TPU v7x, 32 devices: a whole 2x2x4 slice. The times are simulated.
32 devices in a mesh: leaf: 4 (over x, core), dof: 4 (over z), blk: 2 (over y).
Axes of the slice: x: 2, y: 2, z: 4, core: 2. Of those that a mesh axis runs over, the one named last changes fastest.
Arguments:
- modes: bfloat16 [4, 128, 128, 16, 128], P('leaf', 'blk', 'dof'), may hold values from -1.5 to 1.5
- stiffness: float32 [4, 128, 16, 128], P('leaf', 'dof'), may hold values from 0.25 to 2
- density: float32 [4, 128, 16, 128], P('leaf', 'dof'), may hold values from 0.5 to 4
- eigen_blocks: bfloat16 [4, 128, 128], P('leaf', None, 'blk'), may hold values from -0.5 to 0.5
- parent: int32 [4], replicated, may hold values from 0 to 1
Outputs:
- node_stiffness: float32 [2, 128, 128], P(None, 'blk')
- root_stiffness: float32 [128, 128], P('blk')
- leaf_vectors: bfloat16 [4, 128, 128, 16, 128], P('leaf', 'blk', 'dof')
All inputs are finite; a program needn't handle non-finite values.
Results may differ from a plain program's by a relative error of at most 0.0035.
Values may be sent and summed in bfloat16 or wider, within the bound.
No kernel may reach another device: no remote copies, remote signals or barrier semaphores. Data moves between devices by JAX's collectives and lax.ppermute only.
A program may use at most 128 MiB of HBM per device.

v0:
```python
import jax
import jax.numpy as jnp
from jax import lax
from jax.sharding import PartitionSpec as P


def extended(x, sides, width):
    for axis, dim in sides:
        size, length = (lax.axis_size(axis), x.shape[dim])
        up = [(i, (i + 1) % size) for i in range(size - 1)]
        down = [(j, i) for i, j in up]
        last = lax.slice_in_dim(x, length - width, length, axis=dim)
        leading = lax.slice_in_dim(x, 0, width, axis=dim)
        before = lax.ppermute(last, axis, up)
        after = lax.ppermute(leading, axis, down)
        x = jnp.concatenate([before, x, after], axis=dim)
    return x


def neighbours(padded):
    inner = padded[:, 1:-1]
    sides = jnp.pad(inner, ((0, 0), (0, 0), (1, 1), (1, 1)))
    total = padded[:, 2:] + padded[:, :-2]
    total = total + sides[:, :, 2:, 1:-1] + sides[:, :, :-2, 1:-1]
    total = total + sides[:, :, 1:-1, 2:] + sides[:, :, 1:-1, :-2]
    return total


def body(modes, stiffness, density, eigen_blocks, parent):
    own = modes[0]
    rows, cells_x, cells_y, cells_z = own.shape
    cells = cells_x * cells_y * cells_z
    total_modes = rows * lax.axis_size("blk")
    padded = extended(own, (("dof", 1),), 1).astype(jnp.float32)
    field = padded[:, 1:-1]
    stiff = ((6.0 + stiffness[0]) * field - neighbours(padded)).astype(jnp.bfloat16)
    stiff_flat = stiff.reshape(rows, cells)
    own_flat = own.reshape(rows, cells)
    mass_flat = density[0].reshape(cells)
    weighed_own = (mass_flat[None, :] * own_flat.astype(jnp.float32)).astype(jnp.bfloat16)
    diag_own = jnp.einsum("rc,rc->r", weighed_own, own_flat, preferred_element_type=jnp.float32)
    diagonal = lax.all_gather(diag_own, "blk", axis=0, tiled=True)
    blocks = eigen_blocks[0]
    eig_rows = blocks.shape[1]
    piece = lax.all_gather(own_flat, "blk", axis=0, tiled=True)
    columns = lax.dot_general(
        stiff_flat, piece, (((1,), (1,)), ((), ())), preferred_element_type=jnp.float32
    )
    reduced = columns
    vectors = lax.dot_general(
        blocks, piece, (((0,), (0,)), ((), ())), preferred_element_type=jnp.float32
    )
    reduced, vectors = (reduced, vectors)
    vector_flat = vectors.astype(jnp.bfloat16)
    leaf_vectors = vector_flat.reshape(1, eig_rows, cells_x, cells_y, cells_z)
    leaves = lax.axis_size("leaf")
    nodes = leaves // 2
    node_ids = jnp.arange(nodes, dtype=jnp.int32)
    halves = lax.axis_size("dof")
    gathered_rows, gathered_diag = (
        lax.all_gather(reduced[None], ("leaf", "dof"), axis=0, tiled=True),
        lax.all_gather(diagonal[None], ("leaf", "dof"), axis=0, tiled=True),
    )
    leaf_rows = jnp.sum(gathered_rows.reshape(leaves, halves, rows, total_modes), axis=1)
    leaf_diag = jnp.sum(gathered_diag.reshape(leaves, halves, total_modes), axis=1)
    onehot = (parent[:, None] == node_ids[None, :]).astype(jnp.float32)
    node_stiffness = jnp.einsum("lp,lij->pij", onehot, leaf_rows, precision=lax.Precision.HIGHEST)
    node_mass = jnp.einsum("lp,li->pi", onehot, leaf_diag, precision=lax.Precision.HIGHEST)
    scale = 1.0 / jnp.sqrt(node_mass)
    scale_own = lax.dynamic_slice_in_dim(scale, lax.axis_index("blk") * rows, rows, 1)
    root_stiffness = jnp.sum(scale_own[:, :, None] * node_stiffness * scale[:, None, :], axis=0)
    return (node_stiffness, root_stiffness, leaf_vectors)


def solution(mesh):
    in_specs = (
        P("leaf", "blk", "dof", None, None),
        P("leaf", "dof", None, None),
        P("leaf", "dof", None, None),
        P("leaf", None, "blk"),
        P(),
    )
    out_specs = (P(None, "blk", None), P("blk", None), P("leaf", "blk", "dof", None, None))
    return jax.shard_map(body, mesh=mesh, in_specs=in_specs, out_specs=out_specs, check_vma=False)
```

profile of v0, /device:TPU:0, one launch (start us, length us, event | category | flops | bytes accessed | tf_op | source)
XLA Modules:
  0.0 299.1 jit_solution(8625137546150879917)
XLA Ops:
  7.2 0.0 copy-start
  7.2 0.0 copy-start.5
  7.2 0.0 copy-start.2
  7.2 0.0 copy-start.4
  7.2 0.0 all-gather.5.cloned.1.call-start
  7.3 10.4 %reshape_squeeze.3 = bf16[64,65536]{1,0:T(8,128)(2,1)} reshape(bf16[1,64,32,16,128]{4,3,2,1,0:T(8,128)(2,1)} %param.5) | data formatting | bytes 16777216 | tf_op jit(solution)/shard_map/reshape;squeeze | solution.py:38
  17.7 0.0 all-gather.5.cloned.1.call-update
  17.7 1.1 fusion.18
  18.8 4.9 %collective-permute-start = (bf16[64,1,16,128]{3,2,1,0:T(8,128)(2,1)S(1)}, bf16[64,1,16,128]{3,2,1,0:T(8,128)(2,1)S(1)}, u32[]{:S(2)}, u32[]{:S(2)}) collective-permute-start(bf16[64,1,16,128]{3,2,1,0:T(8,128)(2,1)S(1)} %get-tuple-element.9), channel_id=1, source_target_pairs={{0,2},{2,4},{4,6},{1,3},{3,5},{5,7},{8,10},{10,12},{12,14},{9,11},... | collective-permute-start | bytes 786440 | tf_op jit(solution)/shard_map/ppermute | solution.py:14
  23.8 1.3 collective-permute-start.1
  25.1 0.6 dynamic-slice
  26.3 8.1 %fusion.1 = f32[64]{0:T(128)S(1)} fusion(bf16[64,65536]{1,0:T(8,128)(2,1)} %reshape_squeeze.3, f32[65536]{0:T(1024)S(1)} %bitcast.35), kind=kLoop, calls=%fused_computation.8 | loop fusion | flops 25165760 | bytes 8651008 | tf_op jit(solution)/shard_map/rc,rc->r/dot_general | solution.py:41
  34.4 0.2 dynamic-update-slice
  34.7 4.9 %all-reduce.1 = f32[128]{0:T(128)S(1)} all-reduce(f32[128]{0:T(128)S(1)} %dynamic-update-slice), channel_id=1, replica_groups=mesh['leaf'=4,'dof'=4,'blk'=2] {'blk'}, use_global_device_ids=true, to_apply=%add.1 | all-reduce | flops 128 | bytes 1024
  39.6 31.5 %all-gather.2 = f32[16,1,128]{2,1,0:T(1,128)S(1)} all-gather(f32[1,1,128]{2,1,0:T(1,128)S(1)} %bitcast.37), channel_id=3, replica_groups=mesh['leaf'=4,'dof'=4,'blk'=2] {'leaf','dof'}, dimensions={0}, use_global_device_ids=true | all-gather | bytes 8704 | tf_op jit(solution)/shard_map/all_gather | solution.py:62
  71.2 0.1 convolution_rsqrt_fusion
  71.3 0.1 constant_dynamic-slice_fusion
  71.4 0.1 copy.11
  71.5 0.0 copy-done.3
  71.5 0.0 collective-permute-done
  71.5 0.0 collective-permute-done.1
  71.5 4.7 %maximum_convert_fusion = f32[64,34,16,128]{3,2,1,0:T(8,128)S(1)} fusion(bf16[64,1,16,128]{3,2,1,0:T(8,128)(2,1)S(1)} %collective-permute-done.1, bf16[64,32,16,128]{3,2,1,0:T(8,128)(2,1)} %bitcast.32, bf16[64,1,16,128]{3,2,1,0:T(8,128)(2,1)S(1)} %collective-permute-done), kind=kLoop, calls=%fused_computation.16 | loop fusion | flops 13369344 | bytes 26738688 | tf_op jit(solution)/shard_map/convert_element_type | solution.py:34
  76.2 6.1 %copy-done.1 = f32[64,34,16,128]{3,2,1,0:T(8,128)} copy-done((f32[64,34,16,128]{3,2,1,0:T(8,128)}, f32[64,34,16,128]{3,2,1,0:T(8,128)S(1)}, u32[]{:S(2)}) %copy-start.1) | copy-done | bytes 17825816
  82.3 6.2 %slice.39 = f32[64,32,16,128]{3,2,1,0:T(8,128)} slice(f32[64,34,16,128]{3,2,1,0:T(8,128)S(1)} %maximum_convert_fusion), slice={[0:64], [1:33], [0:16], [0:128]} | slice | bytes 33554432 | tf_op jit(solution)/shard_map/slice | solution.py:35
  88.5 40.2 %fusion.7 = bf16[64,32,16,128]{3,2,1,0:T(8,128)(2,1)} fusion(f32[64,32,16,128]{3,2,1,0:T(8,128)} %slice.39, f32[64,34,16,128]{3,2,1,0:T(8,128)} %copy-done.1, f32[32,16,128]{2,1,0:T(8,128)S(1)} %add_bitcast_fusion), kind=kLoop, calls=%fused_computation.14 | loop fusion | flops 33554432 | bytes 58982400 | tf_op jit(solution)/shard_map/convert_element_type | solution.py:36
  128.7 90.8 %all-gather.5.cloned.1.call-done = bf16[128,65536]{1,0:T(8,128)(2,1)} async-done(((bf16[64,65536]{1,0:T(8,128)(2,1)}), bf16[128,65536]{1,0:T(8,128)(2,1)}) %all-gather.5.cloned.1.call-update) | async-done | bytes 16777232 | tf_op jit(solution)/shard_map/all_gather | solution.py:45
  219.5 13.4 %fusion.8 = f32[64,128]{1,0:T(8,128)S(1)} fusion(bf16[128,65536]{1,0:T(8,128)(2,1)} %all-gather.5.cloned.1.call-done, bf16[8,8,512,128]{3,2,1,0:T(8,128)(2,1)} %bitcast.30), kind=kOutput, calls=%fused_computation.17 | convolution fusion | flops 1073741824 | bytes 25198592 | tf_op jit(solution)/shard_map/dot_general | solution.py:46
  232.9 37.2 %all-gather = f32[1024,128]{1,0:T(8,128)S(1)} all-gather(f32[64,128]{1,0:T(8,128)S(1)} %fusion.8), channel_id=2, replica_groups=mesh['leaf'=4,'dof'=4,'blk'=2] {'leaf','dof'}, dimensions={0}, use_global_device_ids=true | all-gather | bytes 557056 | tf_op jit(solution)/shard_map/all_gather | solution.py:61
  270.2 1.0 multiply_reduce_fusion
  271.2 0.6 copy.12
  271.8 11.3 %fusion.11 = bf16[8,8,512,128]{3,1,2,0:T(8,128)(2,1)} fusion(bf16[128,65536]{1,0:T(8,128)(2,1)} %all-gather.5.cloned.1.call-done, bf16[1,128,64]{1,2,0:T(8,128)(2,1)S(1)} %copy-done), kind=kOutput, calls=%fused_computation.20 | convolution fusion | flops 1077936128 | bytes 25182208 | tf_op jit(solution)/shard_map/dot_general | solution.py:50
  283.2 9.1 %copy.19 = bf16[8,8,512,128]{3,2,1,0:T(8,128)(2,1)} copy(bf16[8,8,512,128]{3,1,2,0:T(8,128)(2,1)} %fusion.11) | data formatting | bytes 16777216
  (10 shorter events, 0.1 us)
Async XLA Ops:
  7.2 264.7 %copy-start = (bf16[1,128,64]{1,2,0:T(8,128)(2,1)S(1)}, bf16[1,128,64]{1,2,0:T(8,128)(2,1)}, u32[]{:S(2)}) copy-start(bf16[1,128,64]{1,2,0:T(8,128)(2,1)} %param.8) | copy-start | bytes 49156
  7.2 17.9 %copy-start.5 = (u32[32]{0:T(128)S(1)}, u32[32]{0:T(128)}, u32[]{:S(2)}) copy-start(u32[32]{0:T(128)} %constant.24) | copy-start | bytes 388
  7.2 19.1 %copy-start.2 = (f32[1,32,16,128]{3,2,1,0:T(8,128)S(1)}, f32[1,32,16,128]{3,2,1,0:T(8,128)}, u32[]{:S(2)}) copy-start(f32[1,32,16,128]{3,2,1,0:T(8,128)} %param.7) | copy-start | bytes 786436
  7.2 64.0 %copy-start.4 = (s32[4]{0:T(128)S(1)}, s32[4]{0:T(128)}, u32[]{:S(2)}) copy-start(s32[4]{0:T(128)} %param.9) | copy-start | bytes 52
  7.2 64.2 %copy-start.3 = (f32[1,32,16,128]{3,2,1,0:T(8,128)S(1)}, f32[1,32,16,128]{3,2,1,0:T(8,128)}, u32[]{:S(2)}) copy-start(f32[1,32,16,128]{3,2,1,0:T(8,128)} %param.6) | copy-start | bytes 786436
  7.2 212.3 %all-gather.5.cloned.1.call-start = ((), (), s32[]{:S(2)}) async-start(), calls=%async_computation | async-start | bytes 25165824 | tf_op jit(solution)/shard_map/all_gather | solution.py:45
  18.8 52.7 %collective-permute-start = (bf16[64,1,16,128]{3,2,1,0:T(8,128)(2,1)S(1)}, bf16[64,1,16,128]{3,2,1,0:T(8,128)(2,1)S(1)}, u32[]{:S(2)}, u32[]{:S(2)}) collective-permute-start(bf16[64,1,16,128]{3,2,1,0:T(8,128)(2,1)S(1)} %get-tuple-element.9), channel_id=1, source_target_pairs={{0,2},{2,4},{4,6},{1,3},{3,5},{5,7},{8,10},{10,12},{12,14},{9,11},... | collective-permute-start | bytes 786440 | tf_op jit(solution)/shard_map/ppermute | solution.py:14
  23.8 47.7 %collective-permute-start.1 = (bf16[64,1,16,128]{3,2,1,0:T(8,128)(2,1)S(1)}, bf16[64,1,16,128]{3,2,1,0:T(8,128)(2,1)S(1)}, u32[]{:S(2)}, u32[]{:S(2)}) collective-permute-start(bf16[64,1,16,128]{3,2,1,0:T(8,128)(2,1)S(1)} %get-tuple-element.10), channel_id=1, source_target_pairs={{2,0},{4,2},{6,4},{3,1},{5,3},{7,5},{10,8},{12,10},{14,12},{11,9},... | collective-permute-start | bytes 786440 | tf_op jit(solution)/shard_map/ppermute | solution.py:15
  76.2 6.1 %copy-start.1 = (f32[64,34,16,128]{3,2,1,0:T(8,128)}, f32[64,34,16,128]{3,2,1,0:T(8,128)S(1)}, u32[]{:S(2)}) copy-start(f32[64,34,16,128]{3,2,1,0:T(8,128)S(1)} %maximum_convert_fusion) | copy-start | bytes 53477380
Sparse Core Ops, SparseCore 0:
  17.9 201.5 all-gather.4
where the time goes:
time: 300 us; the launch traced here: 299 us
  waiting for transfers between devices  90.8 us (30%)
  blocking collectives  73.7 us (25%)
  other arithmetic  53 us (18%)
  local copies, waits for them, and re-layouts  34.6 us (12%)
  matrix products  25.9 us (9%)
  between operations  14.8 us (5%)
  starting transfers between devices  6.27 us (2%)
    all_gather x1, waiting for transfers between devices, body(): piece = lax.all_gather(own_flat, 'blk', axis=0, tiled=True)  90.8 us
    convert_element_type x1, other arithmetic, body(): ((6.0 + stiffness[0]) * field - neighbours(padded)).astype(jnp.bfloat16)  40.2 us
    all_gather x1, blocking collectives, body(): lax.all_gather(reduced[None], ('leaf', 'dof'), axis=0, tiled=True)  37.2 us
    all_gather x1, blocking collectives, body(): lax.all_gather(diagonal[None], ('leaf', 'dof'), axis=0, tiled=True)  31.5 us
    unnamed x17, local copies, waits for them, and re-layouts  16.7 us
    dot_general x1, matrix products, body(): lax.dot_general(stiff_flat, piece, (((1,), (1,)), ((), ())), preferred_el...  13.4 us
    dot_general x1, matrix products, body(): lax.dot_general(blocks, piece, (((0,), (0,)), ((), ())), preferred_elemen...  11.3 us
    another operation x1, local copies, waits for them, and re-layouts, body(): own_flat = own.reshape(rows, cells)  10.4 us
  transfers between devices with their start and end apart: 3, of which 1 were waited for; matrix products, arithmetic and copies ran while one was open for 21% of the time, Pallas kernels for 0%

commit v1 on v0

--- a/solution.py
+++ b/solution.py
@@ -1,7 +1,328 @@
+import functools
 import jax
 import jax.numpy as jnp
 from jax import lax
+from jax.experimental import pallas as pl
+from jax.experimental.pallas import tpu as pltpu
 from jax.sharding import PartitionSpec as P
+
+SUB = 8
+VMEM_BYTES = 32 * 1024 * 1024
+
+
+def params(steps):
+    return pltpu.CompilerParams(
+        dimension_semantics=("arbitrary",), vmem_limit_bytes=VMEM_BYTES
+    )
+
+
+def split_rows(x):
+    wide = x.astype(jnp.float32)
+    rows, cells_y, cells_z = wide.shape
+    parts = [
+        wide[:, i * SUB : (i + 1) * SUB].reshape(rows * SUB, cells_z).astype(jnp.bfloat16)
+        for i in range(cells_y // SUB)
+    ]
+    return jnp.concatenate(parts, axis=1)
+
+
+def accumulate(total, left, right):
+    total[...] += lax.dot_general(
+        left, right, (((1,), (1,)), ((), ())), preferred_element_type=jnp.float32
+    )
+
+
+def same_row_sum(total):
+    tall, wide = total.shape
+    row = lax.broadcasted_iota(jnp.int32, (tall, wide), 0) % SUB
+    col = lax.broadcasted_iota(jnp.int32, (tall, wide), 1) % SUB
+    kept = jnp.where(row == col, total, 0.0).reshape(tall // SUB, SUB, wide)
+    folded = jnp.sum(kept, axis=1)
+    group = lax.broadcasted_iota(jnp.int32, (wide, wide // SUB), 0) // SUB
+    pick = (group == lax.broadcasted_iota(jnp.int32, (wide, wide // SUB), 1)).astype(jnp.float32)
+    return jnp.dot(folded, pick, precision=lax.Precision.HIGHEST, preferred_element_type=jnp.float32)
+
+
+def stiff_kernel(own, prev, after, low, high, coefs, masses, stiff, gram, mass, total, flat, acc):
+    layer, last = pl.program_id(0), pl.num_programs(0) - 1
+    rows, _, cells_y, cells_z = own.shape
+
+    @pl.when(layer == 0)
+    def _():
+        total[...] = jnp.zeros_like(total)
+        acc[...] = jnp.zeros_like(acc)
+
+    y = lax.broadcasted_iota(jnp.int32, (SUB, cells_y, cells_z), 1)
+    z = lax.broadcasted_iota(jnp.int32, (SUB, cells_y, cells_z), 2)
+    diagonal = 6.0 + coefs[0]
+    density = masses[0]
+
+    def group(g, carry):
+        modes = pl.ds(g * SUB, SUB)
+        field = own[modes, 0].astype(jnp.float32)
+        before = jnp.where(layer == 0, low[modes, 0], prev[modes, 0]).astype(jnp.float32)
+        behind = jnp.where(layer == last, high[modes, 0], after[modes, 0]).astype(jnp.float32)
+        around = before + behind
+        around += jnp.where(y == 0, 0.0, pltpu.roll(field, 1, 1))
+        around += jnp.where(y == cells_y - 1, 0.0, pltpu.roll(field, cells_y - 1, 1))
+        around += jnp.where(z == 0, 0.0, pltpu.roll(field, 1, 2))
+        around += jnp.where(z == cells_z - 1, 0.0, pltpu.roll(field, cells_z - 1, 2))
+        force = diagonal[None] * field - around
+        weighed = (density[None] * field).astype(jnp.bfloat16).astype(jnp.float32) * field
+        out = pl.ds(g * SUB * SUB, SUB * SUB)
+        part = None
+        for i in range(cells_y // SUB):
+            rows_y, lanes = slice(i * SUB, (i + 1) * SUB), slice(i * cells_z, (i + 1) * cells_z)
+            stiff[0, out, lanes] = force[:, rows_y].reshape(SUB * SUB, cells_z).astype(jnp.bfloat16)
+            flat[out, lanes] = field[:, rows_y].reshape(SUB * SUB, cells_z).astype(jnp.bfloat16)
+            part = weighed[:, rows_y] if part is None else part + weighed[:, rows_y]
+        acc[modes] += part
+        return carry
+
+    lax.fori_loop(0, rows // SUB, group, 0)
+    accumulate(total, stiff[0], flat[...])
+
+    @pl.when(layer == last)
+    def _():
+        gram[...] = same_row_sum(total[...])
+        mass[...] = jnp.broadcast_to(
+            jnp.sum(jnp.sum(acc[...], axis=1), axis=1, keepdims=True), mass.shape
+        )
+
+
+def stiff_terms(own, low, high, coefs, masses):
+    rows, layers, cells_y, cells_z = own.shape
+    tall, wide = rows * SUB, cells_y // SUB * cells_z
+    block = (rows, 1, cells_y, cells_z)
+    cells = (1, cells_y, cells_z)
+    return pl.pallas_call(
+        stiff_kernel,
+        grid=(layers,),
+        in_specs=[
+            pl.BlockSpec(block, lambda g: (0, g, 0, 0)),
+            pl.BlockSpec(block, lambda g: (0, jnp.maximum(g - 1, 0), 0, 0)),
+            pl.BlockSpec(block, lambda g: (0, jnp.minimum(g + 1, layers - 1), 0, 0)),
+            pl.BlockSpec(block, lambda g: (0, 0, 0, 0)),
+            pl.BlockSpec(block, lambda g: (0, 0, 0, 0)),
+            pl.BlockSpec(cells, lambda g: (g, 0, 0)),
+            pl.BlockSpec(cells, lambda g: (g, 0, 0)),
+        ],
+        out_specs=[
+            pl.BlockSpec((1, tall, wide), lambda g: (g, 0, 0)),
+            pl.BlockSpec((rows, rows), lambda g: (0, 0)),
+            pl.BlockSpec((rows, rows), lambda g: (0, 0)),
+        ],
+        out_shape=[
+            jax.ShapeDtypeStruct((layers, tall, wide), jnp.bfloat16),
+            jax.ShapeDtypeStruct((rows, rows), jnp.float32),
+            jax.ShapeDtypeStruct((rows, rows), jnp.float32),
+        ],
+        scratch_shapes=[
+            pltpu.VMEM((tall, tall), jnp.float32),
+            pltpu.VMEM((tall, wide), jnp.bfloat16),
+            pltpu.VMEM((rows, SUB, cells_z), jnp.float32),
+        ],
+        compiler_params=params(layers),
+        cost_estimate=pl.CostEstimate(
+            flops=2 * layers * tall * tall * wide, bytes_accessed=8 * own.size, transcendentals=0
+        ),
+        name="stiff_terms",
+    )(own, own, own, low, high, coefs, masses)
+
+
+def cross_kernel(at, stiff, other, gram, total):
+    step = pl.program_id(0)
+
+    @pl.when(step == 0)
+    def _():
+        total[...] = jnp.zeros_like(total)
+
+    accumulate(total, stiff[0], split_rows(other[:, 0]))
+
+    @pl.when(step == pl.num_programs(0) - 1)
+    def _():
+        gram[...] = same_row_sum(total[...])
+
+
+def cross_terms(stiff, other, at):
+    rows, layers, cells_y, cells_z = other.shape
+    _, tall, wide = stiff.shape
+    return pl.pallas_call(
+        cross_kernel,
+        grid_spec=pltpu.PrefetchScalarGridSpec(
+            num_scalar_prefetch=1,
+            grid=(layers,),
+            in_specs=[
+                pl.BlockSpec((1, tall, wide), lambda g, at: (at[0] + g, 0, 0)),
+                pl.BlockSpec((rows, 1, cells_y, cells_z), lambda g, at: (0, g, 0, 0)),
+            ],
+            out_specs=pl.BlockSpec((rows, rows), lambda g, at: (0, 0)),
+            scratch_shapes=[pltpu.VMEM((tall, tall), jnp.float32)],
+        ),
+        out_shape=jax.ShapeDtypeStruct((rows, rows), jnp.float32),
+        compiler_params=params(layers),
+        cost_estimate=pl.CostEstimate(
+            flops=2 * layers * tall * tall * wide, bytes_accessed=4 * other.size, transcendentals=0
+        ),
+        name="cross_terms",
+    )(at.reshape(1), stiff, other)
+
+
+def vector_kernel(at, spread, own, other, *rest):
+    out = rest[-1]
+    rows, _, cells_y, cells_z = own.shape
+    both = jnp.concatenate([split_rows(own[:, 0]), split_rows(other[:, 0])], axis=0)
+    made = jnp.dot(spread[...], both, preferred_element_type=jnp.float32)
+    eigs = out.shape[0]
+    parts = [
+        made[:, i * cells_z : (i + 1) * cells_z].reshape(eigs, SUB, cells_z)
+        for i in range(cells_y // SUB)
+    ]
+    out[:, 0] = jnp.concatenate(parts, axis=1).astype(out.dtype)
+
+
+def expand(spread, own, other, at, held):
+    rows, layers, cells_y, cells_z = other.shape
+    eigs = spread.shape[0] // SUB
+    inputs = [at.reshape(1), spread, own, other]
+    specs = [
+        pl.BlockSpec(spread.shape, lambda g, at: (0, 0)),
+        pl.BlockSpec((rows, 1, cells_y, cells_z), lambda g, at: (0, at[0] + g, 0, 0)),
+        pl.BlockSpec((rows, 1, cells_y, cells_z), lambda g, at: (0, g, 0, 0)),
+    ]
+    aliases = {}
+    if held is not None:
+        aliases = {len(inputs): 0}
+        inputs.append(held)
+        specs.append(pl.BlockSpec(memory_space=pl.ANY))
+    return pl.pallas_call(
+        vector_kernel,
+        grid_spec=pltpu.PrefetchScalarGridSpec(
+            num_scalar_prefetch=1,
+            grid=(layers,),
+            in_specs=specs,
+            out_specs=pl.BlockSpec((eigs, 1, cells_y, cells_z), lambda g, at: (0, at[0] + g, 0, 0)),
+        ),
+        out_shape=jax.ShapeDtypeStruct((eigs,) + own.shape[1:], jnp.bfloat16),
+        input_output_aliases=aliases,
+        compiler_params=params(layers),
+        cost_estimate=pl.CostEstimate(
+            flops=2 * layers * spread.shape[0] * spread.shape[1] * cells_y // SUB * cells_z,
+            bytes_accessed=6 * other.size,
+            transcendentals=0,
+        ),
+        name="expand",
+    )(*inputs)
+
+
+def tied(x, y):
+    return lax.optimization_barrier((x, y))[0]
+
+
+def swap(x):
+    return lax.ppermute(x, "blk", [(0, 1), (1, 0)])
+
+
+def paired_sum(x, axis):
+    size, step = lax.axis_size(axis), 1
+    while step < size:
+        x = x + lax.ppermute(x, axis, [(i, i ^ step) for i in range(size)])
+        step *= 2
+    return x
+
+
+def line_sum(x, axis):
+    x = x + lax.ppermute(x, axis, [(0, 1), (1, 0), (2, 3), (3, 2)])
+    x = x + lax.ppermute(x, axis, [(1, 2), (2, 1)])
+    outer = lax.ppermute(x, axis, [(1, 0), (2, 3)])
+    place = lax.axis_index(axis)
+    return jnp.where((place == 0) | (place == 3), outer, x)
+
+
+def halved(modes, stiffness, density, eigen_blocks, parent):
+    own = modes[0]
+    rows, layers = own.shape[:2]
+    half = layers // 2
+    blk, dof, leaf = lax.axis_index("blk"), lax.axis_index("dof"), lax.axis_index("leaf")
+    upper = (blk + dof) % 2
+
+    def start(mine, offset, count, top):
+        forward = top == 1 if mine else top == 0
+        return jnp.where(forward, half + offset, half - offset - count).astype(jnp.int32)
+
+    def send(mine, offset, count, after=None):
+        source = own if after is None else tied(own, after)
+        at = start(mine, offset, count, 1 - upper)
+        return swap(lax.dynamic_slice_in_dim(source, at, count, axis=1))
+
+    def place(mine, offset, count):
+        return start(mine, offset, count, upper)
+
+    near, far = half * 3 // 16, half - half * 3 // 16
+    rest = [half * 5 // 16, half * 5 // 16, half * 3 // 16]
+    rest.append(half - 1 - sum(rest))
+    spots = [1, 1 + rest[0], 1 + rest[0] + rest[1], 1 + sum(rest[:3])]
+
+    edge = send(False, 0, 1)
+    first = send(True, 0, near)
+    size = lax.axis_size("dof")
+    low = lax.ppermute(own[:, -1:], "dof", [(i, i + 1) for i in range(size - 1)])
+    high = lax.ppermute(own[:, :1], "dof", [(i + 1, i) for i in range(size - 1)])
+    second = send(True, near, far, edge)
+    stiff, gram, mass = stiff_terms(own, low, high, stiffness[0], density[0])
+
+    blocks = tied(eigen_blocks[0], mass)
+    mine = lax.dynamic_slice_in_dim(blocks, blk * rows, rows, 0)
+    other = lax.dynamic_slice_in_dim(blocks, (1 - blk) * rows, rows, 0)
+    ordered = jnp.concatenate([mine, other], axis=0).T
+    eye = jnp.eye(SUB, dtype=ordered.dtype)
+    spread = (ordered[:, None, :, None] * eye[None, :, None, :]).reshape(
+        ordered.shape[0] * SUB, ordered.shape[1] * SUB
+    )
+
+    third = send(False, spots[0], rest[0], first)
+    inner, outer = place(True, 0, 1), place(False, 0, 1)
+    own_in = lax.dynamic_slice_in_dim(own, inner, 1, axis=1)
+    own_out = lax.dynamic_slice_in_dim(own, outer, 1, axis=1)
+    first_in = lax.dynamic_slice_in_dim(first, inner - place(True, 0, near), 1, axis=1)
+    across = functools.partial(
+        lax.dot_general,
+        dimension_numbers=(((1, 2, 3), (1, 2, 3)), ((), ())),
+        preferred_element_type=jnp.float32,
+    )
+    border = 0.5 * (across(own_out, first_in) - across(own_in, edge))
+    cross = cross_terms(stiff, first, place(True, 0, near))
+    vectors = expand(spread, own, edge, outer, None)
+    vectors = expand(spread, own, first, place(True, 0, near), vectors)
+    cross = cross + border + cross_terms(stiff, second, place(True, near, far))
+
+    fourth = send(False, spots[1], rest[1], cross)
+    theirs = swap(jnp.concatenate([cross, mass], axis=1))
+    vectors = expand(spread, own, second, place(True, near, far), vectors)
+    fifth = send(False, spots[2], rest[2], third)
+    vectors = expand(spread, own, third, place(False, spots[0], rest[0]), vectors)
+    sixth = send(False, spots[3], rest[3], fourth)
+
+    whole = jnp.concatenate([gram, cross + theirs[:, :rows].T, mass, theirs[:, rows:]], axis=1)
+    whole = line_sum(whole, "dof")
+    nodes = lax.axis_size("leaf") // 2
+    belongs = (parent[leaf] == jnp.arange(nodes, dtype=jnp.int32)).astype(jnp.float32)
+    whole = paired_sum(belongs[:, None, None] * whole[None], "leaf")
+    gram, cross = whole[:, :, :rows], whole[:, :, rows : 2 * rows]
+    scale_own = 1.0 / jnp.sqrt(whole[:, :, 2 * rows])
+    scale_other = 1.0 / jnp.sqrt(whole[:, :, 3 * rows])
+
+    def in_order(a, b):
+        return jnp.where(blk == 0, jnp.concatenate([a, b], -1), jnp.concatenate([b, a], -1))
+
+    node_stiffness = in_order(gram, cross)
+    scale = in_order(scale_own, scale_other)
+    root_stiffness = jnp.sum(scale_own[:, :, None] * node_stiffness * scale[:, None, :], axis=0)
+
+    vectors = expand(spread, own, fourth, place(False, spots[1], rest[1]), vectors)
+    vectors = expand(spread, own, fifth, place(False, spots[2], rest[2]), vectors)
+    vectors = expand(spread, own, sixth, place(False, spots[3], rest[3]), vectors)
+    return (node_stiffness, root_stiffness, vectors[None])
 
 
 def extended(x, sides, width):
@@ -26,7 +347,7 @@
     return total
 
 
-def body(modes, stiffness, density, eigen_blocks, parent):
+def gathered(modes, stiffness, density, eigen_blocks, parent):
     own = modes[0]
     rows, cells_x, cells_y, cells_z = own.shape
     cells = cells_x * cells_y * cells_z
@@ -73,6 +394,9 @@
 
 
 def solution(mesh):
+    body = gathered
+    if mesh.shape["blk"] == 2 and mesh.shape["dof"] == 4:
+        body = halved
     in_specs = (
         P("leaf", "blk", "dof", None, None),
         P("leaf", "dof", None, None),

time: 300 us -> 230 us (0.77)
  Pallas kernels: 0 us -> 76.7 us
  blocking collectives: 73.7 us -> 0 us
  other arithmetic: 53 us -> 11.1 us
  waiting for transfers between devices: 90.8 us -> 65 us
  matrix products: 25.9 us -> 0.44 us
  starting transfers between devices: 6.27 us -> 22.7 us
  local copies, waits for them, and re-layouts: 34.6 us -> 50.7 us
  between operations: 14.8 us -> 0.95 us
    all_gather x1 -> x0, waiting for transfers between devices: 90.8 us -> none  [body(): piece = lax.all_gather(own_flat, 'blk', axis=0, tiled=True)]
    pallas_call x0 -> x10, Pallas kernels: none -> 76.7 us  [the longest x1 41.5 us: stiff_terms(): pl.pallas_call(stiff_kernel, grid=(layers,), in_specs=[pl.BlockSpec(block...]
    all_gather x2 -> x0, blocking collectives: 68.8 us -> none  [the longest x1 37.2 us: body(): lax.all_gather(reduced[None], ('leaf', 'dof'), axis=0, tiled=True)]
    ppermute x2 -> x15, waiting for transfers between devices: 0.01 us -> 65 us  [the longest x8 57.7 us: swap(): return lax.ppermute(x, 'blk', [(0, 1), (1, 0)])]
    convert_element_type x2, other arithmetic: 44.9 us -> 1.76 us  [the longest x1 1.17 us: halved(): (parent[leaf] == jnp.arange(nodes, dtype=jnp.int32)).astype(jnp.float32)]
    dot_general x4 -> x2, matrix products: 25.9 us -> 0.44 us  [halved(): border = 0.5 * (across(own_out, first_in) - across(own_in, edge))]
    mul x0 -> x1, local copies, waits for them, and re-layouts: none -> 24.5 us  [halved(): ordered[:, None, :, None] * eye[None, :, None, :]]
    ppermute x2 -> x15, starting transfers between devices: 6.24 us -> 22.7 us  [the longest x8 12 us: swap(): return lax.ppermute(x, 'blk', [(0, 1), (1, 0)])]
  transfers between devices with their start and end apart: 3 -> 15, of which waited for: 1 -> 7; matrix products, arithmetic and copies ran while one was open for 21% -> 20% of each run, Pallas kernels for 0% -> 31%
where the time goes in v1:
time: 230 us; the launch traced here: 228 us
  Pallas kernels  76.7 us (33%)
  waiting for transfers between devices  65 us (28%)
  local copies, waits for them, and re-layouts  50.7 us (22%)
  starting transfers between devices  22.7 us (10%)
  other arithmetic  11.1 us (5%)
    ppermute x8, waiting for transfers between devices, swap(): return lax.ppermute(x, 'blk', [(0, 1), (1, 0)])  57.7 us
    pallas_call x1, Pallas kernels, stiff_terms(): pl.pallas_call(stiff_kernel, grid=(layers,), in_specs=[pl.BlockSpec(block...  41.5 us
    pallas_call x7, Pallas kernels, expand(): pl.pallas_call(vector_kernel, grid_spec=pltpu.PrefetchScalarGridSpec(num_...  26.4 us
    mul x1, local copies, waits for them, and re-layouts, halved(): ordered[:, None, :, None] * eye[None, :, None, :]  24.5 us
    ppermute x8, starting transfers between devices, swap(): return lax.ppermute(x, 'blk', [(0, 1), (1, 0)])  12 us
    dynamic_slice x6, local copies, waits for them, and re-layouts, send(): return swap(lax.dynamic_slice_in_dim(source, at, count, axis=1))  9.44 us
    unnamed x28, local copies, waits for them, and re-layouts  9.4 us
    pallas_call x2, Pallas kernels, cross_terms(): pl.pallas_call(cross_kernel, grid_spec=pltpu.PrefetchScalarGridSpec(num_s...  8.78 us
  transfers between devices with their start and end apart: 15, of which 7 were waited for; matrix products, arithmetic and copies ran while one was open for 20% of the time, Pallas kernels for 31%

profile of v1, /device:TPU:0, one launch (start us, length us, event | category | flops | bytes accessed | tf_op | source)
XLA Modules:
  0.0 227.6 jit_solution(7048136909734078367)
XLA Ops:
  0.7 2.1 constant_dynamic-slice_fusion.8
  2.8 3.0 %collective-permute-start.3 = (bf16[64,1,16,128]{3,2,1,0:T(8,128)(2,1)S(1)}, bf16[64,1,16,128]{3,2,1,0:T(8,128)(2,1)S(1)}, u32[]{:S(2)}, u32[]{:S(2)}) collective-permute-start(bf16[64,1,16,128]{3,2,1,0:T(8,128)(2,1)S(1)} %get-tuple-element.26), channel_id=1, source_target_pairs={{0,1},{1,0},{2,3},{3,2},{4,5},{5,4},{6,7},{7,6},{8,9},{9,8},{10,11... | collective-permute-start | bytes 786440 | tf_op jit(solution)/shard_map/ppermute | solution.py:223
  5.7 6.3 %collective-permute-done.3.other = bf16[64,1,16,128]{3,2,1,0:T(8,128)(2,1)S(1)} collective-permute-done((bf16[64,1,16,128]{3,2,1,0:T(8,128)(2,1)S(1)}, bf16[64,1,16,128]{3,2,1,0:T(8,128)(2,1)S(1)}, u32[]{:S(2)}, u32[]{:S(2)}) %collective-permute-start.3) | collective-permute-done | bytes 262176 | tf_op jit(solution)/shard_map/ppermute | solution.py:223
  12.7 4.3 %constant_dynamic-slice_fusion.6 = bf16[64,13,16,128]{3,2,1,0:T(8,128)(2,1)} fusion(bf16[64,32,16,128]{3,2,1,0:T(8,128)(2,1)} %bitcast.40, s32[]{:T(128)S(6)} %select_n.116), kind=kLoop, calls=%fused_computation.36 | loop fusion | bytes 6815748 | tf_op jit(solution)/shard_map/dynamic_slice | solution.py:256
  17.0 1.7 collective-permute-start.4
  18.8 1.9 fusion.12
  20.7 4.2 %collective-permute-start = (bf16[64,1,16,128]{3,2,1,0:T(8,128)(2,1)}, bf16[64,1,16,128]{3,2,1,0:T(8,128)(2,1)}, u32[]{:S(2)}, u32[]{:S(2)}) collective-permute-start(bf16[64,1,16,128]{3,2,1,0:T(8,128)(2,1)} %get-tuple-element.29), channel_id=1, source_target_pairs={{0,2},{2,4},{4,6},{1,3},{3,5},{5,7},{8,10},{10,12},{12,14},{9,11},... | collective-permute-start | bytes 786440 | tf_op jit(solution)/shard_map/ppermute | solution.py:269
  26.1 2.1 dynamic-slice_bitcast_fusion
  31.1 2.5 %collective-permute-done.1.high = bf16[64,1,16,128]{3,2,1,0:T(8,128)(2,1)} collective-permute-done((bf16[64,1,16,128]{3,2,1,0:T(8,128)(2,1)}, bf16[64,1,16,128]{3,2,1,0:T(8,128)(2,1)}, u32[]{:S(2)}, u32[]{:S(2)}) %collective-permute-start.1) | collective-permute-done | bytes 262176 | tf_op jit(solution)/shard_map/ppermute | solution.py:270
  33.7 3.4 %copy-done = bf16[1,64,32,16,128]{4,3,2,1,0:T(8,128)(2,1)S(1)} copy-done((bf16[1,64,32,16,128]{4,3,2,1,0:T(8,128)(2,1)S(1)}, bf16[1,64,32,16,128]{4,3,2,1,0:T(8,128)(2,1)}, u32[]{:S(2)}) %copy-start) | copy-done | bytes 8388632
  38.9 41.5 %stiff_terms.1 = (bf16[32,512,256]{2,1,0:T(8,128)(2,1)S(1)}, f32[64,64]{1,0:T(8,128)S(1)}, f32[64,64]{1,0:T(8,128)S(1)}) custom-call(bf16[64,32,16,128]{3,2,1,0:T(8,128)(2,1)S(1)} %bitcast.43, bf16[64,32,16,128]{3,2,1,0:T(8,128)(2,1)S(1)} %bitcast.44, bf16[64,32,16,128]{3,2,1,0:T(8,128)(2,1)S(1)} %bitcast.45, ...), custom_call_target="tpu_custom_call" | custom-call | flops 4294967296 | bytes 33554432 | tf_op jit(solution)/shard_map/stiff_terms/pallas_call | solution.py:98
  80.9 28.2 %collective-permute-done.2.other = bf16[64,3,16,128]{3,2,1,0:T(8,128)(2,1)} collective-permute-done((bf16[64,3,16,128]{3,2,1,0:T(8,128)(2,1)}, bf16[64,3,16,128]{3,2,1,0:T(8,128)(2,1)}, u32[]{:S(2)}, u32[]{:S(2)}) %collective-permute-start.2) | collective-permute-done | bytes 786464 | tf_op jit(solution)/shard_map/ppermute | solution.py:223
  109.1 3.3 %cross_terms.2 = f32[64,64]{1,0:T(8,128)S(1)} custom-call(s32[1]{0:T(128)} %bitcast.4.at, bf16[32,512,256]{2,1,0:T(8,128)(2,1)S(1)} %get-tuple-element.13.stiff, bf16[64,3,16,128]{3,2,1,0:T(8,128)(2,1)} %collective-permute-done.2.other), custom_call_target="tpu_custom_call" | custom-call | flops 402653184 | bytes 1572864 | tf_op jit(solution)/shard_map/cross_terms/pallas_call | solution.py:150
  113.7 5.5 %cross_terms.3 = f32[64,64]{1,0:T(8,128)S(1)} custom-call(s32[1]{0:T(128)} %bitcast.13.at, bf16[32,512,256]{2,1,0:T(8,128)(2,1)S(1)} %get-tuple-element.13.stiff, bf16[64,13,16,128]{3,2,1,0:T(8,128)(2,1)S(1)} %collective-permute-done.4.other), custom_call_target="tpu_custom_call" | custom-call | flops 1744830464 | bytes 6815744 | tf_op jit(solution)/shard_map/cross_terms/pallas_call | solution.py:150
  120.7 2.6 %constant_dynamic-slice_fusion.1 = bf16[64,5,16,128]{3,2,1,0:T(8,128)(2,1)} fusion(bf16[64,32,16,128]{3,2,1,0:T(8,128)(2,1)} %bitcast.42, s32[]{:T(128)S(6)} %select_n.127), kind=kLoop, calls=%fused_computation.31 | loop fusion | bytes 2621444 | tf_op jit(solution)/shard_map/dynamic_slice | solution.py:256
  127.9 6.6 %broadcast_multiply_fusion = bf16[64,8,128,8]{3,2,1,0:T(8,128)(2,1)} fusion(bf16[8,8]{1,0:T(8,128)(2,1)} %fusion.11, bf16[64,128]{1,0:T(8,128)(2,1)S(1)} %maximum_bitcast_fusion), kind=kLoop, calls=%fused_computation | loop fusion | flops 524288 | bytes 1065088 | tf_op jit(solution)/shard_map/mul | solution.py:279
  134.5 24.5 %mul.75.spread = bf16[512,1024]{1,0:T(8,128)(2,1)S(1)} reshape(bf16[64,8,128,8]{3,2,1,0:T(8,128)(2,1)} %broadcast_multiply_fusion) | data formatting | bytes 2097152 | tf_op jit(solution)/shard_map/mul | solution.py:279
  159.0 3.4 %copy-done.1 = bf16[1,64,32,16,128]{4,3,2,1,0:T(8,128)(2,1)S(1)} copy-done((bf16[1,64,32,16,128]{4,3,2,1,0:T(8,128)(2,1)S(1)}, bf16[1,64,32,16,128]{4,3,2,1,0:T(8,128)(2,1)}, u32[]{:S(2)}) %copy-start.1) | copy-done | bytes 8388632
  164.4 3.8 %expand.8.rest_0_ = bf16[64,32,16,128]{3,2,1,0:T(8,128)(2,1)} custom-call(s32[1]{0:T(128)} %bitcast.4.at, bf16[512,1024]{1,0:T(8,128)(2,1)S(1)} %mul.75.spread, bf16[64,32,16,128]{3,2,1,0:T(8,128)(2,1)S(1)} %bitcast.47, bf16[64,3,16,128]{3,2,1,0:T(8,128)(2,1)} %collective-permute-done.2.other, ...), custom_call_target="tpu_custom_call", output_to_operand_aliasing={{}: (4, {})} | custom-call | flops 805306368 | bytes 2359296 | tf_op jit(solution)/shard_map/expand/pallas_call | solution.py:198
  169.8 1.6 collective-permute-start.11
  171.4 4.7 %collective-permute-done.8 = f32[64,256]{1,0:T(8,128)S(1)} collective-permute-done((f32[64,256]{1,0:T(8,128)S(1)}, f32[64,256]{1,0:T(8,128)S(1)}, u32[]{:S(2)}, u32[]{:S(2)}) %collective-permute-start.8) | collective-permute-done | bytes 65568 | tf_op jit(solution)/shard_map/ppermute | solution.py:237
  176.4 1.6 collective-permute-start.14
  178.1 1.6 collective-permute-start.10
  179.7 8.4 %expand.9.rest_0_ = bf16[64,32,16,128]{3,2,1,0:T(8,128)(2,1)} custom-call(s32[1]{0:T(128)} %bitcast.13.at, bf16[512,1024]{1,0:T(8,128)(2,1)S(1)} %mul.75.spread, bf16[64,32,16,128]{3,2,1,0:T(8,128)(2,1)S(1)} %bitcast.50, bf16[64,13,16,128]{3,2,1,0:T(8,128)(2,1)S(1)} %copy-done.3, bf16[64,32,16,128]{3,2,1,0:T(8,128)(2,1)} %expand.8.rest_0_), custom_call_target="tpu_custom_call", output_to_operand_aliasing={{}: (4, {})} | custom-call | flops 3489660928 | bytes 10223616 | tf_op jit(solution)/shard_map/expand/pallas_call | solution.py:198
  188.1 5.2 %expand.10.rest_0_ = bf16[64,32,16,128]{3,2,1,0:T(8,128)(2,1)} custom-call(s32[1]{0:T(128)} %bitcast.20.at, bf16[512,1024]{1,0:T(8,128)(2,1)S(1)} %mul.75.spread, bf16[64,32,16,128]{3,2,1,0:T(8,128)(2,1)S(1)} %bitcast.51, bf16[64,5,16,128]{3,2,1,0:T(8,128)(2,1)} %collective-permute-done.13.other, ...), custom_call_target="tpu_custom_call", output_to_operand_aliasing={{}: (4, {})} | custom-call | flops 1342177280 | bytes 3932160 | tf_op jit(solution)/shard_map/expand/pallas_call | solution.py:198
  193.6 8.0 %collective-permute-done.11.other = bf16[64,5,16,128]{3,2,1,0:T(8,128)(2,1)S(1)} collective-permute-done((bf16[64,5,16,128]{3,2,1,0:T(8,128)(2,1)S(1)}, bf16[64,5,16,128]{3,2,1,0:T(8,128)(2,1)S(1)}, u32[]{:S(2)}, u32[]{:S(2)}) %collective-permute-start.11) | collective-permute-done | bytes 1310752 | tf_op jit(solution)/shard_map/ppermute | solution.py:223
  201.6 1.6 collective-permute-start.12
  204.6 3.6 %expand.11.rest_0_ = bf16[64,32,16,128]{3,2,1,0:T(8,128)(2,1)} custom-call(s32[1]{0:T(128)} %bitcast.19.at, bf16[512,1024]{1,0:T(8,128)(2,1)S(1)} %mul.75.spread, bf16[64,32,16,128]{3,2,1,0:T(8,128)(2,1)S(1)} %bitcast.53, bf16[64,5,16,128]{3,2,1,0:T(8,128)(2,1)S(1)} %collective-permute-done.11.other, ...), custom_call_target="tpu_custom_call", output_to_operand_aliasing={{}: (4, {})} | custom-call | flops 1342177280 | bytes 3932160 | tf_op jit(solution)/shard_map/expand/pallas_call | solution.py:198
  208.3 10.2 %collective-permute-done.14.other = bf16[64,3,16,128]{3,2,1,0:T(8,128)(2,1)S(1)} collective-permute-done((bf16[64,3,16,128]{3,2,1,0:T(8,128)(2,1)S(1)}, bf16[64,3,16,128]{3,2,1,0:T(8,128)(2,1)S(1)}, u32[]{:S(2)}, u32[]{:S(2)}) %collective-permute-start.14) | collective-permute-done | bytes 786464 | tf_op jit(solution)/shard_map/ppermute | solution.py:223
  218.4 2.4 %expand.12.rest_0_ = bf16[64,32,16,128]{3,2,1,0:T(8,128)(2,1)} custom-call(s32[1]{0:T(128)} %bitcast.18.at, bf16[512,1024]{1,0:T(8,128)(2,1)S(1)} %mul.75.spread, bf16[64,32,16,128]{3,2,1,0:T(8,128)(2,1)S(1)} %bitcast.54, bf16[64,3,16,128]{3,2,1,0:T(8,128)(2,1)S(1)} %collective-permute-done.14.other, ...), custom_call_target="tpu_custom_call", output_to_operand_aliasing={{}: (4, {})} | custom-call | flops 805306368 | bytes 2359296 | tf_op jit(solution)/shard_map/expand/pallas_call | solution.py:198
  220.9 5.0 %collective-permute-done.12.other = bf16[64,2,16,128]{3,2,1,0:T(8,128)(2,1)S(1)} collective-permute-done((bf16[64,2,16,128]{3,2,1,0:T(8,128)(2,1)S(1)}, bf16[64,2,16,128]{3,2,1,0:T(8,128)(2,1)S(1)}, u32[]{:S(2)}, u32[]{:S(2)}) %collective-permute-start.12) | collective-permute-done | bytes 524320 | tf_op jit(solution)/shard_map/ppermute | solution.py:223
  225.8 1.7 expand.13
  (70 shorter events, 20.1 us)
Async XLA Ops:
  0.6 28.1 %copy-start.13 = (s32[4]{0:T(128)S(1)}, s32[4]{0:T(128)}, u32[]{:S(2)}) copy-start(s32[4]{0:T(128)} %param.9) | copy-start | bytes 52
  2.8 9.3 %collective-permute-start.3 = (bf16[64,1,16,128]{3,2,1,0:T(8,128)(2,1)S(1)}, bf16[64,1,16,128]{3,2,1,0:T(8,128)(2,1)S(1)}, u32[]{:S(2)}, u32[]{:S(2)}) collective-permute-start(bf16[64,1,16,128]{3,2,1,0:T(8,128)(2,1)S(1)} %get-tuple-element.26), channel_id=1, source_target_pairs={{0,1},{1,0},{2,3},{3,2},{4,5},{5,4},{6,7},{7,6},{8,9},{9,8},{10,11... | collective-permute-start | bytes 786440 | tf_op jit(solution)/shard_map/ppermute | solution.py:223
  12.0 0.7 copy-start.6
  17.0 96.6 %collective-permute-start.4 = (bf16[64,13,16,128]{3,2,1,0:T(8,128)(2,1)}, bf16[64,13,16,128]{3,2,1,0:T(8,128)(2,1)S(1)}, u32[]{:S(2)}, u32[]{:S(2)}) collective-permute-start(bf16[64,13,16,128]{3,2,1,0:T(8,128)(2,1)} %constant_dynamic-slice_fusion.6), channel_id=1, source_target_pairs={{0,1},{1,0},{2,3},{3,2},{4,5},{5,4},{6,7},{7,6},{8,9},{9,8},{10,11... | collective-permute-start | bytes 10223624 | tf_op jit(solution)/shard_map/ppermute | solution.py:223
  20.7 10.4 %collective-permute-start = (bf16[64,1,16,128]{3,2,1,0:T(8,128)(2,1)}, bf16[64,1,16,128]{3,2,1,0:T(8,128)(2,1)}, u32[]{:S(2)}, u32[]{:S(2)}) collective-permute-start(bf16[64,1,16,128]{3,2,1,0:T(8,128)(2,1)} %get-tuple-element.29), channel_id=1, source_target_pairs={{0,2},{2,4},{4,6},{1,3},{3,5},{5,7},{8,10},{10,12},{12,14},{9,11},... | collective-permute-start | bytes 786440 | tf_op jit(solution)/shard_map/ppermute | solution.py:269
  24.8 8.8 %collective-permute-start.1 = (bf16[64,1,16,128]{3,2,1,0:T(8,128)(2,1)}, bf16[64,1,16,128]{3,2,1,0:T(8,128)(2,1)}, u32[]{:S(2)}, u32[]{:S(2)}) collective-permute-start(bf16[64,1,16,128]{3,2,1,0:T(8,128)(2,1)} %get-tuple-element.28), channel_id=1, source_target_pairs={{2,0},{4,2},{6,4},{3,1},{5,3},{7,5},{10,8},{12,10},{14,12},{11,9},... | collective-permute-start | bytes 786440 | tf_op jit(solution)/shard_map/ppermute | solution.py:270
  28.3 80.9 %collective-permute-start.2 = (bf16[64,3,16,128]{3,2,1,0:T(8,128)(2,1)}, bf16[64,3,16,128]{3,2,1,0:T(8,128)(2,1)}, u32[]{:S(2)}, u32[]{:S(2)}) collective-permute-start(bf16[64,3,16,128]{3,2,1,0:T(8,128)(2,1)} %dynamic-slice_bitcast_fusion), channel_id=1, source_target_pairs={{0,1},{1,0},{2,3},{3,2},{4,5},{5,4},{6,7},{7,6},{8,9},{9,8},{10,11... | collective-permute-start | bytes 2359304 | tf_op jit(solution)/shard_map/ppermute | solution.py:223
  33.7 3.4 %copy-start = (bf16[1,64,32,16,128]{4,3,2,1,0:T(8,128)(2,1)S(1)}, bf16[1,64,32,16,128]{4,3,2,1,0:T(8,128)(2,1)}, u32[]{:S(2)}) copy-start(bf16[1,64,32,16,128]{4,3,2,1,0:T(8,128)(2,1)} %param.5) | copy-start | bytes 25165828
  37.0 0.9 copy-start.4
  38.0 0.9 copy-start.5
  38.9 41.6 %copy-start.11 = (bf16[1,128,64]{1,2,0:T(8,128)(2,1)S(1)}, bf16[1,128,64]{1,2,0:T(8,128)(2,1)}, u32[]{:S(2)}) copy-start(bf16[1,128,64]{1,2,0:T(8,128)(2,1)} %param.8) | copy-start | bytes 49156
  38.9 41.7 %copy-start.7 = (bf16[64,1,16,128]{3,2,1,0:T(8,128)(2,1)S(1)}, bf16[64,1,16,128]{3,2,1,0:T(8,128)(2,1)}, u32[]{:S(2)}) copy-start(bf16[64,1,16,128]{3,2,1,0:T(8,128)(2,1)} %copy-done.6) | copy-start | bytes 786436
  38.9 41.7 %copy-start.10 = (bf16[1,64,1,16,128]{4,3,2,1,0:T(8,128)(2,1)S(1)}, bf16[1,64,1,16,128]{4,3,2,1,0:T(8,128)(2,1)}, u32[]{:S(2)}) copy-start(bf16[1,64,1,16,128]{4,3,2,1,0:T(8,128)(2,1)} %get-tuple-element.27) | copy-start | bytes 786436
  80.5 33.0 %copy-start.9 = (bf16[1,64,1,16,128]{4,3,2,1,0:T(8,128)(2,1)S(1)}, bf16[1,64,1,16,128]{4,3,2,1,0:T(8,128)(2,1)}, u32[]{:S(2)}) copy-start(bf16[1,64,1,16,128]{4,3,2,1,0:T(8,128)(2,1)} %get-tuple-element.25) | copy-start | bytes 786436
  113.7 14.2 %copy-start.2 = (bf16[64,13,16,128]{3,2,1,0:T(8,128)(2,1)}, bf16[64,13,16,128]{3,2,1,0:T(8,128)(2,1)S(1)}, u32[]{:S(2)}) copy-start(bf16[64,13,16,128]{3,2,1,0:T(8,128)(2,1)S(1)} %collective-permute-done.4.other) | copy-start | bytes 10223620
  119.3 4.7 %collective-permute-start.5 = (f32[64,128]{1,0:T(8,128)S(1)}, f32[64,128]{1,0:T(8,128)S(1)}, u32[]{:S(2)}, u32[]{:S(2)}) collective-permute-start(f32[64,128]{1,0:T(8,128)S(1)} %pad_maximum_fusion.1), channel_id=1, source_target_pairs={{0,1},{1,0},{2,3},{3,2},{4,5},{5,4},{6,7},{7,6},{8,9},{9,8},{10,11... | collective-permute-start | bytes 98312 | tf_op jit(solution)/shard_map/ppermute | solution.py:223
  123.3 44.9 %collective-permute-start.13 = (bf16[64,5,16,128]{3,2,1,0:T(8,128)(2,1)}, bf16[64,5,16,128]{3,2,1,0:T(8,128)(2,1)}, u32[]{:S(2)}, u32[]{:S(2)}) collective-permute-start(bf16[64,5,16,128]{3,2,1,0:T(8,128)(2,1)} %constant_dynamic-slice_fusion.1), channel_id=1, source_target_pairs={{0,1},{1,0},{2,3},{3,2},{4,5},{5,4},{6,7},{7,6},{8,9},{9,8},{10,11... | collective-permute-start | bytes 3932168 | tf_op jit(solution)/shard_map/ppermute | solution.py:223
  126.3 37.2 %collective-permute-start.6 = (f32[64,256]{1,0:T(8,128)S(1)}, f32[64,256]{1,0:T(8,128)S(1)}, u32[]{:S(2)}, u32[]{:S(2)}) collective-permute-start(f32[64,256]{1,0:T(8,128)S(1)} %pad_maximum_fusion), channel_id=1, source_target_pairs={{0,2},{2,0},{4,6},{6,4},{1,3},{3,1},{5,7},{7,5},{8,10},{10,8},{12,... | collective-permute-start | bytes 196616 | tf_op jit(solution)/shard_map/ppermute | solution.py:235
  134.5 24.5 %copy-start.8 = (bf16[64,1,16,128]{3,2,1,0:T(8,128)(2,1)S(1)}, bf16[64,1,16,128]{3,2,1,0:T(8,128)(2,1)}, u32[]{:S(2)}) copy-start(bf16[64,1,16,128]{3,2,1,0:T(8,128)(2,1)} %copy-done.6) | copy-start | bytes 786436
  159.0 3.4 %copy-start.1 = (bf16[1,64,32,16,128]{4,3,2,1,0:T(8,128)(2,1)S(1)}, bf16[1,64,32,16,128]{4,3,2,1,0:T(8,128)(2,1)}, u32[]{:S(2)}) copy-start(bf16[1,64,32,16,128]{4,3,2,1,0:T(8,128)(2,1)} %param.5) | copy-start | bytes 25165828
  163.6 12.6 %copy-start.12 = (f32[2]{0:T(128)S(1)}, f32[2]{0:T(128)}, u32[]{:S(2)}) copy-start(f32[2]{0:T(128)} %compare_convert_fusion) | copy-start | bytes 28
  163.6 16.1 %copy-start.3 = (bf16[64,13,16,128]{3,2,1,0:T(8,128)(2,1)S(1)}, bf16[64,13,16,128]{3,2,1,0:T(8,128)(2,1)}, u32[]{:S(2)}) copy-start(bf16[64,13,16,128]{3,2,1,0:T(8,128)(2,1)} %copy-done.2) | copy-start | bytes 10223620
  163.6 4.6 %collective-permute-start.7 = (f32[64,256]{1,0:T(8,128)S(1)}, f32[64,256]{1,0:T(8,128)S(1)}, u32[]{:S(2)}, u32[]{:S(2)}) collective-permute-start(f32[64,256]{1,0:T(8,128)S(1)} %add.56), channel_id=1, source_target_pairs={{2,4},{4,2},{3,5},{5,3},{10,12},{12,10},{11,13},{13,11},{18,20},{2... | collective-permute-start | bytes 196616 | tf_op jit(solution)/shard_map/ppermute | solution.py:236
  168.2 7.9 %collective-permute-start.8 = (f32[64,256]{1,0:T(8,128)S(1)}, f32[64,256]{1,0:T(8,128)S(1)}, u32[]{:S(2)}, u32[]{:S(2)}) collective-permute-start(f32[64,256]{1,0:T(8,128)S(1)} %add.57), channel_id=1, source_target_pairs={{2,0},{4,6},{3,1},{5,7},{10,8},{12,14},{11,9},{13,15},{18,16},{20,... | collective-permute-start | bytes 196616 | tf_op jit(solution)/shard_map/ppermute | solution.py:237
  169.8 31.8 %collective-permute-start.11 = (bf16[64,5,16,128]{3,2,1,0:T(8,128)(2,1)S(1)}, bf16[64,5,16,128]{3,2,1,0:T(8,128)(2,1)S(1)}, u32[]{:S(2)}, u32[]{:S(2)}) collective-permute-start(bf16[64,5,16,128]{3,2,1,0:T(8,128)(2,1)S(1)} %constant_dynamic-slice_fusion.3), channel_id=1, source_target_pairs={{0,1},{1,0},{2,3},{3,2},{4,5},{5,4},{6,7},{7,6},{8,9},{9,8},{10,11... | collective-permute-start | bytes 3932168 | tf_op jit(solution)/shard_map/ppermute | solution.py:223
  176.2 1.8 collective-permute-start.9
  176.4 42.0 %collective-permute-start.14 = (bf16[64,3,16,128]{3,2,1,0:T(8,128)(2,1)S(1)}, bf16[64,3,16,128]{3,2,1,0:T(8,128)(2,1)S(1)}, u32[]{:S(2)}, u32[]{:S(2)}) collective-permute-start(bf16[64,3,16,128]{3,2,1,0:T(8,128)(2,1)S(1)} %constant_dynamic-slice_fusion), channel_id=1, source_target_pairs={{0,1},{1,0},{2,3},{3,2},{4,5},{5,4},{6,7},{7,6},{8,9},{9,8},{10,11... | collective-permute-start | bytes 2359304 | tf_op jit(solution)/shard_map/ppermute | solution.py:223
  178.1 15.2 %collective-permute-start.10 = (f32[2,64,256]{2,1,0:T(8,128)S(1)}, f32[2,64,256]{2,1,0:T(8,128)S(1)}, u32[]{:S(2)}, u32[]{:S(2)}) collective-permute-start(f32[2,64,256]{2,1,0:T(8,128)S(1)} %fusion.10), channel_id=1, source_target_pairs={{0,16},{8,24},{16,0},{24,8},{1,17},{9,25},{17,1},{25,9},{2,18},{10... | collective-permute-start | bytes 393224 | tf_op jit(solution)/shard_map/ppermute | solution.py:229
  201.6 24.2 %collective-permute-start.12 = (bf16[64,2,16,128]{3,2,1,0:T(8,128)(2,1)S(1)}, bf16[64,2,16,128]{3,2,1,0:T(8,128)(2,1)S(1)}, u32[]{:S(2)}, u32[]{:S(2)}) collective-permute-start(bf16[64,2,16,128]{3,2,1,0:T(8,128)(2,1)S(1)} %constant_dynamic-slice_fusion.2), channel_id=1, source_target_pairs={{0,1},{1,0},{2,3},{3,2},{4,5},{5,4},{6,7},{7,6},{8,9},{9,8},{10,11... | collective-permute-start | bytes 1572872 | tf_op jit(solution)/shard_map/ppermute | solution.py:223

commit v2 on v1

--- a/solution.py
+++ b/solution.py
@@ -8,9 +8,10 @@
 
 SUB = 8
 VMEM_BYTES = 32 * 1024 * 1024
-
-
-def params(steps):
+SMALL = pl.CostEstimate(flops=1024, bytes_accessed=1024, transcendentals=0)
+
+
+def params():
     return pltpu.CompilerParams(
         dimension_semantics=("arbitrary",), vmem_limit_bytes=VMEM_BYTES
     )
@@ -122,15 +123,13 @@
             pltpu.VMEM((tall, wide), jnp.bfloat16),
             pltpu.VMEM((rows, SUB, cells_z), jnp.float32),
         ],
-        compiler_params=params(layers),
-        cost_estimate=pl.CostEstimate(
-            flops=2 * layers * tall * tall * wide, bytes_accessed=8 * own.size, transcendentals=0
-        ),
+        compiler_params=params(),
+        cost_estimate=SMALL,
         name="stiff_terms",
     )(own, own, own, low, high, coefs, masses)
 
 
-def cross_kernel(at, stiff, other, gram, total):
+def cross_kernel(at, skip, stiff, other, gram, total):
     step = pl.program_id(0)
 
     @pl.when(step == 0)
@@ -144,28 +143,125 @@
         gram[...] = same_row_sum(total[...])
 
 
-def cross_terms(stiff, other, at):
-    rows, layers, cells_y, cells_z = other.shape
+def cross_terms(stiff, other, at, skip, layers):
+    rows, _, cells_y, cells_z = other.shape
     _, tall, wide = stiff.shape
     return pl.pallas_call(
         cross_kernel,
         grid_spec=pltpu.PrefetchScalarGridSpec(
-            num_scalar_prefetch=1,
+            num_scalar_prefetch=2,
             grid=(layers,),
             in_specs=[
-                pl.BlockSpec((1, tall, wide), lambda g, at: (at[0] + g, 0, 0)),
-                pl.BlockSpec((rows, 1, cells_y, cells_z), lambda g, at: (0, g, 0, 0)),
+                pl.BlockSpec((1, tall, wide), lambda g, at, skip: (at[0] + g, 0, 0)),
+                pl.BlockSpec((rows, 1, cells_y, cells_z), lambda g, at, skip: (0, skip[0] + g, 0, 0)),
             ],
-            out_specs=pl.BlockSpec((rows, rows), lambda g, at: (0, 0)),
+            out_specs=pl.BlockSpec((rows, rows), lambda g, at, skip: (0, 0)),
             scratch_shapes=[pltpu.VMEM((tall, tall), jnp.float32)],
         ),
         out_shape=jax.ShapeDtypeStruct((rows, rows), jnp.float32),
-        compiler_params=params(layers),
-        cost_estimate=pl.CostEstimate(
-            flops=2 * layers * tall * tall * wide, bytes_accessed=4 * other.size, transcendentals=0
+        compiler_params=params(),
+        cost_estimate=SMALL,
+        name="cross_terms",
+    )(at.reshape(1), skip.reshape(1), stiff, other)
+
+
+def cut_kernel(at, whole, order, out, sem):
+    copy = pltpu.make_async_copy(whole.at[:, pl.ds(at[0], out.shape[1])], out, sem)
+    copy.start()
+    copy.wait()
+
+
+def cut(whole, at, count, order):
+    rows, _, cells_y, cells_z = whole.shape
+    return pl.pallas_call(
+        cut_kernel,
+        grid_spec=pltpu.PrefetchScalarGridSpec(
+            num_scalar_prefetch=1,
+            grid=(1,),
+            in_specs=[pl.BlockSpec(memory_space=pl.ANY)] * 2,
+            out_specs=pl.BlockSpec(memory_space=pl.ANY),
+            scratch_shapes=[pltpu.SemaphoreType.DMA],
         ),
-        name="cross_terms",
-    )(at.reshape(1), stiff, other)
+        out_shape=jax.ShapeDtypeStruct((rows, count, cells_y, cells_z), whole.dtype),
+        compiler_params=params(),
+        cost_estimate=SMALL,
+        name="cut",
+    )(at.reshape(1), whole, order)
+
+
+def merge_kernel(blk, whole, theirs, node, root):
+    nodes, rows, _ = whole.shape
+    first = blk[0] == 0
+    total = None
+    for p in range(nodes):
+        gram = whole[p, :, :rows]
+        cross = whole[p, :, rows : 2 * rows] + theirs[p, :, :rows].T
+        scale = 1.0 / jnp.sqrt(whole[p, :, 2 * rows :])
+        scale_gram = scale.T
+        scale_cross = (1.0 / jnp.sqrt(theirs[p, :, rows:])).T
+        low, high = jnp.where(first, gram, cross), jnp.where(first, cross, gram)
+        scale_low = jnp.where(first, scale_gram, scale_cross)
+        scale_high = jnp.where(first, scale_cross, scale_gram)
+        node[p, :, :rows] = low
+        node[p, :, rows:] = high
+        here = jnp.concatenate([scale * low * scale_low, scale * high * scale_high], axis=1)
+        total = here if total is None else total + here
+    root[...] = total
+
+
+def merge(whole, theirs, blk):
+    nodes, rows, _ = whole.shape
+    return pl.pallas_call(
+        merge_kernel,
+        grid_spec=pltpu.PrefetchScalarGridSpec(
+            num_scalar_prefetch=1,
+            grid=(1,),
+            in_specs=[
+                pl.BlockSpec(whole.shape, lambda g, blk: (0, 0, 0)),
+                pl.BlockSpec(theirs.shape, lambda g, blk: (0, 0, 0)),
+            ],
+            out_specs=[
+                pl.BlockSpec((nodes, rows, 2 * rows), lambda g, blk: (0, 0, 0)),
+                pl.BlockSpec((rows, 2 * rows), lambda g, blk: (0, 0)),
+            ],
+        ),
+        out_shape=[
+            jax.ShapeDtypeStruct((nodes, rows, 2 * rows), jnp.float32),
+            jax.ShapeDtypeStruct((rows, 2 * rows), jnp.float32),
+        ],
+        compiler_params=params(),
+        cost_estimate=SMALL,
+        name="merge",
+    )(blk.astype(jnp.int32).reshape(1), whole, theirs)
+
+
+def spread_kernel(block, out):
+    tall, wide = out.shape
+    eigs, modes = block.shape
+
+    def shape_of(rows, cols, dim):
+        index = lax.broadcasted_iota(jnp.int32, (rows, cols), dim)
+        near = lax.broadcasted_iota(jnp.int32, (rows, cols), 1 - dim)
+        return (index // SUB == near).astype(jnp.bfloat16)
+
+    wider = jnp.dot(block[...], shape_of(modes, wide, 1), preferred_element_type=jnp.float32)
+    full = jnp.dot(
+        shape_of(tall, eigs, 0), wider.astype(jnp.bfloat16), preferred_element_type=jnp.float32
+    )
+    row = lax.broadcasted_iota(jnp.int32, (tall, wide), 0) % SUB
+    col = lax.broadcasted_iota(jnp.int32, (tall, wide), 1) % SUB
+    out[...] = jnp.where(row == col, full, 0.0).astype(out.dtype)
+
+
+def spread_blocks(block):
+    eigs, modes = block.shape
+    return pl.pallas_call(
+        spread_kernel,
+        out_shape=jax.ShapeDtypeStruct((eigs * SUB, modes * SUB), block.dtype),
+        compiler_params=pltpu.CompilerParams(vmem_limit_bytes=VMEM_BYTES),
+        cost_estimate=SMALL,
+        name="spread_blocks",
+    )(block)
 
 
 def vector_kernel(at, spread, own, other, *rest):
@@ -205,18 +301,14 @@
         ),
         out_shape=jax.ShapeDtypeStruct((eigs,) + own.shape[1:], jnp.bfloat16),
         input_output_aliases=aliases,
-        compiler_params=params(layers),
-        cost_estimate=pl.CostEstimate(
-            flops=2 * layers * spread.shape[0] * spread.shape[1] * cells_y // SUB * cells_z,
-            bytes_accessed=6 * other.size,
-            transcendentals=0,
-        ),
+        compiler_params=params(),
+        cost_estimate=SMALL,
         name="expand",
     )(*inputs)
 
 
-def tied(x, y):
-    return lax.optimization_barrier((x, y))[0]
+def shares(total, parts):
+    return [total // parts + (i < total % parts) for i in range(parts)]
 
 
 def swap(x):
@@ -246,82 +338,65 @@
     blk, dof, leaf = lax.axis_index("blk"), lax.axis_index("dof"), lax.axis_index("leaf")
     upper = (blk + dof) % 2
 
-    def start(mine, offset, count, top):
-        forward = top == 1 if mine else top == 0
-        return jnp.where(forward, half + offset, half - offset - count).astype(jnp.int32)
-
-    def send(mine, offset, count, after=None):
-        source = own if after is None else tied(own, after)
-        at = start(mine, offset, count, 1 - upper)
-        return swap(lax.dynamic_slice_in_dim(source, at, count, axis=1))
-
-    def place(mine, offset, count):
-        return start(mine, offset, count, upper)
-
-    near, far = half * 3 // 16, half - half * 3 // 16
-    rest = [half * 5 // 16, half * 5 // 16, half * 3 // 16]
-    rest.append(half - 1 - sum(rest))
-    spots = [1, 1 + rest[0], 1 + rest[0] + rest[1], 1 + sum(rest[:3])]
-
-    edge = send(False, 0, 1)
-    first = send(True, 0, near)
+    def spot(offset, count, top):
+        forward, back = half - 1 + offset, half + 1 - offset - count
+        return jnp.where(top == 1, forward, back).astype(jnp.int32)
+
+    def far_spot(offset, count, top):
+        forward, back = half + 1 + offset, half - 1 - offset - count
+        return jnp.where(top == 0, forward, back).astype(jnp.int32)
+
+    def send(at, count):
+        return swap(lax.dynamic_slice_in_dim(own, at, count, axis=1))
+
+    nears = shares(half + 1, 2)
+    last = half // 8
+    fars = shares(half - 1 - last, 1)
+    near_at = [sum(nears[:i]) for i in range(len(nears))]
+    far_at = [sum(fars[:i]) for i in range(len(fars))]
+
+    near = [send(spot(o, n, 1 - upper), n) for o, n in zip(near_at, nears)]
+    far = [send(far_spot(o, n, 1 - upper), n) for o, n in zip(far_at, fars)]
     size = lax.axis_size("dof")
     low = lax.ppermute(own[:, -1:], "dof", [(i, i + 1) for i in range(size - 1)])
     high = lax.ppermute(own[:, :1], "dof", [(i + 1, i) for i in range(size - 1)])
-    second = send(True, near, far, edge)
     stiff, gram, mass = stiff_terms(own, low, high, stiffness[0], density[0])
 
-    blocks = tied(eigen_blocks[0], mass)
-    mine = lax.dynamic_slice_in_dim(blocks, blk * rows, rows, 0)
-    other = lax.dynamic_slice_in_dim(blocks, (1 - blk) * rows, rows, 0)
-    ordered = jnp.concatenate([mine, other], axis=0).T
-    eye = jnp.eye(SUB, dtype=ordered.dtype)
-    spread = (ordered[:, None, :, None] * eye[None, :, None, :]).reshape(
-        ordered.shape[0] * SUB, ordered.shape[1] * SUB
-    )
-
-    third = send(False, spots[0], rest[0], first)
-    inner, outer = place(True, 0, 1), place(False, 0, 1)
-    own_in = lax.dynamic_slice_in_dim(own, inner, 1, axis=1)
-    own_out = lax.dynamic_slice_in_dim(own, outer, 1, axis=1)
-    first_in = lax.dynamic_slice_in_dim(first, inner - place(True, 0, near), 1, axis=1)
+    mine = lax.dynamic_slice_in_dim(eigen_blocks[0], blk * rows, rows, 0)
+    other = lax.dynamic_slice_in_dim(eigen_blocks[0], (1 - blk) * rows, rows, 0)
+    spread = spread_blocks(jnp.concatenate([mine, other], axis=0).T)
+
+    own_in = lax.dynamic_slice_in_dim(own, spot(1, 1, upper), 1, axis=1)
+    own_out = lax.dynamic_slice_in_dim(own, spot(0, 1, upper), 1, axis=1)
+    first = spot(0, nears[0], upper)
+    near_in = lax.dynamic_slice_in_dim(near[0], spot(1, 1, upper) - first, 1, axis=1)
+    near_out = lax.dynamic_slice_in_dim(near[0], spot(0, 1, upper) - first, 1, axis=1)
     across = functools.partial(
         lax.dot_general,
         dimension_numbers=(((1, 2, 3), (1, 2, 3)), ((), ())),
         preferred_element_type=jnp.float32,
     )
-    border = 0.5 * (across(own_out, first_in) - across(own_in, edge))
-    cross = cross_terms(stiff, first, place(True, 0, near))
-    vectors = expand(spread, own, edge, outer, None)
-    vectors = expand(spread, own, first, place(True, 0, near), vectors)
-    cross = cross + border + cross_terms(stiff, second, place(True, near, far))
-
-    fourth = send(False, spots[1], rest[1], cross)
-    theirs = swap(jnp.concatenate([cross, mass], axis=1))
-    vectors = expand(spread, own, second, place(True, near, far), vectors)
-    fifth = send(False, spots[2], rest[2], third)
-    vectors = expand(spread, own, third, place(False, spots[0], rest[0]), vectors)
-    sixth = send(False, spots[3], rest[3], fourth)
-
-    whole = jnp.concatenate([gram, cross + theirs[:, :rows].T, mass, theirs[:, rows:]], axis=1)
-    whole = line_sum(whole, "dof")
+    cross = 0.5 * (across(own_out, near_in) - across(own_in, near_out))
+    for chunk, offset, count in zip(near, near_at, nears):
+        chunk_at = spot(offset, count, upper)
+        skipped = int(offset == 0)
+        at = spot(offset + skipped, count - skipped, upper)
+        cross = cross + cross_terms(stiff, chunk, at, at - chunk_at, count - skipped)
+
+    whole = line_sum(jnp.concatenate([gram, cross, mass], axis=1), "dof")
     nodes = lax.axis_size("leaf") // 2
     belongs = (parent[leaf] == jnp.arange(nodes, dtype=jnp.int32)).astype(jnp.float32)
     whole = paired_sum(belongs[:, None, None] * whole[None], "leaf")
-    gram, cross = whole[:, :, :rows], whole[:, :, rows : 2 * rows]
-    scale_own = 1.0 / jnp.sqrt(whole[:, :, 2 * rows])
-    scale_other = 1.0 / jnp.sqrt(whole[:, :, 3 * rows])
-
-    def in_order(a, b):
-        return jnp.where(blk == 0, jnp.concatenate([a, b], -1), jnp.concatenate([b, a], -1))
-
-    node_stiffness = in_order(gram, cross)
-    scale = in_order(scale_own, scale_other)
-    root_stiffness = jnp.sum(scale_own[:, :, None] * node_stiffness * scale[:, None, :], axis=0)
-
-    vectors = expand(spread, own, fourth, place(False, spots[1], rest[1]), vectors)
-    vectors = expand(spread, own, fifth, place(False, spots[2], rest[2]), vectors)
-    vectors = expand(spread, own, sixth, place(False, spots[3], rest[3]), vectors)
+    theirs = swap(whole[:, :, rows:])
+    final = swap(cut(own, far_spot(sum(fars), last, 1 - upper), last, whole))
+
+    vectors = None
+    for chunk, offset, count in zip(near, near_at, nears):
+        vectors = expand(spread, own, chunk, spot(offset, count, upper), vectors)
+    for chunk, offset, count in zip(far, far_at, fars):
+        vectors = expand(spread, own, chunk, far_spot(offset, count, upper), vectors)
+    node_stiffness, root_stiffness = merge(whole, theirs, blk)
+    vectors = expand(spread, own, final, far_spot(sum(fars), last, upper), vectors)
     return (node_stiffness, root_stiffness, vectors[None])
 
 

time: 230 us -> 210 us (0.913)
  local copies, waits for them, and re-layouts: 50.7 us -> 32.8 us
  other arithmetic: 11.1 us -> 1.16 us
  waiting for transfers between devices: 65 us -> 73.4 us
  Pallas kernels: 76.7 us -> 81.1 us
  starting transfers between devices: 22.7 us -> 18.7 us
    mul x1 -> x0, local copies, waits for them, and re-layouts: 24.5 us -> none  [halved(): ordered[:, None, :, None] * eye[None, :, None, :]]
    unnamed x28 -> x18, local copies, waits for them, and re-layouts: 9.4 us -> 16.9 us
    mul x1 -> x0, other arithmetic: 6.61 us -> none  [halved(): ordered[:, None, :, None] * eye[None, :, None, :]]
    ppermute x2, waiting for transfers between devices: 0.01 us -> 5.4 us  [paired_sum(): x = x + lax.ppermute(x, axis, [(i, i ^ step) for i in range(size)])]
    ppermute x8 -> x5, starting transfers between devices: 12 us -> 7.08 us  [swap(): return lax.ppermute(x, 'blk', [(0, 1), (1, 0)])]
    ppermute x8 -> x5, waiting for transfers between devices: 57.7 us -> 53.7 us  [swap(): return lax.ppermute(x, 'blk', [(0, 1), (1, 0)])]
    ppermute x1, waiting for transfers between devices: 4.74 us -> 8.46 us  [line_sum(): outer = lax.ppermute(x, axis, [(1, 0), (2, 3)])]
    pallas_call x0 -> x3, Pallas kernels: none -> 3.24 us  [the longest x1 1.87 us: merge(): pl.pallas_call(merge_kernel, grid_spec=pltpu.PrefetchScalarGridSpec(num_s...]
  transfers between devices with their start and end apart: 15 -> 12, of which waited for: 7 -> 8; matrix products, arithmetic and copies ran while one was open for 20% -> 7% of each run, Pallas kernels for 31% -> 38%
where the time goes in v2:
time: 210 us; the launch traced here: 209 us
  Pallas kernels  81.1 us (39%)
  waiting for transfers between devices  73.4 us (35%)
  local copies, waits for them, and re-layouts  32.8 us (16%)
  starting transfers between devices  18.7 us (9%)
    ppermute x5, waiting for transfers between devices, swap(): return lax.ppermute(x, 'blk', [(0, 1), (1, 0)])  53.7 us
    pallas_call x1, Pallas kernels, stiff_terms(): pl.pallas_call(stiff_kernel, grid=(layers,), in_specs=[pl.BlockSpec(block...  40.6 us
    pallas_call x4, Pallas kernels, expand(): pl.pallas_call(vector_kernel, grid_spec=pltpu.PrefetchScalarGridSpec(num_...  27.3 us
    unnamed x18, local copies, waits for them, and re-layouts  16.9 us
    dynamic_slice x3, local copies, waits for them, and re-layouts, send(): return swap(lax.dynamic_slice_in_dim(own, at, count, axis=1))  11.4 us
    pallas_call x2, Pallas kernels, cross_terms(): pl.pallas_call(cross_kernel, grid_spec=pltpu.PrefetchScalarGridSpec(num_s...  10 us
    ppermute x1, waiting for transfers between devices, line_sum(): outer = lax.ppermute(x, axis, [(1, 0), (2, 3)])  8.46 us
    ppermute x5, starting transfers between devices, swap(): return lax.ppermute(x, 'blk', [(0, 1), (1, 0)])  7.08 us
  transfers between devices with their start and end apart: 12, of which 8 were waited for; matrix products, arithmetic and copies ran while one was open for 7% of the time, Pallas kernels for 38%

profile of v2, /device:TPU:0, one launch (start us, length us, event | category | flops | bytes accessed | tf_op | source)
XLA Modules:
  0.0 208.5 jit_solution(11969708883834056631)
XLA Ops:
  0.7 3.5 %dynamic-slice_bitcast_fusion.1 = bf16[64,9,16,128]{3,2,1,0:T(8,128)(2,1)} fusion(bf16[1,64,32,16,128]{4,3,2,1,0:T(8,128)(2,1)} %param.5, s32[]{:T(128)S(6)} %select_n.79), kind=kLoop, calls=%fused_computation.1 | loop fusion | bytes 4718596 | tf_op jit(solution)/shard_map/dynamic_slice | solution.py:350
  4.2 3.0 %collective-permute-start.2 = (bf16[64,9,16,128]{3,2,1,0:T(8,128)(2,1)}, bf16[64,9,16,128]{3,2,1,0:T(8,128)(2,1)S(1)}, u32[]{:S(2)}, u32[]{:S(2)}) collective-permute-start(bf16[64,9,16,128]{3,2,1,0:T(8,128)(2,1)} %dynamic-slice_bitcast_fusion.1), channel_id=1, source_target_pairs={{0,1},{1,0},{2,3},{3,2},{4,5},{5,4},{6,7},{7,6},{8,9},{9,8},{10,11... | collective-permute-start | bytes 7077896 | tf_op jit(solution)/shard_map/ppermute | solution.py:315
  7.2 3.6 %dynamic-slice_bitcast_fusion.2 = bf16[64,8,16,128]{3,2,1,0:T(8,128)(2,1)} fusion(bf16[1,64,32,16,128]{4,3,2,1,0:T(8,128)(2,1)} %param.5, s32[]{:T(128)S(6)} %select_n.86), kind=kLoop, calls=%fused_computation.2 | loop fusion | bytes 4194308 | tf_op jit(solution)/shard_map/dynamic_slice | solution.py:350
  10.8 4.3 %dynamic-slice_bitcast_fusion = bf16[64,13,16,128]{3,2,1,0:T(8,128)(2,1)} fusion(bf16[1,64,32,16,128]{4,3,2,1,0:T(8,128)(2,1)} %param.5, s32[]{:T(128)S(6)} %select_n.93), kind=kLoop, calls=%fused_computation | loop fusion | bytes 6815748 | tf_op jit(solution)/shard_map/dynamic_slice | solution.py:350
  15.1 2.0 collective-permute-start.11
  17.1 1.9 fusion.11
  20.2 4.6 %collective-permute-start = (bf16[64,1,16,128]{3,2,1,0:T(8,128)(2,1)}, bf16[64,1,16,128]{3,2,1,0:T(8,128)(2,1)S(1)}, u32[]{:S(2)}, u32[]{:S(2)}) collective-permute-start(bf16[64,1,16,128]{3,2,1,0:T(8,128)(2,1)} %get-tuple-element.16), channel_id=1, source_target_pairs={{0,2},{2,4},{4,6},{1,3},{3,5},{5,7},{8,10},{10,12},{12,14},{9,11},... | collective-permute-start | bytes 786440 | tf_op jit(solution)/shard_map/ppermute | solution.py:361
  25.9 2.3 %collective-permute-done.1.high = bf16[64,1,16,128]{3,2,1,0:T(8,128)(2,1)S(1)} collective-permute-done((bf16[64,1,16,128]{3,2,1,0:T(8,128)(2,1)}, bf16[64,1,16,128]{3,2,1,0:T(8,128)(2,1)S(1)}, u32[]{:S(2)}, u32[]{:S(2)}) %collective-permute-start.1) | collective-permute-done | bytes 262176 | tf_op jit(solution)/shard_map/ppermute | solution.py:362
  28.3 1.3 collective-permute-done.low
  29.5 3.4 %copy-done = bf16[1,64,32,16,128]{4,3,2,1,0:T(8,128)(2,1)S(1)} copy-done((bf16[1,64,32,16,128]{4,3,2,1,0:T(8,128)(2,1)S(1)}, bf16[1,64,32,16,128]{4,3,2,1,0:T(8,128)(2,1)}, u32[]{:S(2)}) %copy-start) | copy-done | bytes 8388632
  32.9 40.6 %stiff_terms.1 = (bf16[32,512,256]{2,1,0:T(8,128)(2,1)S(1)}, f32[64,64]{1,0:T(8,128)S(1)}, f32[64,64]{1,0:T(8,128)S(1)}) custom-call(bf16[64,32,16,128]{3,2,1,0:T(8,128)(2,1)S(1)} %bitcast.48, bf16[64,32,16,128]{3,2,1,0:T(8,128)(2,1)S(1)} %bitcast.49, bf16[64,32,16,128]{3,2,1,0:T(8,128)(2,1)S(1)} %bitcast.50, ...), custom_call_target="tpu_custom_call" | custom-call | flops 1024 | bytes 1024 | tf_op jit(solution)/shard_map/stiff_terms/pallas_call | solution.py:99
  73.5 31.0 %collective-permute-done.3.other = bf16[64,8,16,128]{3,2,1,0:T(8,128)(2,1)} collective-permute-done((bf16[64,8,16,128]{3,2,1,0:T(8,128)(2,1)}, bf16[64,8,16,128]{3,2,1,0:T(8,128)(2,1)}, u32[]{:S(2)}, u32[]{:S(2)}) %collective-permute-start.3) | collective-permute-done | bytes 2097184 | tf_op jit(solution)/shard_map/ppermute | solution.py:315
  104.5 6.3 %cross_terms.3 = f32[64,64]{1,0:T(8,128)S(1)} custom-call(s32[1]{0:T(128)} %bitcast.14.at, s32[1]{0:T(128)} %constant.61.clone.1.skip, bf16[32,512,256]{2,1,0:T(8,128)(2,1)S(1)} %get-tuple-element.9.stiff, bf16[64,8,16,128]{3,2,1,0:T(8,128)(2,1)} %collective-permute-done.3.other), custom_call_target="tpu_custom_call" | custom-call | flops 1024 | bytes 1024 | tf_op jit(solution)/shard_map/cross_terms/pallas_call | solution.py:149
  110.9 3.7 %cross_terms.2 = f32[64,64]{1,0:T(8,128)S(1)} custom-call(s32[1]{0:T(128)} %bitcast.12.at, s32[1]{0:T(128)} %bitcast.13.skip, bf16[32,512,256]{2,1,0:T(8,128)(2,1)S(1)} %get-tuple-element.9.stiff, bf16[64,9,16,128]{3,2,1,0:T(8,128)(2,1)S(1)} %collective-permute-done.2.other), custom_call_target="tpu_custom_call" | custom-call | flops 1024 | bytes 1024 | tf_op jit(solution)/shard_map/cross_terms/pallas_call | solution.py:149
  115.2 2.2 %collective-permute-start.4 = (f32[64,192]{1,0:T(8,128)S(1)}, f32[64,192]{1,0:T(8,128)S(1)}, u32[]{:S(2)}, u32[]{:S(2)}) collective-permute-start(f32[64,192]{1,0:T(8,128)S(1)} %pad_maximum_fusion), channel_id=1, source_target_pairs={{0,2},{2,0},{4,6},{6,4},{1,3},{3,1},{5,7},{7,5},{8,10},{10,8},{12,... | collective-permute-start | bytes 147464 | tf_op jit(solution)/shard_map/ppermute | solution.py:327
  117.4 2.2 %collective-permute-done.4 = f32[64,192]{1,0:T(8,128)S(1)} collective-permute-done((f32[64,192]{1,0:T(8,128)S(1)}, f32[64,192]{1,0:T(8,128)S(1)}, u32[]{:S(2)}, u32[]{:S(2)}) %collective-permute-start.4) | collective-permute-done | bytes 49184 | tf_op jit(solution)/shard_map/ppermute | solution.py:327
  121.0 1.3 collective-permute-start.6
  123.0 8.5 %collective-permute-done.6 = f32[64,192]{1,0:T(8,128)S(1)} collective-permute-done((f32[64,192]{1,0:T(8,128)S(1)}, f32[64,192]{1,0:T(8,128)S(1)}, u32[]{:S(2)}, u32[]{:S(2)}) %collective-permute-start.6) | collective-permute-done | bytes 49184 | tf_op jit(solution)/shard_map/ppermute | solution.py:329
  131.6 1.3 collective-permute-done.7
  133.0 1.6 collective-permute-start.8
  134.6 4.1 %collective-permute-done.8 = f32[2,64,192]{2,1,0:T(8,128)S(1)} collective-permute-done((f32[2,64,192]{2,1,0:T(8,128)S(1)}, f32[2,64,192]{2,1,0:T(8,128)S(1)}, u32[]{:S(2)}, u32[]{:S(2)}) %collective-permute-start.8) | collective-permute-done | bytes 98336 | tf_op jit(solution)/shard_map/ppermute | solution.py:321
  138.8 3.4 %copy-done.1 = bf16[1,64,32,16,128]{4,3,2,1,0:T(8,128)(2,1)S(1)} copy-done((bf16[1,64,32,16,128]{4,3,2,1,0:T(8,128)(2,1)S(1)}, bf16[1,64,32,16,128]{4,3,2,1,0:T(8,128)(2,1)}, u32[]{:S(2)}) %copy-start.1) | copy-done | bytes 8388632
  142.9 1.6 collective-permute-start.10
  146.5 3.4 %copy-done.2 = bf16[1,64,32,16,128]{4,3,2,1,0:T(8,128)(2,1)S(1)} copy-done((bf16[1,64,32,16,128]{4,3,2,1,0:T(8,128)(2,1)S(1)}, bf16[1,64,32,16,128]{4,3,2,1,0:T(8,128)(2,1)}, u32[]{:S(2)}) %copy-start.2) | copy-done | bytes 8388632
  149.9 6.0 %expand.4.rest_0_ = bf16[64,32,16,128]{3,2,1,0:T(8,128)(2,1)} custom-call(s32[1]{0:T(128)} %bitcast.23.at, bf16[512,1024]{1,0:T(8,128)(2,1)S(1)} %spread_blocks.1.spread, bf16[64,32,16,128]{3,2,1,0:T(8,128)(2,1)S(1)} %bitcast.52, bf16[64,9,16,128]{3,2,1,0:T(8,128)(2,1)S(1)} %collective-permute-done.2.other), custom_call_target="tpu_custom_call" | custom-call | flops 1024 | bytes 1024 | tf_op jit(solution)/shard_map/expand/pallas_call | solution.py:294
  155.9 3.4 %copy-done.3 = bf16[1,64,32,16,128]{4,3,2,1,0:T(8,128)(2,1)S(1)} copy-done((bf16[1,64,32,16,128]{4,3,2,1,0:T(8,128)(2,1)S(1)}, bf16[1,64,32,16,128]{4,3,2,1,0:T(8,128)(2,1)}, u32[]{:S(2)}) %copy-start.3) | copy-done | bytes 8388632
  159.3 7.3 %expand.5.rest_0_ = bf16[64,32,16,128]{3,2,1,0:T(8,128)(2,1)} custom-call(s32[1]{0:T(128)} %bitcast.14.at, bf16[512,1024]{1,0:T(8,128)(2,1)S(1)} %spread_blocks.1.spread, bf16[64,32,16,128]{3,2,1,0:T(8,128)(2,1)S(1)} %bitcast.53, bf16[64,8,16,128]{3,2,1,0:T(8,128)(2,1)} %collective-permute-done.3.other, ...), custom_call_target="tpu_custom_call", output_to_operand_aliasing={{}: (4, {})} | custom-call | flops 1024 | bytes 1024 | tf_op jit(solution)/shard_map/expand/pallas_call | solution.py:294
  166.6 22.7 %collective-permute-done.9.theirs = f32[2,64,128]{2,1,0:T(8,128)} collective-permute-done((f32[2,64,128]{2,1,0:T(8,128)}, f32[2,64,128]{2,1,0:T(8,128)}, u32[]{:S(2)}, u32[]{:S(2)}) %collective-permute-start.9) | collective-permute-done | bytes 65568 | tf_op jit(solution)/shard_map/ppermute | solution.py:315
  189.4 1.9 merge.1
  191.2 3.4 %copy-done.4 = bf16[1,64,32,16,128]{4,3,2,1,0:T(8,128)(2,1)S(1)} copy-done((bf16[1,64,32,16,128]{4,3,2,1,0:T(8,128)(2,1)S(1)}, bf16[1,64,32,16,128]{4,3,2,1,0:T(8,128)(2,1)}, u32[]{:S(2)}) %copy-start.4) | copy-done | bytes 8388632
  194.6 11.3 %expand.6.rest_0_ = bf16[64,32,16,128]{3,2,1,0:T(8,128)(2,1)} custom-call(s32[1]{0:T(128)} %bitcast.21.at, bf16[512,1024]{1,0:T(8,128)(2,1)S(1)} %spread_blocks.1.spread, bf16[64,32,16,128]{3,2,1,0:T(8,128)(2,1)S(1)} %bitcast.54, bf16[64,13,16,128]{3,2,1,0:T(8,128)(2,1)} %collective-permute-done.11.other, ...), custom_call_target="tpu_custom_call", output_to_operand_aliasing={{}: (4, {})} | custom-call | flops 1024 | bytes 1024 | tf_op jit(solution)/shard_map/expand/pallas_call | solution.py:294
  205.9 2.6 %expand.7 = bf16[64,32,16,128]{3,2,1,0:T(8,128)(2,1)} custom-call(s32[1]{0:T(128)} %bitcast.16.at, bf16[512,1024]{1,0:T(8,128)(2,1)S(1)} %spread_blocks.1.spread, bf16[64,32,16,128]{3,2,1,0:T(8,128)(2,1)S(1)} %bitcast.55, bf16[64,2,16,128]{3,2,1,0:T(8,128)(2,1)} %collective-permute-done.10.other, ...), custom_call_target="tpu_custom_call", output_to_operand_aliasing={{}: (4, {})} | custom-call | flops 1024 | bytes 1024 | tf_op jit(solution)/shard_map/expand/pallas_call | solution.py:294
  (40 shorter events, 8.1 us)
Async XLA Ops:
  0.7 28.9 %copy-start.5 = (f32[1,32,16,128]{3,2,1,0:T(8,128)S(1)}, f32[1,32,16,128]{3,2,1,0:T(8,128)}, u32[]{:S(2)}) copy-start(f32[1,32,16,128]{3,2,1,0:T(8,128)} %param.6) | copy-start | bytes 786436
  0.7 28.9 %copy-start.6 = (f32[1,32,16,128]{3,2,1,0:T(8,128)S(1)}, f32[1,32,16,128]{3,2,1,0:T(8,128)}, u32[]{:S(2)}) copy-start(f32[1,32,16,128]{3,2,1,0:T(8,128)} %param.7) | copy-start | bytes 786436
  4.2 106.7 %collective-permute-start.2 = (bf16[64,9,16,128]{3,2,1,0:T(8,128)(2,1)}, bf16[64,9,16,128]{3,2,1,0:T(8,128)(2,1)S(1)}, u32[]{:S(2)}, u32[]{:S(2)}) collective-permute-start(bf16[64,9,16,128]{3,2,1,0:T(8,128)(2,1)} %dynamic-slice_bitcast_fusion.1), channel_id=1, source_target_pairs={{0,1},{1,0},{2,3},{3,2},{4,5},{5,4},{6,7},{7,6},{8,9},{9,8},{10,11... | collective-permute-start | bytes 7077896 | tf_op jit(solution)/shard_map/ppermute | solution.py:315
  10.8 93.7 %collective-permute-start.3 = (bf16[64,8,16,128]{3,2,1,0:T(8,128)(2,1)}, bf16[64,8,16,128]{3,2,1,0:T(8,128)(2,1)}, u32[]{:S(2)}, u32[]{:S(2)}) collective-permute-start(bf16[64,8,16,128]{3,2,1,0:T(8,128)(2,1)} %dynamic-slice_bitcast_fusion.2), channel_id=1, source_target_pairs={{0,1},{1,0},{2,3},{3,2},{4,5},{5,4},{6,7},{7,6},{8,9},{9,8},{10,11... | collective-permute-start | bytes 6291464 | tf_op jit(solution)/shard_map/ppermute | solution.py:315
  15.1 176.2 %collective-permute-start.11 = (bf16[64,13,16,128]{3,2,1,0:T(8,128)(2,1)}, bf16[64,13,16,128]{3,2,1,0:T(8,128)(2,1)}, u32[]{:S(2)}, u32[]{:S(2)}) collective-permute-start(bf16[64,13,16,128]{3,2,1,0:T(8,128)(2,1)} %dynamic-slice_bitcast_fusion), channel_id=1, source_target_pairs={{0,1},{1,0},{2,3},{3,2},{4,5},{5,4},{6,7},{7,6},{8,9},{9,8},{10,11... | collective-permute-start | bytes 10223624 | tf_op jit(solution)/shard_map/ppermute | solution.py:315
  19.0 9.3 %collective-permute-start.1 = (bf16[64,1,16,128]{3,2,1,0:T(8,128)(2,1)}, bf16[64,1,16,128]{3,2,1,0:T(8,128)(2,1)S(1)}, u32[]{:S(2)}, u32[]{:S(2)}) collective-permute-start(bf16[64,1,16,128]{3,2,1,0:T(8,128)(2,1)} %get-tuple-element.15), channel_id=1, source_target_pairs={{2,0},{4,2},{6,4},{3,1},{5,3},{7,5},{10,8},{12,10},{14,12},{11,9},... | collective-permute-start | bytes 786440 | tf_op jit(solution)/shard_map/ppermute | solution.py:362
  20.2 9.3 %collective-permute-start = (bf16[64,1,16,128]{3,2,1,0:T(8,128)(2,1)}, bf16[64,1,16,128]{3,2,1,0:T(8,128)(2,1)S(1)}, u32[]{:S(2)}, u32[]{:S(2)}) collective-permute-start(bf16[64,1,16,128]{3,2,1,0:T(8,128)(2,1)} %get-tuple-element.16), channel_id=1, source_target_pairs={{0,2},{2,4},{4,6},{1,3},{3,5},{5,7},{8,10},{10,12},{12,14},{9,11},... | collective-permute-start | bytes 786440 | tf_op jit(solution)/shard_map/ppermute | solution.py:361
  29.5 3.4 %copy-start = (bf16[1,64,32,16,128]{4,3,2,1,0:T(8,128)(2,1)S(1)}, bf16[1,64,32,16,128]{4,3,2,1,0:T(8,128)(2,1)}, u32[]{:S(2)}) copy-start(bf16[1,64,32,16,128]{4,3,2,1,0:T(8,128)(2,1)} %param.5) | copy-start | bytes 25165828
  110.9 9.5 %copy-start.8 = (s32[4]{0:T(128)S(1)}, s32[4]{0:T(128)}, u32[]{:S(2)}) copy-start(s32[4]{0:T(128)} %param.9) | copy-start | bytes 52
  114.6 30.0 %copy-start.7 = (bf16[1,128,64]{1,2,0:T(8,128)(2,1)S(1)}, bf16[1,128,64]{1,2,0:T(8,128)(2,1)}, u32[]{:S(2)}) copy-start(bf16[1,128,64]{1,2,0:T(8,128)(2,1)} %param.8) | copy-start | bytes 49156
  115.2 4.4 %collective-permute-start.4 = (f32[64,192]{1,0:T(8,128)S(1)}, f32[64,192]{1,0:T(8,128)S(1)}, u32[]{:S(2)}, u32[]{:S(2)}) collective-permute-start(f32[64,192]{1,0:T(8,128)S(1)} %pad_maximum_fusion), channel_id=1, source_target_pairs={{0,2},{2,0},{4,6},{6,4},{1,3},{3,1},{5,7},{7,5},{8,10},{10,8},{12,... | collective-permute-start | bytes 147464 | tf_op jit(solution)/shard_map/ppermute | solution.py:327
  119.7 1.3 collective-permute-start.5
  121.0 10.4 %collective-permute-start.6 = (f32[64,192]{1,0:T(8,128)S(1)}, f32[64,192]{1,0:T(8,128)S(1)}, u32[]{:S(2)}, u32[]{:S(2)}) collective-permute-start(f32[64,192]{1,0:T(8,128)S(1)} %add.53), channel_id=1, source_target_pairs={{2,0},{4,6},{3,1},{5,7},{10,8},{12,14},{11,9},{13,15},{18,16},{20,... | collective-permute-start | bytes 147464 | tf_op jit(solution)/shard_map/ppermute | solution.py:329
  131.5 1.4 collective-permute-start.7
  133.0 5.6 %collective-permute-start.8 = (f32[2,64,192]{2,1,0:T(8,128)S(1)}, f32[2,64,192]{2,1,0:T(8,128)S(1)}, u32[]{:S(2)}, u32[]{:S(2)}) collective-permute-start(f32[2,64,192]{2,1,0:T(8,128)S(1)} %fusion.10), channel_id=1, source_target_pairs={{0,16},{8,24},{16,0},{24,8},{1,17},{9,25},{17,1},{25,9},{2,18},{10... | collective-permute-start | bytes 294920 | tf_op jit(solution)/shard_map/ppermute | solution.py:321
  138.7 3.4 %copy-start.1 = (bf16[1,64,32,16,128]{4,3,2,1,0:T(8,128)(2,1)S(1)}, bf16[1,64,32,16,128]{4,3,2,1,0:T(8,128)(2,1)}, u32[]{:S(2)}) copy-start(bf16[1,64,32,16,128]{4,3,2,1,0:T(8,128)(2,1)} %param.5) | copy-start | bytes 25165828
  142.9 63.0 %collective-permute-start.10 = (bf16[64,2,16,128]{3,2,1,0:T(8,128)(2,1)}, bf16[64,2,16,128]{3,2,1,0:T(8,128)(2,1)}, u32[]{:S(2)}, u32[]{:S(2)}) collective-permute-start(bf16[64,2,16,128]{3,2,1,0:T(8,128)(2,1)} %cut.1), channel_id=1, source_target_pairs={{0,1},{1,0},{2,3},{3,2},{4,5},{5,4},{6,7},{7,6},{8,9},{9,8},{10,11... | collective-permute-start | bytes 1572872 | tf_op jit(solution)/shard_map/ppermute | solution.py:315
  145.4 44.0 %collective-permute-start.9 = (f32[2,64,128]{2,1,0:T(8,128)}, f32[2,64,128]{2,1,0:T(8,128)}, u32[]{:S(2)}, u32[]{:S(2)}) collective-permute-start(f32[2,64,128]{2,1,0:T(8,128)} %slice.14), channel_id=1, source_target_pairs={{0,1},{1,0},{2,3},{3,2},{4,5},{5,4},{6,7},{7,6},{8,9},{9,8},{10,11... | collective-permute-start | bytes 196616 | tf_op jit(solution)/shard_map/ppermute | solution.py:315
  146.5 3.4 %copy-start.2 = (bf16[1,64,32,16,128]{4,3,2,1,0:T(8,128)(2,1)S(1)}, bf16[1,64,32,16,128]{4,3,2,1,0:T(8,128)(2,1)}, u32[]{:S(2)}) copy-start(bf16[1,64,32,16,128]{4,3,2,1,0:T(8,128)(2,1)} %param.5) | copy-start | bytes 25165828
  155.9 3.4 %copy-start.3 = (bf16[1,64,32,16,128]{4,3,2,1,0:T(8,128)(2,1)S(1)}, bf16[1,64,32,16,128]{4,3,2,1,0:T(8,128)(2,1)}, u32[]{:S(2)}) copy-start(bf16[1,64,32,16,128]{4,3,2,1,0:T(8,128)(2,1)} %param.5) | copy-start | bytes 25165828
  191.2 3.4 %copy-start.4 = (bf16[1,64,32,16,128]{4,3,2,1,0:T(8,128)(2,1)S(1)}, bf16[1,64,32,16,128]{4,3,2,1,0:T(8,128)(2,1)}, u32[]{:S(2)}) copy-start(bf16[1,64,32,16,128]{4,3,2,1,0:T(8,128)(2,1)} %param.5) | copy-start | bytes 25165828

commit v3 on v2

--- a/solution.py
+++ b/solution.py
@@ -7,7 +7,7 @@
 from jax.sharding import PartitionSpec as P
 
 SUB = 8
-VMEM_BYTES = 32 * 1024 * 1024
+VMEM_BYTES = 48 * 1024 * 1024
 SMALL = pl.CostEstimate(flops=1024, bytes_accessed=1024, transcendentals=0)
 
 
@@ -165,20 +165,21 @@
     )(at.reshape(1), skip.reshape(1), stiff, other)
 
 
-def cut_kernel(at, whole, order, out, sem):
+def cut_kernel(at, whole, *rest):
+    out, sem = rest[-2:]
     copy = pltpu.make_async_copy(whole.at[:, pl.ds(at[0], out.shape[1])], out, sem)
     copy.start()
     copy.wait()
 
 
-def cut(whole, at, count, order):
+def cut(whole, at, count, *orders):
     rows, _, cells_y, cells_z = whole.shape
     return pl.pallas_call(
         cut_kernel,
         grid_spec=pltpu.PrefetchScalarGridSpec(
             num_scalar_prefetch=1,
             grid=(1,),
-            in_specs=[pl.BlockSpec(memory_space=pl.ANY)] * 2,
+            in_specs=[pl.BlockSpec(memory_space=pl.ANY)] * (1 + len(orders)),
             out_specs=pl.BlockSpec(memory_space=pl.ANY),
             scratch_shapes=[pltpu.SemaphoreType.DMA],
         ),
@@ -186,10 +187,10 @@
         compiler_params=params(),
         cost_estimate=SMALL,
         name="cut",
-    )(at.reshape(1), whole, order)
-
-
-def merge_kernel(blk, whole, theirs, node, root):
+    )(at.reshape(1), whole, *orders)
+
+
+def merge_kernel(blk, whole, theirs, order, node, root):
     nodes, rows, _ = whole.shape
     first = blk[0] == 0
     total = None
@@ -209,7 +210,7 @@
     root[...] = total
 
 
-def merge(whole, theirs, blk):
+def merge(whole, theirs, blk, order):
     nodes, rows, _ = whole.shape
     return pl.pallas_call(
         merge_kernel,
@@ -219,6 +220,7 @@
             in_specs=[
                 pl.BlockSpec(whole.shape, lambda g, blk: (0, 0, 0)),
                 pl.BlockSpec(theirs.shape, lambda g, blk: (0, 0, 0)),
+                pl.BlockSpec(memory_space=pl.ANY),
             ],
             out_specs=[
                 pl.BlockSpec((nodes, rows, 2 * rows), lambda g, blk: (0, 0, 0)),
@@ -232,7 +234,7 @@
         compiler_params=params(),
         cost_estimate=SMALL,
         name="merge",
-    )(blk.astype(jnp.int32).reshape(1), whole, theirs)
+    )(blk.astype(jnp.int32).reshape(1), whole, theirs, order)
 
 
 def spread_kernel(block, out):
@@ -265,7 +267,8 @@
 
 
 def vector_kernel(at, spread, own, other, *rest):
-    out = rest[-1]
+    out, order = rest[-2:]
+    order[...] = jnp.zeros_like(order)
     rows, _, cells_y, cells_z = own.shape
     both = jnp.concatenate([split_rows(own[:, 0]), split_rows(other[:, 0])], axis=0)
     made = jnp.dot(spread[...], both, preferred_element_type=jnp.float32)
@@ -297,9 +300,15 @@
             num_scalar_prefetch=1,
             grid=(layers,),
             in_specs=specs,
-            out_specs=pl.BlockSpec((eigs, 1, cells_y, cells_z), lambda g, at: (0, at[0] + g, 0, 0)),
+            out_specs=[
+                pl.BlockSpec((eigs, 1, cells_y, cells_z), lambda g, at: (0, at[0] + g, 0, 0)),
+                pl.BlockSpec((SUB, cells_z), lambda g, at: (0, 0)),
+            ],
         ),
-        out_shape=jax.ShapeDtypeStruct((eigs,) + own.shape[1:], jnp.bfloat16),
+        out_shape=[
+            jax.ShapeDtypeStruct((eigs,) + own.shape[1:], jnp.bfloat16),
+            jax.ShapeDtypeStruct((SUB, cells_z), jnp.float32),
+        ],
         input_output_aliases=aliases,
         compiler_params=params(),
         cost_estimate=SMALL,
@@ -346,17 +355,18 @@
         forward, back = half + 1 + offset, half - 1 - offset - count
         return jnp.where(top == 0, forward, back).astype(jnp.int32)
 
-    def send(at, count):
-        return swap(lax.dynamic_slice_in_dim(own, at, count, axis=1))
+    def send(at, count, *orders):
+        return swap(cut(own, at, count, *orders))
 
     nears = shares(half + 1, 2)
-    last = half // 8
-    fars = shares(half - 1 - last, 1)
+    last = half // 16
+    middle = half // 4
+    fars = [half - 1 - middle - last, middle, last]
     near_at = [sum(nears[:i]) for i in range(len(nears))]
     far_at = [sum(fars[:i]) for i in range(len(fars))]
 
     near = [send(spot(o, n, 1 - upper), n) for o, n in zip(near_at, nears)]
-    far = [send(far_spot(o, n, 1 - upper), n) for o, n in zip(far_at, fars)]
+    far = [send(far_spot(far_at[0], fars[0], 1 - upper), fars[0])]
     size = lax.axis_size("dof")
     low = lax.ppermute(own[:, -1:], "dof", [(i, i + 1) for i in range(size - 1)])
     high = lax.ppermute(own[:, :1], "dof", [(i + 1, i) for i in range(size - 1)])
@@ -388,15 +398,16 @@
     belongs = (parent[leaf] == jnp.arange(nodes, dtype=jnp.int32)).astype(jnp.float32)
     whole = paired_sum(belongs[:, None, None] * whole[None], "leaf")
     theirs = swap(whole[:, :, rows:])
-    final = swap(cut(own, far_spot(sum(fars), last, 1 - upper), last, whole))
+    far += [send(far_spot(o, n, 1 - upper), n, whole) for o, n in zip(far_at[1:], fars[1:])]
 
     vectors = None
     for chunk, offset, count in zip(near, near_at, nears):
-        vectors = expand(spread, own, chunk, spot(offset, count, upper), vectors)
-    for chunk, offset, count in zip(far, far_at, fars):
-        vectors = expand(spread, own, chunk, far_spot(offset, count, upper), vectors)
-    node_stiffness, root_stiffness = merge(whole, theirs, blk)
-    vectors = expand(spread, own, final, far_spot(sum(fars), last, upper), vectors)
+        vectors, _ = expand(spread, own, chunk, spot(offset, count, upper), vectors)
+    places = [far_spot(o, n, upper) for o, n in zip(far_at, fars)]
+    for chunk, at in zip(far[:-1], places[:-1]):
+        vectors, order = expand(spread, own, chunk, at, vectors)
+    node_stiffness, root_stiffness = merge(whole, theirs, blk, order)
+    vectors, _ = expand(spread, own, far[-1], places[-1], vectors)
     return (node_stiffness, root_stiffness, vectors[None])
 
 

time: 210 us -> 391 us (1.86)
  Pallas kernels: 81.1 us -> 347 us
  waiting for transfers between devices: 73.4 us -> 16.1 us
  local copies, waits for them, and re-layouts: 32.8 us -> 4.47 us
    pallas_call x1 -> x5, Pallas kernels: 0.81 us -> 260 us  [cut(): pl.pallas_call(cut_kernel, grid_spec=pltpu.PrefetchScalarGridSpec(num_sca...]
    ppermute x5 -> x6, waiting for transfers between devices: 53.7 us -> 0.02 us  [swap(): return lax.ppermute(x, 'blk', [(0, 1), (1, 0)])]
    unnamed x18 -> x8, local copies, waits for them, and re-layouts: 16.9 us -> 0.03 us
    dynamic_slice x3 -> x0, local copies, waits for them, and re-layouts: 11.4 us -> none  [send(): return swap(lax.dynamic_slice_in_dim(own, at, count, axis=1))]
    pallas_call x4 -> x5, Pallas kernels: 27.3 us -> 31.8 us  [expand(): pl.pallas_call(vector_kernel, grid_spec=pltpu.PrefetchScalarGridSpec(num_...]
  transfers between devices with their start and end apart: 12 -> 13, of which waited for: 8 -> 4; matrix products, arithmetic and copies ran while one was open for 7% -> 2% of each run, Pallas kernels for 38% -> 70%
where the time goes in v3:
time: 391 us; the launch traced here: 389 us
  Pallas kernels  347 us (89%)
  starting transfers between devices  18.9 us (5%)
  waiting for transfers between devices  16.1 us (4%)
  local copies, waits for them, and re-layouts  4.47 us (1%)
    pallas_call x5, Pallas kernels, cut(): pl.pallas_call(cut_kernel, grid_spec=pltpu.PrefetchScalarGridSpec(num_sca...  260 us
    pallas_call x1, Pallas kernels, stiff_terms(): pl.pallas_call(stiff_kernel, grid=(layers,), in_specs=[pl.BlockSpec(block...  40.1 us
    pallas_call x5, Pallas kernels, expand(): pl.pallas_call(vector_kernel, grid_spec=pltpu.PrefetchScalarGridSpec(num_...  31.8 us
    pallas_call x2, Pallas kernels, cross_terms(): pl.pallas_call(cross_kernel, grid_spec=pltpu.PrefetchScalarGridSpec(num_s...  13.1 us
    ppermute x1, waiting for transfers between devices, line_sum(): outer = lax.ppermute(x, axis, [(1, 0), (2, 3)])  8.46 us
  transfers between devices with their start and end apart: 13, of which 4 were waited for; matrix products, arithmetic and copies ran while one was open for 2% of the time, Pallas kernels for 70%

profile of v3, /device:TPU:0, one launch (start us, length us, event | category | flops | bytes accessed | tf_op | source)
XLA Modules:
  0.0 389.1 jit_solution(3363521185259808567)
XLA Ops:
  0.6 72.6 %cut.5 = bf16[64,9,16,128]{3,2,1,0:T(8,128)(2,1)} custom-call(s32[1]{0:T(128)} %bitcast.6.at, bf16[64,32,16,128]{3,2,1,0:T(8,128)(2,1)} %bitcast.48), custom_call_target="tpu_custom_call" | custom-call | flops 1024 | bytes 1024 | tf_op jit(solution)/shard_map/cut/pallas_call | solution.py:177
  73.2 3.0 collective-permute-start.2
  76.3 64.6 %cut.6 = bf16[64,8,16,128]{3,2,1,0:T(8,128)(2,1)} custom-call(s32[1]{0:T(128)} %bitcast.15.at, bf16[64,32,16,128]{3,2,1,0:T(8,128)(2,1)} %bitcast.49), custom_call_target="tpu_custom_call" | custom-call | flops 1024 | bytes 1024 | tf_op jit(solution)/shard_map/cut/pallas_call | solution.py:177
  141.0 1.9 fusion.11
  142.9 3.9 %collective-permute-start = (bf16[64,1,16,128]{3,2,1,0:T(8,128)(2,1)}, bf16[64,1,16,128]{3,2,1,0:T(8,128)(2,1)S(1)}, u32[]{:S(2)}, u32[]{:S(2)}) collective-permute-start(bf16[64,1,16,128]{3,2,1,0:T(8,128)(2,1)} %get-tuple-element.28), channel_id=1, source_target_pairs={{0,2},{2,4},{4,6},{1,3},{3,5},{5,7},{8,10},{10,12},{12,14},{9,11},... | collective-permute-start | bytes 786440 | tf_op jit(solution)/shard_map/ppermute | solution.py:371
  146.9 1.3 collective-permute-start.1
  148.2 80.5 %cut.8 = bf16[64,10,16,128]{3,2,1,0:T(8,128)(2,1)} custom-call(s32[1]{0:T(128)} %bitcast.22.at, bf16[64,32,16,128]{3,2,1,0:T(8,128)(2,1)} %bitcast.51), custom_call_target="tpu_custom_call" | custom-call | flops 1024 | bytes 1024 | tf_op jit(solution)/shard_map/cut/pallas_call | solution.py:177
  228.7 1.6 collective-permute-start.11
  230.3 1.1 constant_dynamic-slice_fusion.1
  231.4 40.1 %stiff_terms.1 = (bf16[32,512,256]{2,1,0:T(8,128)(2,1)}, f32[64,64]{1,0:T(8,128)S(1)}, f32[64,64]{1,0:T(8,128)S(1)}) custom-call(bf16[64,32,16,128]{3,2,1,0:T(8,128)(2,1)} %bitcast.52, bf16[64,32,16,128]{3,2,1,0:T(8,128)(2,1)} %bitcast.53, bf16[64,32,16,128]{3,2,1,0:T(8,128)(2,1)} %bitcast.54, bf16[64,1,16,128]{3,2,1,0:T(8,128)(2,1)S(1)} %collective-permute-done.low, ...), custom_call_target="tpu_custom_call" | custom-call | flops 1024 | bytes 1024 | tf_op jit(solution)/shard_map/stiff_terms/pallas_call | solution.py:99
  271.5 6.7 %cross_terms.3 = f32[64,64]{1,0:T(8,128)S(1)} custom-call(s32[1]{0:T(128)} %bitcast.14.at, s32[1]{0:T(128)} %constant.57.clone.1.skip, bf16[32,512,256]{2,1,0:T(8,128)(2,1)} %get-tuple-element.15.stiff, bf16[64,8,16,128]{3,2,1,0:T(8,128)(2,1)} %collective-permute-done.3.other), custom_call_target="tpu_custom_call" | custom-call | flops 1024 | bytes 1024 | tf_op jit(solution)/shard_map/cross_terms/pallas_call | solution.py:149
  278.6 6.3 %cross_terms.2 = f32[64,64]{1,0:T(8,128)S(1)} custom-call(s32[1]{0:T(128)} %bitcast.12.at, s32[1]{0:T(128)} %bitcast.13.skip, bf16[32,512,256]{2,1,0:T(8,128)(2,1)} %get-tuple-element.15.stiff, bf16[64,9,16,128]{3,2,1,0:T(8,128)(2,1)S(1)} %collective-permute-done.2.other), custom_call_target="tpu_custom_call" | custom-call | flops 1024 | bytes 1024 | tf_op jit(solution)/shard_map/cross_terms/pallas_call | solution.py:149
  285.3 2.7 collective-permute-start.4
  287.9 2.2 collective-permute-done.4
  290.3 0.7 collective-permute-start.5
  291.6 1.3 collective-permute-start.6
  292.9 0.7 compare_convert_fusion
  293.5 8.5 %collective-permute-done.6 = f32[64,192]{1,0:T(8,128)S(1)} collective-permute-done((f32[64,192]{1,0:T(8,128)S(1)}, f32[64,192]{1,0:T(8,128)S(1)}, u32[]{:S(2)}, u32[]{:S(2)}) %collective-permute-start.6) | collective-permute-done | bytes 49184 | tf_op jit(solution)/shard_map/ppermute | solution.py:338
  302.2 1.3 collective-permute-done.7
  303.6 1.6 collective-permute-start.8
  305.1 4.1 %collective-permute-done.8 = f32[2,64,192]{2,1,0:T(8,128)S(1)} collective-permute-done((f32[2,64,192]{2,1,0:T(8,128)S(1)}, f32[2,64,192]{2,1,0:T(8,128)S(1)}, u32[]{:S(2)}, u32[]{:S(2)}) %collective-permute-start.8) | collective-permute-done | bytes 98336 | tf_op jit(solution)/shard_map/ppermute | solution.py:330
  309.3 32.9 %cut.7 = bf16[64,4,16,128]{3,2,1,0:T(8,128)(2,1)} custom-call(s32[1]{0:T(128)} %bitcast.20.at, bf16[64,32,16,128]{3,2,1,0:T(8,128)(2,1)} %bitcast.55, f32[2,64,192]{2,1,0:T(8,128)S(1)} %fusion.12.rest_0_.whole), custom_call_target="tpu_custom_call" | custom-call | flops 1024 | bytes 1024 | tf_op jit(solution)/shard_map/cut/pallas_call | solution.py:177
  342.2 0.6 collective-permute-start.10
  342.8 9.0 %cut.9 = bf16[64,1,16,128]{3,2,1,0:T(8,128)(2,1)} custom-call(s32[1]{0:T(128)} %bitcast.25.at, bf16[64,32,16,128]{3,2,1,0:T(8,128)(2,1)} %bitcast.56, f32[2,64,192]{2,1,0:T(8,128)S(1)} %fusion.12.rest_0_.whole), custom_call_target="tpu_custom_call" | custom-call | flops 1024 | bytes 1024 | tf_op jit(solution)/shard_map/cut/pallas_call | solution.py:177
  351.9 1.6 collective-permute-start.12
  353.5 0.7 slice.14
  355.4 8.2 %expand.5 = (bf16[64,32,16,128]{3,2,1,0:T(8,128)(2,1)}, f32[8,128]{1,0:T(8,128)}) custom-call(s32[1]{0:T(128)} %bitcast.23.at, bf16[512,1024]{1,0:T(8,128)(2,1)S(1)} %spread_blocks.1.spread, bf16[64,32,16,128]{3,2,1,0:T(8,128)(2,1)} %bitcast.57, bf16[64,9,16,128]{3,2,1,0:T(8,128)(2,1)S(1)} %collective-permute-done.2.other), custom_call_target="tpu_custom_call" | custom-call | flops 1024 | bytes 1024 | tf_op jit(solution)/shard_map/expand/pallas_call | solution.py:297
  363.7 7.7 %expand.6 = (bf16[64,32,16,128]{3,2,1,0:T(8,128)(2,1)}, f32[8,128]{1,0:T(8,128)}) custom-call(s32[1]{0:T(128)} %bitcast.14.at, bf16[512,1024]{1,0:T(8,128)(2,1)S(1)} %spread_blocks.1.spread, bf16[64,32,16,128]{3,2,1,0:T(8,128)(2,1)} %bitcast.58, bf16[64,8,16,128]{3,2,1,0:T(8,128)(2,1)} %collective-permute-done.3.other, ...), custom_call_target="tpu_custom_call", output_to_operand_aliasing={{0}: (4, {})} | custom-call | flops 1024 | bytes 1024 | tf_op jit(solution)/shard_map/expand/pallas_call | solution.py:297
  371.3 9.3 %expand.7 = (bf16[64,32,16,128]{3,2,1,0:T(8,128)(2,1)}, f32[8,128]{1,0:T(8,128)}) custom-call(s32[1]{0:T(128)} %bitcast.21.at, bf16[512,1024]{1,0:T(8,128)(2,1)S(1)} %spread_blocks.1.spread, bf16[64,32,16,128]{3,2,1,0:T(8,128)(2,1)} %bitcast.59, bf16[64,10,16,128]{3,2,1,0:T(8,128)(2,1)} %collective-permute-done.11.other, ...), custom_call_target="tpu_custom_call", output_to_operand_aliasing={{0}: (4, {})} | custom-call | flops 1024 | bytes 1024 | tf_op jit(solution)/shard_map/expand/pallas_call | solution.py:297
  380.6 4.4 %expand.8 = (bf16[64,32,16,128]{3,2,1,0:T(8,128)(2,1)}, f32[8,128]{1,0:T(8,128)S(1)}) custom-call(s32[1]{0:T(128)} %bitcast.16.at, bf16[512,1024]{1,0:T(8,128)(2,1)S(1)} %spread_blocks.1.spread, bf16[64,32,16,128]{3,2,1,0:T(8,128)(2,1)} %bitcast.60, bf16[64,4,16,128]{3,2,1,0:T(8,128)(2,1)} %collective-permute-done.10.other, ...), custom_call_target="tpu_custom_call", output_to_operand_aliasing={{0}: (4, {})} | custom-call | flops 1024 | bytes 1024 | tf_op jit(solution)/shard_map/expand/pallas_call | solution.py:297
  385.1 1.9 merge.1
  386.9 2.2 expand.9
  (34 shorter events, 3.0 us)
Async XLA Ops:
  73.2 205.0 %collective-permute-start.2 = (bf16[64,9,16,128]{3,2,1,0:T(8,128)(2,1)}, bf16[64,9,16,128]{3,2,1,0:T(8,128)(2,1)S(1)}, u32[]{:S(2)}, u32[]{:S(2)}) collective-permute-start(bf16[64,9,16,128]{3,2,1,0:T(8,128)(2,1)} %cut.5), channel_id=1, source_target_pairs={{0,1},{1,0},{2,3},{3,2},{4,5},{5,4},{6,7},{7,6},{8,9},{9,8},{10,11... | collective-permute-start | bytes 7077896 | tf_op jit(solution)/shard_map/ppermute | solution.py:324
  140.9 90.5 %copy-start = (f32[1,32,16,128]{3,2,1,0:T(8,128)S(1)}, f32[1,32,16,128]{3,2,1,0:T(8,128)}, u32[]{:S(2)}) copy-start(f32[1,32,16,128]{3,2,1,0:T(8,128)} %param.6) | copy-start | bytes 786436
  140.9 90.5 %copy-start.1 = (f32[1,32,16,128]{3,2,1,0:T(8,128)S(1)}, f32[1,32,16,128]{3,2,1,0:T(8,128)}, u32[]{:S(2)}) copy-start(f32[1,32,16,128]{3,2,1,0:T(8,128)} %param.7) | copy-start | bytes 786436
  140.9 130.6 %collective-permute-start.3 = (bf16[64,8,16,128]{3,2,1,0:T(8,128)(2,1)}, bf16[64,8,16,128]{3,2,1,0:T(8,128)(2,1)}, u32[]{:S(2)}, u32[]{:S(2)}) collective-permute-start(bf16[64,8,16,128]{3,2,1,0:T(8,128)(2,1)} %cut.6), channel_id=1, source_target_pairs={{0,1},{1,0},{2,3},{3,2},{4,5},{5,4},{6,7},{7,6},{8,9},{9,8},{10,11... | collective-permute-start | bytes 6291464 | tf_op jit(solution)/shard_map/ppermute | solution.py:324
  142.9 88.4 %collective-permute-start = (bf16[64,1,16,128]{3,2,1,0:T(8,128)(2,1)}, bf16[64,1,16,128]{3,2,1,0:T(8,128)(2,1)S(1)}, u32[]{:S(2)}, u32[]{:S(2)}) collective-permute-start(bf16[64,1,16,128]{3,2,1,0:T(8,128)(2,1)} %get-tuple-element.28), channel_id=1, source_target_pairs={{0,2},{2,4},{4,6},{1,3},{3,5},{5,7},{8,10},{10,12},{12,14},{9,11},... | collective-permute-start | bytes 786440 | tf_op jit(solution)/shard_map/ppermute | solution.py:371
  146.9 84.5 %collective-permute-start.1 = (bf16[64,1,16,128]{3,2,1,0:T(8,128)(2,1)}, bf16[64,1,16,128]{3,2,1,0:T(8,128)(2,1)S(1)}, u32[]{:S(2)}, u32[]{:S(2)}) collective-permute-start(bf16[64,1,16,128]{3,2,1,0:T(8,128)(2,1)} %get-tuple-element.27), channel_id=1, source_target_pairs={{2,0},{4,2},{6,4},{3,1},{5,3},{7,5},{10,8},{12,10},{14,12},{11,9},... | collective-permute-start | bytes 786440 | tf_op jit(solution)/shard_map/ppermute | solution.py:372
  228.7 142.6 %collective-permute-start.11 = (bf16[64,10,16,128]{3,2,1,0:T(8,128)(2,1)}, bf16[64,10,16,128]{3,2,1,0:T(8,128)(2,1)}, u32[]{:S(2)}, u32[]{:S(2)}) collective-permute-start(bf16[64,10,16,128]{3,2,1,0:T(8,128)(2,1)} %cut.8), channel_id=1, source_target_pairs={{0,1},{1,0},{2,3},{3,2},{4,5},{5,4},{6,7},{7,6},{8,9},{9,8},{10,11... | collective-permute-start | bytes 7864328 | tf_op jit(solution)/shard_map/ppermute | solution.py:324
  278.3 12.7 %copy-start.3 = (s32[4]{0:T(128)S(1)}, s32[4]{0:T(128)}, u32[]{:S(2)}) copy-start(s32[4]{0:T(128)} %param.9) | copy-start | bytes 52
  285.3 4.9 %collective-permute-start.4 = (f32[64,192]{1,0:T(8,128)S(1)}, f32[64,192]{1,0:T(8,128)S(1)}, u32[]{:S(2)}, u32[]{:S(2)}) collective-permute-start(f32[64,192]{1,0:T(8,128)S(1)} %pad_maximum_fusion), channel_id=1, source_target_pairs={{0,2},{2,0},{4,6},{6,4},{1,3},{3,1},{5,7},{7,5},{8,10},{10,8},{12,... | collective-permute-start | bytes 147464 | tf_op jit(solution)/shard_map/ppermute | solution.py:336
  290.3 1.3 collective-permute-start.5
  291.6 10.4 %collective-permute-start.6 = (f32[64,192]{1,0:T(8,128)S(1)}, f32[64,192]{1,0:T(8,128)S(1)}, u32[]{:S(2)}, u32[]{:S(2)}) collective-permute-start(f32[64,192]{1,0:T(8,128)S(1)} %add.50), channel_id=1, source_target_pairs={{2,0},{4,6},{3,1},{5,7},{10,8},{12,14},{11,9},{13,15},{18,16},{20,... | collective-permute-start | bytes 147464 | tf_op jit(solution)/shard_map/ppermute | solution.py:338
  302.1 1.4 collective-permute-start.7
  303.6 5.6 %collective-permute-start.8 = (f32[2,64,192]{2,1,0:T(8,128)S(1)}, f32[2,64,192]{2,1,0:T(8,128)S(1)}, u32[]{:S(2)}, u32[]{:S(2)}) collective-permute-start(f32[2,64,192]{2,1,0:T(8,128)S(1)} %fusion.10), channel_id=1, source_target_pairs={{0,16},{8,24},{16,0},{24,8},{1,17},{9,25},{17,1},{25,9},{2,18},{10... | collective-permute-start | bytes 294920 | tf_op jit(solution)/shard_map/ppermute | solution.py:330
  309.3 44.1 %copy-start.2 = (bf16[1,128,64]{1,2,0:T(8,128)(2,1)S(1)}, bf16[1,128,64]{1,2,0:T(8,128)(2,1)}, u32[]{:S(2)}) copy-start(bf16[1,128,64]{1,2,0:T(8,128)(2,1)} %param.8) | copy-start | bytes 49156
  342.2 38.5 %collective-permute-start.10 = (bf16[64,4,16,128]{3,2,1,0:T(8,128)(2,1)}, bf16[64,4,16,128]{3,2,1,0:T(8,128)(2,1)}, u32[]{:S(2)}, u32[]{:S(2)}) collective-permute-start(bf16[64,4,16,128]{3,2,1,0:T(8,128)(2,1)} %cut.7), channel_id=1, source_target_pairs={{0,1},{1,0},{2,3},{3,2},{4,5},{5,4},{6,7},{7,6},{8,9},{9,8},{10,11... | collective-permute-start | bytes 3145736 | tf_op jit(solution)/shard_map/ppermute | solution.py:324
  351.9 35.1 %collective-permute-start.12 = (bf16[64,1,16,128]{3,2,1,0:T(8,128)(2,1)}, bf16[64,1,16,128]{3,2,1,0:T(8,128)(2,1)}, u32[]{:S(2)}, u32[]{:S(2)}) collective-permute-start(bf16[64,1,16,128]{3,2,1,0:T(8,128)(2,1)} %cut.9), channel_id=1, source_target_pairs={{0,1},{1,0},{2,3},{3,2},{4,5},{5,4},{6,7},{7,6},{8,9},{9,8},{10,11... | collective-permute-start | bytes 786440 | tf_op jit(solution)/shard_map/ppermute | solution.py:324
  354.2 30.9 %collective-permute-start.9 = (f32[2,64,128]{2,1,0:T(8,128)}, f32[2,64,128]{2,1,0:T(8,128)}, u32[]{:S(2)}, u32[]{:S(2)}) collective-permute-start(f32[2,64,128]{2,1,0:T(8,128)} %slice.14), channel_id=1, source_target_pairs={{0,1},{1,0},{2,3},{3,2},{4,5},{5,4},{6,7},{7,6},{8,9},{9,8},{10,11... | collective-permute-start | bytes 196616 | tf_op jit(solution)/shard_map/ppermute | solution.py:324

commit v4 on v3

--- a/solution.py
+++ b/solution.py
@@ -166,14 +166,31 @@
 
 
 def cut_kernel(at, whole, *rest):
-    out, sem = rest[-2:]
-    copy = pltpu.make_async_copy(whole.at[:, pl.ds(at[0], out.shape[1])], out, sem)
-    copy.start()
-    copy.wait()
+    out, held, reads, writes = rest[-4:]
+    pieces = held.shape[0]
+    layers = out.shape[1]
+    bounds = [layers * i // pieces for i in range(pieces + 1)]
+    ins, outs = [], []
+    for i in range(pieces):
+        start, size = bounds[i], bounds[i + 1] - bounds[i]
+        piece = held.at[i, :, pl.ds(0, size)]
+        ins.append(
+            pltpu.make_async_copy(whole.at[:, pl.ds(at[0] + start, size)], piece, reads.at[i])
+        )
+        outs.append(pltpu.make_async_copy(piece, out.at[:, pl.ds(start, size)], writes.at[i]))
+    for copy in ins:
+        copy.start()
+    for i in range(pieces):
+        ins[i].wait()
+        outs[i].start()
+    for copy in outs:
+        copy.wait()
 
 
 def cut(whole, at, count, *orders):
     rows, _, cells_y, cells_z = whole.shape
+    pieces = min(4, count)
+    longest = -(-count // pieces)
     return pl.pallas_call(
         cut_kernel,
         grid_spec=pltpu.PrefetchScalarGridSpec(
@@ -181,7 +198,11 @@
             grid=(1,),
             in_specs=[pl.BlockSpec(memory_space=pl.ANY)] * (1 + len(orders)),
             out_specs=pl.BlockSpec(memory_space=pl.ANY),
-            scratch_shapes=[pltpu.SemaphoreType.DMA],
+            scratch_shapes=[
+                pltpu.VMEM((pieces, rows, longest, cells_y, cells_z), whole.dtype),
+                pltpu.SemaphoreType.DMA((pieces,)),
+                pltpu.SemaphoreType.DMA((pieces,)),
+            ],
         ),
         out_shape=jax.ShapeDtypeStruct((rows, count, cells_y, cells_z), whole.dtype),
         compiler_params=params(),

time: 391 us -> 195 us (0.50)
  Pallas kernels: 347 us -> 99 us
  waiting for transfers between devices: 16.1 us -> 67.2 us
    pallas_call x5, Pallas kernels: 260 us -> 11.6 us  [cut(): pl.pallas_call(cut_kernel, grid_spec=pltpu.PrefetchScalarGridSpec(num_sca...]
    ppermute x6, waiting for transfers between devices: 0.02 us -> 48.5 us  [swap(): return lax.ppermute(x, 'blk', [(0, 1), (1, 0)])]
  transfers between devices with their start and end apart: 13 -> 13, of which waited for: 4 -> 8; matrix products, arithmetic and copies ran while one was open for 2% -> 3% of each run, Pallas kernels for 70% -> 49%
where the time goes in v4:
time: 195 us; the launch traced here: 193 us
  Pallas kernels  99 us (51%)
  waiting for transfers between devices  67.2 us (34%)
  starting transfers between devices  19.4 us (10%)
  local copies, waits for them, and re-layouts  4.47 us (2%)
    ppermute x6, waiting for transfers between devices, swap(): return lax.ppermute(x, 'blk', [(0, 1), (1, 0)])  48.5 us
    pallas_call x1, Pallas kernels, stiff_terms(): pl.pallas_call(stiff_kernel, grid=(layers,), in_specs=[pl.BlockSpec(block...  40.1 us
    pallas_call x5, Pallas kernels, expand(): pl.pallas_call(vector_kernel, grid_spec=pltpu.PrefetchScalarGridSpec(num_...  31.8 us
    pallas_call x2, Pallas kernels, cross_terms(): pl.pallas_call(cross_kernel, grid_spec=pltpu.PrefetchScalarGridSpec(num_s...  13.1 us
    pallas_call x5, Pallas kernels, cut(): pl.pallas_call(cut_kernel, grid_spec=pltpu.PrefetchScalarGridSpec(num_sca...  11.6 us
    ppermute x1, waiting for transfers between devices, line_sum(): outer = lax.ppermute(x, axis, [(1, 0), (2, 3)])  8.46 us
    ppermute x6, starting transfers between devices, swap(): return lax.ppermute(x, 'blk', [(0, 1), (1, 0)])  8.41 us
    ppermute x2, waiting for transfers between devices, paired_sum(): x = x + lax.ppermute(x, axis, [(i, i ^ step) for i in range(size)])  5.39 us
  transfers between devices with their start and end apart: 13, of which 8 were waited for; matrix products, arithmetic and copies ran while one was open for 3% of the time, Pallas kernels for 49%

profile of v4, /device:TPU:0, one launch (start us, length us, event | category | flops | bytes accessed | tf_op | source)
XLA Modules:
  0.0 192.5 jit_solution(16465232075533386339)
XLA Ops:
  0.6 2.6 %cut.5 = bf16[64,9,16,128]{3,2,1,0:T(8,128)(2,1)} custom-call(s32[1]{0:T(128)} %bitcast.6.at, bf16[64,32,16,128]{3,2,1,0:T(8,128)(2,1)} %bitcast.48), custom_call_target="tpu_custom_call" | custom-call | flops 1024 | bytes 1024 | tf_op jit(solution)/shard_map/cut/pallas_call | solution.py:194
  3.3 3.0 %collective-permute-start.2 = (bf16[64,9,16,128]{3,2,1,0:T(8,128)(2,1)}, bf16[64,9,16,128]{3,2,1,0:T(8,128)(2,1)S(1)}, u32[]{:S(2)}, u32[]{:S(2)}) collective-permute-start(bf16[64,9,16,128]{3,2,1,0:T(8,128)(2,1)} %cut.5), channel_id=1, source_target_pairs={{0,1},{1,0},{2,3},{3,2},{4,5},{5,4},{6,7},{7,6},{8,9},{9,8},{10,11... | collective-permute-start | bytes 7077896 | tf_op jit(solution)/shard_map/ppermute | solution.py:345
  6.3 2.5 %cut.6 = bf16[64,8,16,128]{3,2,1,0:T(8,128)(2,1)} custom-call(s32[1]{0:T(128)} %bitcast.15.at, bf16[64,32,16,128]{3,2,1,0:T(8,128)(2,1)} %bitcast.49), custom_call_target="tpu_custom_call" | custom-call | flops 1024 | bytes 1024 | tf_op jit(solution)/shard_map/cut/pallas_call | solution.py:194
  8.9 1.9 fusion.11
  10.8 3.9 %collective-permute-start = (bf16[64,1,16,128]{3,2,1,0:T(8,128)(2,1)}, bf16[64,1,16,128]{3,2,1,0:T(8,128)(2,1)S(1)}, u32[]{:S(2)}, u32[]{:S(2)}) collective-permute-start(bf16[64,1,16,128]{3,2,1,0:T(8,128)(2,1)} %get-tuple-element.28), channel_id=1, source_target_pairs={{0,2},{2,4},{4,6},{1,3},{3,5},{5,7},{8,10},{10,12},{12,14},{9,11},... | collective-permute-start | bytes 786440 | tf_op jit(solution)/shard_map/ppermute | solution.py:392
  14.8 1.3 collective-permute-start.1
  16.1 2.7 %cut.8 = bf16[64,10,16,128]{3,2,1,0:T(8,128)(2,1)} custom-call(s32[1]{0:T(128)} %bitcast.22.at, bf16[64,32,16,128]{3,2,1,0:T(8,128)(2,1)} %bitcast.51), custom_call_target="tpu_custom_call" | custom-call | flops 1024 | bytes 1024 | tf_op jit(solution)/shard_map/cut/pallas_call | solution.py:194
  18.8 1.6 collective-permute-start.11
  21.5 2.6 %collective-permute-done.1.high = bf16[64,1,16,128]{3,2,1,0:T(8,128)(2,1)S(1)} collective-permute-done((bf16[64,1,16,128]{3,2,1,0:T(8,128)(2,1)}, bf16[64,1,16,128]{3,2,1,0:T(8,128)(2,1)S(1)}, u32[]{:S(2)}, u32[]{:S(2)}) %collective-permute-start.1) | collective-permute-done | bytes 262176 | tf_op jit(solution)/shard_map/ppermute | solution.py:393
  24.1 40.1 %stiff_terms.1 = (bf16[32,512,256]{2,1,0:T(8,128)(2,1)}, f32[64,64]{1,0:T(8,128)S(1)}, f32[64,64]{1,0:T(8,128)S(1)}) custom-call(bf16[64,32,16,128]{3,2,1,0:T(8,128)(2,1)} %bitcast.52, bf16[64,32,16,128]{3,2,1,0:T(8,128)(2,1)} %bitcast.53, bf16[64,32,16,128]{3,2,1,0:T(8,128)(2,1)} %bitcast.54, bf16[64,1,16,128]{3,2,1,0:T(8,128)(2,1)S(1)} %collective-permute-done.low, ...), custom_call_target="tpu_custom_call" | custom-call | flops 1024 | bytes 1024 | tf_op jit(solution)/shard_map/stiff_terms/pallas_call | solution.py:99
  64.2 39.5 %collective-permute-done.3.other = bf16[64,8,16,128]{3,2,1,0:T(8,128)(2,1)} collective-permute-done((bf16[64,8,16,128]{3,2,1,0:T(8,128)(2,1)}, bf16[64,8,16,128]{3,2,1,0:T(8,128)(2,1)}, u32[]{:S(2)}, u32[]{:S(2)}) %collective-permute-start.3) | collective-permute-done | bytes 2097184 | tf_op jit(solution)/shard_map/ppermute | solution.py:345
  103.6 6.7 %cross_terms.3 = f32[64,64]{1,0:T(8,128)S(1)} custom-call(s32[1]{0:T(128)} %bitcast.14.at, s32[1]{0:T(128)} %constant.57.clone.1.skip, bf16[32,512,256]{2,1,0:T(8,128)(2,1)} %get-tuple-element.15.stiff, bf16[64,8,16,128]{3,2,1,0:T(8,128)(2,1)} %collective-permute-done.3.other), custom_call_target="tpu_custom_call" | custom-call | flops 1024 | bytes 1024 | tf_op jit(solution)/shard_map/cross_terms/pallas_call | solution.py:149
  110.7 6.3 %cross_terms.2 = f32[64,64]{1,0:T(8,128)S(1)} custom-call(s32[1]{0:T(128)} %bitcast.12.at, s32[1]{0:T(128)} %bitcast.13.skip, bf16[32,512,256]{2,1,0:T(8,128)(2,1)} %get-tuple-element.15.stiff, bf16[64,9,16,128]{3,2,1,0:T(8,128)(2,1)S(1)} %collective-permute-done.2.other), custom_call_target="tpu_custom_call" | custom-call | flops 1024 | bytes 1024 | tf_op jit(solution)/shard_map/cross_terms/pallas_call | solution.py:149
  117.4 2.1 %collective-permute-start.4 = (f32[64,192]{1,0:T(8,128)S(1)}, f32[64,192]{1,0:T(8,128)S(1)}, u32[]{:S(2)}, u32[]{:S(2)}) collective-permute-start(f32[64,192]{1,0:T(8,128)S(1)} %pad_maximum_fusion), channel_id=1, source_target_pairs={{0,2},{2,0},{4,6},{6,4},{1,3},{3,1},{5,7},{7,5},{8,10},{10,8},{12,... | collective-permute-start | bytes 147464 | tf_op jit(solution)/shard_map/ppermute | solution.py:357
  119.5 2.2 %collective-permute-done.4 = f32[64,192]{1,0:T(8,128)S(1)} collective-permute-done((f32[64,192]{1,0:T(8,128)S(1)}, f32[64,192]{1,0:T(8,128)S(1)}, u32[]{:S(2)}, u32[]{:S(2)}) %collective-permute-start.4) | collective-permute-done | bytes 49184 | tf_op jit(solution)/shard_map/ppermute | solution.py:357
  123.2 1.3 collective-permute-start.6
  125.1 8.5 %collective-permute-done.6 = f32[64,192]{1,0:T(8,128)S(1)} collective-permute-done((f32[64,192]{1,0:T(8,128)S(1)}, f32[64,192]{1,0:T(8,128)S(1)}, u32[]{:S(2)}, u32[]{:S(2)}) %collective-permute-start.6) | collective-permute-done | bytes 49184 | tf_op jit(solution)/shard_map/ppermute | solution.py:359
  133.8 1.3 collective-permute-done.7
  135.2 1.6 collective-permute-start.8
  136.7 4.1 %collective-permute-done.8 = f32[2,64,192]{2,1,0:T(8,128)S(1)} collective-permute-done((f32[2,64,192]{2,1,0:T(8,128)S(1)}, f32[2,64,192]{2,1,0:T(8,128)S(1)}, u32[]{:S(2)}, u32[]{:S(2)}) %collective-permute-start.8) | collective-permute-done | bytes 98336 | tf_op jit(solution)/shard_map/ppermute | solution.py:351
  140.9 2.0 %cut.7 = bf16[64,4,16,128]{3,2,1,0:T(8,128)(2,1)} custom-call(s32[1]{0:T(128)} %bitcast.20.at, bf16[64,32,16,128]{3,2,1,0:T(8,128)(2,1)} %bitcast.55, f32[2,64,192]{2,1,0:T(8,128)S(1)} %fusion.12.rest_0_.whole), custom_call_target="tpu_custom_call" | custom-call | flops 1024 | bytes 1024 | tf_op jit(solution)/shard_map/cut/pallas_call | solution.py:194
  142.9 1.6 collective-permute-start.10
  144.6 1.7 cut.9
  147.6 1.6 collective-permute-start.9
  149.8 8.2 %expand.5 = (bf16[64,32,16,128]{3,2,1,0:T(8,128)(2,1)}, f32[8,128]{1,0:T(8,128)}) custom-call(s32[1]{0:T(128)} %bitcast.23.at, bf16[512,1024]{1,0:T(8,128)(2,1)S(1)} %spread_blocks.1.spread, bf16[64,32,16,128]{3,2,1,0:T(8,128)(2,1)} %bitcast.57, bf16[64,9,16,128]{3,2,1,0:T(8,128)(2,1)S(1)} %collective-permute-done.2.other), custom_call_target="tpu_custom_call" | custom-call | flops 1024 | bytes 1024 | tf_op jit(solution)/shard_map/expand/pallas_call | solution.py:318
  158.0 7.7 %expand.6 = (bf16[64,32,16,128]{3,2,1,0:T(8,128)(2,1)}, f32[8,128]{1,0:T(8,128)}) custom-call(s32[1]{0:T(128)} %bitcast.14.at, bf16[512,1024]{1,0:T(8,128)(2,1)S(1)} %spread_blocks.1.spread, bf16[64,32,16,128]{3,2,1,0:T(8,128)(2,1)} %bitcast.58, bf16[64,8,16,128]{3,2,1,0:T(8,128)(2,1)} %collective-permute-done.3.other, ...), custom_call_target="tpu_custom_call", output_to_operand_aliasing={{0}: (4, {})} | custom-call | flops 1024 | bytes 1024 | tf_op jit(solution)/shard_map/expand/pallas_call | solution.py:318
  165.7 9.3 %expand.7 = (bf16[64,32,16,128]{3,2,1,0:T(8,128)(2,1)}, f32[8,128]{1,0:T(8,128)}) custom-call(s32[1]{0:T(128)} %bitcast.21.at, bf16[512,1024]{1,0:T(8,128)(2,1)S(1)} %spread_blocks.1.spread, bf16[64,32,16,128]{3,2,1,0:T(8,128)(2,1)} %bitcast.59, bf16[64,10,16,128]{3,2,1,0:T(8,128)(2,1)} %collective-permute-done.11.other, ...), custom_call_target="tpu_custom_call", output_to_operand_aliasing={{0}: (4, {})} | custom-call | flops 1024 | bytes 1024 | tf_op jit(solution)/shard_map/expand/pallas_call | solution.py:318
  175.0 7.3 %collective-permute-done.10.other = bf16[64,4,16,128]{3,2,1,0:T(8,128)(2,1)} collective-permute-done((bf16[64,4,16,128]{3,2,1,0:T(8,128)(2,1)}, bf16[64,4,16,128]{3,2,1,0:T(8,128)(2,1)}, u32[]{:S(2)}, u32[]{:S(2)}) %collective-permute-start.10) | collective-permute-done | bytes 1048608 | tf_op jit(solution)/shard_map/ppermute | solution.py:345
  182.3 4.4 %expand.8 = (bf16[64,32,16,128]{3,2,1,0:T(8,128)(2,1)}, f32[8,128]{1,0:T(8,128)S(1)}) custom-call(s32[1]{0:T(128)} %bitcast.16.at, bf16[512,1024]{1,0:T(8,128)(2,1)S(1)} %spread_blocks.1.spread, bf16[64,32,16,128]{3,2,1,0:T(8,128)(2,1)} %bitcast.60, bf16[64,4,16,128]{3,2,1,0:T(8,128)(2,1)} %collective-permute-done.10.other, ...), custom_call_target="tpu_custom_call", output_to_operand_aliasing={{0}: (4, {})} | custom-call | flops 1024 | bytes 1024 | tf_op jit(solution)/shard_map/expand/pallas_call | solution.py:318
  186.7 1.8 collective-permute-done.9.theirs
  188.5 1.9 merge.1
  190.4 2.2 %expand.9 = (bf16[64,32,16,128]{3,2,1,0:T(8,128)(2,1)}, f32[8,128]{1,0:T(8,128)}) custom-call(s32[1]{0:T(128)} %bitcast.24.at, bf16[512,1024]{1,0:T(8,128)(2,1)S(1)} %spread_blocks.1.spread, bf16[64,32,16,128]{3,2,1,0:T(8,128)(2,1)} %bitcast.61, bf16[64,1,16,128]{3,2,1,0:T(8,128)(2,1)} %collective-permute-done.12.other, ...), custom_call_target="tpu_custom_call", output_to_operand_aliasing={{0}: (4, {})} | custom-call | flops 1024 | bytes 1024 | tf_op jit(solution)/shard_map/expand/pallas_call | solution.py:318
  (34 shorter events, 6.1 us)
Async XLA Ops:
  3.3 107.1 %collective-permute-start.2 = (bf16[64,9,16,128]{3,2,1,0:T(8,128)(2,1)}, bf16[64,9,16,128]{3,2,1,0:T(8,128)(2,1)S(1)}, u32[]{:S(2)}, u32[]{:S(2)}) collective-permute-start(bf16[64,9,16,128]{3,2,1,0:T(8,128)(2,1)} %cut.5), channel_id=1, source_target_pairs={{0,1},{1,0},{2,3},{3,2},{4,5},{5,4},{6,7},{7,6},{8,9},{9,8},{10,11... | collective-permute-start | bytes 7077896 | tf_op jit(solution)/shard_map/ppermute | solution.py:345
  8.8 15.3 %copy-start = (f32[1,32,16,128]{3,2,1,0:T(8,128)S(1)}, f32[1,32,16,128]{3,2,1,0:T(8,128)}, u32[]{:S(2)}) copy-start(f32[1,32,16,128]{3,2,1,0:T(8,128)} %param.6) | copy-start | bytes 786436
  8.8 15.3 %copy-start.1 = (f32[1,32,16,128]{3,2,1,0:T(8,128)S(1)}, f32[1,32,16,128]{3,2,1,0:T(8,128)}, u32[]{:S(2)}) copy-start(f32[1,32,16,128]{3,2,1,0:T(8,128)} %param.7) | copy-start | bytes 786436
  8.8 94.8 %collective-permute-start.3 = (bf16[64,8,16,128]{3,2,1,0:T(8,128)(2,1)}, bf16[64,8,16,128]{3,2,1,0:T(8,128)(2,1)}, u32[]{:S(2)}, u32[]{:S(2)}) collective-permute-start(bf16[64,8,16,128]{3,2,1,0:T(8,128)(2,1)} %cut.6), channel_id=1, source_target_pairs={{0,1},{1,0},{2,3},{3,2},{4,5},{5,4},{6,7},{7,6},{8,9},{9,8},{10,11... | collective-permute-start | bytes 6291464 | tf_op jit(solution)/shard_map/ppermute | solution.py:345
  10.8 10.7 %collective-permute-start = (bf16[64,1,16,128]{3,2,1,0:T(8,128)(2,1)}, bf16[64,1,16,128]{3,2,1,0:T(8,128)(2,1)S(1)}, u32[]{:S(2)}, u32[]{:S(2)}) collective-permute-start(bf16[64,1,16,128]{3,2,1,0:T(8,128)(2,1)} %get-tuple-element.28), channel_id=1, source_target_pairs={{0,2},{2,4},{4,6},{1,3},{3,5},{5,7},{8,10},{10,12},{12,14},{9,11},... | collective-permute-start | bytes 786440 | tf_op jit(solution)/shard_map/ppermute | solution.py:392
  14.8 9.3 %collective-permute-start.1 = (bf16[64,1,16,128]{3,2,1,0:T(8,128)(2,1)}, bf16[64,1,16,128]{3,2,1,0:T(8,128)(2,1)S(1)}, u32[]{:S(2)}, u32[]{:S(2)}) collective-permute-start(bf16[64,1,16,128]{3,2,1,0:T(8,128)(2,1)} %get-tuple-element.27), channel_id=1, source_target_pairs={{2,0},{4,2},{6,4},{3,1},{5,3},{7,5},{10,8},{12,10},{14,12},{11,9},... | collective-permute-start | bytes 786440 | tf_op jit(solution)/shard_map/ppermute | solution.py:393
  18.8 146.9 %collective-permute-start.11 = (bf16[64,10,16,128]{3,2,1,0:T(8,128)(2,1)}, bf16[64,10,16,128]{3,2,1,0:T(8,128)(2,1)}, u32[]{:S(2)}, u32[]{:S(2)}) collective-permute-start(bf16[64,10,16,128]{3,2,1,0:T(8,128)(2,1)} %cut.8), channel_id=1, source_target_pairs={{0,1},{1,0},{2,3},{3,2},{4,5},{5,4},{6,7},{7,6},{8,9},{9,8},{10,11... | collective-permute-start | bytes 7864328 | tf_op jit(solution)/shard_map/ppermute | solution.py:345
  110.4 12.2 %copy-start.3 = (s32[4]{0:T(128)S(1)}, s32[4]{0:T(128)}, u32[]{:S(2)}) copy-start(s32[4]{0:T(128)} %param.9) | copy-start | bytes 52
  117.4 4.4 %collective-permute-start.4 = (f32[64,192]{1,0:T(8,128)S(1)}, f32[64,192]{1,0:T(8,128)S(1)}, u32[]{:S(2)}, u32[]{:S(2)}) collective-permute-start(f32[64,192]{1,0:T(8,128)S(1)} %pad_maximum_fusion), channel_id=1, source_target_pairs={{0,2},{2,0},{4,6},{6,4},{1,3},{3,1},{5,7},{7,5},{8,10},{10,8},{12,... | collective-permute-start | bytes 147464 | tf_op jit(solution)/shard_map/ppermute | solution.py:357
  121.9 1.3 collective-permute-start.5
  123.2 10.4 %collective-permute-start.6 = (f32[64,192]{1,0:T(8,128)S(1)}, f32[64,192]{1,0:T(8,128)S(1)}, u32[]{:S(2)}, u32[]{:S(2)}) collective-permute-start(f32[64,192]{1,0:T(8,128)S(1)} %add.50), channel_id=1, source_target_pairs={{2,0},{4,6},{3,1},{5,7},{10,8},{12,14},{11,9},{13,15},{18,16},{20,... | collective-permute-start | bytes 147464 | tf_op jit(solution)/shard_map/ppermute | solution.py:359
  133.7 1.4 collective-permute-start.7
  135.2 5.6 %collective-permute-start.8 = (f32[2,64,192]{2,1,0:T(8,128)S(1)}, f32[2,64,192]{2,1,0:T(8,128)S(1)}, u32[]{:S(2)}, u32[]{:S(2)}) collective-permute-start(f32[2,64,192]{2,1,0:T(8,128)S(1)} %fusion.10), channel_id=1, source_target_pairs={{0,16},{8,24},{16,0},{24,8},{1,17},{9,25},{17,1},{25,9},{2,18},{10... | collective-permute-start | bytes 294920 | tf_op jit(solution)/shard_map/ppermute | solution.py:351
  140.9 5.9 %copy-start.2 = (bf16[1,128,64]{1,2,0:T(8,128)(2,1)S(1)}, bf16[1,128,64]{1,2,0:T(8,128)(2,1)}, u32[]{:S(2)}) copy-start(bf16[1,128,64]{1,2,0:T(8,128)(2,1)} %param.8) | copy-start | bytes 49156
  142.9 39.3 %collective-permute-start.10 = (bf16[64,4,16,128]{3,2,1,0:T(8,128)(2,1)}, bf16[64,4,16,128]{3,2,1,0:T(8,128)(2,1)}, u32[]{:S(2)}, u32[]{:S(2)}) collective-permute-start(bf16[64,4,16,128]{3,2,1,0:T(8,128)(2,1)} %cut.7), channel_id=1, source_target_pairs={{0,1},{1,0},{2,3},{3,2},{4,5},{5,4},{6,7},{7,6},{8,9},{9,8},{10,11... | collective-permute-start | bytes 3145736 | tf_op jit(solution)/shard_map/ppermute | solution.py:345
  146.2 44.1 %collective-permute-start.12 = (bf16[64,1,16,128]{3,2,1,0:T(8,128)(2,1)}, bf16[64,1,16,128]{3,2,1,0:T(8,128)(2,1)}, u32[]{:S(2)}, u32[]{:S(2)}) collective-permute-start(bf16[64,1,16,128]{3,2,1,0:T(8,128)(2,1)} %cut.9), channel_id=1, source_target_pairs={{0,1},{1,0},{2,3},{3,2},{4,5},{5,4},{6,7},{7,6},{8,9},{9,8},{10,11... | collective-permute-start | bytes 786440 | tf_op jit(solution)/shard_map/ppermute | solution.py:345
  147.6 40.9 %collective-permute-start.9 = (f32[2,64,128]{2,1,0:T(8,128)}, f32[2,64,128]{2,1,0:T(8,128)}, u32[]{:S(2)}, u32[]{:S(2)}) collective-permute-start(f32[2,64,128]{2,1,0:T(8,128)} %slice.14), channel_id=1, source_target_pairs={{0,1},{1,0},{2,3},{3,2},{4,5},{5,4},{6,7},{7,6},{8,9},{9,8},{10,11... | collective-permute-start | bytes 196616 | tf_op jit(solution)/shard_map/ppermute | solution.py:345

commit v5 on v4

--- a/solution.py
+++ b/solution.py
@@ -8,6 +8,8 @@
 
 SUB = 8
 VMEM_BYTES = 48 * 1024 * 1024
+LAST_BYTES = 16 * 1024 * 1024
+PARTS = 5
 SMALL = pl.CostEstimate(flops=1024, bytes_accessed=1024, transcendentals=0)
 
 
@@ -44,7 +46,7 @@
     return jnp.dot(folded, pick, precision=lax.Precision.HIGHEST, preferred_element_type=jnp.float32)
 
 
-def stiff_kernel(own, prev, after, low, high, coefs, masses, stiff, gram, mass, total, flat, acc):
+def stiff_kernel(own, prev, after, low, high, coefs, masses, order, stiff, gram, mass, total, flat, acc):
     layer, last = pl.program_id(0), pl.num_programs(0) - 1
     rows, _, cells_y, cells_z = own.shape
 
@@ -86,12 +88,11 @@
     @pl.when(layer == last)
     def _():
         gram[...] = same_row_sum(total[...])
-        mass[...] = jnp.broadcast_to(
-            jnp.sum(jnp.sum(acc[...], axis=1), axis=1, keepdims=True), mass.shape
-        )
-
-
-def stiff_terms(own, low, high, coefs, masses):
+        column = jnp.sum(jnp.sum(acc[...], axis=1), axis=1, keepdims=True)
+        mass[...] = jnp.broadcast_to(column, (rows, rows)).T[: mass.shape[0]]
+
+
+def stiff_terms(own, low, high, coefs, masses, order):
     rows, layers, cells_y, cells_z = own.shape
     tall, wide = rows * SUB, cells_y // SUB * cells_z
     block = (rows, 1, cells_y, cells_z)
@@ -107,16 +108,17 @@
             pl.BlockSpec(block, lambda g: (0, 0, 0, 0)),
             pl.BlockSpec(cells, lambda g: (g, 0, 0)),
             pl.BlockSpec(cells, lambda g: (g, 0, 0)),
+            pl.BlockSpec(memory_space=pl.ANY),
         ],
         out_specs=[
             pl.BlockSpec((1, tall, wide), lambda g: (g, 0, 0)),
             pl.BlockSpec((rows, rows), lambda g: (0, 0)),
-            pl.BlockSpec((rows, rows), lambda g: (0, 0)),
+            pl.BlockSpec((2 * SUB, rows), lambda g: (0, 0)),
         ],
         out_shape=[
             jax.ShapeDtypeStruct((layers, tall, wide), jnp.bfloat16),
             jax.ShapeDtypeStruct((rows, rows), jnp.float32),
-            jax.ShapeDtypeStruct((rows, rows), jnp.float32),
+            jax.ShapeDtypeStruct((2 * SUB, rows), jnp.float32),
         ],
         scratch_shapes=[
             pltpu.VMEM((tall, tall), jnp.float32),
@@ -126,7 +128,7 @@
         compiler_params=params(),
         cost_estimate=SMALL,
         name="stiff_terms",
-    )(own, own, own, low, high, coefs, masses)
+    )(own, own, own, low, high, coefs, masses, order)
 
 
 def cross_kernel(at, skip, stiff, other, gram, total):
@@ -211,28 +213,31 @@
     )(at.reshape(1), whole, *orders)
 
 
-def merge_kernel(blk, whole, theirs, order, node, root):
-    nodes, rows, _ = whole.shape
+def merge_kernel(blk, whole, theirs, node, root):
+    nodes, _, both = whole.shape
+    rows = both // 2
     first = blk[0] == 0
     total = None
     for p in range(nodes):
-        gram = whole[p, :, :rows]
-        cross = whole[p, :, rows : 2 * rows] + theirs[p, :, :rows].T
-        scale = 1.0 / jnp.sqrt(whole[p, :, 2 * rows :])
-        scale_gram = scale.T
-        scale_cross = (1.0 / jnp.sqrt(theirs[p, :, rows:])).T
+        here = slice(p * rows, (p + 1) * rows)
+        gram = whole[p, :rows, :rows]
+        cross = whole[p, :rows, rows:] + theirs[:rows, here].T
+        scale_gram = 1.0 / jnp.sqrt(whole[p, rows : rows + 1, :rows])
+        scale_cross = 1.0 / jnp.sqrt(theirs[rows : rows + 1, here])
+        scale = jnp.broadcast_to(scale_gram, (rows, rows)).T
         low, high = jnp.where(first, gram, cross), jnp.where(first, cross, gram)
         scale_low = jnp.where(first, scale_gram, scale_cross)
         scale_high = jnp.where(first, scale_cross, scale_gram)
         node[p, :, :rows] = low
         node[p, :, rows:] = high
-        here = jnp.concatenate([scale * low * scale_low, scale * high * scale_high], axis=1)
-        total = here if total is None else total + here
+        scaled = jnp.concatenate([scale * low * scale_low, scale * high * scale_high], axis=1)
+        total = scaled if total is None else total + scaled
     root[...] = total
 
 
-def merge(whole, theirs, blk, order):
-    nodes, rows, _ = whole.shape
+def merge(whole, theirs, blk):
+    nodes, _, both = whole.shape
+    rows = both // 2
     return pl.pallas_call(
         merge_kernel,
         grid_spec=pltpu.PrefetchScalarGridSpec(
@@ -240,8 +245,7 @@
             grid=(1,),
             in_specs=[
                 pl.BlockSpec(whole.shape, lambda g, blk: (0, 0, 0)),
-                pl.BlockSpec(theirs.shape, lambda g, blk: (0, 0, 0)),
-                pl.BlockSpec(memory_space=pl.ANY),
+                pl.BlockSpec(theirs.shape, lambda g, blk: (0, 0)),
             ],
             out_specs=[
                 pl.BlockSpec((nodes, rows, 2 * rows), lambda g, blk: (0, 0, 0)),
@@ -255,7 +259,7 @@
         compiler_params=params(),
         cost_estimate=SMALL,
         name="merge",
-    )(blk.astype(jnp.int32).reshape(1), whole, theirs, order)
+    )(blk.astype(jnp.int32).reshape(1), whole, theirs)
 
 
 def spread_kernel(block, out):
@@ -288,8 +292,7 @@
 
 
 def vector_kernel(at, spread, own, other, *rest):
-    out, order = rest[-2:]
-    order[...] = jnp.zeros_like(order)
+    out = rest[-1]
     rows, _, cells_y, cells_z = own.shape
     both = jnp.concatenate([split_rows(own[:, 0]), split_rows(other[:, 0])], axis=0)
     made = jnp.dot(spread[...], both, preferred_element_type=jnp.float32)
@@ -301,7 +304,7 @@
     out[:, 0] = jnp.concatenate(parts, axis=1).astype(out.dtype)
 
 
-def expand(spread, own, other, at, held):
+def expand(spread, own, other, at, held, *orders):
     rows, layers, cells_y, cells_z = other.shape
     eigs = spread.shape[0] // SUB
     inputs = [at.reshape(1), spread, own, other]
@@ -314,22 +317,17 @@
     if held is not None:
         aliases = {len(inputs): 0}
         inputs.append(held)
-        specs.append(pl.BlockSpec(memory_space=pl.ANY))
+    inputs += orders
+    specs += [pl.BlockSpec(memory_space=pl.ANY)] * (len(inputs) - 1 - len(specs))
     return pl.pallas_call(
         vector_kernel,
         grid_spec=pltpu.PrefetchScalarGridSpec(
             num_scalar_prefetch=1,
             grid=(layers,),
             in_specs=specs,
-            out_specs=[
-                pl.BlockSpec((eigs, 1, cells_y, cells_z), lambda g, at: (0, at[0] + g, 0, 0)),
-                pl.BlockSpec((SUB, cells_z), lambda g, at: (0, 0)),
-            ],
+            out_specs=pl.BlockSpec((eigs, 1, cells_y, cells_z), lambda g, at: (0, at[0] + g, 0, 0)),
         ),
-        out_shape=[
-            jax.ShapeDtypeStruct((eigs,) + own.shape[1:], jnp.bfloat16),
-            jax.ShapeDtypeStruct((SUB, cells_z), jnp.float32),
-        ],
+        out_shape=jax.ShapeDtypeStruct((eigs,) + own.shape[1:], jnp.bfloat16),
         input_output_aliases=aliases,
         compiler_params=params(),
         cost_estimate=SMALL,
@@ -337,12 +335,71 @@
     )(*inputs)
 
 
+def last_kernel(at, spread, own, other, held, out, made, sems):
+    rows, layers, cells_y, cells_z = own.shape
+    eigs = out.shape[0]
+    parts = made.shape[0]
+    copies = []
+    for layer in range(layers):
+        both = jnp.concatenate([split_rows(own[:, layer]), split_rows(other[:, layer])], axis=0)
+        for part in range(parts):
+            size = eigs // parts
+            some = jnp.dot(
+                spread[part * size * SUB : (part + 1) * size * SUB],
+                both,
+                preferred_element_type=jnp.float32,
+            )
+            tiles = [
+                some[:, i * cells_z : (i + 1) * cells_z].reshape(size, SUB, cells_z)
+                for i in range(cells_y // SUB)
+            ]
+            made[part, :, layer] = jnp.concatenate(tiles, axis=1).astype(made.dtype)
+            if layer == layers - 1:
+                place = out.at[pl.ds(part * size, size), pl.ds(at[0], layers)]
+                copies.append(pltpu.make_async_copy(made.at[part], place, sems.at[part]))
+                copies[-1].start()
+    for copy in copies:
+        copy.wait()
+
+
+def expand_last(spread, own, other, at, held):
+    rows, layers, cells_y, cells_z = other.shape
+    eigs, parts = spread.shape[0] // SUB, 2
+    inside = pl.BlockSpec(memory_space=pltpu.VMEM)
+    return pl.pallas_call(
+        last_kernel,
+        in_specs=[pl.BlockSpec(memory_space=pltpu.SMEM), inside, inside, inside, pl.BlockSpec(memory_space=pl.ANY)],
+        out_specs=pl.BlockSpec(memory_space=pl.ANY),
+        out_shape=jax.ShapeDtypeStruct(held.shape, held.dtype),
+        scratch_shapes=[
+            pltpu.VMEM((parts, eigs // parts, layers, cells_y, cells_z), held.dtype),
+            pltpu.SemaphoreType.DMA((parts,)),
+        ],
+        input_output_aliases={4: 0},
+        compiler_params=pltpu.CompilerParams(vmem_limit_bytes=LAST_BYTES),
+        cost_estimate=SMALL,
+        name="expand_last",
+    )(at.reshape(1), spread, own, other, held)
+
+
 def shares(total, parts):
     return [total // parts + (i < total % parts) for i in range(parts)]
 
 
 def swap(x):
     return lax.ppermute(x, "blk", [(0, 1), (1, 0)])
+
+
+def crossed(x):
+    leaves, leaf = lax.axis_size("leaf"), lax.axis_index("leaf")
+    pairs = [(2 * i + j, 2 * (i ^ (leaves // 2)) + 1 - j) for i in range(leaves) for j in range(2)]
+    count = x.shape[0] // 2
+    part = lax.dynamic_slice_in_dim(x, leaf % 2 * count, count, 0)
+    part = lax.ppermute(part, ("leaf", "blk"), pairs)
+    rest = lax.ppermute(part, "leaf", [(i, i ^ 1) for i in range(leaves)])
+    return jnp.where(
+        leaf % 2 == 0, jnp.concatenate([part, rest], 0), jnp.concatenate([rest, part], 0)
+    )
 
 
 def paired_sum(x, axis):
@@ -379,56 +436,56 @@
     def send(at, count, *orders):
         return swap(cut(own, at, count, *orders))
 
-    nears = shares(half + 1, 2)
     last = half // 16
-    middle = half // 4
+    middle = half // 8
     fars = [half - 1 - middle - last, middle, last]
-    near_at = [sum(nears[:i]) for i in range(len(nears))]
     far_at = [sum(fars[:i]) for i in range(len(fars))]
 
+    pair = own[:, half - 1 : half + 1]
+    met = swap(pair)
+    nears = shares(half - 1, PARTS)
+    near_at = [2 + sum(nears[:i]) for i in range(len(nears))]
     near = [send(spot(o, n, 1 - upper), n) for o, n in zip(near_at, nears)]
     far = [send(far_spot(far_at[0], fars[0], 1 - upper), fars[0])]
     size = lax.axis_size("dof")
     low = lax.ppermute(own[:, -1:], "dof", [(i, i + 1) for i in range(size - 1)])
     high = lax.ppermute(own[:, :1], "dof", [(i + 1, i) for i in range(size - 1)])
-    stiff, gram, mass = stiff_terms(own, low, high, stiffness[0], density[0])
+    stiff, gram, mass = stiff_terms(own, low, high, stiffness[0], density[0], met)
 
     mine = lax.dynamic_slice_in_dim(eigen_blocks[0], blk * rows, rows, 0)
     other = lax.dynamic_slice_in_dim(eigen_blocks[0], (1 - blk) * rows, rows, 0)
     spread = spread_blocks(jnp.concatenate([mine, other], axis=0).T)
 
-    own_in = lax.dynamic_slice_in_dim(own, spot(1, 1, upper), 1, axis=1)
-    own_out = lax.dynamic_slice_in_dim(own, spot(0, 1, upper), 1, axis=1)
-    first = spot(0, nears[0], upper)
-    near_in = lax.dynamic_slice_in_dim(near[0], spot(1, 1, upper) - first, 1, axis=1)
-    near_out = lax.dynamic_slice_in_dim(near[0], spot(0, 1, upper) - first, 1, axis=1)
     across = functools.partial(
         lax.dot_general,
-        dimension_numbers=(((1, 2, 3), (1, 2, 3)), ((), ())),
+        dimension_numbers=(((1, 2), (1, 2)), ((), ())),
         preferred_element_type=jnp.float32,
     )
-    cross = 0.5 * (across(own_out, near_in) - across(own_in, near_out))
+    border = across(pair[:, 0], met[:, 1]) - across(pair[:, 1], met[:, 0])
+    cross = jnp.where(upper == 1, 0.5 * border, -0.5 * border)
+    cross = cross + cross_terms(stiff, met, half - 1 + upper, upper, 1)
     for chunk, offset, count in zip(near, near_at, nears):
-        chunk_at = spot(offset, count, upper)
-        skipped = int(offset == 0)
-        at = spot(offset + skipped, count - skipped, upper)
-        cross = cross + cross_terms(stiff, chunk, at, at - chunk_at, count - skipped)
-
-    whole = line_sum(jnp.concatenate([gram, cross, mass], axis=1), "dof")
+        at = spot(offset, count, upper)
+        cross = cross + cross_terms(stiff, chunk, at, jnp.zeros_like(at), count)
+
+    tops, masses = jnp.concatenate([gram, cross], axis=1), jnp.concatenate([mass, mass], axis=1)
+    whole = line_sum(jnp.concatenate([tops, masses], axis=0), "dof")
     nodes = lax.axis_size("leaf") // 2
     belongs = (parent[leaf] == jnp.arange(nodes, dtype=jnp.int32)).astype(jnp.float32)
     whole = paired_sum(belongs[:, None, None] * whole[None], "leaf")
-    theirs = swap(whole[:, :, rows:])
+    theirs = crossed(jnp.concatenate([whole[p, :, rows:] for p in range(nodes)], axis=1))
     far += [send(far_spot(o, n, 1 - upper), n, whole) for o, n in zip(far_at[1:], fars[1:])]
 
-    vectors = None
+    vectors = expand(spread, own, met, jnp.full_like(upper, half - 1), None)
     for chunk, offset, count in zip(near, near_at, nears):
-        vectors, _ = expand(spread, own, chunk, spot(offset, count, upper), vectors)
+        vectors = expand(spread, own, chunk, spot(offset, count, upper), vectors)
+    node_stiffness, root_stiffness = merge(whole, theirs, blk)
     places = [far_spot(o, n, upper) for o, n in zip(far_at, fars)]
+    order = (root_stiffness,)
     for chunk, at in zip(far[:-1], places[:-1]):
-        vectors, order = expand(spread, own, chunk, at, vectors)
-    node_stiffness, root_stiffness = merge(whole, theirs, blk, order)
-    vectors, _ = expand(spread, own, far[-1], places[-1], vectors)
+        vectors = expand(spread, own, chunk, at, vectors, *order)
+        order = ()
+    vectors = expand_last(spread, cut(own, places[-1], last, whole), far[-1], places[-1], vectors)
     return (node_stiffness, root_stiffness, vectors[None])
 
 
@@ -502,7 +559,7 @@
 
 def solution(mesh):
     body = gathered
-    if mesh.shape["blk"] == 2 and mesh.shape["dof"] == 4:
+    if dict(mesh.shape) == {"leaf": 4, "dof": 4, "blk": 2}:
         body = halved
     in_specs = (
         P("leaf", "blk", "dof", None, None),

time: 195 us -> 190 us (0.974)
  waiting for transfers between devices: 67.2 us -> 39.4 us
  Pallas kernels: 99 us -> 114 us
  starting transfers between devices: 19.4 us -> 24.6 us
  local copies, waits for them, and re-layouts: 4.47 us -> 7.52 us
    ppermute x6 -> x9, waiting for transfers between devices: 48.5 us -> 25.4 us  [swap(): return lax.ppermute(x, 'blk', [(0, 1), (1, 0)])]
    pallas_call x2 -> x6, Pallas kernels: 13.1 us -> 18.9 us  [cross_terms(): pl.pallas_call(cross_kernel, grid_spec=pltpu.PrefetchScalarGridSpec(num_s...]
    pallas_call x5 -> x9, Pallas kernels: 11.6 us -> 17.1 us  [cut(): pl.pallas_call(cut_kernel, grid_spec=pltpu.PrefetchScalarGridSpec(num_sca...]
    ppermute x6 -> x9, starting transfers between devices: 8.41 us -> 12 us  [swap(): return lax.ppermute(x, 'blk', [(0, 1), (1, 0)])]
    pallas_call x5 -> x8, Pallas kernels: 31.8 us -> 34.7 us  [expand(): pl.pallas_call(vector_kernel, grid_spec=pltpu.PrefetchScalarGridSpec(num_...]
    unnamed x8 -> x26, local copies, waits for them, and re-layouts: 0.03 us -> 2.69 us
    ppermute x1, waiting for transfers between devices: 2.57 us -> 0.01 us  [halved(): lax.ppermute(own[:, :1], 'dof', [(i + 1, i) for i in range(size - 1)])]
    squeeze x0 -> x3, local copies, waits for them, and re-layouts: none -> 2.28 us  [the longest x2 2.21 us: halved(): border = across(pair[:, 0], met[:, 1]) - across(pair[:, 1], met[:, 0])]
  transfers between devices with their start and end apart: 13 -> 18, of which waited for: 8 -> 8; matrix products, arithmetic and copies ran while one was open for 3% -> 3% of each run, Pallas kernels for 49% -> 59%
where the time goes in v5:
time: 190 us; the launch traced here: 188 us
  Pallas kernels  114 us (60%)
  waiting for transfers between devices  39.4 us (21%)
  starting transfers between devices  24.6 us (13%)
  local copies, waits for them, and re-layouts  7.52 us (4%)
    pallas_call x1, Pallas kernels, stiff_terms(): pl.pallas_call(stiff_kernel, grid=(layers,), in_specs=[pl.BlockSpec(block...  40.1 us
    pallas_call x8, Pallas kernels, expand(): pl.pallas_call(vector_kernel, grid_spec=pltpu.PrefetchScalarGridSpec(num_...  34.7 us
    ppermute x9, waiting for transfers between devices, swap(): return lax.ppermute(x, 'blk', [(0, 1), (1, 0)])  25.4 us
    pallas_call x6, Pallas kernels, cross_terms(): pl.pallas_call(cross_kernel, grid_spec=pltpu.PrefetchScalarGridSpec(num_s...  18.9 us
    pallas_call x9, Pallas kernels, cut(): pl.pallas_call(cut_kernel, grid_spec=pltpu.PrefetchScalarGridSpec(num_sca...  17.1 us
    ppermute x9, starting transfers between devices, swap(): return lax.ppermute(x, 'blk', [(0, 1), (1, 0)])  12 us
    ppermute x1, waiting for transfers between devices, line_sum(): outer = lax.ppermute(x, axis, [(1, 0), (2, 3)])  7.73 us
    ppermute x2, waiting for transfers between devices, paired_sum(): x = x + lax.ppermute(x, axis, [(i, i ^ step) for i in range(size)])  4.27 us
  transfers between devices with their start and end apart: 18, of which 8 were waited for; matrix products, arithmetic and copies ran while one was open for 3% of the time, Pallas kernels for 59%

profile of v5, /device:TPU:0, one launch (start us, length us, event | category | flops | bytes accessed | tf_op | source)
XLA Modules:
  0.0 188.0 jit_solution(14225386394109048543)
XLA Ops:
  0.6 1.9 %cut.12 = bf16[64,3,16,128]{3,2,1,0:T(8,128)(2,1)} custom-call(s32[1]{0:T(128)} %bitcast.20.at, bf16[64,32,16,128]{3,2,1,0:T(8,128)(2,1)} %bitcast.50), custom_call_target="tpu_custom_call" | custom-call | flops 1024 | bytes 1024 | tf_op jit(solution)/shard_map/cut/pallas_call | solution.py:196
  2.6 3.0 %collective-permute-start.6 = (bf16[64,3,16,128]{3,2,1,0:T(8,128)(2,1)}, bf16[64,3,16,128]{3,2,1,0:T(8,128)(2,1)S(1)}, u32[]{:S(2)}, u32[]{:S(2)}) collective-permute-start(bf16[64,3,16,128]{3,2,1,0:T(8,128)(2,1)} %cut.12), channel_id=1, source_target_pairs={{0,1},{1,0},{2,3},{3,2},{4,5},{5,4},{6,7},{7,6},{8,9},{9,8},{10,11... | collective-permute-start | bytes 2359304 | tf_op jit(solution)/shard_map/ppermute | solution.py:390
  5.6 1.9 slice.40
  7.5 2.2 %slice_bitcast_fusion.3 = (bf16[64,16,128]{2,1,0:T(8,128)(2,1)}, bf16[64,16,128]{2,1,0:T(8,128)(2,1)}, bf16[64,1,16,128]{3,2,1,0:T(8,128)(2,1)S(1)}, bf16[64,1,16,128]{3,2,1,0:T(8,128)(2,1)S(1)}) fusion(bf16[64,32,16,128]{3,2,1,0:T(8,128)(2,1)} %bitcast.52), kind=kLoop, calls=%fused_computation.6 | loop fusion | bytes 2097152 | tf_op jit(solution)/shard_map/squeeze | solution.py:464
  9.7 4.0 %collective-permute-start = (bf16[64,1,16,128]{3,2,1,0:T(8,128)(2,1)S(1)}, bf16[64,1,16,128]{3,2,1,0:T(8,128)(2,1)S(1)}, u32[]{:S(2)}, u32[]{:S(2)}) collective-permute-start(bf16[64,1,16,128]{3,2,1,0:T(8,128)(2,1)S(1)} %get-tuple-element.16), channel_id=1, source_target_pairs={{0,2},{2,4},{4,6},{1,3},{3,5},{5,7},{8,10},{10,12},{12,14},{9,11},... | collective-permute-start | bytes 786440 | tf_op jit(solution)/shard_map/ppermute | solution.py:451
  15.0 2.0 %cut.9 = bf16[64,3,16,128]{3,2,1,0:T(8,128)(2,1)} custom-call(s32[1]{0:T(128)} %bitcast.14.at, bf16[64,32,16,128]{3,2,1,0:T(8,128)(2,1)} %bitcast.53), custom_call_target="tpu_custom_call" | custom-call | flops 1024 | bytes 1024 | tf_op jit(solution)/shard_map/cut/pallas_call | solution.py:196
  18.5 1.9 %cut.10 = bf16[64,3,16,128]{3,2,1,0:T(8,128)(2,1)} custom-call(s32[1]{0:T(128)} %bitcast.16.at, bf16[64,32,16,128]{3,2,1,0:T(8,128)(2,1)} %bitcast.54), custom_call_target="tpu_custom_call" | custom-call | flops 1024 | bytes 1024 | tf_op jit(solution)/shard_map/cut/pallas_call | solution.py:196
  20.4 1.9 %cut.11 = bf16[64,3,16,128]{3,2,1,0:T(8,128)(2,1)} custom-call(s32[1]{0:T(128)} %bitcast.18.at, bf16[64,32,16,128]{3,2,1,0:T(8,128)(2,1)} %bitcast.55), custom_call_target="tpu_custom_call" | custom-call | flops 1024 | bytes 1024 | tf_op jit(solution)/shard_map/cut/pallas_call | solution.py:196
  24.5 2.0 %cut.13 = bf16[64,3,16,128]{3,2,1,0:T(8,128)(2,1)} custom-call(s32[1]{0:T(128)} %bitcast.22.at, bf16[64,32,16,128]{3,2,1,0:T(8,128)(2,1)} %bitcast.56), custom_call_target="tpu_custom_call" | custom-call | flops 1024 | bytes 1024 | tf_op jit(solution)/shard_map/cut/pallas_call | solution.py:196
  26.5 8.9 %collective-permute-done.2.order.other = bf16[64,2,16,128]{3,2,1,0:T(8,128)(2,1)S(1)} collective-permute-done((bf16[64,2,16,128]{3,2,1,0:T(8,128)(2,1)}, bf16[64,2,16,128]{3,2,1,0:T(8,128)(2,1)S(1)}, u32[]{:S(2)}, u32[]{:S(2)}) %collective-permute-start.2) | collective-permute-done | bytes 524320 | tf_op jit(solution)/shard_map/ppermute | solution.py:390
  35.4 2.1 %collective-permute-start.7 = (bf16[64,3,16,128]{3,2,1,0:T(8,128)(2,1)}, bf16[64,3,16,128]{3,2,1,0:T(8,128)(2,1)S(1)}, u32[]{:S(2)}, u32[]{:S(2)}) collective-permute-start(bf16[64,3,16,128]{3,2,1,0:T(8,128)(2,1)} %cut.13), channel_id=1, source_target_pairs={{0,1},{1,0},{2,3},{3,2},{4,5},{5,4},{6,7},{7,6},{8,9},{9,8},{10,11... | collective-permute-start | bytes 2359304 | tf_op jit(solution)/shard_map/ppermute | solution.py:390
  37.5 2.9 %cut.17 = bf16[64,12,16,128]{3,2,1,0:T(8,128)(2,1)} custom-call(s32[1]{0:T(128)} %bitcast.33.at, bf16[64,32,16,128]{3,2,1,0:T(8,128)(2,1)} %bitcast.57), custom_call_target="tpu_custom_call" | custom-call | flops 1024 | bytes 1024 | tf_op jit(solution)/shard_map/cut/pallas_call | solution.py:196
  42.3 40.1 %stiff_terms.1 = (bf16[32,512,256]{2,1,0:T(8,128)(2,1)}, f32[64,64]{1,0:T(8,128)S(1)}, f32[16,64]{1,0:T(8,128)S(1)}) custom-call(bf16[64,32,16,128]{3,2,1,0:T(8,128)(2,1)} %bitcast.58, bf16[64,32,16,128]{3,2,1,0:T(8,128)(2,1)} %bitcast.59, bf16[64,32,16,128]{3,2,1,0:T(8,128)(2,1)} %bitcast.60, bf16[64,1,16,128]{3,2,1,0:T(8,128)(2,1)S(1)} %copy-done.5, ...), custom_call_target="tpu_custom_call" | custom-call | flops 1024 | bytes 1024 | tf_op jit(solution)/shard_map/stiff_terms/pallas_call | solution.py:100
  84.8 3.3 %cross_terms.10 = f32[64,64]{1,0:T(8,128)S(1)} custom-call(s32[1]{0:T(128)} %bitcast.19.at, s32[1]{0:T(128)} %constant.61.clone.1.skip, bf16[32,512,256]{2,1,0:T(8,128)(2,1)} %get-tuple-element.9.stiff, bf16[64,3,16,128]{3,2,1,0:T(8,128)(2,1)S(1)} %collective-permute-done.6.other), custom_call_target="tpu_custom_call" | custom-call | flops 1024 | bytes 1024 | tf_op jit(solution)/shard_map/cross_terms/pallas_call | solution.py:151
  88.2 3.3 %cross_terms.7 = f32[64,64]{1,0:T(8,128)S(1)} custom-call(s32[1]{0:T(128)} %bitcast.13.at, s32[1]{0:T(128)} %constant.61.clone.1.skip, bf16[32,512,256]{2,1,0:T(8,128)(2,1)} %get-tuple-element.9.stiff, bf16[64,3,16,128]{3,2,1,0:T(8,128)(2,1)S(1)} %collective-permute-done.3.other), custom_call_target="tpu_custom_call" | custom-call | flops 1024 | bytes 1024 | tf_op jit(solution)/shard_map/cross_terms/pallas_call | solution.py:151
  91.5 3.5 %cross_terms.8 = f32[64,64]{1,0:T(8,128)S(1)} custom-call(s32[1]{0:T(128)} %bitcast.15.at, s32[1]{0:T(128)} %constant.61.clone.1.skip, bf16[32,512,256]{2,1,0:T(8,128)(2,1)} %get-tuple-element.9.stiff, bf16[64,3,16,128]{3,2,1,0:T(8,128)(2,1)} %collective-permute-done.4.other), custom_call_target="tpu_custom_call" | custom-call | flops 1024 | bytes 1024 | tf_op jit(solution)/shard_map/cross_terms/pallas_call | solution.py:151
  95.1 3.5 %cross_terms.9 = f32[64,64]{1,0:T(8,128)S(1)} custom-call(s32[1]{0:T(128)} %bitcast.17.at, s32[1]{0:T(128)} %constant.61.clone.1.skip, bf16[32,512,256]{2,1,0:T(8,128)(2,1)} %get-tuple-element.9.stiff, bf16[64,3,16,128]{3,2,1,0:T(8,128)(2,1)} %collective-permute-done.5.other), custom_call_target="tpu_custom_call" | custom-call | flops 1024 | bytes 1024 | tf_op jit(solution)/shard_map/cross_terms/pallas_call | solution.py:151
  98.6 4.3 %collective-permute-done.7.other = bf16[64,3,16,128]{3,2,1,0:T(8,128)(2,1)S(1)} collective-permute-done((bf16[64,3,16,128]{3,2,1,0:T(8,128)(2,1)}, bf16[64,3,16,128]{3,2,1,0:T(8,128)(2,1)S(1)}, u32[]{:S(2)}, u32[]{:S(2)}) %collective-permute-start.7) | collective-permute-done | bytes 786464 | tf_op jit(solution)/shard_map/ppermute | solution.py:390
  102.8 3.5 %cross_terms.11 = f32[64,64]{1,0:T(8,128)S(1)} custom-call(s32[1]{0:T(128)} %bitcast.21.at, s32[1]{0:T(128)} %constant.61.clone.1.skip, bf16[32,512,256]{2,1,0:T(8,128)(2,1)} %get-tuple-element.9.stiff, bf16[64,3,16,128]{3,2,1,0:T(8,128)(2,1)S(1)} %collective-permute-done.7.other), custom_call_target="tpu_custom_call" | custom-call | flops 1024 | bytes 1024 | tf_op jit(solution)/shard_map/cross_terms/pallas_call | solution.py:151
  106.4 2.1 %collective-permute-start.8 = (f32[80,128]{1,0:T(8,128)S(1)}, f32[80,128]{1,0:T(8,128)S(1)}, u32[]{:S(2)}, u32[]{:S(2)}) collective-permute-start(f32[80,128]{1,0:T(8,128)S(1)} %maximum_maximum_fusion), channel_id=1, source_target_pairs={{0,2},{2,0},{4,6},{6,4},{1,3},{3,1},{5,7},{7,5},{8,10},{10,8},{12,... | collective-permute-start | bytes 122888 | tf_op jit(solution)/shard_map/ppermute | solution.py:414
  108.6 2.0 %collective-permute-done.8 = f32[80,128]{1,0:T(8,128)S(1)} collective-permute-done((f32[80,128]{1,0:T(8,128)S(1)}, f32[80,128]{1,0:T(8,128)S(1)}, u32[]{:S(2)}, u32[]{:S(2)}) %collective-permute-start.8) | collective-permute-done | bytes 40992 | tf_op jit(solution)/shard_map/ppermute | solution.py:414
  114.0 7.7 %collective-permute-done.10 = f32[80,128]{1,0:T(8,128)S(1)} collective-permute-done((f32[80,128]{1,0:T(8,128)S(1)}, f32[80,128]{1,0:T(8,128)S(1)}, u32[]{:S(2)}, u32[]{:S(2)}) %collective-permute-start.10) | collective-permute-done | bytes 40992 | tf_op jit(solution)/shard_map/ppermute | solution.py:416
  124.8 3.0 %collective-permute-done.12 = f32[2,80,128]{2,1,0:T(8,128)S(1)} collective-permute-done((f32[2,80,128]{2,1,0:T(8,128)S(1)}, f32[2,80,128]{2,1,0:T(8,128)S(1)}, u32[]{:S(2)}, u32[]{:S(2)}) %collective-permute-start.12) | collective-permute-done | bytes 81952 | tf_op jit(solution)/shard_map/ppermute | solution.py:408
  137.0 2.6 %expand.8.rest_0_ = bf16[64,32,16,128]{3,2,1,0:T(8,128)(2,1)} custom-call(s32[1]{0:T(128)} %constant.73.clone.1.at, bf16[512,1024]{1,0:T(8,128)(2,1)S(1)} %spread_blocks.1.spread, bf16[64,32,16,128]{3,2,1,0:T(8,128)(2,1)} %bitcast.63, bf16[64,2,16,128]{3,2,1,0:T(8,128)(2,1)S(1)} %collective-permute-done.2.order.other), custom_call_target="tpu_custom_call" | custom-call | flops 1024 | bytes 1024 | tf_op jit(solution)/shard_map/expand/pallas_call | solution.py:322
  139.6 3.6 %expand.9.rest_0_ = bf16[64,32,16,128]{3,2,1,0:T(8,128)(2,1)} custom-call(s32[1]{0:T(128)} %bitcast.13.at, bf16[512,1024]{1,0:T(8,128)(2,1)S(1)} %spread_blocks.1.spread, bf16[64,32,16,128]{3,2,1,0:T(8,128)(2,1)} %bitcast.64, bf16[64,3,16,128]{3,2,1,0:T(8,128)(2,1)S(1)} %collective-permute-done.3.other, ...), custom_call_target="tpu_custom_call", output_to_operand_aliasing={{}: (4, {})} | custom-call | flops 1024 | bytes 1024 | tf_op jit(solution)/shard_map/expand/pallas_call | solution.py:322
  143.2 3.8 %expand.10.rest_0_ = bf16[64,32,16,128]{3,2,1,0:T(8,128)(2,1)} custom-call(s32[1]{0:T(128)} %bitcast.15.at, bf16[512,1024]{1,0:T(8,128)(2,1)S(1)} %spread_blocks.1.spread, bf16[64,32,16,128]{3,2,1,0:T(8,128)(2,1)} %bitcast.65, bf16[64,3,16,128]{3,2,1,0:T(8,128)(2,1)} %collective-permute-done.4.other, ...), custom_call_target="tpu_custom_call", output_to_operand_aliasing={{}: (4, {})} | custom-call | flops 1024 | bytes 1024 | tf_op jit(solution)/shard_map/expand/pallas_call | solution.py:322
  147.0 3.8 %expand.11.rest_0_ = bf16[64,32,16,128]{3,2,1,0:T(8,128)(2,1)} custom-call(s32[1]{0:T(128)} %bitcast.17.at, bf16[512,1024]{1,0:T(8,128)(2,1)S(1)} %spread_blocks.1.spread, bf16[64,32,16,128]{3,2,1,0:T(8,128)(2,1)} %bitcast.66, bf16[64,3,16,128]{3,2,1,0:T(8,128)(2,1)} %collective-permute-done.5.other, ...), custom_call_target="tpu_custom_call", output_to_operand_aliasing={{}: (4, {})} | custom-call | flops 1024 | bytes 1024 | tf_op jit(solution)/shard_map/expand/pallas_call | solution.py:322
  150.8 3.7 %expand.12.rest_0_ = bf16[64,32,16,128]{3,2,1,0:T(8,128)(2,1)} custom-call(s32[1]{0:T(128)} %bitcast.19.at, bf16[512,1024]{1,0:T(8,128)(2,1)S(1)} %spread_blocks.1.spread, bf16[64,32,16,128]{3,2,1,0:T(8,128)(2,1)} %bitcast.67, bf16[64,3,16,128]{3,2,1,0:T(8,128)(2,1)S(1)} %collective-permute-done.6.other, ...), custom_call_target="tpu_custom_call", output_to_operand_aliasing={{}: (4, {})} | custom-call | flops 1024 | bytes 1024 | tf_op jit(solution)/shard_map/expand/pallas_call | solution.py:322
  154.5 3.6 %expand.13.rest_0_ = bf16[64,32,16,128]{3,2,1,0:T(8,128)(2,1)} custom-call(s32[1]{0:T(128)} %bitcast.21.at, bf16[512,1024]{1,0:T(8,128)(2,1)S(1)} %spread_blocks.1.spread, bf16[64,32,16,128]{3,2,1,0:T(8,128)(2,1)} %bitcast.68, bf16[64,3,16,128]{3,2,1,0:T(8,128)(2,1)S(1)} %copy-done.1, ...), custom_call_target="tpu_custom_call", output_to_operand_aliasing={{}: (4, {})} | custom-call | flops 1024 | bytes 1024 | tf_op jit(solution)/shard_map/expand/pallas_call | solution.py:322
  160.2 10.6 %collective-permute-done.17.other = bf16[64,12,16,128]{3,2,1,0:T(8,128)(2,1)} collective-permute-done((bf16[64,12,16,128]{3,2,1,0:T(8,128)(2,1)}, bf16[64,12,16,128]{3,2,1,0:T(8,128)(2,1)}, u32[]{:S(2)}, u32[]{:S(2)}) %collective-permute-start.17) | collective-permute-done | bytes 3145760 | tf_op jit(solution)/shard_map/ppermute | solution.py:390
  171.6 10.9 %expand.14.rest_0_ = bf16[64,32,16,128]{3,2,1,0:T(8,128)(2,1)} custom-call(s32[1]{0:T(128)} %bitcast.32.at, bf16[512,1024]{1,0:T(8,128)(2,1)S(1)} %spread_blocks.1.spread, bf16[64,32,16,128]{3,2,1,0:T(8,128)(2,1)} %bitcast.70, bf16[64,12,16,128]{3,2,1,0:T(8,128)(2,1)} %collective-permute-done.17.other, ...), custom_call_target="tpu_custom_call", output_to_operand_aliasing={{}: (4, {})} | custom-call | flops 1024 | bytes 1024 | tf_op jit(solution)/shard_map/expand/pallas_call | solution.py:322
  182.5 2.7 %expand.15.held = bf16[64,32,16,128]{3,2,1,0:T(8,128)(2,1)} custom-call(s32[1]{0:T(128)} %bitcast.30.at, bf16[512,1024]{1,0:T(8,128)(2,1)S(1)} %spread_blocks.1.spread, bf16[64,32,16,128]{3,2,1,0:T(8,128)(2,1)} %bitcast.71, bf16[64,2,16,128]{3,2,1,0:T(8,128)(2,1)} %collective-permute-done.16.other, ...), custom_call_target="tpu_custom_call", output_to_operand_aliasing={{}: (4, {})} | custom-call | flops 1024 | bytes 1024 | tf_op jit(solution)/shard_map/expand/pallas_call | solution.py:322
  (77 shorter events, 30.5 us)
Async XLA Ops:
  2.6 81.7 %collective-permute-start.6 = (bf16[64,3,16,128]{3,2,1,0:T(8,128)(2,1)}, bf16[64,3,16,128]{3,2,1,0:T(8,128)(2,1)S(1)}, u32[]{:S(2)}, u32[]{:S(2)}) collective-permute-start(bf16[64,3,16,128]{3,2,1,0:T(8,128)(2,1)} %cut.12), channel_id=1, source_target_pairs={{0,1},{1,0},{2,3},{3,2},{4,5},{5,4},{6,7},{7,6},{8,9},{9,8},{10,11... | collective-permute-start | bytes 2359304 | tf_op jit(solution)/shard_map/ppermute | solution.py:390
  7.5 27.9 %collective-permute-start.2 = (bf16[64,2,16,128]{3,2,1,0:T(8,128)(2,1)}, bf16[64,2,16,128]{3,2,1,0:T(8,128)(2,1)S(1)}, u32[]{:S(2)}, u32[]{:S(2)}) collective-permute-start(bf16[64,2,16,128]{3,2,1,0:T(8,128)(2,1)} %slice.40), channel_id=1, source_target_pairs={{0,1},{1,0},{2,3},{3,2},{4,5},{5,4},{6,7},{7,6},{8,9},{9,8},{10,11... | collective-permute-start | bytes 1572872 | tf_op jit(solution)/shard_map/ppermute | solution.py:390
  9.7 12.7 %collective-permute-start = (bf16[64,1,16,128]{3,2,1,0:T(8,128)(2,1)S(1)}, bf16[64,1,16,128]{3,2,1,0:T(8,128)(2,1)S(1)}, u32[]{:S(2)}, u32[]{:S(2)}) collective-permute-start(bf16[64,1,16,128]{3,2,1,0:T(8,128)(2,1)S(1)} %get-tuple-element.16), channel_id=1, source_target_pairs={{0,2},{2,4},{4,6},{1,3},{3,5},{5,7},{8,10},{10,12},{12,14},{9,11},... | collective-permute-start | bytes 786440 | tf_op jit(solution)/shard_map/ppermute | solution.py:451
  13.7 9.3 %collective-permute-start.1 = (bf16[64,1,16,128]{3,2,1,0:T(8,128)(2,1)S(1)}, bf16[64,1,16,128]{3,2,1,0:T(8,128)(2,1)S(1)}, u32[]{:S(2)}, u32[]{:S(2)}) collective-permute-start(bf16[64,1,16,128]{3,2,1,0:T(8,128)(2,1)S(1)} %get-tuple-element.15), channel_id=1, source_target_pairs={{2,0},{4,2},{6,4},{3,1},{5,3},{7,5},{10,8},{12,10},{14,12},{11,9},... | collective-permute-start | bytes 786440 | tf_op jit(solution)/shard_map/ppermute | solution.py:452
  16.9 71.3 %collective-permute-start.3 = (bf16[64,3,16,128]{3,2,1,0:T(8,128)(2,1)}, bf16[64,3,16,128]{3,2,1,0:T(8,128)(2,1)S(1)}, u32[]{:S(2)}, u32[]{:S(2)}) collective-permute-start(bf16[64,3,16,128]{3,2,1,0:T(8,128)(2,1)} %cut.9), channel_id=1, source_target_pairs={{0,1},{1,0},{2,3},{3,2},{4,5},{5,4},{6,7},{7,6},{8,9},{9,8},{10,11... | collective-permute-start | bytes 2359304 | tf_op jit(solution)/shard_map/ppermute | solution.py:390
  22.4 4.1 %copy-start.4 = (bf16[64,1,16,128]{3,2,1,0:T(8,128)(2,1)}, bf16[64,1,16,128]{3,2,1,0:T(8,128)(2,1)S(1)}, u32[]{:S(2)}) copy-start(bf16[64,1,16,128]{3,2,1,0:T(8,128)(2,1)S(1)} %collective-permute-done.low) | copy-start | bytes 786436
  22.4 69.1 %collective-permute-start.4 = (bf16[64,3,16,128]{3,2,1,0:T(8,128)(2,1)}, bf16[64,3,16,128]{3,2,1,0:T(8,128)(2,1)}, u32[]{:S(2)}, u32[]{:S(2)}) collective-permute-start(bf16[64,3,16,128]{3,2,1,0:T(8,128)(2,1)} %cut.10), channel_id=1, source_target_pairs={{0,1},{1,0},{2,3},{3,2},{4,5},{5,4},{6,7},{7,6},{8,9},{9,8},{10,11... | collective-permute-start | bytes 2359304 | tf_op jit(solution)/shard_map/ppermute | solution.py:390
  23.0 3.5 %copy-start.6 = (bf16[64,1,16,128]{3,2,1,0:T(8,128)(2,1)}, bf16[64,1,16,128]{3,2,1,0:T(8,128)(2,1)S(1)}, u32[]{:S(2)}) copy-start(bf16[64,1,16,128]{3,2,1,0:T(8,128)(2,1)S(1)} %collective-permute-done.1.high) | copy-start | bytes 786436
  23.0 72.1 %collective-permute-start.5 = (bf16[64,3,16,128]{3,2,1,0:T(8,128)(2,1)}, bf16[64,3,16,128]{3,2,1,0:T(8,128)(2,1)}, u32[]{:S(2)}, u32[]{:S(2)}) collective-permute-start(bf16[64,3,16,128]{3,2,1,0:T(8,128)(2,1)} %cut.11), channel_id=1, source_target_pairs={{0,1},{1,0},{2,3},{3,2},{4,5},{5,4},{6,7},{7,6},{8,9},{9,8},{10,11... | collective-permute-start | bytes 2359304 | tf_op jit(solution)/shard_map/ppermute | solution.py:390
  24.5 15.9 %copy-start.2 = (f32[1,32,16,128]{3,2,1,0:T(8,128)S(1)}, f32[1,32,16,128]{3,2,1,0:T(8,128)}, u32[]{:S(2)}) copy-start(f32[1,32,16,128]{3,2,1,0:T(8,128)} %param.6) | copy-start | bytes 786436
  24.5 15.9 %copy-start.3 = (f32[1,32,16,128]{3,2,1,0:T(8,128)S(1)}, f32[1,32,16,128]{3,2,1,0:T(8,128)}, u32[]{:S(2)}) copy-start(f32[1,32,16,128]{3,2,1,0:T(8,128)} %param.7) | copy-start | bytes 786436
  35.4 67.4 %collective-permute-start.7 = (bf16[64,3,16,128]{3,2,1,0:T(8,128)(2,1)}, bf16[64,3,16,128]{3,2,1,0:T(8,128)(2,1)S(1)}, u32[]{:S(2)}, u32[]{:S(2)}) collective-permute-start(bf16[64,3,16,128]{3,2,1,0:T(8,128)(2,1)} %cut.13), channel_id=1, source_target_pairs={{0,1},{1,0},{2,3},{3,2},{4,5},{5,4},{6,7},{7,6},{8,9},{9,8},{10,11... | collective-permute-start | bytes 2359304 | tf_op jit(solution)/shard_map/ppermute | solution.py:390
  40.4 1.0 copy-start.5
  41.4 0.9 copy-start.7
  82.4 1.9 %copy-start.10 = (bf16[64,16,128]{2,1,0:T(8,128)(2,1)S(1)}, bf16[64,16,128]{2,1,0:T(8,128)(2,1)}, u32[]{:S(2)}) copy-start(bf16[64,16,128]{2,1,0:T(8,128)(2,1)} %get-tuple-element.14) | copy-start | bytes 786436
  82.4 2.2 %copy-start.9 = (bf16[64,16,128]{2,1,0:T(8,128)(2,1)S(1)}, bf16[64,16,128]{2,1,0:T(8,128)(2,1)}, u32[]{:S(2)}) copy-start(bf16[64,16,128]{2,1,0:T(8,128)(2,1)} %get-tuple-element.13) | copy-start | bytes 786436
  84.2 86.6 %collective-permute-start.17 = (bf16[64,12,16,128]{3,2,1,0:T(8,128)(2,1)}, bf16[64,12,16,128]{3,2,1,0:T(8,128)(2,1)}, u32[]{:S(2)}, u32[]{:S(2)}) collective-permute-start(bf16[64,12,16,128]{3,2,1,0:T(8,128)(2,1)} %cut.17), channel_id=1, source_target_pairs={{0,1},{1,0},{2,3},{3,2},{4,5},{5,4},{6,7},{7,6},{8,9},{9,8},{10,11... | collective-permute-start | bytes 9437192 | tf_op jit(solution)/shard_map/ppermute | solution.py:390
  95.0 16.2 %copy-start.12 = (s32[4]{0:T(128)S(1)}, s32[4]{0:T(128)}, u32[]{:S(2)}) copy-start(s32[4]{0:T(128)} %param.9) | copy-start | bytes 52
  102.8 26.9 %copy-start = (bf16[64,3,16,128]{3,2,1,0:T(8,128)(2,1)}, bf16[64,3,16,128]{3,2,1,0:T(8,128)(2,1)S(1)}, u32[]{:S(2)}) copy-start(bf16[64,3,16,128]{3,2,1,0:T(8,128)(2,1)S(1)} %collective-permute-done.7.other) | copy-start | bytes 2359300
  106.4 4.1 %collective-permute-start.8 = (f32[80,128]{1,0:T(8,128)S(1)}, f32[80,128]{1,0:T(8,128)S(1)}, u32[]{:S(2)}, u32[]{:S(2)}) collective-permute-start(f32[80,128]{1,0:T(8,128)S(1)} %maximum_maximum_fusion), channel_id=1, source_target_pairs={{0,2},{2,0},{4,6},{6,4},{1,3},{3,1},{5,7},{7,5},{8,10},{10,8},{12,... | collective-permute-start | bytes 122888 | tf_op jit(solution)/shard_map/ppermute | solution.py:414
  110.6 1.3 collective-permute-start.9
  111.9 9.9 %collective-permute-start.10 = (f32[80,128]{1,0:T(8,128)S(1)}, f32[80,128]{1,0:T(8,128)S(1)}, u32[]{:S(2)}, u32[]{:S(2)}) collective-permute-start(f32[80,128]{1,0:T(8,128)S(1)} %add.67), channel_id=1, source_target_pairs={{2,0},{4,6},{3,1},{5,7},{10,8},{12,14},{11,9},{13,15},{18,16},{20,... | collective-permute-start | bytes 122888 | tf_op jit(solution)/shard_map/ppermute | solution.py:416
  121.9 1.3 collective-permute-start.11
  123.2 4.5 %collective-permute-start.12 = (f32[2,80,128]{2,1,0:T(8,128)S(1)}, f32[2,80,128]{2,1,0:T(8,128)S(1)}, u32[]{:S(2)}, u32[]{:S(2)}) collective-permute-start(f32[2,80,128]{2,1,0:T(8,128)S(1)} %fusion.6), channel_id=1, source_target_pairs={{0,16},{8,24},{16,0},{24,8},{1,17},{9,25},{17,1},{25,9},{2,18},{10... | collective-permute-start | bytes 245768 | tf_op jit(solution)/shard_map/ppermute | solution.py:408
  127.8 8.3 %copy-start.11 = (bf16[1,128,64]{1,2,0:T(8,128)(2,1)S(1)}, bf16[1,128,64]{1,2,0:T(8,128)(2,1)}, u32[]{:S(2)}) copy-start(bf16[1,128,64]{1,2,0:T(8,128)(2,1)} %param.8) | copy-start | bytes 49156
  129.7 52.8 %collective-permute-start.16 = (bf16[64,2,16,128]{3,2,1,0:T(8,128)(2,1)}, bf16[64,2,16,128]{3,2,1,0:T(8,128)(2,1)}, u32[]{:S(2)}, u32[]{:S(2)}) collective-permute-start(bf16[64,2,16,128]{3,2,1,0:T(8,128)(2,1)} %cut.16), channel_id=1, source_target_pairs={{0,1},{1,0},{2,3},{3,2},{4,5},{5,4},{6,7},{7,6},{8,9},{9,8},{10,11... | collective-permute-start | bytes 1572872 | tf_op jit(solution)/shard_map/ppermute | solution.py:390
  131.5 4.8 %collective-permute-start.13 = (f32[40,128]{1,0:T(8,128)S(1)}, f32[40,128]{1,0:T(8,128)S(1)}, u32[]{:S(2)}, u32[]{:S(2)}) collective-permute-start(f32[40,128]{1,0:T(8,128)S(1)} %fusion.5), channel_id=1, source_target_pairs={{0,17},{1,16},{8,25},{9,24},{16,1},{17,0},{24,9},{25,8},{2,19},{3,... | collective-permute-start | bytes 61448 | tf_op jit(solution)/shard_map/ppermute | solution.py:398
  134.6 52.1 %collective-permute-start.15 = (bf16[64,1,16,128]{3,2,1,0:T(8,128)(2,1)}, bf16[64,1,16,128]{3,2,1,0:T(8,128)(2,1)S(1)}, u32[]{:S(2)}, u32[]{:S(2)}) collective-permute-start(bf16[64,1,16,128]{3,2,1,0:T(8,128)(2,1)} %cut.15), channel_id=1, source_target_pairs={{0,1},{1,0},{2,3},{3,2},{4,5},{5,4},{6,7},{7,6},{8,9},{9,8},{10,11... | collective-permute-start | bytes 786440 | tf_op jit(solution)/shard_map/ppermute | solution.py:390
  136.3 22.8 %collective-permute-start.14 = (f32[40,128]{1,0:T(8,128)S(1)}, f32[40,128]{1,0:T(8,128)S(1)}, u32[]{:S(2)}, u32[]{:S(2)}) collective-permute-start(f32[40,128]{1,0:T(8,128)S(1)} %collective-permute-done.13), channel_id=1, source_target_pairs={{0,8},{8,0},{16,24},{24,16},{1,9},{9,1},{17,25},{25,17},{2,10},{10... | collective-permute-start | bytes 61448 | tf_op jit(solution)/shard_map/ppermute | solution.py:399
  150.8 3.7 %copy-start.1 = (bf16[64,3,16,128]{3,2,1,0:T(8,128)(2,1)S(1)}, bf16[64,3,16,128]{3,2,1,0:T(8,128)(2,1)}, u32[]{:S(2)}) copy-start(bf16[64,3,16,128]{3,2,1,0:T(8,128)(2,1)} %copy-done) | copy-start | bytes 2359300
  170.8 0.8 copy-start.8

commit v6 on v5

--- a/solution.py
+++ b/solution.py
@@ -167,50 +167,19 @@
     )(at.reshape(1), skip.reshape(1), stiff, other)
 
 
-def cut_kernel(at, whole, *rest):
-    out, held, reads, writes = rest[-4:]
-    pieces = held.shape[0]
-    layers = out.shape[1]
-    bounds = [layers * i // pieces for i in range(pieces + 1)]
-    ins, outs = [], []
-    for i in range(pieces):
-        start, size = bounds[i], bounds[i + 1] - bounds[i]
-        piece = held.at[i, :, pl.ds(0, size)]
-        ins.append(
-            pltpu.make_async_copy(whole.at[:, pl.ds(at[0] + start, size)], piece, reads.at[i])
-        )
-        outs.append(pltpu.make_async_copy(piece, out.at[:, pl.ds(start, size)], writes.at[i]))
-    for copy in ins:
-        copy.start()
-    for i in range(pieces):
-        ins[i].wait()
-        outs[i].start()
-    for copy in outs:
-        copy.wait()
-
-
-def cut(whole, at, count, *orders):
-    rows, _, cells_y, cells_z = whole.shape
-    pieces = min(4, count)
-    longest = -(-count // pieces)
-    return pl.pallas_call(
-        cut_kernel,
-        grid_spec=pltpu.PrefetchScalarGridSpec(
-            num_scalar_prefetch=1,
-            grid=(1,),
-            in_specs=[pl.BlockSpec(memory_space=pl.ANY)] * (1 + len(orders)),
-            out_specs=pl.BlockSpec(memory_space=pl.ANY),
-            scratch_shapes=[
-                pltpu.VMEM((pieces, rows, longest, cells_y, cells_z), whole.dtype),
-                pltpu.SemaphoreType.DMA((pieces,)),
-                pltpu.SemaphoreType.DMA((pieces,)),
-            ],
-        ),
-        out_shape=jax.ShapeDtypeStruct((rows, count, cells_y, cells_z), whole.dtype),
-        compiler_params=params(),
-        cost_estimate=SMALL,
-        name="cut",
-    )(at.reshape(1), whole, *orders)
+def after_kernel(at, order, out):
+    out[0] = at[0]
+
+
+def after(at, order):
+    return pl.pallas_call(
+        after_kernel,
+        in_specs=[pl.BlockSpec(memory_space=pltpu.SMEM), pl.BlockSpec(memory_space=pl.ANY)],
+        out_specs=pl.BlockSpec(memory_space=pltpu.SMEM),
+        out_shape=jax.ShapeDtypeStruct((1,), jnp.int32),
+        cost_estimate=SMALL,
+        name="after",
+    )(at.reshape(1), order)[0]
 
 
 def merge_kernel(blk, whole, theirs, node, root):
@@ -411,6 +380,8 @@
 
 
 def line_sum(x, axis):
+    if lax.axis_size(axis) != 4:
+        return lax.psum(x, axis)
     x = x + lax.ppermute(x, axis, [(0, 1), (1, 0), (2, 3), (3, 2)])
     x = x + lax.ppermute(x, axis, [(1, 2), (2, 1)])
     outer = lax.ppermute(x, axis, [(1, 0), (2, 3)])
@@ -433,8 +404,11 @@
         forward, back = half + 1 + offset, half - 1 - offset - count
         return jnp.where(top == 0, forward, back).astype(jnp.int32)
 
-    def send(at, count, *orders):
-        return swap(cut(own, at, count, *orders))
+    def cut(at, count):
+        return lax.dynamic_slice_in_dim(own, at, count, axis=1)
+
+    def send(at, count):
+        return swap(cut(at, count))
 
     last = half // 16
     middle = half // 8
@@ -474,7 +448,7 @@
     belongs = (parent[leaf] == jnp.arange(nodes, dtype=jnp.int32)).astype(jnp.float32)
     whole = paired_sum(belongs[:, None, None] * whole[None], "leaf")
     theirs = crossed(jnp.concatenate([whole[p, :, rows:] for p in range(nodes)], axis=1))
-    far += [send(far_spot(o, n, 1 - upper), n, whole) for o, n in zip(far_at[1:], fars[1:])]
+    far += [send(after(far_spot(o, n, 1 - upper), whole), n) for o, n in zip(far_at[1:], fars[1:])]
 
     vectors = expand(spread, own, met, jnp.full_like(upper, half - 1), None)
     for chunk, offset, count in zip(near, near_at, nears):
@@ -485,7 +459,7 @@
     for chunk, at in zip(far[:-1], places[:-1]):
         vectors = expand(spread, own, chunk, at, vectors, *order)
         order = ()
-    vectors = expand_last(spread, cut(own, places[-1], last, whole), far[-1], places[-1], vectors)
+    vectors = expand_last(spread, cut(after(places[-1], whole), last), far[-1], places[-1], vectors)
     return (node_stiffness, root_stiffness, vectors[None])
 
 
@@ -557,10 +531,17 @@
     return (node_stiffness, root_stiffness, leaf_vectors)
 
 
+def body(modes, *others):
+    leaves = lax.axis_size("leaf")
+    paired = leaves >= 4 and leaves & (leaves - 1) == 0
+    layers, cells_y = modes.shape[2:4]
+    fits = layers % 2 == 0 and layers >= 32 and cells_y % SUB == 0 and modes.shape[1] % SUB == 0
+    if lax.axis_size("blk") == 2 and paired and fits:
+        return halved(modes, *others)
+    return gathered(modes, *others)
+
+
 def solution(mesh):
-    body = gathered
-    if dict(mesh.shape) == {"leaf": 4, "dof": 4, "blk": 2}:
-        body = halved
     in_specs = (
         P("leaf", "blk", "dof", None, None),
         P("leaf", "dof", None, None),

time: 190 us -> 191 us (level)
  Pallas kernels: 114 us -> 98.9 us
  local copies, waits for them, and re-layouts: 7.52 us -> 18.3 us
  between operations: 1.27 us -> 7.02 us
  waiting for transfers between devices: 39.4 us -> 37.1 us
    pallas_call x9 -> x3, Pallas kernels: 17.1 us -> 1.56 us  [after(): pl.pallas_call(after_kernel, in_specs=[pl.BlockSpec(memory_space=pltpu.SM...]
    dynamic_slice x0 -> x4, local copies, waits for them, and re-layouts: none -> 11.9 us  [cut(): return lax.dynamic_slice_in_dim(own, at, count, axis=1)]
    ppermute x9, waiting for transfers between devices: 25.4 us -> 18.2 us  [swap(): return lax.ppermute(x, 'blk', [(0, 1), (1, 0)])]
    ppermute x1, waiting for transfers between devices: 0.01 us -> 2.5 us  [halved(): lax.ppermute(own[:, :1], 'dof', [(i + 1, i) for i in range(size - 1)])]
    ppermute x1, waiting for transfers between devices: 0.01 us -> 2.4 us  [halved(): lax.ppermute(own[:, -1:], 'dof', [(i, i + 1) for i in range(size - 1)])]
  transfers between devices with their start and end apart: 18 -> 18, of which waited for: 8 -> 10; matrix products, arithmetic and copies ran while one was open for 3% -> 9% of each run, Pallas kernels for 59% -> 51%
where the time goes in v6:
time: 191 us; the launch traced here: 189 us
  Pallas kernels  98.9 us (52%)
  waiting for transfers between devices  37.1 us (19%)
  starting transfers between devices  25.3 us (13%)
  local copies, waits for them, and re-layouts  18.3 us (10%)
  between operations  7.02 us (4%)
    pallas_call x1, Pallas kernels, stiff_terms(): pl.pallas_call(stiff_kernel, grid=(layers,), in_specs=[pl.BlockSpec(block...  40.1 us
    pallas_call x8, Pallas kernels, expand(): pl.pallas_call(vector_kernel, grid_spec=pltpu.PrefetchScalarGridSpec(num_...  34.6 us
    pallas_call x6, Pallas kernels, cross_terms(): pl.pallas_call(cross_kernel, grid_spec=pltpu.PrefetchScalarGridSpec(num_s...  18.9 us
    ppermute x9, waiting for transfers between devices, swap(): return lax.ppermute(x, 'blk', [(0, 1), (1, 0)])  18.2 us
    ppermute x9, starting transfers between devices, swap(): return lax.ppermute(x, 'blk', [(0, 1), (1, 0)])  12.8 us
    dynamic_slice x4, local copies, waits for them, and re-layouts, cut(): return lax.dynamic_slice_in_dim(own, at, count, axis=1)  11.9 us
    ppermute x1, waiting for transfers between devices, line_sum(): outer = lax.ppermute(x, axis, [(1, 0), (2, 3)])  7.73 us
    ppermute x2, waiting for transfers between devices, paired_sum(): x = x + lax.ppermute(x, axis, [(i, i ^ step) for i in range(size)])  4.28 us
  transfers between devices with their start and end apart: 18, of which 10 were waited for; matrix products, arithmetic and copies ran while one was open for 9% of the time, Pallas kernels for 51%

profile of v6, /device:TPU:0, one launch (start us, length us, event | category | flops | bytes accessed | tf_op | source)
XLA Modules:
  0.0 189.0 jit_solution(14218962648285246872)
XLA Ops:
  0.6 1.9 slice.40
  2.5 3.0 %collective-permute-start.2 = (bf16[64,2,16,128]{3,2,1,0:T(8,128)(2,1)}, bf16[64,2,16,128]{3,2,1,0:T(8,128)(2,1)S(1)}, u32[]{:S(2)}, u32[]{:S(2)}) collective-permute-start(bf16[64,2,16,128]{3,2,1,0:T(8,128)(2,1)} %slice.40), channel_id=1, source_target_pairs={{0,1},{1,0},{2,3},{3,2},{4,5},{5,4},{6,7},{7,6},{8,9},{9,8},{10,11... | collective-permute-start | bytes 1572872 | tf_op jit(solution)/shard_map/ppermute | solution.py:359
  5.5 4.1 %dynamic-slice_bitcast_fusion.5 = (bf16[64,3,16,128]{3,2,1,0:T(8,128)(2,1)}, bf16[64,3,16,128]{3,2,1,0:T(8,128)(2,1)}, bf16[64,3,16,128]{3,2,1,0:T(8,128)(2,1)},...) fusion(bf16[1,64,32,16,128]{4,3,2,1,0:T(8,128)(2,1)} %param.5, s32[]{:T(128)S(6)} %select_n.122, ...), kind=kLoop, calls=%fused_computation.8 | loop fusion | bytes 7864340 | tf_op jit(solution)/shard_map/dynamic_slice | solution.py:408
  9.7 2.2 %slice_bitcast_fusion.3 = (bf16[64,16,128]{2,1,0:T(8,128)(2,1)S(1)}, bf16[64,16,128]{2,1,0:T(8,128)(2,1)}, bf16[64,1,16,128]{3,2,1,0:T(8,128)(2,1)}, bf16[64,1,16,128]{3,2,1,0:T(8,128)(2,1)}) fusion(bf16[64,32,16,128]{3,2,1,0:T(8,128)(2,1)} %bitcast.66), kind=kLoop, calls=%fused_computation.13 | loop fusion | bytes 2097152 | tf_op jit(solution)/shard_map/squeeze | solution.py:438
  11.9 3.9 %collective-permute-start = (bf16[64,1,16,128]{3,2,1,0:T(8,128)(2,1)}, bf16[64,1,16,128]{3,2,1,0:T(8,128)(2,1)S(1)}, u32[]{:S(2)}, u32[]{:S(2)}) collective-permute-start(bf16[64,1,16,128]{3,2,1,0:T(8,128)(2,1)} %get-tuple-element.18), channel_id=1, source_target_pairs={{0,2},{2,4},{4,6},{1,3},{3,5},{5,7},{8,10},{10,12},{12,14},{9,11},... | collective-permute-start | bytes 786440 | tf_op jit(solution)/shard_map/ppermute | solution.py:425
  18.7 2.4 %collective-permute-done.low = bf16[64,1,16,128]{3,2,1,0:T(8,128)(2,1)S(1)} collective-permute-done((bf16[64,1,16,128]{3,2,1,0:T(8,128)(2,1)}, bf16[64,1,16,128]{3,2,1,0:T(8,128)(2,1)S(1)}, u32[]{:S(2)}, u32[]{:S(2)}) %collective-permute-start) | collective-permute-done | bytes 262176 | tf_op jit(solution)/shard_map/ppermute | solution.py:425
  22.6 2.5 %collective-permute-done.1.high = bf16[64,1,16,128]{3,2,1,0:T(8,128)(2,1)S(1)} collective-permute-done((bf16[64,1,16,128]{3,2,1,0:T(8,128)(2,1)}, bf16[64,1,16,128]{3,2,1,0:T(8,128)(2,1)S(1)}, u32[]{:S(2)}, u32[]{:S(2)}) %collective-permute-start.1) | collective-permute-done | bytes 262176 | tf_op jit(solution)/shard_map/ppermute | solution.py:426
  27.1 4.1 %dynamic-slice_bitcast_fusion = bf16[64,12,16,128]{3,2,1,0:T(8,128)(2,1)} fusion(bf16[1,64,32,16,128]{4,3,2,1,0:T(8,128)(2,1)} %param.5, s32[]{:T(128)S(6)} %select_n.146), kind=kLoop, calls=%fused_computation | loop fusion | bytes 6291460 | tf_op jit(solution)/shard_map/dynamic_slice | solution.py:408
  31.2 40.1 %stiff_terms.1 = (bf16[32,512,256]{2,1,0:T(8,128)(2,1)}, f32[64,64]{1,0:T(8,128)S(1)}, f32[16,64]{1,0:T(8,128)S(1)}) custom-call(bf16[64,32,16,128]{3,2,1,0:T(8,128)(2,1)} %bitcast.67, bf16[64,32,16,128]{3,2,1,0:T(8,128)(2,1)} %bitcast.68, bf16[64,32,16,128]{3,2,1,0:T(8,128)(2,1)} %bitcast.69, bf16[64,1,16,128]{3,2,1,0:T(8,128)(2,1)S(1)} %collective-permute-done.low, ...), custom_call_target="tpu_custom_call" | custom-call | flops 1024 | bytes 1024 | tf_op jit(solution)/shard_map/stiff_terms/pallas_call | solution.py:100
  71.3 1.8 cross_terms.6
  75.2 3.3 %cross_terms.7 = f32[64,64]{1,0:T(8,128)S(1)} custom-call(s32[1]{0:T(128)} %bitcast.13.at, s32[1]{0:T(128)} %constant.77.clone.1.skip, bf16[32,512,256]{2,1,0:T(8,128)(2,1)} %get-tuple-element.9.stiff, bf16[64,3,16,128]{3,2,1,0:T(8,128)(2,1)S(1)} %collective-permute-done.3.other), custom_call_target="tpu_custom_call" | custom-call | flops 1024 | bytes 1024 | tf_op jit(solution)/shard_map/cross_terms/pallas_call | solution.py:151
  78.5 3.3 %cross_terms.8 = f32[64,64]{1,0:T(8,128)S(1)} custom-call(s32[1]{0:T(128)} %bitcast.15.at, s32[1]{0:T(128)} %constant.77.clone.1.skip, bf16[32,512,256]{2,1,0:T(8,128)(2,1)} %get-tuple-element.9.stiff, bf16[64,3,16,128]{3,2,1,0:T(8,128)(2,1)S(1)} %collective-permute-done.4.other), custom_call_target="tpu_custom_call" | custom-call | flops 1024 | bytes 1024 | tf_op jit(solution)/shard_map/cross_terms/pallas_call | solution.py:151
  81.9 3.5 %cross_terms.9 = f32[64,64]{1,0:T(8,128)S(1)} custom-call(s32[1]{0:T(128)} %bitcast.17.at, s32[1]{0:T(128)} %constant.77.clone.1.skip, bf16[32,512,256]{2,1,0:T(8,128)(2,1)} %get-tuple-element.9.stiff, bf16[64,3,16,128]{3,2,1,0:T(8,128)(2,1)S(1)} %collective-permute-done.5.other), custom_call_target="tpu_custom_call" | custom-call | flops 1024 | bytes 1024 | tf_op jit(solution)/shard_map/cross_terms/pallas_call | solution.py:151
  85.9 3.5 %cross_terms.10 = f32[64,64]{1,0:T(8,128)S(1)} custom-call(s32[1]{0:T(128)} %bitcast.19.at, s32[1]{0:T(128)} %constant.77.clone.1.skip, bf16[32,512,256]{2,1,0:T(8,128)(2,1)} %get-tuple-element.9.stiff, bf16[64,3,16,128]{3,2,1,0:T(8,128)(2,1)S(1)} %collective-permute-done.6.other), custom_call_target="tpu_custom_call" | custom-call | flops 1024 | bytes 1024 | tf_op jit(solution)/shard_map/cross_terms/pallas_call | solution.py:151
  89.4 13.3 %collective-permute-done.7.other = bf16[64,3,16,128]{3,2,1,0:T(8,128)(2,1)S(1)} collective-permute-done((bf16[64,3,16,128]{3,2,1,0:T(8,128)(2,1)}, bf16[64,3,16,128]{3,2,1,0:T(8,128)(2,1)S(1)}, u32[]{:S(2)}, u32[]{:S(2)}) %collective-permute-start.7) | collective-permute-done | bytes 786464 | tf_op jit(solution)/shard_map/ppermute | solution.py:359
  102.7 3.5 %cross_terms.11 = f32[64,64]{1,0:T(8,128)S(1)} custom-call(s32[1]{0:T(128)} %bitcast.21.at, s32[1]{0:T(128)} %constant.77.clone.1.skip, bf16[32,512,256]{2,1,0:T(8,128)(2,1)} %get-tuple-element.9.stiff, bf16[64,3,16,128]{3,2,1,0:T(8,128)(2,1)S(1)} %collective-permute-done.7.other), custom_call_target="tpu_custom_call" | custom-call | flops 1024 | bytes 1024 | tf_op jit(solution)/shard_map/cross_terms/pallas_call | solution.py:151
  106.3 2.1 %collective-permute-start.8 = (f32[80,128]{1,0:T(8,128)S(1)}, f32[80,128]{1,0:T(8,128)S(1)}, u32[]{:S(2)}, u32[]{:S(2)}) collective-permute-start(f32[80,128]{1,0:T(8,128)S(1)} %maximum_maximum_fusion), channel_id=1, source_target_pairs={{0,2},{2,0},{4,6},{6,4},{1,3},{3,1},{5,7},{7,5},{8,10},{10,8},{12,... | collective-permute-start | bytes 122888 | tf_op jit(solution)/shard_map/ppermute | solution.py:385
  108.5 2.0 %collective-permute-done.8 = f32[80,128]{1,0:T(8,128)S(1)} collective-permute-done((f32[80,128]{1,0:T(8,128)S(1)}, f32[80,128]{1,0:T(8,128)S(1)}, u32[]{:S(2)}, u32[]{:S(2)}) %collective-permute-start.8) | collective-permute-done | bytes 40992 | tf_op jit(solution)/shard_map/ppermute | solution.py:385
  113.9 7.7 %collective-permute-done.10 = f32[80,128]{1,0:T(8,128)S(1)} collective-permute-done((f32[80,128]{1,0:T(8,128)S(1)}, f32[80,128]{1,0:T(8,128)S(1)}, u32[]{:S(2)}, u32[]{:S(2)}) %collective-permute-start.10) | collective-permute-done | bytes 40992 | tf_op jit(solution)/shard_map/ppermute | solution.py:387
  124.6 3.0 %collective-permute-done.12 = f32[2,80,128]{2,1,0:T(8,128)S(1)} collective-permute-done((f32[2,80,128]{2,1,0:T(8,128)S(1)}, f32[2,80,128]{2,1,0:T(8,128)S(1)}, u32[]{:S(2)}, u32[]{:S(2)}) %collective-permute-start.12) | collective-permute-done | bytes 81952 | tf_op jit(solution)/shard_map/ppermute | solution.py:377
  134.6 1.9 %dynamic-slice_bitcast_fusion.6 = bf16[64,2,16,128]{3,2,1,0:T(8,128)(2,1)} fusion(bf16[1,64,32,16,128]{4,3,2,1,0:T(8,128)(2,1)} %param.5, s32[]{:T(128)S(6)} %select_n.144), kind=kLoop, calls=%fused_computation.9 | loop fusion | bytes 1048580 | tf_op jit(solution)/shard_map/dynamic_slice | solution.py:408
  141.7 1.8 dynamic-slice_bitcast_fusion.7
  145.8 2.6 %expand.8.rest_0_ = bf16[64,32,16,128]{3,2,1,0:T(8,128)(2,1)} custom-call(s32[1]{0:T(128)} %constant.90.clone.1.at, bf16[512,1024]{1,0:T(8,128)(2,1)S(1)} %spread_blocks.1.spread, bf16[64,32,16,128]{3,2,1,0:T(8,128)(2,1)} %bitcast.70, bf16[64,2,16,128]{3,2,1,0:T(8,128)(2,1)S(1)} %collective-permute-done.2.order.other), custom_call_target="tpu_custom_call" | custom-call | flops 1024 | bytes 1024 | tf_op jit(solution)/shard_map/expand/pallas_call | solution.py:291
  148.4 3.6 %expand.9.rest_0_ = bf16[64,32,16,128]{3,2,1,0:T(8,128)(2,1)} custom-call(s32[1]{0:T(128)} %bitcast.13.at, bf16[512,1024]{1,0:T(8,128)(2,1)S(1)} %spread_blocks.1.spread, bf16[64,32,16,128]{3,2,1,0:T(8,128)(2,1)} %bitcast.71, bf16[64,3,16,128]{3,2,1,0:T(8,128)(2,1)S(1)} %collective-permute-done.3.other, ...), custom_call_target="tpu_custom_call", output_to_operand_aliasing={{}: (4, {})} | custom-call | flops 1024 | bytes 1024 | tf_op jit(solution)/shard_map/expand/pallas_call | solution.py:291
  152.0 3.7 %expand.10.rest_0_ = bf16[64,32,16,128]{3,2,1,0:T(8,128)(2,1)} custom-call(s32[1]{0:T(128)} %bitcast.15.at, bf16[512,1024]{1,0:T(8,128)(2,1)S(1)} %spread_blocks.1.spread, bf16[64,32,16,128]{3,2,1,0:T(8,128)(2,1)} %bitcast.72, bf16[64,3,16,128]{3,2,1,0:T(8,128)(2,1)S(1)} %collective-permute-done.4.other, ...), custom_call_target="tpu_custom_call", output_to_operand_aliasing={{}: (4, {})} | custom-call | flops 1024 | bytes 1024 | tf_op jit(solution)/shard_map/expand/pallas_call | solution.py:291
  155.7 3.7 %expand.11.rest_0_ = bf16[64,32,16,128]{3,2,1,0:T(8,128)(2,1)} custom-call(s32[1]{0:T(128)} %bitcast.17.at, bf16[512,1024]{1,0:T(8,128)(2,1)S(1)} %spread_blocks.1.spread, bf16[64,32,16,128]{3,2,1,0:T(8,128)(2,1)} %bitcast.73, bf16[64,3,16,128]{3,2,1,0:T(8,128)(2,1)S(1)} %copy-done.1, ...), custom_call_target="tpu_custom_call", output_to_operand_aliasing={{}: (4, {})} | custom-call | flops 1024 | bytes 1024 | tf_op jit(solution)/shard_map/expand/pallas_call | solution.py:291
  159.4 3.7 %expand.12.rest_0_ = bf16[64,32,16,128]{3,2,1,0:T(8,128)(2,1)} custom-call(s32[1]{0:T(128)} %bitcast.19.at, bf16[512,1024]{1,0:T(8,128)(2,1)S(1)} %spread_blocks.1.spread, bf16[64,32,16,128]{3,2,1,0:T(8,128)(2,1)} %bitcast.74, bf16[64,3,16,128]{3,2,1,0:T(8,128)(2,1)S(1)} %copy-done.3, ...), custom_call_target="tpu_custom_call", output_to_operand_aliasing={{}: (4, {})} | custom-call | flops 1024 | bytes 1024 | tf_op jit(solution)/shard_map/expand/pallas_call | solution.py:291
  163.2 3.7 %expand.13.rest_0_ = bf16[64,32,16,128]{3,2,1,0:T(8,128)(2,1)} custom-call(s32[1]{0:T(128)} %bitcast.21.at, bf16[512,1024]{1,0:T(8,128)(2,1)S(1)} %spread_blocks.1.spread, bf16[64,32,16,128]{3,2,1,0:T(8,128)(2,1)} %bitcast.75, bf16[64,3,16,128]{3,2,1,0:T(8,128)(2,1)S(1)} %copy-done.5, ...), custom_call_target="tpu_custom_call", output_to_operand_aliasing={{}: (4, {})} | custom-call | flops 1024 | bytes 1024 | tf_op jit(solution)/shard_map/expand/pallas_call | solution.py:291
  167.9 2.8 %collective-permute-done.17.other = bf16[64,12,16,128]{3,2,1,0:T(8,128)(2,1)} collective-permute-done((bf16[64,12,16,128]{3,2,1,0:T(8,128)(2,1)}, bf16[64,12,16,128]{3,2,1,0:T(8,128)(2,1)}, u32[]{:S(2)}, u32[]{:S(2)}) %collective-permute-start.17) | collective-permute-done | bytes 3145760 | tf_op jit(solution)/shard_map/ppermute | solution.py:359
  171.4 10.9 %expand.14.rest_0_ = bf16[64,32,16,128]{3,2,1,0:T(8,128)(2,1)} custom-call(s32[1]{0:T(128)} %bitcast.38.at, bf16[512,1024]{1,0:T(8,128)(2,1)S(1)} %spread_blocks.1.spread, bf16[64,32,16,128]{3,2,1,0:T(8,128)(2,1)} %bitcast.76, bf16[64,12,16,128]{3,2,1,0:T(8,128)(2,1)} %collective-permute-done.17.other, ...), custom_call_target="tpu_custom_call", output_to_operand_aliasing={{}: (4, {})} | custom-call | flops 1024 | bytes 1024 | tf_op jit(solution)/shard_map/expand/pallas_call | solution.py:291
  182.4 2.7 %expand.15.held = bf16[64,32,16,128]{3,2,1,0:T(8,128)(2,1)} custom-call(s32[1]{0:T(128)} %bitcast.34.at, bf16[512,1024]{1,0:T(8,128)(2,1)S(1)} %spread_blocks.1.spread, bf16[64,32,16,128]{3,2,1,0:T(8,128)(2,1)} %bitcast.77, bf16[64,2,16,128]{3,2,1,0:T(8,128)(2,1)} %collective-permute-done.16.other, ...), custom_call_target="tpu_custom_call", output_to_operand_aliasing={{}: (4, {})} | custom-call | flops 1024 | bytes 1024 | tf_op jit(solution)/shard_map/expand/pallas_call | solution.py:291
  186.7 2.1 %expand_last.1 = bf16[64,32,16,128]{3,2,1,0:T(8,128)(2,1)} custom-call(s32[1]{0:T(128)} %bitcast.25.at, bf16[512,1024]{1,0:T(8,128)(2,1)S(1)} %spread_blocks.1.spread, bf16[64,1,16,128]{3,2,1,0:T(8,128)(2,1)S(1)} %get-tuple-element.14.own, bf16[64,1,16,128]{3,2,1,0:T(8,128)(2,1)} %collective-permute-done.15.other, ...), custom_call_target="tpu_custom_call", output_to_operand_aliasing={{}: (4, {})} | custom-call | flops 1024 | bytes 1024 | tf_op jit(solution)/shard_map/expand_last/pallas_call | solution.py:338
  (75 shorter events, 27.6 us)
Async XLA Ops:
  2.5 28.7 %copy-start.7 = (f32[1,32,16,128]{3,2,1,0:T(8,128)S(1)}, f32[1,32,16,128]{3,2,1,0:T(8,128)}, u32[]{:S(2)}) copy-start(f32[1,32,16,128]{3,2,1,0:T(8,128)} %param.6) | copy-start | bytes 786436
  2.5 28.7 %copy-start.8 = (f32[1,32,16,128]{3,2,1,0:T(8,128)S(1)}, f32[1,32,16,128]{3,2,1,0:T(8,128)}, u32[]{:S(2)}) copy-start(f32[1,32,16,128]{3,2,1,0:T(8,128)} %param.7) | copy-start | bytes 786436
  2.5 24.1 %collective-permute-start.2 = (bf16[64,2,16,128]{3,2,1,0:T(8,128)(2,1)}, bf16[64,2,16,128]{3,2,1,0:T(8,128)(2,1)S(1)}, u32[]{:S(2)}, u32[]{:S(2)}) collective-permute-start(bf16[64,2,16,128]{3,2,1,0:T(8,128)(2,1)} %slice.40), channel_id=1, source_target_pairs={{0,1},{1,0},{2,3},{3,2},{4,5},{5,4},{6,7},{7,6},{8,9},{9,8},{10,11... | collective-permute-start | bytes 1572872 | tf_op jit(solution)/shard_map/ppermute | solution.py:359
  9.6 63.5 %collective-permute-start.3 = (bf16[64,3,16,128]{3,2,1,0:T(8,128)(2,1)}, bf16[64,3,16,128]{3,2,1,0:T(8,128)(2,1)S(1)}, u32[]{:S(2)}, u32[]{:S(2)}) collective-permute-start(bf16[64,3,16,128]{3,2,1,0:T(8,128)(2,1)} %get-tuple-element.19), channel_id=1, source_target_pairs={{0,1},{1,0},{2,3},{3,2},{4,5},{5,4},{6,7},{7,6},{8,9},{9,8},{10,11... | collective-permute-start | bytes 2359304 | tf_op jit(solution)/shard_map/ppermute | solution.py:359
  11.9 9.2 %collective-permute-start = (bf16[64,1,16,128]{3,2,1,0:T(8,128)(2,1)}, bf16[64,1,16,128]{3,2,1,0:T(8,128)(2,1)S(1)}, u32[]{:S(2)}, u32[]{:S(2)}) collective-permute-start(bf16[64,1,16,128]{3,2,1,0:T(8,128)(2,1)} %get-tuple-element.18), channel_id=1, source_target_pairs={{0,2},{2,4},{4,6},{1,3},{3,5},{5,7},{8,10},{10,12},{12,14},{9,11},... | collective-permute-start | bytes 786440 | tf_op jit(solution)/shard_map/ppermute | solution.py:425
  15.8 9.3 %collective-permute-start.1 = (bf16[64,1,16,128]{3,2,1,0:T(8,128)(2,1)}, bf16[64,1,16,128]{3,2,1,0:T(8,128)(2,1)S(1)}, u32[]{:S(2)}, u32[]{:S(2)}) collective-permute-start(bf16[64,1,16,128]{3,2,1,0:T(8,128)(2,1)} %get-tuple-element.17), channel_id=1, source_target_pairs={{2,0},{4,2},{6,4},{3,1},{5,3},{7,5},{10,8},{12,10},{14,12},{11,9},... | collective-permute-start | bytes 786440 | tf_op jit(solution)/shard_map/ppermute | solution.py:426
  17.1 61.4 %collective-permute-start.4 = (bf16[64,3,16,128]{3,2,1,0:T(8,128)(2,1)}, bf16[64,3,16,128]{3,2,1,0:T(8,128)(2,1)S(1)}, u32[]{:S(2)}, u32[]{:S(2)}) collective-permute-start(bf16[64,3,16,128]{3,2,1,0:T(8,128)(2,1)} %get-tuple-element.23), channel_id=1, source_target_pairs={{0,1},{1,0},{2,3},{3,2},{4,5},{5,4},{6,7},{7,6},{8,9},{9,8},{10,11... | collective-permute-start | bytes 2359304 | tf_op jit(solution)/shard_map/ppermute | solution.py:359
  21.1 60.8 %collective-permute-start.5 = (bf16[64,3,16,128]{3,2,1,0:T(8,128)(2,1)}, bf16[64,3,16,128]{3,2,1,0:T(8,128)(2,1)S(1)}, u32[]{:S(2)}, u32[]{:S(2)}) collective-permute-start(bf16[64,3,16,128]{3,2,1,0:T(8,128)(2,1)} %get-tuple-element.22), channel_id=1, source_target_pairs={{0,1},{1,0},{2,3},{3,2},{4,5},{5,4},{6,7},{7,6},{8,9},{9,8},{10,11... | collective-permute-start | bytes 2359304 | tf_op jit(solution)/shard_map/ppermute | solution.py:359
  25.1 60.8 %collective-permute-start.6 = (bf16[64,3,16,128]{3,2,1,0:T(8,128)(2,1)}, bf16[64,3,16,128]{3,2,1,0:T(8,128)(2,1)S(1)}, u32[]{:S(2)}, u32[]{:S(2)}) collective-permute-start(bf16[64,3,16,128]{3,2,1,0:T(8,128)(2,1)} %get-tuple-element.21), channel_id=1, source_target_pairs={{0,1},{1,0},{2,3},{3,2},{4,5},{5,4},{6,7},{7,6},{8,9},{9,8},{10,11... | collective-permute-start | bytes 2359304 | tf_op jit(solution)/shard_map/ppermute | solution.py:359
  26.6 76.1 %collective-permute-start.7 = (bf16[64,3,16,128]{3,2,1,0:T(8,128)(2,1)}, bf16[64,3,16,128]{3,2,1,0:T(8,128)(2,1)S(1)}, u32[]{:S(2)}, u32[]{:S(2)}) collective-permute-start(bf16[64,3,16,128]{3,2,1,0:T(8,128)(2,1)} %get-tuple-element.20), channel_id=1, source_target_pairs={{0,1},{1,0},{2,3},{3,2},{4,5},{5,4},{6,7},{7,6},{8,9},{9,8},{10,11... | collective-permute-start | bytes 2359304 | tf_op jit(solution)/shard_map/ppermute | solution.py:359
  71.3 3.4 %copy-start.10 = (bf16[64,16,128]{2,1,0:T(8,128)(2,1)S(1)}, bf16[64,16,128]{2,1,0:T(8,128)(2,1)}, u32[]{:S(2)}) copy-start(bf16[64,16,128]{2,1,0:T(8,128)(2,1)} %get-tuple-element.16) | copy-start | bytes 786436
  73.2 97.5 %collective-permute-start.17 = (bf16[64,12,16,128]{3,2,1,0:T(8,128)(2,1)}, bf16[64,12,16,128]{3,2,1,0:T(8,128)(2,1)}, u32[]{:S(2)}, u32[]{:S(2)}) collective-permute-start(bf16[64,12,16,128]{3,2,1,0:T(8,128)(2,1)} %dynamic-slice_bitcast_fusion), channel_id=1, source_target_pairs={{0,1},{1,0},{2,3},{3,2},{4,5},{5,4},{6,7},{7,6},{8,9},{9,8},{10,11... | collective-permute-start | bytes 9437192 | tf_op jit(solution)/shard_map/ppermute | solution.py:359
  81.9 7.5 %copy-start = (bf16[64,3,16,128]{3,2,1,0:T(8,128)(2,1)}, bf16[64,3,16,128]{3,2,1,0:T(8,128)(2,1)S(1)}, u32[]{:S(2)}) copy-start(bf16[64,3,16,128]{3,2,1,0:T(8,128)(2,1)S(1)} %collective-permute-done.5.other) | copy-start | bytes 2359300
  85.9 20.3 %copy-start.2 = (bf16[64,3,16,128]{3,2,1,0:T(8,128)(2,1)}, bf16[64,3,16,128]{3,2,1,0:T(8,128)(2,1)S(1)}, u32[]{:S(2)}) copy-start(bf16[64,3,16,128]{3,2,1,0:T(8,128)(2,1)S(1)} %collective-permute-done.6.other) | copy-start | bytes 2359300
  85.9 25.3 %copy-start.12 = (s32[4]{0:T(128)S(1)}, s32[4]{0:T(128)}, u32[]{:S(2)}) copy-start(s32[4]{0:T(128)} %param.9) | copy-start | bytes 52
  89.4 55.6 %copy-start.11 = (bf16[1,128,64]{1,2,0:T(8,128)(2,1)S(1)}, bf16[1,128,64]{1,2,0:T(8,128)(2,1)}, u32[]{:S(2)}) copy-start(bf16[1,128,64]{1,2,0:T(8,128)(2,1)} %param.8) | copy-start | bytes 49156
  102.7 3.5 %copy-start.4 = (bf16[64,3,16,128]{3,2,1,0:T(8,128)(2,1)}, bf16[64,3,16,128]{3,2,1,0:T(8,128)(2,1)S(1)}, u32[]{:S(2)}) copy-start(bf16[64,3,16,128]{3,2,1,0:T(8,128)(2,1)S(1)} %collective-permute-done.7.other) | copy-start | bytes 2359300
  106.3 4.1 %collective-permute-start.8 = (f32[80,128]{1,0:T(8,128)S(1)}, f32[80,128]{1,0:T(8,128)S(1)}, u32[]{:S(2)}, u32[]{:S(2)}) collective-permute-start(f32[80,128]{1,0:T(8,128)S(1)} %maximum_maximum_fusion), channel_id=1, source_target_pairs={{0,2},{2,0},{4,6},{6,4},{1,3},{3,1},{5,7},{7,5},{8,10},{10,8},{12,... | collective-permute-start | bytes 122888 | tf_op jit(solution)/shard_map/ppermute | solution.py:385
  110.5 1.3 collective-permute-start.9
  111.8 9.9 %collective-permute-start.10 = (f32[80,128]{1,0:T(8,128)S(1)}, f32[80,128]{1,0:T(8,128)S(1)}, u32[]{:S(2)}, u32[]{:S(2)}) collective-permute-start(f32[80,128]{1,0:T(8,128)S(1)} %add.82), channel_id=1, source_target_pairs={{2,0},{4,6},{3,1},{5,7},{10,8},{12,14},{11,9},{13,15},{18,16},{20,... | collective-permute-start | bytes 122888 | tf_op jit(solution)/shard_map/ppermute | solution.py:387
  121.8 1.3 collective-permute-start.11
  123.1 4.5 %collective-permute-start.12 = (f32[2,80,128]{2,1,0:T(8,128)S(1)}, f32[2,80,128]{2,1,0:T(8,128)S(1)}, u32[]{:S(2)}, u32[]{:S(2)}) collective-permute-start(f32[2,80,128]{2,1,0:T(8,128)S(1)} %fusion.6), channel_id=1, source_target_pairs={{0,16},{8,24},{16,0},{24,8},{1,17},{9,25},{17,1},{25,9},{2,18},{10... | collective-permute-start | bytes 245768 | tf_op jit(solution)/shard_map/ppermute | solution.py:377
  136.5 45.9 %collective-permute-start.16 = (bf16[64,2,16,128]{3,2,1,0:T(8,128)(2,1)}, bf16[64,2,16,128]{3,2,1,0:T(8,128)(2,1)}, u32[]{:S(2)}, u32[]{:S(2)}) collective-permute-start(bf16[64,2,16,128]{3,2,1,0:T(8,128)(2,1)} %dynamic-slice_bitcast_fusion.6), channel_id=1, source_target_pairs={{0,1},{1,0},{2,3},{3,2},{4,5},{5,4},{6,7},{7,6},{8,9},{9,8},{10,11... | collective-permute-start | bytes 1572872 | tf_op jit(solution)/shard_map/ppermute | solution.py:359
  139.0 6.1 %collective-permute-start.13 = (f32[40,128]{1,0:T(8,128)S(1)}, f32[40,128]{1,0:T(8,128)S(1)}, u32[]{:S(2)}, u32[]{:S(2)}) collective-permute-start(f32[40,128]{1,0:T(8,128)S(1)} %fusion.5), channel_id=1, source_target_pairs={{0,17},{1,16},{8,25},{9,24},{16,1},{17,0},{24,9},{25,8},{2,19},{3,... | collective-permute-start | bytes 61448 | tf_op jit(solution)/shard_map/ppermute | solution.py:367
  143.5 43.2 %collective-permute-start.15 = (bf16[64,1,16,128]{3,2,1,0:T(8,128)(2,1)}, bf16[64,1,16,128]{3,2,1,0:T(8,128)(2,1)}, u32[]{:S(2)}, u32[]{:S(2)}) collective-permute-start(bf16[64,1,16,128]{3,2,1,0:T(8,128)(2,1)} %get-tuple-element.13), channel_id=1, source_target_pairs={{0,1},{1,0},{2,3},{3,2},{4,5},{5,4},{6,7},{7,6},{8,9},{9,8},{10,11... | collective-permute-start | bytes 786440 | tf_op jit(solution)/shard_map/ppermute | solution.py:359
  145.1 21.7 %collective-permute-start.14 = (f32[40,128]{1,0:T(8,128)S(1)}, f32[40,128]{1,0:T(8,128)S(1)}, u32[]{:S(2)}, u32[]{:S(2)}) collective-permute-start(f32[40,128]{1,0:T(8,128)S(1)} %collective-permute-done.13), channel_id=1, source_target_pairs={{0,8},{8,0},{16,24},{24,16},{1,9},{9,1},{17,25},{25,17},{2,10},{10... | collective-permute-start | bytes 61448 | tf_op jit(solution)/shard_map/ppermute | solution.py:368
  152.0 3.7 %copy-start.1 = (bf16[64,3,16,128]{3,2,1,0:T(8,128)(2,1)S(1)}, bf16[64,3,16,128]{3,2,1,0:T(8,128)(2,1)}, u32[]{:S(2)}) copy-start(bf16[64,3,16,128]{3,2,1,0:T(8,128)(2,1)} %copy-done) | copy-start | bytes 2359300
  155.7 3.7 %copy-start.3 = (bf16[64,3,16,128]{3,2,1,0:T(8,128)(2,1)S(1)}, bf16[64,3,16,128]{3,2,1,0:T(8,128)(2,1)}, u32[]{:S(2)}) copy-start(bf16[64,3,16,128]{3,2,1,0:T(8,128)(2,1)} %copy-done.2) | copy-start | bytes 2359300
  159.4 3.7 %copy-start.5 = (bf16[64,3,16,128]{3,2,1,0:T(8,128)(2,1)S(1)}, bf16[64,3,16,128]{3,2,1,0:T(8,128)(2,1)}, u32[]{:S(2)}) copy-start(bf16[64,3,16,128]{3,2,1,0:T(8,128)(2,1)} %copy-done.4) | copy-start | bytes 2359300
  163.1 3.7 %copy-start.6 = (f32[2,80,128]{2,1,0:T(8,128)S(1)}, f32[2,80,128]{2,1,0:T(8,128)}, u32[]{:S(2)}) copy-start(f32[2,80,128]{2,1,0:T(8,128)} %fusion.7.whole.order) | copy-start | bytes 245764
  170.7 0.8 copy-start.9

commit v7 on v5

--- a/solution.py
+++ b/solution.py
@@ -131,7 +131,7 @@
     )(own, own, own, low, high, coefs, masses, order)
 
 
-def cross_kernel(at, skip, stiff, other, gram, total):
+def cross_kernel(at, skip, stiff, other, order, gram, total):
     step = pl.program_id(0)
 
     @pl.when(step == 0)
@@ -145,7 +145,7 @@
         gram[...] = same_row_sum(total[...])
 
 
-def cross_terms(stiff, other, at, skip, layers):
+def cross_terms(stiff, other, at, skip, layers, order):
     rows, _, cells_y, cells_z = other.shape
     _, tall, wide = stiff.shape
     return pl.pallas_call(
@@ -156,6 +156,7 @@
             in_specs=[
                 pl.BlockSpec((1, tall, wide), lambda g, at, skip: (at[0] + g, 0, 0)),
                 pl.BlockSpec((rows, 1, cells_y, cells_z), lambda g, at, skip: (0, skip[0] + g, 0, 0)),
+                pl.BlockSpec(memory_space=pl.ANY),
             ],
             out_specs=pl.BlockSpec((rows, rows), lambda g, at, skip: (0, 0)),
             scratch_shapes=[pltpu.VMEM((tall, tall), jnp.float32)],
@@ -164,7 +165,7 @@
         compiler_params=params(),
         cost_estimate=SMALL,
         name="cross_terms",
-    )(at.reshape(1), skip.reshape(1), stiff, other)
+    )(at.reshape(1), skip.reshape(1), stiff, other, order)
 
 
 def cut_kernel(at, whole, *rest):
@@ -213,6 +214,41 @@
     )(at.reshape(1), whole, *orders)
 
 
+def cut_middle_kernel(start, whole, out, held, reads, writes):
+    layers = out.shape[1]
+    ins, outs = [], []
+    for i in range(layers):
+        piece = held.at[:, pl.ds(i, 1)]
+        ins.append(pltpu.make_async_copy(whole.at[:, pl.ds(start + i, 1)], piece, reads.at[i]))
+        outs.append(pltpu.make_async_copy(piece, out.at[:, pl.ds(i, 1)], writes.at[i]))
+    for copy in ins:
+        copy.start()
+    for i in range(layers):
+        ins[i].wait()
+        outs[i].start()
+    for copy in outs:
+        copy.wait()
+
+
+def cut_middle(whole, count):
+    rows, layers, cells_y, cells_z = whole.shape
+    shape = (rows, count, cells_y, cells_z)
+    return pl.pallas_call(
+        functools.partial(cut_middle_kernel, (layers - count) // 2),
+        in_specs=[pl.BlockSpec(memory_space=pl.ANY)],
+        out_specs=pl.BlockSpec(memory_space=pl.ANY),
+        scratch_shapes=[
+            pltpu.VMEM(shape, whole.dtype),
+            pltpu.SemaphoreType.DMA((count,)),
+            pltpu.SemaphoreType.DMA((count,)),
+        ],
+        out_shape=jax.ShapeDtypeStruct(shape, whole.dtype),
+        compiler_params=pltpu.CompilerParams(vmem_limit_bytes=VMEM_BYTES),
+        cost_estimate=SMALL,
+        name="cut_middle",
+    )(whole)
+
+
 def merge_kernel(blk, whole, theirs, node, root):
     nodes, _, both = whole.shape
     rows = both // 2
@@ -292,7 +328,8 @@
 
 
 def vector_kernel(at, spread, own, other, *rest):
-    out = rest[-1]
+    out, done = rest[-2:]
+    done[...] = jnp.zeros_like(done)
     rows, _, cells_y, cells_z = own.shape
     both = jnp.concatenate([split_rows(own[:, 0]), split_rows(other[:, 0])], axis=0)
     made = jnp.dot(spread[...], both, preferred_element_type=jnp.float32)
@@ -325,9 +362,15 @@
             num_scalar_prefetch=1,
             grid=(layers,),
             in_specs=specs,
-            out_specs=pl.BlockSpec((eigs, 1, cells_y, cells_z), lambda g, at: (0, at[0] + g, 0, 0)),
+            out_specs=[
+                pl.BlockSpec((eigs, 1, cells_y, cells_z), lambda g, at: (0, at[0] + g, 0, 0)),
+                pl.BlockSpec((SUB, cells_z), lambda g, at: (0, 0)),
+            ],
         ),
-        out_shape=jax.ShapeDtypeStruct((eigs,) + own.shape[1:], jnp.bfloat16),
+        out_shape=[
+            jax.ShapeDtypeStruct((eigs,) + own.shape[1:], jnp.bfloat16),
+            jax.ShapeDtypeStruct((SUB, cells_z), jnp.float32),
+        ],
         input_output_aliases=aliases,
         compiler_params=params(),
         cost_estimate=SMALL,
@@ -411,6 +454,8 @@
 
 
 def line_sum(x, axis):
+    if lax.axis_size(axis) != 4:
+        return lax.psum(x, axis)
     x = x + lax.ppermute(x, axis, [(0, 1), (1, 0), (2, 3), (3, 2)])
     x = x + lax.ppermute(x, axis, [(1, 2), (2, 1)])
     outer = lax.ppermute(x, axis, [(1, 0), (2, 3)])
@@ -436,17 +481,16 @@
     def send(at, count, *orders):
         return swap(cut(own, at, count, *orders))
 
-    last = half // 16
-    middle = half // 8
-    fars = [half - 1 - middle - last, middle, last]
-    far_at = [sum(fars[:i]) for i in range(len(fars))]
-
-    pair = own[:, half - 1 : half + 1]
-    met = swap(pair)
-    nears = shares(half - 1, PARTS)
-    near_at = [2 + sum(nears[:i]) for i in range(len(nears))]
-    near = [send(spot(o, n, 1 - upper), n) for o, n in zip(near_at, nears)]
-    far = [send(far_spot(far_at[0], fars[0], 1 - upper), fars[0])]
+    last, middle, reach = half // 16, half // 8, half // 8
+    fars = [half - reach - middle - last, middle, last]
+    far_at = [reach - 1 + sum(fars[:i]) for i in range(len(fars))]
+    nears = shares(half - reach, PARTS)
+    near_at = [reach + 1 + sum(nears[:i]) for i in range(len(nears))]
+
+    core = cut_middle(own, 2 * reach)
+    met = swap(core)
+    near = [send(spot(o, n, 1 - upper), n, core) for o, n in zip(near_at, nears)]
+    far = [send(far_spot(far_at[0], fars[0], 1 - upper), fars[0], core)]
     size = lax.axis_size("dof")
     low = lax.ppermute(own[:, -1:], "dof", [(i, i + 1) for i in range(size - 1)])
     high = lax.ppermute(own[:, :1], "dof", [(i + 1, i) for i in range(size - 1)])
@@ -461,12 +505,15 @@
         dimension_numbers=(((1, 2), (1, 2)), ((), ())),
         preferred_element_type=jnp.float32,
     )
-    border = across(pair[:, 0], met[:, 1]) - across(pair[:, 1], met[:, 0])
+    border = across(core[:, reach - 1], met[:, reach]) - across(core[:, reach], met[:, reach - 1])
     cross = jnp.where(upper == 1, 0.5 * border, -0.5 * border)
-    cross = cross + cross_terms(stiff, met, half - 1 + upper, upper, 1)
+    within = upper * reach
+    vectors, order = expand(spread, own, met, jnp.full_like(upper, half - reach), None, mass)
+    cross = cross + cross_terms(stiff, met, half - reach + within, within, reach, order)
     for chunk, offset, count in zip(near, near_at, nears):
         at = spot(offset, count, upper)
-        cross = cross + cross_terms(stiff, chunk, at, jnp.zeros_like(at), count)
+        vectors, order = expand(spread, own, chunk, at, vectors)
+        cross = cross + cross_terms(stiff, chunk, at, jnp.zeros_like(at), count, order)
 
     tops, masses = jnp.concatenate([gram, cross], axis=1), jnp.concatenate([mass, mass], axis=1)
     whole = line_sum(jnp.concatenate([tops, masses], axis=0), "dof")
@@ -476,14 +523,11 @@
     theirs = crossed(jnp.concatenate([whole[p, :, rows:] for p in range(nodes)], axis=1))
     far += [send(far_spot(o, n, 1 - upper), n, whole) for o, n in zip(far_at[1:], fars[1:])]
 
-    vectors = expand(spread, own, met, jnp.full_like(upper, half - 1), None)
-    for chunk, offset, count in zip(near, near_at, nears):
-        vectors = expand(spread, own, chunk, spot(offset, count, upper), vectors)
     node_stiffness, root_stiffness = merge(whole, theirs, blk)
     places = [far_spot(o, n, upper) for o, n in zip(far_at, fars)]
     order = (root_stiffness,)
     for chunk, at in zip(far[:-1], places[:-1]):
-        vectors = expand(spread, own, chunk, at, vectors, *order)
+        vectors, _ = expand(spread, own, chunk, at, vectors, *order)
         order = ()
     vectors = expand_last(spread, cut(own, places[-1], last, whole), far[-1], places[-1], vectors)
     return (node_stiffness, root_stiffness, vectors[None])
@@ -557,10 +601,17 @@
     return (node_stiffness, root_stiffness, leaf_vectors)
 
 
+def body(modes, *others):
+    leaves = lax.axis_size("leaf")
+    paired = leaves >= 4 and leaves & (leaves - 1) == 0
+    layers, cells_y = modes.shape[2:4]
+    fits = layers % 2 == 0 and layers >= 32 and cells_y % SUB == 0 and modes.shape[1] % SUB == 0
+    if lax.axis_size("blk") == 2 and paired and fits:
+        return halved(modes, *others)
+    return gathered(modes, *others)
+
+
 def solution(mesh):
-    body = gathered
-    if dict(mesh.shape) == {"leaf": 4, "dof": 4, "blk": 2}:
-        body = halved
     in_specs = (
         P("leaf", "blk", "dof", None, None),
         P("leaf", "dof", None, None),

time: 190 us -> 189 us (level)
  local copies, waits for them, and re-layouts: 7.52 us -> 5.52 us
    ppermute x1, waiting for transfers between devices: 0.01 us -> 2.36 us  [crossed(): part = lax.ppermute(part, ('leaf', 'blk'), pairs)]
    squeeze x2, local copies, waits for them, and re-layouts: 2.21 us -> 0.07 us  [the longest x1 0.04 us: halved(): core[:, reach - 1]]
  transfers between devices with their start and end apart: 18 -> 18, of which waited for: 8 -> 12; matrix products, arithmetic and copies ran while one was open for 3% -> 2% of each run, Pallas kernels for 59% -> 59%
where the time goes in v7:
time: 189 us; the launch traced here: 187 us
  Pallas kernels  113 us (60%)
  waiting for transfers between devices  41 us (22%)
  starting transfers between devices  24.4 us (13%)
  local copies, waits for them, and re-layouts  5.52 us (3%)
    pallas_call x1, Pallas kernels, stiff_terms(): pl.pallas_call(stiff_kernel, grid=(layers,), in_specs=[pl.BlockSpec(block...  40.1 us
    pallas_call x8, Pallas kernels, expand(): pl.pallas_call(vector_kernel, grid_spec=pltpu.PrefetchScalarGridSpec(num_...  34.9 us
    ppermute x9, waiting for transfers between devices, swap(): return lax.ppermute(x, 'blk', [(0, 1), (1, 0)])  24.2 us
    pallas_call x6, Pallas kernels, cross_terms(): pl.pallas_call(cross_kernel, grid_spec=pltpu.PrefetchScalarGridSpec(num_s...  18.8 us
    pallas_call x9, Pallas kernels, cut(): pl.pallas_call(cut_kernel, grid_spec=pltpu.PrefetchScalarGridSpec(num_sca...  15.4 us
    ppermute x9, starting transfers between devices, swap(): return lax.ppermute(x, 'blk', [(0, 1), (1, 0)])  11.6 us
    ppermute x1, waiting for transfers between devices, line_sum(): outer = lax.ppermute(x, axis, [(1, 0), (2, 3)])  7.92 us
    ppermute x2, waiting for transfers between devices, paired_sum(): x = x + lax.ppermute(x, axis, [(i, i ^ step) for i in range(size)])  4.29 us
  transfers between devices with their start and end apart: 18, of which 12 were waited for; matrix products, arithmetic and copies ran while one was open for 2% of the time, Pallas kernels for 59%

profile of v7, /device:TPU:0, one launch (start us, length us, event | category | flops | bytes accessed | tf_op | source)
XLA Modules:
  0.0 187.0 jit_solution(5372329691373753077)
XLA Ops:
  2.0 3.0 %collective-permute-start.2 = (bf16[64,4,16,128]{3,2,1,0:T(8,128)(2,1)S(1)}, bf16[64,4,16,128]{3,2,1,0:T(8,128)(2,1)S(1)}, u32[]{:S(2)}, u32[]{:S(2)}) collective-permute-start(bf16[64,4,16,128]{3,2,1,0:T(8,128)(2,1)S(1)} %cut_middle.1.rest_0_), channel_id=1, source_target_pairs={{0,1},{1,0},{2,3},{3,2},{4,5},{5,4},{6,7},{7,6},{8,9},{9,8},{10,11... | collective-permute-start | bytes 3145736 | tf_op jit(solution)/shard_map/ppermute | solution.py:433
  6.1 3.5 %collective-permute-start = (bf16[64,1,16,128]{3,2,1,0:T(8,128)(2,1)S(1)}, bf16[64,1,16,128]{3,2,1,0:T(8,128)(2,1)S(1)}, u32[]{:S(2)}, u32[]{:S(2)}) collective-permute-start(bf16[64,1,16,128]{3,2,1,0:T(8,128)(2,1)S(1)} %get-tuple-element.42), channel_id=1, source_target_pairs={{0,2},{2,4},{4,6},{1,3},{3,5},{5,7},{8,10},{10,12},{12,14},{9,11},... | collective-permute-start | bytes 786440 | tf_op jit(solution)/shard_map/ppermute | solution.py:495
  10.9 1.9 %cut.9 = bf16[64,3,16,128]{3,2,1,0:T(8,128)(2,1)} custom-call(s32[1]{0:T(128)} %bitcast.17.at, bf16[64,32,16,128]{3,2,1,0:T(8,128)(2,1)} %bitcast.52, bf16[64,4,16,128]{3,2,1,0:T(8,128)(2,1)S(1)} %cut_middle.1.rest_0_), custom_call_target="tpu_custom_call" | custom-call | flops 1024 | bytes 1024 | tf_op jit(solution)/shard_map/cut/pallas_call | solution.py:197
  19.4 1.9 %cut.12 = bf16[64,3,16,128]{3,2,1,0:T(8,128)(2,1)} custom-call(s32[1]{0:T(128)} %bitcast.23.at, bf16[64,32,16,128]{3,2,1,0:T(8,128)(2,1)} %bitcast.55, bf16[64,4,16,128]{3,2,1,0:T(8,128)(2,1)S(1)} %cut_middle.1.rest_0_), custom_call_target="tpu_custom_call" | custom-call | flops 1024 | bytes 1024 | tf_op jit(solution)/shard_map/cut/pallas_call | solution.py:197
  24.8 4.2 %collective-permute-done.2.order.other = bf16[64,4,16,128]{3,2,1,0:T(8,128)(2,1)S(1)} collective-permute-done((bf16[64,4,16,128]{3,2,1,0:T(8,128)(2,1)S(1)}, bf16[64,4,16,128]{3,2,1,0:T(8,128)(2,1)S(1)}, u32[]{:S(2)}, u32[]{:S(2)}) %collective-permute-start.2) | collective-permute-done | bytes 1048608 | tf_op jit(solution)/shard_map/ppermute | solution.py:433
  29.0 2.1 %collective-permute-start.7 = (bf16[64,2,16,128]{3,2,1,0:T(8,128)(2,1)}, bf16[64,2,16,128]{3,2,1,0:T(8,128)(2,1)}, u32[]{:S(2)}, u32[]{:S(2)}) collective-permute-start(bf16[64,2,16,128]{3,2,1,0:T(8,128)(2,1)} %cut.13), channel_id=1, source_target_pairs={{0,1},{1,0},{2,3},{3,2},{4,5},{5,4},{6,7},{7,6},{8,9},{9,8},{10,11... | collective-permute-start | bytes 1572872 | tf_op jit(solution)/shard_map/ppermute | solution.py:433
  31.8 2.8 %cut.17 = bf16[64,11,16,128]{3,2,1,0:T(8,128)(2,1)} custom-call(s32[1]{0:T(128)} %bitcast.33.at, bf16[64,32,16,128]{3,2,1,0:T(8,128)(2,1)} %bitcast.57, bf16[64,4,16,128]{3,2,1,0:T(8,128)(2,1)S(1)} %cut_middle.1.rest_0_), custom_call_target="tpu_custom_call" | custom-call | flops 1024 | bytes 1024 | tf_op jit(solution)/shard_map/cut/pallas_call | solution.py:197
  37.5 40.1 %stiff_terms.1 = (bf16[32,512,256]{2,1,0:T(8,128)(2,1)}, f32[64,64]{1,0:T(8,128)S(1)}, f32[16,64]{1,0:T(8,128)S(1)}) custom-call(bf16[64,32,16,128]{3,2,1,0:T(8,128)(2,1)} %bitcast.58, bf16[64,32,16,128]{3,2,1,0:T(8,128)(2,1)} %bitcast.59, bf16[64,32,16,128]{3,2,1,0:T(8,128)(2,1)} %bitcast.60, bf16[64,1,16,128]{3,2,1,0:T(8,128)(2,1)S(1)} %copy-done.3, ...), custom_call_target="tpu_custom_call" | custom-call | flops 1024 | bytes 1024 | tf_op jit(solution)/shard_map/stiff_terms/pallas_call | solution.py:100
  77.7 4.2 %expand.8 = (bf16[64,32,16,128]{3,2,1,0:T(8,128)(2,1)}, f32[8,128]{1,0:T(8,128)S(1)}) custom-call(s32[1]{0:T(128)} %constant.60.clone.1.at, bf16[512,1024]{1,0:T(8,128)(2,1)S(1)} %spread_blocks.1.spread, bf16[64,32,16,128]{3,2,1,0:T(8,128)(2,1)} %bitcast.61, bf16[64,4,16,128]{3,2,1,0:T(8,128)(2,1)S(1)} %collective-permute-done.2.order.other, ...), custom_call_target="tpu_custom_call" | custom-call | flops 1024 | bytes 1024 | tf_op jit(solution)/shard_map/expand/pallas_call | solution.py:359
  81.9 3.8 %expand.9 = (bf16[64,32,16,128]{3,2,1,0:T(8,128)(2,1)}, f32[8,128]{1,0:T(8,128)S(1)}) custom-call(s32[1]{0:T(128)} %bitcast.16.at, bf16[512,1024]{1,0:T(8,128)(2,1)S(1)} %spread_blocks.1.spread, bf16[64,32,16,128]{3,2,1,0:T(8,128)(2,1)} %bitcast.62, bf16[64,3,16,128]{3,2,1,0:T(8,128)(2,1)} %collective-permute-done.3.other, ...), custom_call_target="tpu_custom_call", output_to_operand_aliasing={{0}: (4, {})} | custom-call | flops 1024 | bytes 1024 | tf_op jit(solution)/shard_map/expand/pallas_call | solution.py:359
  85.7 3.8 %expand.10 = (bf16[64,32,16,128]{3,2,1,0:T(8,128)(2,1)}, f32[8,128]{1,0:T(8,128)S(1)}) custom-call(s32[1]{0:T(128)} %bitcast.18.at, bf16[512,1024]{1,0:T(8,128)(2,1)S(1)} %spread_blocks.1.spread, bf16[64,32,16,128]{3,2,1,0:T(8,128)(2,1)} %bitcast.63, bf16[64,3,16,128]{3,2,1,0:T(8,128)(2,1)} %collective-permute-done.4.other, ...), custom_call_target="tpu_custom_call", output_to_operand_aliasing={{0}: (4, {})} | custom-call | flops 1024 | bytes 1024 | tf_op jit(solution)/shard_map/expand/pallas_call | solution.py:359
  89.5 3.8 %expand.11 = (bf16[64,32,16,128]{3,2,1,0:T(8,128)(2,1)}, f32[8,128]{1,0:T(8,128)S(1)}) custom-call(s32[1]{0:T(128)} %bitcast.20.at, bf16[512,1024]{1,0:T(8,128)(2,1)S(1)} %spread_blocks.1.spread, bf16[64,32,16,128]{3,2,1,0:T(8,128)(2,1)} %bitcast.64, bf16[64,3,16,128]{3,2,1,0:T(8,128)(2,1)} %collective-permute-done.5.other, ...), custom_call_target="tpu_custom_call", output_to_operand_aliasing={{0}: (4, {})} | custom-call | flops 1024 | bytes 1024 | tf_op jit(solution)/shard_map/expand/pallas_call | solution.py:359
  93.3 3.2 %collective-permute-done.6.other = bf16[64,3,16,128]{3,2,1,0:T(8,128)(2,1)} collective-permute-done((bf16[64,3,16,128]{3,2,1,0:T(8,128)(2,1)}, bf16[64,3,16,128]{3,2,1,0:T(8,128)(2,1)}, u32[]{:S(2)}, u32[]{:S(2)}) %collective-permute-start.6) | collective-permute-done | bytes 786464 | tf_op jit(solution)/shard_map/ppermute | solution.py:433
  96.5 3.8 %expand.12 = (bf16[64,32,16,128]{3,2,1,0:T(8,128)(2,1)}, f32[8,128]{1,0:T(8,128)S(1)}) custom-call(s32[1]{0:T(128)} %bitcast.22.at, bf16[512,1024]{1,0:T(8,128)(2,1)S(1)} %spread_blocks.1.spread, bf16[64,32,16,128]{3,2,1,0:T(8,128)(2,1)} %bitcast.65, bf16[64,3,16,128]{3,2,1,0:T(8,128)(2,1)} %collective-permute-done.6.other, ...), custom_call_target="tpu_custom_call", output_to_operand_aliasing={{0}: (4, {})} | custom-call | flops 1024 | bytes 1024 | tf_op jit(solution)/shard_map/expand/pallas_call | solution.py:359
  100.3 3.5 %cross_terms.10 = f32[64,64]{1,0:T(8,128)S(1)} custom-call(s32[1]{0:T(128)} %bitcast.22.at, s32[1]{0:T(128)} %constant.65.clone.1.skip, bf16[32,512,256]{2,1,0:T(8,128)(2,1)} %get-tuple-element.23.stiff, bf16[64,3,16,128]{3,2,1,0:T(8,128)(2,1)} %collective-permute-done.6.other, f32[8,128]{1,0:T(8,128)S(1)} %get-tuple-element.33.order), custom_call_target="tpu_custom_call" | custom-call | flops 1024 | bytes 1024 | tf_op jit(solution)/shard_map/cross_terms/pallas_call | solution.py:151
  103.8 4.0 %collective-permute-done.7.other = bf16[64,2,16,128]{3,2,1,0:T(8,128)(2,1)} collective-permute-done((bf16[64,2,16,128]{3,2,1,0:T(8,128)(2,1)}, bf16[64,2,16,128]{3,2,1,0:T(8,128)(2,1)}, u32[]{:S(2)}, u32[]{:S(2)}) %collective-permute-start.7) | collective-permute-done | bytes 524320 | tf_op jit(solution)/shard_map/ppermute | solution.py:433
  107.7 2.7 %expand.13 = (bf16[64,32,16,128]{3,2,1,0:T(8,128)(2,1)}, f32[8,128]{1,0:T(8,128)S(1)}) custom-call(s32[1]{0:T(128)} %bitcast.24.at, bf16[512,1024]{1,0:T(8,128)(2,1)S(1)} %spread_blocks.1.spread, bf16[64,32,16,128]{3,2,1,0:T(8,128)(2,1)} %bitcast.66, bf16[64,2,16,128]{3,2,1,0:T(8,128)(2,1)} %collective-permute-done.7.other, ...), custom_call_target="tpu_custom_call", output_to_operand_aliasing={{0}: (4, {})} | custom-call | flops 1024 | bytes 1024 | tf_op jit(solution)/shard_map/expand/pallas_call | solution.py:359
  110.4 2.5 %cross_terms.11 = f32[64,64]{1,0:T(8,128)S(1)} custom-call(s32[1]{0:T(128)} %bitcast.24.at, s32[1]{0:T(128)} %constant.65.clone.1.skip, bf16[32,512,256]{2,1,0:T(8,128)(2,1)} %get-tuple-element.23.stiff, bf16[64,2,16,128]{3,2,1,0:T(8,128)(2,1)} %collective-permute-done.7.other, f32[8,128]{1,0:T(8,128)S(1)} %get-tuple-element.35.order), custom_call_target="tpu_custom_call" | custom-call | flops 1024 | bytes 1024 | tf_op jit(solution)/shard_map/cross_terms/pallas_call | solution.py:151
  112.8 3.5 %cross_terms.9 = f32[64,64]{1,0:T(8,128)S(1)} custom-call(s32[1]{0:T(128)} %bitcast.20.at, s32[1]{0:T(128)} %constant.65.clone.1.skip, bf16[32,512,256]{2,1,0:T(8,128)(2,1)} %get-tuple-element.23.stiff, bf16[64,3,16,128]{3,2,1,0:T(8,128)(2,1)} %collective-permute-done.5.other, f32[8,128]{1,0:T(8,128)S(1)} %get-tuple-element.31.order), custom_call_target="tpu_custom_call" | custom-call | flops 1024 | bytes 1024 | tf_op jit(solution)/shard_map/cross_terms/pallas_call | solution.py:151
  116.4 3.5 %cross_terms.8 = f32[64,64]{1,0:T(8,128)S(1)} custom-call(s32[1]{0:T(128)} %bitcast.18.at, s32[1]{0:T(128)} %constant.65.clone.1.skip, bf16[32,512,256]{2,1,0:T(8,128)(2,1)} %get-tuple-element.23.stiff, bf16[64,3,16,128]{3,2,1,0:T(8,128)(2,1)} %collective-permute-done.4.other, f32[8,128]{1,0:T(8,128)S(1)} %get-tuple-element.29.order), custom_call_target="tpu_custom_call" | custom-call | flops 1024 | bytes 1024 | tf_op jit(solution)/shard_map/cross_terms/pallas_call | solution.py:151
  119.9 3.5 %cross_terms.7 = f32[64,64]{1,0:T(8,128)S(1)} custom-call(s32[1]{0:T(128)} %bitcast.16.at, s32[1]{0:T(128)} %constant.65.clone.1.skip, bf16[32,512,256]{2,1,0:T(8,128)(2,1)} %get-tuple-element.23.stiff, bf16[64,3,16,128]{3,2,1,0:T(8,128)(2,1)} %collective-permute-done.3.other, f32[8,128]{1,0:T(8,128)S(1)} %get-tuple-element.27.order), custom_call_target="tpu_custom_call" | custom-call | flops 1024 | bytes 1024 | tf_op jit(solution)/shard_map/cross_terms/pallas_call | solution.py:151
  123.4 2.4 %cross_terms.6 = f32[64,64]{1,0:T(8,128)S(1)} custom-call(s32[1]{0:T(128)} %bitcast.11.at, s32[1]{0:T(128)} %bitcast.12.skip, bf16[32,512,256]{2,1,0:T(8,128)(2,1)} %get-tuple-element.23.stiff, bf16[64,4,16,128]{3,2,1,0:T(8,128)(2,1)S(1)} %collective-permute-done.2.order.other, f32[8,128]{1,0:T(8,128)S(1)} %get-tuple-element.25.order), custom_call_target="tpu_custom_call" | custom-call | flops 1024 | bytes 1024 | tf_op jit(solution)/shard_map/cross_terms/pallas_call | solution.py:151
  126.4 2.2 %collective-permute-start.8 = (f32[80,128]{1,0:T(8,128)S(1)}, f32[80,128]{1,0:T(8,128)S(1)}, u32[]{:S(2)}, u32[]{:S(2)}) collective-permute-start(f32[80,128]{1,0:T(8,128)S(1)} %maximum_maximum_fusion), channel_id=1, source_target_pairs={{0,2},{2,0},{4,6},{6,4},{1,3},{3,1},{5,7},{7,5},{8,10},{10,8},{12,... | collective-permute-start | bytes 122888 | tf_op jit(solution)/shard_map/ppermute | solution.py:459
  128.6 2.0 %collective-permute-done.8 = f32[80,128]{1,0:T(8,128)S(1)} collective-permute-done((f32[80,128]{1,0:T(8,128)S(1)}, f32[80,128]{1,0:T(8,128)S(1)}, u32[]{:S(2)}, u32[]{:S(2)}) %collective-permute-start.8) | collective-permute-done | bytes 40992 | tf_op jit(solution)/shard_map/ppermute | solution.py:459
  133.9 7.9 %collective-permute-done.10 = f32[80,128]{1,0:T(8,128)S(1)} collective-permute-done((f32[80,128]{1,0:T(8,128)S(1)}, f32[80,128]{1,0:T(8,128)S(1)}, u32[]{:S(2)}, u32[]{:S(2)}) %collective-permute-start.10) | collective-permute-done | bytes 40992 | tf_op jit(solution)/shard_map/ppermute | solution.py:461
  144.7 3.0 %collective-permute-done.12 = f32[2,80,128]{2,1,0:T(8,128)S(1)} collective-permute-done((f32[2,80,128]{2,1,0:T(8,128)S(1)}, f32[2,80,128]{2,1,0:T(8,128)S(1)}, u32[]{:S(2)}, u32[]{:S(2)}) %collective-permute-start.12) | collective-permute-done | bytes 81952 | tf_op jit(solution)/shard_map/ppermute | solution.py:451
  152.3 2.4 %collective-permute-start.13 = (f32[40,128]{1,0:T(8,128)S(1)}, f32[40,128]{1,0:T(8,128)S(1)}, u32[]{:S(2)}, u32[]{:S(2)}) collective-permute-start(f32[40,128]{1,0:T(8,128)S(1)} %fusion.5), channel_id=1, source_target_pairs={{0,17},{1,16},{8,25},{9,24},{16,1},{17,0},{24,9},{25,8},{2,19},{3,... | collective-permute-start | bytes 61448 | tf_op jit(solution)/shard_map/ppermute | solution.py:441
  154.7 2.4 %collective-permute-done.13 = f32[40,128]{1,0:T(8,128)S(1)} collective-permute-done((f32[40,128]{1,0:T(8,128)S(1)}, f32[40,128]{1,0:T(8,128)S(1)}, u32[]{:S(2)}, u32[]{:S(2)}) %collective-permute-start.13) | collective-permute-done | bytes 20512 | tf_op jit(solution)/shard_map/ppermute | solution.py:441
  159.3 10.6 %collective-permute-done.17.other = bf16[64,11,16,128]{3,2,1,0:T(8,128)(2,1)} collective-permute-done((bf16[64,11,16,128]{3,2,1,0:T(8,128)(2,1)}, bf16[64,11,16,128]{3,2,1,0:T(8,128)(2,1)}, u32[]{:S(2)}, u32[]{:S(2)}) %collective-permute-start.17) | collective-permute-done | bytes 2883616 | tf_op jit(solution)/shard_map/ppermute | solution.py:433
  170.7 10.3 %expand.14 = (bf16[64,32,16,128]{3,2,1,0:T(8,128)(2,1)}, f32[8,128]{1,0:T(8,128)}) custom-call(s32[1]{0:T(128)} %bitcast.32.at, bf16[512,1024]{1,0:T(8,128)(2,1)S(1)} %spread_blocks.1.spread, bf16[64,32,16,128]{3,2,1,0:T(8,128)(2,1)} %bitcast.70, bf16[64,11,16,128]{3,2,1,0:T(8,128)(2,1)} %collective-permute-done.17.other, ...), custom_call_target="tpu_custom_call", output_to_operand_aliasing={{0}: (4, {})} | custom-call | flops 1024 | bytes 1024 | tf_op jit(solution)/shard_map/expand/pallas_call | solution.py:359
  181.1 2.6 %expand.15 = (bf16[64,32,16,128]{3,2,1,0:T(8,128)(2,1)}, f32[8,128]{1,0:T(8,128)}) custom-call(s32[1]{0:T(128)} %bitcast.30.at, bf16[512,1024]{1,0:T(8,128)(2,1)S(1)} %spread_blocks.1.spread, bf16[64,32,16,128]{3,2,1,0:T(8,128)(2,1)} %bitcast.71, bf16[64,2,16,128]{3,2,1,0:T(8,128)(2,1)S(1)} %collective-permute-done.16.other, ...), custom_call_target="tpu_custom_call", output_to_operand_aliasing={{0}: (4, {})} | custom-call | flops 1024 | bytes 1024 | tf_op jit(solution)/shard_map/expand/pallas_call | solution.py:359
  183.7 2.2 %collective-permute-done.15.other = bf16[64,1,16,128]{3,2,1,0:T(8,128)(2,1)S(1)} collective-permute-done((bf16[64,1,16,128]{3,2,1,0:T(8,128)(2,1)S(1)}, bf16[64,1,16,128]{3,2,1,0:T(8,128)(2,1)S(1)}, u32[]{:S(2)}, u32[]{:S(2)}) %collective-permute-start.15) | collective-permute-done | bytes 262176 | tf_op jit(solution)/shard_map/ppermute | solution.py:433
  (70 shorter events, 32.8 us)
Async XLA Ops:
  2.0 27.0 %collective-permute-start.2 = (bf16[64,4,16,128]{3,2,1,0:T(8,128)(2,1)S(1)}, bf16[64,4,16,128]{3,2,1,0:T(8,128)(2,1)S(1)}, u32[]{:S(2)}, u32[]{:S(2)}) collective-permute-start(bf16[64,4,16,128]{3,2,1,0:T(8,128)(2,1)S(1)} %cut_middle.1.rest_0_), channel_id=1, source_target_pairs={{0,1},{1,0},{2,3},{3,2},{4,5},{5,4},{6,7},{7,6},{8,9},{9,8},{10,11... | collective-permute-start | bytes 3145736 | tf_op jit(solution)/shard_map/ppermute | solution.py:433
  6.1 12.8 %collective-permute-start = (bf16[64,1,16,128]{3,2,1,0:T(8,128)(2,1)S(1)}, bf16[64,1,16,128]{3,2,1,0:T(8,128)(2,1)S(1)}, u32[]{:S(2)}, u32[]{:S(2)}) collective-permute-start(bf16[64,1,16,128]{3,2,1,0:T(8,128)(2,1)S(1)} %get-tuple-element.42), channel_id=1, source_target_pairs={{0,2},{2,4},{4,6},{1,3},{3,5},{5,7},{8,10},{10,12},{12,14},{9,11},... | collective-permute-start | bytes 786440 | tf_op jit(solution)/shard_map/ppermute | solution.py:495
  9.6 11.8 %collective-permute-start.1 = (bf16[64,1,16,128]{3,2,1,0:T(8,128)(2,1)S(1)}, bf16[64,1,16,128]{3,2,1,0:T(8,128)(2,1)S(1)}, u32[]{:S(2)}, u32[]{:S(2)}) collective-permute-start(bf16[64,1,16,128]{3,2,1,0:T(8,128)(2,1)S(1)} %get-tuple-element.41), channel_id=1, source_target_pairs={{2,0},{4,2},{6,4},{3,1},{5,3},{7,5},{10,8},{12,10},{14,12},{11,9},... | collective-permute-start | bytes 786440 | tf_op jit(solution)/shard_map/ppermute | solution.py:496
  12.8 69.0 %collective-permute-start.3 = (bf16[64,3,16,128]{3,2,1,0:T(8,128)(2,1)}, bf16[64,3,16,128]{3,2,1,0:T(8,128)(2,1)}, u32[]{:S(2)}, u32[]{:S(2)}) collective-permute-start(bf16[64,3,16,128]{3,2,1,0:T(8,128)(2,1)} %cut.9), channel_id=1, source_target_pairs={{0,1},{1,0},{2,3},{3,2},{4,5},{5,4},{6,7},{7,6},{8,9},{9,8},{10,11... | collective-permute-start | bytes 2359304 | tf_op jit(solution)/shard_map/ppermute | solution.py:433
  15.3 70.4 %collective-permute-start.4 = (bf16[64,3,16,128]{3,2,1,0:T(8,128)(2,1)}, bf16[64,3,16,128]{3,2,1,0:T(8,128)(2,1)}, u32[]{:S(2)}, u32[]{:S(2)}) collective-permute-start(bf16[64,3,16,128]{3,2,1,0:T(8,128)(2,1)} %cut.10), channel_id=1, source_target_pairs={{0,1},{1,0},{2,3},{3,2},{4,5},{5,4},{6,7},{7,6},{8,9},{9,8},{10,11... | collective-permute-start | bytes 2359304 | tf_op jit(solution)/shard_map/ppermute | solution.py:433
  18.9 5.9 %copy-start.2 = (bf16[64,1,16,128]{3,2,1,0:T(8,128)(2,1)}, bf16[64,1,16,128]{3,2,1,0:T(8,128)(2,1)S(1)}, u32[]{:S(2)}) copy-start(bf16[64,1,16,128]{3,2,1,0:T(8,128)(2,1)S(1)} %collective-permute-done.low) | copy-start | bytes 786436
  18.9 70.6 %collective-permute-start.5 = (bf16[64,3,16,128]{3,2,1,0:T(8,128)(2,1)}, bf16[64,3,16,128]{3,2,1,0:T(8,128)(2,1)}, u32[]{:S(2)}, u32[]{:S(2)}) collective-permute-start(bf16[64,3,16,128]{3,2,1,0:T(8,128)(2,1)} %cut.11), channel_id=1, source_target_pairs={{0,1},{1,0},{2,3},{3,2},{4,5},{5,4},{6,7},{7,6},{8,9},{9,8},{10,11... | collective-permute-start | bytes 2359304 | tf_op jit(solution)/shard_map/ppermute | solution.py:433
  19.4 11.6 %copy-start.7 = (bf16[1,128,64]{1,2,0:T(8,128)(2,1)S(1)}, bf16[1,128,64]{1,2,0:T(8,128)(2,1)}, u32[]{:S(2)}) copy-start(bf16[1,128,64]{1,2,0:T(8,128)(2,1)} %param.8) | copy-start | bytes 49156
  21.4 9.7 %copy-start.4 = (bf16[64,1,16,128]{3,2,1,0:T(8,128)(2,1)}, bf16[64,1,16,128]{3,2,1,0:T(8,128)(2,1)S(1)}, u32[]{:S(2)}) copy-start(bf16[64,1,16,128]{3,2,1,0:T(8,128)(2,1)S(1)} %collective-permute-done.1.high) | copy-start | bytes 786436
  21.4 75.1 %collective-permute-start.6 = (bf16[64,3,16,128]{3,2,1,0:T(8,128)(2,1)}, bf16[64,3,16,128]{3,2,1,0:T(8,128)(2,1)}, u32[]{:S(2)}, u32[]{:S(2)}) collective-permute-start(bf16[64,3,16,128]{3,2,1,0:T(8,128)(2,1)} %cut.12), channel_id=1, source_target_pairs={{0,1},{1,0},{2,3},{3,2},{4,5},{5,4},{6,7},{7,6},{8,9},{9,8},{10,11... | collective-permute-start | bytes 2359304 | tf_op jit(solution)/shard_map/ppermute | solution.py:433
  24.8 9.9 %copy-start = (f32[1,32,16,128]{3,2,1,0:T(8,128)S(1)}, f32[1,32,16,128]{3,2,1,0:T(8,128)}, u32[]{:S(2)}) copy-start(f32[1,32,16,128]{3,2,1,0:T(8,128)} %param.6) | copy-start | bytes 786436
  29.0 78.8 %collective-permute-start.7 = (bf16[64,2,16,128]{3,2,1,0:T(8,128)(2,1)}, bf16[64,2,16,128]{3,2,1,0:T(8,128)(2,1)}, u32[]{:S(2)}, u32[]{:S(2)}) collective-permute-start(bf16[64,2,16,128]{3,2,1,0:T(8,128)(2,1)} %cut.13), channel_id=1, source_target_pairs={{0,1},{1,0},{2,3},{3,2},{4,5},{5,4},{6,7},{7,6},{8,9},{9,8},{10,11... | collective-permute-start | bytes 1572872 | tf_op jit(solution)/shard_map/ppermute | solution.py:433
  34.7 1.0 copy-start.1
  35.6 0.9 copy-start.3
  36.6 0.9 copy-start.5
  81.9 88.1 %collective-permute-start.17 = (bf16[64,11,16,128]{3,2,1,0:T(8,128)(2,1)}, bf16[64,11,16,128]{3,2,1,0:T(8,128)(2,1)}, u32[]{:S(2)}, u32[]{:S(2)}) collective-permute-start(bf16[64,11,16,128]{3,2,1,0:T(8,128)(2,1)} %cut.17), channel_id=1, source_target_pairs={{0,1},{1,0},{2,3},{3,2},{4,5},{5,4},{6,7},{7,6},{8,9},{9,8},{10,11... | collective-permute-start | bytes 8650760 | tf_op jit(solution)/shard_map/ppermute | solution.py:433
  123.4 7.9 %copy-start.8 = (s32[4]{0:T(128)S(1)}, s32[4]{0:T(128)}, u32[]{:S(2)}) copy-start(s32[4]{0:T(128)} %param.9) | copy-start | bytes 52
  126.4 4.1 %collective-permute-start.8 = (f32[80,128]{1,0:T(8,128)S(1)}, f32[80,128]{1,0:T(8,128)S(1)}, u32[]{:S(2)}, u32[]{:S(2)}) collective-permute-start(f32[80,128]{1,0:T(8,128)S(1)} %maximum_maximum_fusion), channel_id=1, source_target_pairs={{0,2},{2,0},{4,6},{6,4},{1,3},{3,1},{5,7},{7,5},{8,10},{10,8},{12,... | collective-permute-start | bytes 122888 | tf_op jit(solution)/shard_map/ppermute | solution.py:459
  130.6 1.3 collective-permute-start.9
  131.9 9.9 %collective-permute-start.10 = (f32[80,128]{1,0:T(8,128)S(1)}, f32[80,128]{1,0:T(8,128)S(1)}, u32[]{:S(2)}, u32[]{:S(2)}) collective-permute-start(f32[80,128]{1,0:T(8,128)S(1)} %add.69), channel_id=1, source_target_pairs={{2,0},{4,6},{3,1},{5,7},{10,8},{12,14},{11,9},{13,15},{18,16},{20,... | collective-permute-start | bytes 122888 | tf_op jit(solution)/shard_map/ppermute | solution.py:461
  141.9 1.3 collective-permute-start.11
  143.2 4.5 %collective-permute-start.12 = (f32[2,80,128]{2,1,0:T(8,128)S(1)}, f32[2,80,128]{2,1,0:T(8,128)S(1)}, u32[]{:S(2)}, u32[]{:S(2)}) collective-permute-start(f32[2,80,128]{2,1,0:T(8,128)S(1)} %fusion.6), channel_id=1, source_target_pairs={{0,16},{8,24},{16,0},{24,8},{1,17},{9,25},{17,1},{25,9},{2,18},{10... | collective-permute-start | bytes 245768 | tf_op jit(solution)/shard_map/ppermute | solution.py:451
  149.0 32.1 %collective-permute-start.16 = (bf16[64,2,16,128]{3,2,1,0:T(8,128)(2,1)S(1)}, bf16[64,2,16,128]{3,2,1,0:T(8,128)(2,1)S(1)}, u32[]{:S(2)}, u32[]{:S(2)}) collective-permute-start(bf16[64,2,16,128]{3,2,1,0:T(8,128)(2,1)S(1)} %cut.16), channel_id=1, source_target_pairs={{0,1},{1,0},{2,3},{3,2},{4,5},{5,4},{6,7},{7,6},{8,9},{9,8},{10,11... | collective-permute-start | bytes 1572872 | tf_op jit(solution)/shard_map/ppermute | solution.py:433
  151.5 34.3 %collective-permute-start.15 = (bf16[64,1,16,128]{3,2,1,0:T(8,128)(2,1)S(1)}, bf16[64,1,16,128]{3,2,1,0:T(8,128)(2,1)S(1)}, u32[]{:S(2)}, u32[]{:S(2)}) collective-permute-start(bf16[64,1,16,128]{3,2,1,0:T(8,128)(2,1)S(1)} %cut.15), channel_id=1, source_target_pairs={{0,1},{1,0},{2,3},{3,2},{4,5},{5,4},{6,7},{7,6},{8,9},{9,8},{10,11... | collective-permute-start | bytes 786440 | tf_op jit(solution)/shard_map/ppermute | solution.py:433
  152.3 4.8 %collective-permute-start.13 = (f32[40,128]{1,0:T(8,128)S(1)}, f32[40,128]{1,0:T(8,128)S(1)}, u32[]{:S(2)}, u32[]{:S(2)}) collective-permute-start(f32[40,128]{1,0:T(8,128)S(1)} %fusion.5), channel_id=1, source_target_pairs={{0,17},{1,16},{8,25},{9,24},{16,1},{17,0},{24,9},{25,8},{2,19},{3,... | collective-permute-start | bytes 61448 | tf_op jit(solution)/shard_map/ppermute | solution.py:441
  157.1 1.2 collective-permute-start.14
  170.0 0.8 copy-start.6

commit v8 on v7

--- a/solution.py
+++ b/solution.py
@@ -407,7 +407,7 @@
 
 def expand_last(spread, own, other, at, held):
     rows, layers, cells_y, cells_z = other.shape
-    eigs, parts = spread.shape[0] // SUB, 2
+    eigs, parts = spread.shape[0] // SUB, 4
     inside = pl.BlockSpec(memory_space=pltpu.VMEM)
     return pl.pallas_call(
         last_kernel,
@@ -435,14 +435,22 @@
 
 def crossed(x):
     leaves, leaf = lax.axis_size("leaf"), lax.axis_index("leaf")
+    places, place = lax.axis_size("dof"), lax.axis_index("dof")
     pairs = [(2 * i + j, 2 * (i ^ (leaves // 2)) + 1 - j) for i in range(leaves) for j in range(2)]
-    count = x.shape[0] // 2
-    part = lax.dynamic_slice_in_dim(x, leaf % 2 * count, count, 0)
+    count = x.shape[0] // (2 * places)
+    part = lax.dynamic_slice_in_dim(x, (leaf % 2 * places + place) * count, count, 0)
     part = lax.ppermute(part, ("leaf", "blk"), pairs)
-    rest = lax.ppermute(part, "leaf", [(i, i ^ 1) for i in range(leaves)])
-    return jnp.where(
-        leaf % 2 == 0, jnp.concatenate([part, rest], 0), jnp.concatenate([rest, part], 0)
-    )
+    step = 1
+    while step < places:
+        part = joined(part, "dof", step)
+        step *= 2
+    return joined(part, "leaf", 1)
+
+
+def joined(part, axis, step):
+    rest = lax.ppermute(part, axis, [(i, i ^ step) for i in range(lax.axis_size(axis))])
+    first = lax.axis_index(axis) // step % 2 == 0
+    return jnp.where(first, jnp.concatenate([part, rest], 0), jnp.concatenate([rest, part], 0))
 
 
 def paired_sum(x, axis):

time: 189 us -> 189 us (level)
    ppermute x9, waiting for transfers between devices: 24.2 us -> 17.3 us  [swap(): return lax.ppermute(x, 'blk', [(0, 1), (1, 0)])]
    ppermute x1 -> x3, waiting for transfers between devices: 0.19 us -> 5.81 us  [joined(): lax.ppermute(part, axis, [(i, i ^ step) for i in range(lax.axis_size(axis...]
  transfers between devices with their start and end apart: 18 -> 20, of which waited for: 12 -> 14; matrix products, arithmetic and copies ran while one was open for 2% -> 2% of each run, Pallas kernels for 59% -> 59%
where the time goes in v8:
time: 189 us; the launch traced here: 187 us
  Pallas kernels  113 us (60%)
  waiting for transfers between devices  40.5 us (21%)
  starting transfers between devices  24.6 us (13%)
  local copies, waits for them, and re-layouts  5.52 us (3%)
    pallas_call x1, Pallas kernels, stiff_terms(): pl.pallas_call(stiff_kernel, grid=(layers,), in_specs=[pl.BlockSpec(block...  40.1 us
    pallas_call x8, Pallas kernels, expand(): pl.pallas_call(vector_kernel, grid_spec=pltpu.PrefetchScalarGridSpec(num_...  34.9 us
    pallas_call x6, Pallas kernels, cross_terms(): pl.pallas_call(cross_kernel, grid_spec=pltpu.PrefetchScalarGridSpec(num_s...  18.9 us
    ppermute x9, waiting for transfers between devices, swap(): return lax.ppermute(x, 'blk', [(0, 1), (1, 0)])  17.3 us
    pallas_call x9, Pallas kernels, cut(): pl.pallas_call(cut_kernel, grid_spec=pltpu.PrefetchScalarGridSpec(num_sca...  15.3 us
    ppermute x9, starting transfers between devices, swap(): return lax.ppermute(x, 'blk', [(0, 1), (1, 0)])  11.6 us
    ppermute x1, waiting for transfers between devices, line_sum(): outer = lax.ppermute(x, axis, [(1, 0), (2, 3)])  7.91 us
    ppermute x3, waiting for transfers between devices, joined(): lax.ppermute(part, axis, [(i, i ^ step) for i in range(lax.axis_size(axis...  5.81 us
  transfers between devices with their start and end apart: 20, of which 14 were waited for; matrix products, arithmetic and copies ran while one was open for 2% of the time, Pallas kernels for 59%

profile of v8, /device:TPU:0, one launch (start us, length us, event | category | flops | bytes accessed | tf_op | source)
XLA Modules:
  0.0 186.8 jit_solution(8502120315021793218)
XLA Ops:
  2.0 3.0 %collective-permute-start.2 = (bf16[64,4,16,128]{3,2,1,0:T(8,128)(2,1)S(1)}, bf16[64,4,16,128]{3,2,1,0:T(8,128)(2,1)S(1)}, u32[]{:S(2)}, u32[]{:S(2)}) collective-permute-start(bf16[64,4,16,128]{3,2,1,0:T(8,128)(2,1)S(1)} %cut_middle.1.rest_0_), channel_id=1, source_target_pairs={{0,1},{1,0},{2,3},{3,2},{4,5},{5,4},{6,7},{7,6},{8,9},{9,8},{10,11... | collective-permute-start | bytes 3145736 | tf_op jit(solution)/shard_map/ppermute | solution.py:433
  6.1 3.5 %collective-permute-start = (bf16[64,1,16,128]{3,2,1,0:T(8,128)(2,1)S(1)}, bf16[64,1,16,128]{3,2,1,0:T(8,128)(2,1)S(1)}, u32[]{:S(2)}, u32[]{:S(2)}) collective-permute-start(bf16[64,1,16,128]{3,2,1,0:T(8,128)(2,1)S(1)} %get-tuple-element.42), channel_id=1, source_target_pairs={{0,2},{2,4},{4,6},{1,3},{3,5},{5,7},{8,10},{10,12},{12,14},{9,11},... | collective-permute-start | bytes 786440 | tf_op jit(solution)/shard_map/ppermute | solution.py:503
  16.9 1.9 %cut.11 = bf16[64,3,16,128]{3,2,1,0:T(8,128)(2,1)} custom-call(s32[1]{0:T(128)} %bitcast.21.at, bf16[64,32,16,128]{3,2,1,0:T(8,128)(2,1)} %bitcast.54, bf16[64,4,16,128]{3,2,1,0:T(8,128)(2,1)S(1)} %cut_middle.1.rest_0_), custom_call_target="tpu_custom_call" | custom-call | flops 1024 | bytes 1024 | tf_op jit(solution)/shard_map/cut/pallas_call | solution.py:197
  24.8 4.1 %collective-permute-done.2.order.other = bf16[64,4,16,128]{3,2,1,0:T(8,128)(2,1)S(1)} collective-permute-done((bf16[64,4,16,128]{3,2,1,0:T(8,128)(2,1)S(1)}, bf16[64,4,16,128]{3,2,1,0:T(8,128)(2,1)S(1)}, u32[]{:S(2)}, u32[]{:S(2)}) %collective-permute-start.2) | collective-permute-done | bytes 1048608 | tf_op jit(solution)/shard_map/ppermute | solution.py:433
  29.0 2.1 %collective-permute-start.7 = (bf16[64,2,16,128]{3,2,1,0:T(8,128)(2,1)}, bf16[64,2,16,128]{3,2,1,0:T(8,128)(2,1)}, u32[]{:S(2)}, u32[]{:S(2)}) collective-permute-start(bf16[64,2,16,128]{3,2,1,0:T(8,128)(2,1)} %cut.13), channel_id=1, source_target_pairs={{0,1},{1,0},{2,3},{3,2},{4,5},{5,4},{6,7},{7,6},{8,9},{9,8},{10,11... | collective-permute-start | bytes 1572872 | tf_op jit(solution)/shard_map/ppermute | solution.py:433
  31.7 2.8 %cut.17 = bf16[64,11,16,128]{3,2,1,0:T(8,128)(2,1)} custom-call(s32[1]{0:T(128)} %bitcast.33.at, bf16[64,32,16,128]{3,2,1,0:T(8,128)(2,1)} %bitcast.57, bf16[64,4,16,128]{3,2,1,0:T(8,128)(2,1)S(1)} %cut_middle.1.rest_0_), custom_call_target="tpu_custom_call" | custom-call | flops 1024 | bytes 1024 | tf_op jit(solution)/shard_map/cut/pallas_call | solution.py:197
  37.5 40.1 %stiff_terms.1 = (bf16[32,512,256]{2,1,0:T(8,128)(2,1)}, f32[64,64]{1,0:T(8,128)S(1)}, f32[16,64]{1,0:T(8,128)S(1)}) custom-call(bf16[64,32,16,128]{3,2,1,0:T(8,128)(2,1)} %bitcast.58, bf16[64,32,16,128]{3,2,1,0:T(8,128)(2,1)} %bitcast.59, bf16[64,32,16,128]{3,2,1,0:T(8,128)(2,1)} %bitcast.60, bf16[64,1,16,128]{3,2,1,0:T(8,128)(2,1)S(1)} %copy-done.3, ...), custom_call_target="tpu_custom_call" | custom-call | flops 1024 | bytes 1024 | tf_op jit(solution)/shard_map/stiff_terms/pallas_call | solution.py:100
  77.6 4.2 %expand.8 = (bf16[64,32,16,128]{3,2,1,0:T(8,128)(2,1)}, f32[8,128]{1,0:T(8,128)S(1)}) custom-call(s32[1]{0:T(128)} %constant.95.clone.1.at, bf16[512,1024]{1,0:T(8,128)(2,1)S(1)} %spread_blocks.1.spread, bf16[64,32,16,128]{3,2,1,0:T(8,128)(2,1)} %bitcast.61, bf16[64,4,16,128]{3,2,1,0:T(8,128)(2,1)S(1)} %collective-permute-done.2.order.other, ...), custom_call_target="tpu_custom_call" | custom-call | flops 1024 | bytes 1024 | tf_op jit(solution)/shard_map/expand/pallas_call | solution.py:359
  81.8 3.8 %expand.9 = (bf16[64,32,16,128]{3,2,1,0:T(8,128)(2,1)}, f32[8,128]{1,0:T(8,128)S(1)}) custom-call(s32[1]{0:T(128)} %bitcast.16.at, bf16[512,1024]{1,0:T(8,128)(2,1)S(1)} %spread_blocks.1.spread, bf16[64,32,16,128]{3,2,1,0:T(8,128)(2,1)} %bitcast.62, bf16[64,3,16,128]{3,2,1,0:T(8,128)(2,1)} %collective-permute-done.3.other, ...), custom_call_target="tpu_custom_call", output_to_operand_aliasing={{0}: (4, {})} | custom-call | flops 1024 | bytes 1024 | tf_op jit(solution)/shard_map/expand/pallas_call | solution.py:359
  85.6 3.8 %expand.10 = (bf16[64,32,16,128]{3,2,1,0:T(8,128)(2,1)}, f32[8,128]{1,0:T(8,128)S(1)}) custom-call(s32[1]{0:T(128)} %bitcast.18.at, bf16[512,1024]{1,0:T(8,128)(2,1)S(1)} %spread_blocks.1.spread, bf16[64,32,16,128]{3,2,1,0:T(8,128)(2,1)} %bitcast.63, bf16[64,3,16,128]{3,2,1,0:T(8,128)(2,1)} %collective-permute-done.4.other, ...), custom_call_target="tpu_custom_call", output_to_operand_aliasing={{0}: (4, {})} | custom-call | flops 1024 | bytes 1024 | tf_op jit(solution)/shard_map/expand/pallas_call | solution.py:359
  89.4 3.8 %expand.11 = (bf16[64,32,16,128]{3,2,1,0:T(8,128)(2,1)}, f32[8,128]{1,0:T(8,128)S(1)}) custom-call(s32[1]{0:T(128)} %bitcast.20.at, bf16[512,1024]{1,0:T(8,128)(2,1)S(1)} %spread_blocks.1.spread, bf16[64,32,16,128]{3,2,1,0:T(8,128)(2,1)} %bitcast.64, bf16[64,3,16,128]{3,2,1,0:T(8,128)(2,1)} %collective-permute-done.5.other, ...), custom_call_target="tpu_custom_call", output_to_operand_aliasing={{0}: (4, {})} | custom-call | flops 1024 | bytes 1024 | tf_op jit(solution)/shard_map/expand/pallas_call | solution.py:359
  93.2 3.3 %collective-permute-done.6.other = bf16[64,3,16,128]{3,2,1,0:T(8,128)(2,1)} collective-permute-done((bf16[64,3,16,128]{3,2,1,0:T(8,128)(2,1)}, bf16[64,3,16,128]{3,2,1,0:T(8,128)(2,1)}, u32[]{:S(2)}, u32[]{:S(2)}) %collective-permute-start.6) | collective-permute-done | bytes 786464 | tf_op jit(solution)/shard_map/ppermute | solution.py:433
  96.5 3.8 %expand.12 = (bf16[64,32,16,128]{3,2,1,0:T(8,128)(2,1)}, f32[8,128]{1,0:T(8,128)S(1)}) custom-call(s32[1]{0:T(128)} %bitcast.22.at, bf16[512,1024]{1,0:T(8,128)(2,1)S(1)} %spread_blocks.1.spread, bf16[64,32,16,128]{3,2,1,0:T(8,128)(2,1)} %bitcast.65, bf16[64,3,16,128]{3,2,1,0:T(8,128)(2,1)} %collective-permute-done.6.other, ...), custom_call_target="tpu_custom_call", output_to_operand_aliasing={{0}: (4, {})} | custom-call | flops 1024 | bytes 1024 | tf_op jit(solution)/shard_map/expand/pallas_call | solution.py:359
  100.3 3.5 %cross_terms.10 = f32[64,64]{1,0:T(8,128)S(1)} custom-call(s32[1]{0:T(128)} %bitcast.22.at, s32[1]{0:T(128)} %constant.100.clone.1.skip, bf16[32,512,256]{2,1,0:T(8,128)(2,1)} %get-tuple-element.23.stiff, bf16[64,3,16,128]{3,2,1,0:T(8,128)(2,1)} %collective-permute-done.6.other, f32[8,128]{1,0:T(8,128)S(1)} %get-tuple-element.33.order), custom_call_target="tpu_custom_call" | custom-call | flops 1024 | bytes 1024 | tf_op jit(solution)/shard_map/cross_terms/pallas_call | solution.py:151
  103.8 3.9 %collective-permute-done.7.other = bf16[64,2,16,128]{3,2,1,0:T(8,128)(2,1)} collective-permute-done((bf16[64,2,16,128]{3,2,1,0:T(8,128)(2,1)}, bf16[64,2,16,128]{3,2,1,0:T(8,128)(2,1)}, u32[]{:S(2)}, u32[]{:S(2)}) %collective-permute-start.7) | collective-permute-done | bytes 524320 | tf_op jit(solution)/shard_map/ppermute | solution.py:433
  107.7 2.7 %expand.13 = (bf16[64,32,16,128]{3,2,1,0:T(8,128)(2,1)}, f32[8,128]{1,0:T(8,128)S(1)}) custom-call(s32[1]{0:T(128)} %bitcast.24.at, bf16[512,1024]{1,0:T(8,128)(2,1)S(1)} %spread_blocks.1.spread, bf16[64,32,16,128]{3,2,1,0:T(8,128)(2,1)} %bitcast.66, bf16[64,2,16,128]{3,2,1,0:T(8,128)(2,1)} %collective-permute-done.7.other, ...), custom_call_target="tpu_custom_call", output_to_operand_aliasing={{0}: (4, {})} | custom-call | flops 1024 | bytes 1024 | tf_op jit(solution)/shard_map/expand/pallas_call | solution.py:359
  110.4 2.5 %cross_terms.11 = f32[64,64]{1,0:T(8,128)S(1)} custom-call(s32[1]{0:T(128)} %bitcast.24.at, s32[1]{0:T(128)} %constant.100.clone.1.skip, bf16[32,512,256]{2,1,0:T(8,128)(2,1)} %get-tuple-element.23.stiff, bf16[64,2,16,128]{3,2,1,0:T(8,128)(2,1)} %collective-permute-done.7.other, f32[8,128]{1,0:T(8,128)S(1)} %get-tuple-element.35.order), custom_call_target="tpu_custom_call" | custom-call | flops 1024 | bytes 1024 | tf_op jit(solution)/shard_map/cross_terms/pallas_call | solution.py:151
  112.8 3.5 %cross_terms.9 = f32[64,64]{1,0:T(8,128)S(1)} custom-call(s32[1]{0:T(128)} %bitcast.20.at, s32[1]{0:T(128)} %constant.100.clone.1.skip, bf16[32,512,256]{2,1,0:T(8,128)(2,1)} %get-tuple-element.23.stiff, bf16[64,3,16,128]{3,2,1,0:T(8,128)(2,1)} %collective-permute-done.5.other, f32[8,128]{1,0:T(8,128)S(1)} %get-tuple-element.31.order), custom_call_target="tpu_custom_call" | custom-call | flops 1024 | bytes 1024 | tf_op jit(solution)/shard_map/cross_terms/pallas_call | solution.py:151
  116.4 3.5 %cross_terms.8 = f32[64,64]{1,0:T(8,128)S(1)} custom-call(s32[1]{0:T(128)} %bitcast.18.at, s32[1]{0:T(128)} %constant.100.clone.1.skip, bf16[32,512,256]{2,1,0:T(8,128)(2,1)} %get-tuple-element.23.stiff, bf16[64,3,16,128]{3,2,1,0:T(8,128)(2,1)} %collective-permute-done.4.other, f32[8,128]{1,0:T(8,128)S(1)} %get-tuple-element.29.order), custom_call_target="tpu_custom_call" | custom-call | flops 1024 | bytes 1024 | tf_op jit(solution)/shard_map/cross_terms/pallas_call | solution.py:151
  119.9 3.5 %cross_terms.7 = f32[64,64]{1,0:T(8,128)S(1)} custom-call(s32[1]{0:T(128)} %bitcast.16.at, s32[1]{0:T(128)} %constant.100.clone.1.skip, bf16[32,512,256]{2,1,0:T(8,128)(2,1)} %get-tuple-element.23.stiff, bf16[64,3,16,128]{3,2,1,0:T(8,128)(2,1)} %collective-permute-done.3.other, f32[8,128]{1,0:T(8,128)S(1)} %get-tuple-element.27.order), custom_call_target="tpu_custom_call" | custom-call | flops 1024 | bytes 1024 | tf_op jit(solution)/shard_map/cross_terms/pallas_call | solution.py:151
  123.4 2.4 %cross_terms.6 = f32[64,64]{1,0:T(8,128)S(1)} custom-call(s32[1]{0:T(128)} %bitcast.11.at, s32[1]{0:T(128)} %bitcast.12.skip, bf16[32,512,256]{2,1,0:T(8,128)(2,1)} %get-tuple-element.23.stiff, bf16[64,4,16,128]{3,2,1,0:T(8,128)(2,1)S(1)} %collective-permute-done.2.order.other, f32[8,128]{1,0:T(8,128)S(1)} %get-tuple-element.25.order), custom_call_target="tpu_custom_call" | custom-call | flops 1024 | bytes 1024 | tf_op jit(solution)/shard_map/cross_terms/pallas_call | solution.py:151
  126.4 2.1 %collective-permute-start.8 = (f32[80,128]{1,0:T(8,128)S(1)}, f32[80,128]{1,0:T(8,128)S(1)}, u32[]{:S(2)}, u32[]{:S(2)}) collective-permute-start(f32[80,128]{1,0:T(8,128)S(1)} %maximum_maximum_fusion), channel_id=1, source_target_pairs={{0,2},{2,0},{4,6},{6,4},{1,3},{3,1},{5,7},{7,5},{8,10},{10,8},{12,... | collective-permute-start | bytes 122888 | tf_op jit(solution)/shard_map/ppermute | solution.py:467
  128.5 2.0 %collective-permute-done.8 = f32[80,128]{1,0:T(8,128)S(1)} collective-permute-done((f32[80,128]{1,0:T(8,128)S(1)}, f32[80,128]{1,0:T(8,128)S(1)}, u32[]{:S(2)}, u32[]{:S(2)}) %collective-permute-start.8) | collective-permute-done | bytes 40992 | tf_op jit(solution)/shard_map/ppermute | solution.py:467
  133.8 7.9 %collective-permute-done.10 = f32[80,128]{1,0:T(8,128)S(1)} collective-permute-done((f32[80,128]{1,0:T(8,128)S(1)}, f32[80,128]{1,0:T(8,128)S(1)}, u32[]{:S(2)}, u32[]{:S(2)}) %collective-permute-start.10) | collective-permute-done | bytes 40992 | tf_op jit(solution)/shard_map/ppermute | solution.py:469
  144.7 3.0 %collective-permute-done.12 = f32[2,80,128]{2,1,0:T(8,128)S(1)} collective-permute-done((f32[2,80,128]{2,1,0:T(8,128)S(1)}, f32[2,80,128]{2,1,0:T(8,128)S(1)}, u32[]{:S(2)}, u32[]{:S(2)}) %collective-permute-start.12) | collective-permute-done | bytes 81952 | tf_op jit(solution)/shard_map/ppermute | solution.py:459
  152.1 3.2 %collective-permute-done.13 = f32[10,128]{1,0:T(8,128)S(1)} collective-permute-done((f32[10,128]{1,0:T(8,128)S(1)}, f32[10,128]{1,0:T(8,128)S(1)}, u32[]{:S(2)}, u32[]{:S(2)}) %collective-permute-start.13) | collective-permute-done | bytes 5152 | tf_op jit(solution)/shard_map/ppermute | solution.py:442
  156.9 2.1 %collective-permute-done.14 = f32[10,128]{1,0:T(8,128)S(1)} collective-permute-done((f32[10,128]{1,0:T(8,128)S(1)}, f32[10,128]{1,0:T(8,128)S(1)}, u32[]{:S(2)}, u32[]{:S(2)}) %collective-permute-start.14) | collective-permute-done | bytes 5152 | tf_op jit(solution)/shard_map/ppermute | solution.py:451
  160.1 3.6 %collective-permute-done.15 = f32[20,128]{1,0:T(8,128)S(1)} collective-permute-done((f32[20,128]{1,0:T(8,128)S(1)}, f32[20,128]{1,0:T(8,128)S(1)}, u32[]{:S(2)}, u32[]{:S(2)}) %collective-permute-start.15) | collective-permute-done | bytes 10272 | tf_op jit(solution)/shard_map/ppermute | solution.py:451
  166.0 3.7 %collective-permute-done.19.other = bf16[64,11,16,128]{3,2,1,0:T(8,128)(2,1)} collective-permute-done((bf16[64,11,16,128]{3,2,1,0:T(8,128)(2,1)}, bf16[64,11,16,128]{3,2,1,0:T(8,128)(2,1)}, u32[]{:S(2)}, u32[]{:S(2)}) %collective-permute-start.19) | collective-permute-done | bytes 2883616 | tf_op jit(solution)/shard_map/ppermute | solution.py:433
  170.5 10.3 %expand.14 = (bf16[64,32,16,128]{3,2,1,0:T(8,128)(2,1)}, f32[8,128]{1,0:T(8,128)}) custom-call(s32[1]{0:T(128)} %bitcast.32.at, bf16[512,1024]{1,0:T(8,128)(2,1)S(1)} %spread_blocks.1.spread, bf16[64,32,16,128]{3,2,1,0:T(8,128)(2,1)} %bitcast.70, bf16[64,11,16,128]{3,2,1,0:T(8,128)(2,1)} %collective-permute-done.19.other, ...), custom_call_target="tpu_custom_call", output_to_operand_aliasing={{0}: (4, {})} | custom-call | flops 1024 | bytes 1024 | tf_op jit(solution)/shard_map/expand/pallas_call | solution.py:359
  180.8 2.6 %expand.15 = (bf16[64,32,16,128]{3,2,1,0:T(8,128)(2,1)}, f32[8,128]{1,0:T(8,128)}) custom-call(s32[1]{0:T(128)} %bitcast.30.at, bf16[512,1024]{1,0:T(8,128)(2,1)S(1)} %spread_blocks.1.spread, bf16[64,32,16,128]{3,2,1,0:T(8,128)(2,1)} %bitcast.71, bf16[64,2,16,128]{3,2,1,0:T(8,128)(2,1)S(1)} %collective-permute-done.18.other, ...), custom_call_target="tpu_custom_call", output_to_operand_aliasing={{0}: (4, {})} | custom-call | flops 1024 | bytes 1024 | tf_op jit(solution)/shard_map/expand/pallas_call | solution.py:359
  183.4 2.2 %collective-permute-done.17.other = bf16[64,1,16,128]{3,2,1,0:T(8,128)(2,1)S(1)} collective-permute-done((bf16[64,1,16,128]{3,2,1,0:T(8,128)(2,1)S(1)}, bf16[64,1,16,128]{3,2,1,0:T(8,128)(2,1)S(1)}, u32[]{:S(2)}, u32[]{:S(2)}) %collective-permute-start.17) | collective-permute-done | bytes 262176 | tf_op jit(solution)/shard_map/ppermute | solution.py:433
  (76 shorter events, 37.3 us)
Async XLA Ops:
  2.0 27.0 %collective-permute-start.2 = (bf16[64,4,16,128]{3,2,1,0:T(8,128)(2,1)S(1)}, bf16[64,4,16,128]{3,2,1,0:T(8,128)(2,1)S(1)}, u32[]{:S(2)}, u32[]{:S(2)}) collective-permute-start(bf16[64,4,16,128]{3,2,1,0:T(8,128)(2,1)S(1)} %cut_middle.1.rest_0_), channel_id=1, source_target_pairs={{0,1},{1,0},{2,3},{3,2},{4,5},{5,4},{6,7},{7,6},{8,9},{9,8},{10,11... | collective-permute-start | bytes 3145736 | tf_op jit(solution)/shard_map/ppermute | solution.py:433
  6.1 12.7 %collective-permute-start = (bf16[64,1,16,128]{3,2,1,0:T(8,128)(2,1)S(1)}, bf16[64,1,16,128]{3,2,1,0:T(8,128)(2,1)S(1)}, u32[]{:S(2)}, u32[]{:S(2)}) collective-permute-start(bf16[64,1,16,128]{3,2,1,0:T(8,128)(2,1)S(1)} %get-tuple-element.42), channel_id=1, source_target_pairs={{0,2},{2,4},{4,6},{1,3},{3,5},{5,7},{8,10},{10,12},{12,14},{9,11},... | collective-permute-start | bytes 786440 | tf_op jit(solution)/shard_map/ppermute | solution.py:503
  9.6 11.8 %collective-permute-start.1 = (bf16[64,1,16,128]{3,2,1,0:T(8,128)(2,1)S(1)}, bf16[64,1,16,128]{3,2,1,0:T(8,128)(2,1)S(1)}, u32[]{:S(2)}, u32[]{:S(2)}) collective-permute-start(bf16[64,1,16,128]{3,2,1,0:T(8,128)(2,1)S(1)} %get-tuple-element.41), channel_id=1, source_target_pairs={{2,0},{4,2},{6,4},{3,1},{5,3},{7,5},{10,8},{12,10},{14,12},{11,9},... | collective-permute-start | bytes 786440 | tf_op jit(solution)/shard_map/ppermute | solution.py:504
  12.8 69.0 %collective-permute-start.3 = (bf16[64,3,16,128]{3,2,1,0:T(8,128)(2,1)}, bf16[64,3,16,128]{3,2,1,0:T(8,128)(2,1)}, u32[]{:S(2)}, u32[]{:S(2)}) collective-permute-start(bf16[64,3,16,128]{3,2,1,0:T(8,128)(2,1)} %cut.9), channel_id=1, source_target_pairs={{0,1},{1,0},{2,3},{3,2},{4,5},{5,4},{6,7},{7,6},{8,9},{9,8},{10,11... | collective-permute-start | bytes 2359304 | tf_op jit(solution)/shard_map/ppermute | solution.py:433
  15.3 70.3 %collective-permute-start.4 = (bf16[64,3,16,128]{3,2,1,0:T(8,128)(2,1)}, bf16[64,3,16,128]{3,2,1,0:T(8,128)(2,1)}, u32[]{:S(2)}, u32[]{:S(2)}) collective-permute-start(bf16[64,3,16,128]{3,2,1,0:T(8,128)(2,1)} %cut.10), channel_id=1, source_target_pairs={{0,1},{1,0},{2,3},{3,2},{4,5},{5,4},{6,7},{7,6},{8,9},{9,8},{10,11... | collective-permute-start | bytes 2359304 | tf_op jit(solution)/shard_map/ppermute | solution.py:433
  18.8 5.9 %copy-start.2 = (bf16[64,1,16,128]{3,2,1,0:T(8,128)(2,1)}, bf16[64,1,16,128]{3,2,1,0:T(8,128)(2,1)S(1)}, u32[]{:S(2)}) copy-start(bf16[64,1,16,128]{3,2,1,0:T(8,128)(2,1)S(1)} %collective-permute-done.low) | copy-start | bytes 786436
  18.8 70.6 %collective-permute-start.5 = (bf16[64,3,16,128]{3,2,1,0:T(8,128)(2,1)}, bf16[64,3,16,128]{3,2,1,0:T(8,128)(2,1)}, u32[]{:S(2)}, u32[]{:S(2)}) collective-permute-start(bf16[64,3,16,128]{3,2,1,0:T(8,128)(2,1)} %cut.11), channel_id=1, source_target_pairs={{0,1},{1,0},{2,3},{3,2},{4,5},{5,4},{6,7},{7,6},{8,9},{9,8},{10,11... | collective-permute-start | bytes 2359304 | tf_op jit(solution)/shard_map/ppermute | solution.py:433
  19.4 5.4 %copy-start.7 = (bf16[1,128,64]{1,2,0:T(8,128)(2,1)S(1)}, bf16[1,128,64]{1,2,0:T(8,128)(2,1)}, u32[]{:S(2)}) copy-start(bf16[1,128,64]{1,2,0:T(8,128)(2,1)} %param.8) | copy-start | bytes 49156
  21.3 9.7 %copy-start.4 = (bf16[64,1,16,128]{3,2,1,0:T(8,128)(2,1)}, bf16[64,1,16,128]{3,2,1,0:T(8,128)(2,1)S(1)}, u32[]{:S(2)}) copy-start(bf16[64,1,16,128]{3,2,1,0:T(8,128)(2,1)S(1)} %collective-permute-done.1.high) | copy-start | bytes 786436
  21.3 75.1 %collective-permute-start.6 = (bf16[64,3,16,128]{3,2,1,0:T(8,128)(2,1)}, bf16[64,3,16,128]{3,2,1,0:T(8,128)(2,1)}, u32[]{:S(2)}, u32[]{:S(2)}) collective-permute-start(bf16[64,3,16,128]{3,2,1,0:T(8,128)(2,1)} %cut.12), channel_id=1, source_target_pairs={{0,1},{1,0},{2,3},{3,2},{4,5},{5,4},{6,7},{7,6},{8,9},{9,8},{10,11... | collective-permute-start | bytes 2359304 | tf_op jit(solution)/shard_map/ppermute | solution.py:433
  24.7 9.9 %copy-start = (f32[1,32,16,128]{3,2,1,0:T(8,128)S(1)}, f32[1,32,16,128]{3,2,1,0:T(8,128)}, u32[]{:S(2)}) copy-start(f32[1,32,16,128]{3,2,1,0:T(8,128)} %param.6) | copy-start | bytes 786436
  29.0 78.8 %collective-permute-start.7 = (bf16[64,2,16,128]{3,2,1,0:T(8,128)(2,1)}, bf16[64,2,16,128]{3,2,1,0:T(8,128)(2,1)}, u32[]{:S(2)}, u32[]{:S(2)}) collective-permute-start(bf16[64,2,16,128]{3,2,1,0:T(8,128)(2,1)} %cut.13), channel_id=1, source_target_pairs={{0,1},{1,0},{2,3},{3,2},{4,5},{5,4},{6,7},{7,6},{8,9},{9,8},{10,11... | collective-permute-start | bytes 1572872 | tf_op jit(solution)/shard_map/ppermute | solution.py:433
  34.6 1.0 copy-start.1
  35.6 0.9 copy-start.3
  36.5 0.9 copy-start.5
  81.8 87.9 %collective-permute-start.19 = (bf16[64,11,16,128]{3,2,1,0:T(8,128)(2,1)}, bf16[64,11,16,128]{3,2,1,0:T(8,128)(2,1)}, u32[]{:S(2)}, u32[]{:S(2)}) collective-permute-start(bf16[64,11,16,128]{3,2,1,0:T(8,128)(2,1)} %cut.17), channel_id=1, source_target_pairs={{0,1},{1,0},{2,3},{3,2},{4,5},{5,4},{6,7},{7,6},{8,9},{9,8},{10,11... | collective-permute-start | bytes 8650760 | tf_op jit(solution)/shard_map/ppermute | solution.py:433
  119.9 11.4 %copy-start.8 = (s32[4]{0:T(128)S(1)}, s32[4]{0:T(128)}, u32[]{:S(2)}) copy-start(s32[4]{0:T(128)} %param.9) | copy-start | bytes 52
  126.4 4.1 %collective-permute-start.8 = (f32[80,128]{1,0:T(8,128)S(1)}, f32[80,128]{1,0:T(8,128)S(1)}, u32[]{:S(2)}, u32[]{:S(2)}) collective-permute-start(f32[80,128]{1,0:T(8,128)S(1)} %maximum_maximum_fusion), channel_id=1, source_target_pairs={{0,2},{2,0},{4,6},{6,4},{1,3},{3,1},{5,7},{7,5},{8,10},{10,8},{12,... | collective-permute-start | bytes 122888 | tf_op jit(solution)/shard_map/ppermute | solution.py:467
  130.6 1.3 collective-permute-start.9
  131.9 9.9 %collective-permute-start.10 = (f32[80,128]{1,0:T(8,128)S(1)}, f32[80,128]{1,0:T(8,128)S(1)}, u32[]{:S(2)}, u32[]{:S(2)}) collective-permute-start(f32[80,128]{1,0:T(8,128)S(1)} %add.81), channel_id=1, source_target_pairs={{2,0},{4,6},{3,1},{5,7},{10,8},{12,14},{11,9},{13,15},{18,16},{20,... | collective-permute-start | bytes 122888 | tf_op jit(solution)/shard_map/ppermute | solution.py:469
  141.8 1.3 collective-permute-start.11
  143.2 4.5 %collective-permute-start.12 = (f32[2,80,128]{2,1,0:T(8,128)S(1)}, f32[2,80,128]{2,1,0:T(8,128)S(1)}, u32[]{:S(2)}, u32[]{:S(2)}) collective-permute-start(f32[2,80,128]{2,1,0:T(8,128)S(1)} %fusion.6), channel_id=1, source_target_pairs={{0,16},{8,24},{16,0},{24,8},{1,17},{9,25},{17,1},{25,9},{2,18},{10... | collective-permute-start | bytes 245768 | tf_op jit(solution)/shard_map/ppermute | solution.py:459
  148.9 31.9 %collective-permute-start.18 = (bf16[64,2,16,128]{3,2,1,0:T(8,128)(2,1)S(1)}, bf16[64,2,16,128]{3,2,1,0:T(8,128)(2,1)S(1)}, u32[]{:S(2)}, u32[]{:S(2)}) collective-permute-start(bf16[64,2,16,128]{3,2,1,0:T(8,128)(2,1)S(1)} %cut.16), channel_id=1, source_target_pairs={{0,1},{1,0},{2,3},{3,2},{4,5},{5,4},{6,7},{7,6},{8,9},{9,8},{10,11... | collective-permute-start | bytes 1572872 | tf_op jit(solution)/shard_map/ppermute | solution.py:433
  150.7 4.7 %collective-permute-start.13 = (f32[10,128]{1,0:T(8,128)S(1)}, f32[10,128]{1,0:T(8,128)S(1)}, u32[]{:S(2)}, u32[]{:S(2)}) collective-permute-start(f32[10,128]{1,0:T(8,128)S(1)} %fusion.5), channel_id=1, source_target_pairs={{0,17},{1,16},{8,25},{9,24},{16,1},{17,0},{24,9},{25,8},{2,19},{3,... | collective-permute-start | bytes 15368 | tf_op jit(solution)/shard_map/ppermute | solution.py:442
  155.3 3.7 %collective-permute-start.14 = (f32[10,128]{1,0:T(8,128)S(1)}, f32[10,128]{1,0:T(8,128)S(1)}, u32[]{:S(2)}, u32[]{:S(2)}) collective-permute-start(f32[10,128]{1,0:T(8,128)S(1)} %collective-permute-done.13), channel_id=1, source_target_pairs={{0,2},{2,0},{4,6},{6,4},{1,3},{3,1},{5,7},{7,5},{8,10},{10,8},{12,... | collective-permute-start | bytes 15368 | tf_op jit(solution)/shard_map/ppermute | solution.py:451
  156.3 29.3 %collective-permute-start.17 = (bf16[64,1,16,128]{3,2,1,0:T(8,128)(2,1)S(1)}, bf16[64,1,16,128]{3,2,1,0:T(8,128)(2,1)S(1)}, u32[]{:S(2)}, u32[]{:S(2)}) collective-permute-start(bf16[64,1,16,128]{3,2,1,0:T(8,128)(2,1)S(1)} %cut.15), channel_id=1, source_target_pairs={{0,1},{1,0},{2,3},{3,2},{4,5},{5,4},{6,7},{7,6},{8,9},{9,8},{10,11... | collective-permute-start | bytes 786440 | tf_op jit(solution)/shard_map/ppermute | solution.py:433
  159.0 4.7 %collective-permute-start.15 = (f32[20,128]{1,0:T(8,128)S(1)}, f32[20,128]{1,0:T(8,128)S(1)}, u32[]{:S(2)}, u32[]{:S(2)}) collective-permute-start(f32[20,128]{1,0:T(8,128)S(1)} %maximum_select_fusion.2), channel_id=1, source_target_pairs={{0,4},{2,6},{4,0},{6,2},{1,5},{3,7},{5,1},{7,3},{8,12},{10,14},{12... | collective-permute-start | bytes 30728 | tf_op jit(solution)/shard_map/ppermute | solution.py:451
  163.7 1.3 collective-permute-start.16
  169.7 0.8 copy-start.6

commit v9 on v8

--- a/solution.py
+++ b/solution.py
@@ -214,35 +214,20 @@
     )(at.reshape(1), whole, *orders)
 
 
-def cut_middle_kernel(start, whole, out, held, reads, writes):
-    layers = out.shape[1]
-    ins, outs = [], []
-    for i in range(layers):
-        piece = held.at[:, pl.ds(i, 1)]
-        ins.append(pltpu.make_async_copy(whole.at[:, pl.ds(start + i, 1)], piece, reads.at[i]))
-        outs.append(pltpu.make_async_copy(piece, out.at[:, pl.ds(i, 1)], writes.at[i]))
-    for copy in ins:
-        copy.start()
-    for i in range(layers):
-        ins[i].wait()
-        outs[i].start()
-    for copy in outs:
-        copy.wait()
+def cut_middle_kernel(start, whole, out, sem):
+    copy = pltpu.make_async_copy(whole.at[:, pl.ds(start, out.shape[1])], out, sem)
+    copy.start()
+    copy.wait()
 
 
 def cut_middle(whole, count):
     rows, layers, cells_y, cells_z = whole.shape
-    shape = (rows, count, cells_y, cells_z)
     return pl.pallas_call(
         functools.partial(cut_middle_kernel, (layers - count) // 2),
         in_specs=[pl.BlockSpec(memory_space=pl.ANY)],
         out_specs=pl.BlockSpec(memory_space=pl.ANY),
-        scratch_shapes=[
-            pltpu.VMEM(shape, whole.dtype),
-            pltpu.SemaphoreType.DMA((count,)),
-            pltpu.SemaphoreType.DMA((count,)),
-        ],
-        out_shape=jax.ShapeDtypeStruct(shape, whole.dtype),
+        scratch_shapes=[pltpu.SemaphoreType.DMA],
+        out_shape=jax.ShapeDtypeStruct((rows, count, cells_y, cells_z), whole.dtype),
         compiler_params=pltpu.CompilerParams(vmem_limit_bytes=VMEM_BYTES),
         cost_estimate=SMALL,
         name="cut_middle",
@@ -378,51 +363,67 @@
     )(*inputs)
 
 
-def last_kernel(at, spread, own, other, held, out, made, sems):
+def halves(spread):
+    middle = spread.shape[1] // 2
+    return slice(0, middle), slice(middle, 2 * middle)
+
+
+def early_kernel(spread, own, made):
+    mine, _ = halves(spread)
+    for layer in range(own.shape[1]):
+        flat = split_rows(own[:, layer])
+        made[layer] = jnp.dot(spread[:, mine], flat, preferred_element_type=jnp.float32)
+
+
+def expand_early(spread, own):
     rows, layers, cells_y, cells_z = own.shape
-    eigs = out.shape[0]
-    parts = made.shape[0]
-    copies = []
+    inside = pl.BlockSpec(memory_space=pltpu.VMEM)
+    shape = (layers, spread.shape[0], cells_y // SUB * cells_z)
+    return pl.pallas_call(
+        early_kernel,
+        in_specs=[inside, inside],
+        out_specs=inside,
+        out_shape=jax.ShapeDtypeStruct(shape, jnp.float32),
+        compiler_params=pltpu.CompilerParams(vmem_limit_bytes=LAST_BYTES),
+        cost_estimate=SMALL,
+        name="expand_early",
+    )(spread, own)
+
+
+def last_kernel(at, spread, early, other, held, out, made, sem):
+    rows, layers, cells_y, cells_z = other.shape
+    _, theirs = halves(spread)
     for layer in range(layers):
-        both = jnp.concatenate([split_rows(own[:, layer]), split_rows(other[:, layer])], axis=0)
-        for part in range(parts):
-            size = eigs // parts
-            some = jnp.dot(
-                spread[part * size * SUB : (part + 1) * size * SUB],
-                both,
-                preferred_element_type=jnp.float32,
-            )
-            tiles = [
-                some[:, i * cells_z : (i + 1) * cells_z].reshape(size, SUB, cells_z)
-                for i in range(cells_y // SUB)
-            ]
-            made[part, :, layer] = jnp.concatenate(tiles, axis=1).astype(made.dtype)
-            if layer == layers - 1:
-                place = out.at[pl.ds(part * size, size), pl.ds(at[0], layers)]
-                copies.append(pltpu.make_async_copy(made.at[part], place, sems.at[part]))
-                copies[-1].start()
-    for copy in copies:
-        copy.wait()
-
-
-def expand_last(spread, own, other, at, held):
+        flat = split_rows(other[:, layer])
+        whole = early[layer] + jnp.dot(spread[:, theirs], flat, preferred_element_type=jnp.float32)
+        tiles = [
+            whole[:, i * cells_z : (i + 1) * cells_z].reshape(out.shape[0], SUB, cells_z)
+            for i in range(cells_y // SUB)
+        ]
+        made[:, layer] = jnp.concatenate(tiles, axis=1).astype(made.dtype)
+    copy = pltpu.make_async_copy(made, out.at[:, pl.ds(at[0], layers)], sem)
+    copy.start()
+    copy.wait()
+
+
+def expand_last(spread, early, other, at, held):
     rows, layers, cells_y, cells_z = other.shape
-    eigs, parts = spread.shape[0] // SUB, 4
-    inside = pl.BlockSpec(memory_space=pltpu.VMEM)
+    eigs = spread.shape[0] // SUB
+    inside, outside = pl.BlockSpec(memory_space=pltpu.VMEM), pl.BlockSpec(memory_space=pl.ANY)
     return pl.pallas_call(
         last_kernel,
-        in_specs=[pl.BlockSpec(memory_space=pltpu.SMEM), inside, inside, inside, pl.BlockSpec(memory_space=pl.ANY)],
-        out_specs=pl.BlockSpec(memory_space=pl.ANY),
+        in_specs=[pl.BlockSpec(memory_space=pltpu.SMEM), inside, inside, inside, outside],
+        out_specs=outside,
         out_shape=jax.ShapeDtypeStruct(held.shape, held.dtype),
         scratch_shapes=[
-            pltpu.VMEM((parts, eigs // parts, layers, cells_y, cells_z), held.dtype),
-            pltpu.SemaphoreType.DMA((parts,)),
+            pltpu.VMEM((eigs, layers, cells_y, cells_z), held.dtype),
+            pltpu.SemaphoreType.DMA,
         ],
         input_output_aliases={4: 0},
         compiler_params=pltpu.CompilerParams(vmem_limit_bytes=LAST_BYTES),
         cost_estimate=SMALL,
         name="expand_last",
-    )(at.reshape(1), spread, own, other, held)
+    )(at.reshape(1), spread, early, other, held)
 
 
 def shares(total, parts):
@@ -537,7 +538,8 @@
     for chunk, at in zip(far[:-1], places[:-1]):
         vectors, _ = expand(spread, own, chunk, at, vectors, *order)
         order = ()
-    vectors = expand_last(spread, cut(own, places[-1], last, whole), far[-1], places[-1], vectors)
+    early = expand_early(spread, cut(own, places[-1], last, whole))
+    vectors = expand_last(spread, early, far[-1], places[-1], vectors)
     return (node_stiffness, root_stiffness, vectors[None])
 
 

time: 189 us -> 189 us (level)
  transfers between devices with their start and end apart: 20 -> 20, of which waited for: 14 -> 13; matrix products, arithmetic and copies ran while one was open for 2% -> 2% of each run, Pallas kernels for 59% -> 60%
where the time goes in v9:
time: 189 us; the launch traced here: 187 us
  Pallas kernels  113 us (60%)
  waiting for transfers between devices  40 us (21%)
  starting transfers between devices  24.7 us (13%)
  local copies, waits for them, and re-layouts  5.52 us (3%)
    pallas_call x1, Pallas kernels, stiff_terms(): pl.pallas_call(stiff_kernel, grid=(layers,), in_specs=[pl.BlockSpec(block...  40.1 us
    pallas_call x8, Pallas kernels, expand(): pl.pallas_call(vector_kernel, grid_spec=pltpu.PrefetchScalarGridSpec(num_...  34.9 us
    pallas_call x6, Pallas kernels, cross_terms(): pl.pallas_call(cross_kernel, grid_spec=pltpu.PrefetchScalarGridSpec(num_s...  18.9 us
    ppermute x9, waiting for transfers between devices, swap(): return lax.ppermute(x, 'blk', [(0, 1), (1, 0)])  17.1 us
    pallas_call x9, Pallas kernels, cut(): pl.pallas_call(cut_kernel, grid_spec=pltpu.PrefetchScalarGridSpec(num_sca...  15.3 us
    ppermute x9, starting transfers between devices, swap(): return lax.ppermute(x, 'blk', [(0, 1), (1, 0)])  11.6 us
    ppermute x1, waiting for transfers between devices, line_sum(): outer = lax.ppermute(x, axis, [(1, 0), (2, 3)])  7.73 us
    ppermute x3, waiting for transfers between devices, joined(): lax.ppermute(part, axis, [(i, i ^ step) for i in range(lax.axis_size(axis...  5.66 us
  transfers between devices with their start and end apart: 20, of which 13 were waited for; matrix products, arithmetic and copies ran while one was open for 2% of the time, Pallas kernels for 60%

profile of v9, /device:TPU:0, one launch (start us, length us, event | category | flops | bytes accessed | tf_op | source)
XLA Modules:
  0.0 186.7 jit_solution(8031846205533719465)
XLA Ops:
  1.9 3.0 %collective-permute-start.2 = (bf16[64,4,16,128]{3,2,1,0:T(8,128)(2,1)S(1)}, bf16[64,4,16,128]{3,2,1,0:T(8,128)(2,1)S(1)}, u32[]{:S(2)}, u32[]{:S(2)}) collective-permute-start(bf16[64,4,16,128]{3,2,1,0:T(8,128)(2,1)S(1)} %cut_middle.1.rest_0_), channel_id=1, source_target_pairs={{0,1},{1,0},{2,3},{3,2},{4,5},{5,4},{6,7},{7,6},{8,9},{9,8},{10,11... | collective-permute-start | bytes 3145736 | tf_op jit(solution)/shard_map/ppermute | solution.py:434
  6.0 3.5 %collective-permute-start = (bf16[64,1,16,128]{3,2,1,0:T(8,128)(2,1)S(1)}, bf16[64,1,16,128]{3,2,1,0:T(8,128)(2,1)S(1)}, u32[]{:S(2)}, u32[]{:S(2)}) collective-permute-start(bf16[64,1,16,128]{3,2,1,0:T(8,128)(2,1)S(1)} %get-tuple-element.42), channel_id=1, source_target_pairs={{0,2},{2,4},{4,6},{1,3},{3,5},{5,7},{8,10},{10,12},{12,14},{9,11},... | collective-permute-start | bytes 786440 | tf_op jit(solution)/shard_map/ppermute | solution.py:504
  16.8 1.9 %cut.11 = bf16[64,3,16,128]{3,2,1,0:T(8,128)(2,1)} custom-call(s32[1]{0:T(128)} %bitcast.21.at, bf16[64,32,16,128]{3,2,1,0:T(8,128)(2,1)} %bitcast.54, bf16[64,4,16,128]{3,2,1,0:T(8,128)(2,1)S(1)} %cut_middle.1.rest_0_), custom_call_target="tpu_custom_call" | custom-call | flops 1024 | bytes 1024 | tf_op jit(solution)/shard_map/cut/pallas_call | solution.py:197
  24.8 4.1 %collective-permute-done.2.order.other = bf16[64,4,16,128]{3,2,1,0:T(8,128)(2,1)S(1)} collective-permute-done((bf16[64,4,16,128]{3,2,1,0:T(8,128)(2,1)S(1)}, bf16[64,4,16,128]{3,2,1,0:T(8,128)(2,1)S(1)}, u32[]{:S(2)}, u32[]{:S(2)}) %collective-permute-start.2) | collective-permute-done | bytes 1048608 | tf_op jit(solution)/shard_map/ppermute | solution.py:434
  28.9 2.1 %collective-permute-start.7 = (bf16[64,2,16,128]{3,2,1,0:T(8,128)(2,1)}, bf16[64,2,16,128]{3,2,1,0:T(8,128)(2,1)}, u32[]{:S(2)}, u32[]{:S(2)}) collective-permute-start(bf16[64,2,16,128]{3,2,1,0:T(8,128)(2,1)} %cut.13), channel_id=1, source_target_pairs={{0,1},{1,0},{2,3},{3,2},{4,5},{5,4},{6,7},{7,6},{8,9},{9,8},{10,11... | collective-permute-start | bytes 1572872 | tf_op jit(solution)/shard_map/ppermute | solution.py:434
  31.6 2.8 %cut.17 = bf16[64,11,16,128]{3,2,1,0:T(8,128)(2,1)} custom-call(s32[1]{0:T(128)} %bitcast.33.at, bf16[64,32,16,128]{3,2,1,0:T(8,128)(2,1)} %bitcast.57, bf16[64,4,16,128]{3,2,1,0:T(8,128)(2,1)S(1)} %cut_middle.1.rest_0_), custom_call_target="tpu_custom_call" | custom-call | flops 1024 | bytes 1024 | tf_op jit(solution)/shard_map/cut/pallas_call | solution.py:197
  37.4 40.1 %stiff_terms.1 = (bf16[32,512,256]{2,1,0:T(8,128)(2,1)}, f32[64,64]{1,0:T(8,128)S(1)}, f32[16,64]{1,0:T(8,128)S(1)}) custom-call(bf16[64,32,16,128]{3,2,1,0:T(8,128)(2,1)} %bitcast.58, bf16[64,32,16,128]{3,2,1,0:T(8,128)(2,1)} %bitcast.59, bf16[64,32,16,128]{3,2,1,0:T(8,128)(2,1)} %bitcast.60, bf16[64,1,16,128]{3,2,1,0:T(8,128)(2,1)S(1)} %copy-done.3, ...), custom_call_target="tpu_custom_call" | custom-call | flops 1024 | bytes 1024 | tf_op jit(solution)/shard_map/stiff_terms/pallas_call | solution.py:100
  77.5 4.2 %expand.8 = (bf16[64,32,16,128]{3,2,1,0:T(8,128)(2,1)}, f32[8,128]{1,0:T(8,128)S(1)}) custom-call(s32[1]{0:T(128)} %constant.95.clone.1.at, bf16[512,1024]{1,0:T(8,128)(2,1)S(1)} %spread_blocks.1.spread, bf16[64,32,16,128]{3,2,1,0:T(8,128)(2,1)} %bitcast.61, bf16[64,4,16,128]{3,2,1,0:T(8,128)(2,1)S(1)} %collective-permute-done.2.order.other, ...), custom_call_target="tpu_custom_call" | custom-call | flops 1024 | bytes 1024 | tf_op jit(solution)/shard_map/expand/pallas_call | solution.py:344
  81.7 3.8 %expand.9 = (bf16[64,32,16,128]{3,2,1,0:T(8,128)(2,1)}, f32[8,128]{1,0:T(8,128)S(1)}) custom-call(s32[1]{0:T(128)} %bitcast.16.at, bf16[512,1024]{1,0:T(8,128)(2,1)S(1)} %spread_blocks.1.spread, bf16[64,32,16,128]{3,2,1,0:T(8,128)(2,1)} %bitcast.62, bf16[64,3,16,128]{3,2,1,0:T(8,128)(2,1)} %collective-permute-done.3.other, ...), custom_call_target="tpu_custom_call", output_to_operand_aliasing={{0}: (4, {})} | custom-call | flops 1024 | bytes 1024 | tf_op jit(solution)/shard_map/expand/pallas_call | solution.py:344
  85.5 3.8 %expand.10 = (bf16[64,32,16,128]{3,2,1,0:T(8,128)(2,1)}, f32[8,128]{1,0:T(8,128)S(1)}) custom-call(s32[1]{0:T(128)} %bitcast.18.at, bf16[512,1024]{1,0:T(8,128)(2,1)S(1)} %spread_blocks.1.spread, bf16[64,32,16,128]{3,2,1,0:T(8,128)(2,1)} %bitcast.63, bf16[64,3,16,128]{3,2,1,0:T(8,128)(2,1)} %collective-permute-done.4.other, ...), custom_call_target="tpu_custom_call", output_to_operand_aliasing={{0}: (4, {})} | custom-call | flops 1024 | bytes 1024 | tf_op jit(solution)/shard_map/expand/pallas_call | solution.py:344
  89.3 3.8 %expand.11 = (bf16[64,32,16,128]{3,2,1,0:T(8,128)(2,1)}, f32[8,128]{1,0:T(8,128)S(1)}) custom-call(s32[1]{0:T(128)} %bitcast.20.at, bf16[512,1024]{1,0:T(8,128)(2,1)S(1)} %spread_blocks.1.spread, bf16[64,32,16,128]{3,2,1,0:T(8,128)(2,1)} %bitcast.64, bf16[64,3,16,128]{3,2,1,0:T(8,128)(2,1)} %collective-permute-done.5.other, ...), custom_call_target="tpu_custom_call", output_to_operand_aliasing={{0}: (4, {})} | custom-call | flops 1024 | bytes 1024 | tf_op jit(solution)/shard_map/expand/pallas_call | solution.py:344
  93.1 3.3 %collective-permute-done.6.other = bf16[64,3,16,128]{3,2,1,0:T(8,128)(2,1)} collective-permute-done((bf16[64,3,16,128]{3,2,1,0:T(8,128)(2,1)}, bf16[64,3,16,128]{3,2,1,0:T(8,128)(2,1)}, u32[]{:S(2)}, u32[]{:S(2)}) %collective-permute-start.6) | collective-permute-done | bytes 786464 | tf_op jit(solution)/shard_map/ppermute | solution.py:434
  96.4 3.8 %expand.12 = (bf16[64,32,16,128]{3,2,1,0:T(8,128)(2,1)}, f32[8,128]{1,0:T(8,128)S(1)}) custom-call(s32[1]{0:T(128)} %bitcast.22.at, bf16[512,1024]{1,0:T(8,128)(2,1)S(1)} %spread_blocks.1.spread, bf16[64,32,16,128]{3,2,1,0:T(8,128)(2,1)} %bitcast.65, bf16[64,3,16,128]{3,2,1,0:T(8,128)(2,1)} %collective-permute-done.6.other, ...), custom_call_target="tpu_custom_call", output_to_operand_aliasing={{0}: (4, {})} | custom-call | flops 1024 | bytes 1024 | tf_op jit(solution)/shard_map/expand/pallas_call | solution.py:344
  100.2 3.5 %cross_terms.10 = f32[64,64]{1,0:T(8,128)S(1)} custom-call(s32[1]{0:T(128)} %bitcast.22.at, s32[1]{0:T(128)} %constant.100.clone.1.skip, bf16[32,512,256]{2,1,0:T(8,128)(2,1)} %get-tuple-element.23.stiff, bf16[64,3,16,128]{3,2,1,0:T(8,128)(2,1)} %collective-permute-done.6.other, f32[8,128]{1,0:T(8,128)S(1)} %get-tuple-element.33.order), custom_call_target="tpu_custom_call" | custom-call | flops 1024 | bytes 1024 | tf_op jit(solution)/shard_map/cross_terms/pallas_call | solution.py:151
  103.7 3.9 %collective-permute-done.7.other = bf16[64,2,16,128]{3,2,1,0:T(8,128)(2,1)} collective-permute-done((bf16[64,2,16,128]{3,2,1,0:T(8,128)(2,1)}, bf16[64,2,16,128]{3,2,1,0:T(8,128)(2,1)}, u32[]{:S(2)}, u32[]{:S(2)}) %collective-permute-start.7) | collective-permute-done | bytes 524320 | tf_op jit(solution)/shard_map/ppermute | solution.py:434
  107.6 2.7 %expand.13 = (bf16[64,32,16,128]{3,2,1,0:T(8,128)(2,1)}, f32[8,128]{1,0:T(8,128)S(1)}) custom-call(s32[1]{0:T(128)} %bitcast.24.at, bf16[512,1024]{1,0:T(8,128)(2,1)S(1)} %spread_blocks.1.spread, bf16[64,32,16,128]{3,2,1,0:T(8,128)(2,1)} %bitcast.66, bf16[64,2,16,128]{3,2,1,0:T(8,128)(2,1)} %collective-permute-done.7.other, ...), custom_call_target="tpu_custom_call", output_to_operand_aliasing={{0}: (4, {})} | custom-call | flops 1024 | bytes 1024 | tf_op jit(solution)/shard_map/expand/pallas_call | solution.py:344
  110.3 2.5 %cross_terms.11 = f32[64,64]{1,0:T(8,128)S(1)} custom-call(s32[1]{0:T(128)} %bitcast.24.at, s32[1]{0:T(128)} %constant.100.clone.1.skip, bf16[32,512,256]{2,1,0:T(8,128)(2,1)} %get-tuple-element.23.stiff, bf16[64,2,16,128]{3,2,1,0:T(8,128)(2,1)} %collective-permute-done.7.other, f32[8,128]{1,0:T(8,128)S(1)} %get-tuple-element.35.order), custom_call_target="tpu_custom_call" | custom-call | flops 1024 | bytes 1024 | tf_op jit(solution)/shard_map/cross_terms/pallas_call | solution.py:151
  112.8 3.5 %cross_terms.9 = f32[64,64]{1,0:T(8,128)S(1)} custom-call(s32[1]{0:T(128)} %bitcast.20.at, s32[1]{0:T(128)} %constant.100.clone.1.skip, bf16[32,512,256]{2,1,0:T(8,128)(2,1)} %get-tuple-element.23.stiff, bf16[64,3,16,128]{3,2,1,0:T(8,128)(2,1)} %collective-permute-done.5.other, f32[8,128]{1,0:T(8,128)S(1)} %get-tuple-element.31.order), custom_call_target="tpu_custom_call" | custom-call | flops 1024 | bytes 1024 | tf_op jit(solution)/shard_map/cross_terms/pallas_call | solution.py:151
  116.3 3.5 %cross_terms.8 = f32[64,64]{1,0:T(8,128)S(1)} custom-call(s32[1]{0:T(128)} %bitcast.18.at, s32[1]{0:T(128)} %constant.100.clone.1.skip, bf16[32,512,256]{2,1,0:T(8,128)(2,1)} %get-tuple-element.23.stiff, bf16[64,3,16,128]{3,2,1,0:T(8,128)(2,1)} %collective-permute-done.4.other, f32[8,128]{1,0:T(8,128)S(1)} %get-tuple-element.29.order), custom_call_target="tpu_custom_call" | custom-call | flops 1024 | bytes 1024 | tf_op jit(solution)/shard_map/cross_terms/pallas_call | solution.py:151
  119.8 3.5 %cross_terms.7 = f32[64,64]{1,0:T(8,128)S(1)} custom-call(s32[1]{0:T(128)} %bitcast.16.at, s32[1]{0:T(128)} %constant.100.clone.1.skip, bf16[32,512,256]{2,1,0:T(8,128)(2,1)} %get-tuple-element.23.stiff, bf16[64,3,16,128]{3,2,1,0:T(8,128)(2,1)} %collective-permute-done.3.other, f32[8,128]{1,0:T(8,128)S(1)} %get-tuple-element.27.order), custom_call_target="tpu_custom_call" | custom-call | flops 1024 | bytes 1024 | tf_op jit(solution)/shard_map/cross_terms/pallas_call | solution.py:151
  123.3 2.4 %cross_terms.6 = f32[64,64]{1,0:T(8,128)S(1)} custom-call(s32[1]{0:T(128)} %bitcast.11.at, s32[1]{0:T(128)} %bitcast.12.skip, bf16[32,512,256]{2,1,0:T(8,128)(2,1)} %get-tuple-element.23.stiff, bf16[64,4,16,128]{3,2,1,0:T(8,128)(2,1)S(1)} %collective-permute-done.2.order.other, f32[8,128]{1,0:T(8,128)S(1)} %get-tuple-element.25.order), custom_call_target="tpu_custom_call" | custom-call | flops 1024 | bytes 1024 | tf_op jit(solution)/shard_map/cross_terms/pallas_call | solution.py:151
  126.3 2.1 %collective-permute-start.8 = (f32[80,128]{1,0:T(8,128)S(1)}, f32[80,128]{1,0:T(8,128)S(1)}, u32[]{:S(2)}, u32[]{:S(2)}) collective-permute-start(f32[80,128]{1,0:T(8,128)S(1)} %maximum_maximum_fusion), channel_id=1, source_target_pairs={{0,2},{2,0},{4,6},{6,4},{1,3},{3,1},{5,7},{7,5},{8,10},{10,8},{12,... | collective-permute-start | bytes 122888 | tf_op jit(solution)/shard_map/ppermute | solution.py:468
  128.4 2.0 %collective-permute-done.8 = f32[80,128]{1,0:T(8,128)S(1)} collective-permute-done((f32[80,128]{1,0:T(8,128)S(1)}, f32[80,128]{1,0:T(8,128)S(1)}, u32[]{:S(2)}, u32[]{:S(2)}) %collective-permute-start.8) | collective-permute-done | bytes 40992 | tf_op jit(solution)/shard_map/ppermute | solution.py:468
  133.9 7.7 %collective-permute-done.10 = f32[80,128]{1,0:T(8,128)S(1)} collective-permute-done((f32[80,128]{1,0:T(8,128)S(1)}, f32[80,128]{1,0:T(8,128)S(1)}, u32[]{:S(2)}, u32[]{:S(2)}) %collective-permute-start.10) | collective-permute-done | bytes 40992 | tf_op jit(solution)/shard_map/ppermute | solution.py:470
  144.6 3.0 %collective-permute-done.12 = f32[2,80,128]{2,1,0:T(8,128)S(1)} collective-permute-done((f32[2,80,128]{2,1,0:T(8,128)S(1)}, f32[2,80,128]{2,1,0:T(8,128)S(1)}, u32[]{:S(2)}, u32[]{:S(2)}) %collective-permute-start.12) | collective-permute-done | bytes 81952 | tf_op jit(solution)/shard_map/ppermute | solution.py:460
  152.0 3.2 %collective-permute-done.13 = f32[10,128]{1,0:T(8,128)S(1)} collective-permute-done((f32[10,128]{1,0:T(8,128)S(1)}, f32[10,128]{1,0:T(8,128)S(1)}, u32[]{:S(2)}, u32[]{:S(2)}) %collective-permute-start.13) | collective-permute-done | bytes 5152 | tf_op jit(solution)/shard_map/ppermute | solution.py:443
  156.8 2.1 %collective-permute-done.14 = f32[10,128]{1,0:T(8,128)S(1)} collective-permute-done((f32[10,128]{1,0:T(8,128)S(1)}, f32[10,128]{1,0:T(8,128)S(1)}, u32[]{:S(2)}, u32[]{:S(2)}) %collective-permute-start.14) | collective-permute-done | bytes 5152 | tf_op jit(solution)/shard_map/ppermute | solution.py:452
  160.0 3.6 %collective-permute-done.15 = f32[20,128]{1,0:T(8,128)S(1)} collective-permute-done((f32[20,128]{1,0:T(8,128)S(1)}, f32[20,128]{1,0:T(8,128)S(1)}, u32[]{:S(2)}, u32[]{:S(2)}) %collective-permute-start.15) | collective-permute-done | bytes 10272 | tf_op jit(solution)/shard_map/ppermute | solution.py:452
  166.1 3.5 %collective-permute-done.19.other = bf16[64,11,16,128]{3,2,1,0:T(8,128)(2,1)} collective-permute-done((bf16[64,11,16,128]{3,2,1,0:T(8,128)(2,1)}, bf16[64,11,16,128]{3,2,1,0:T(8,128)(2,1)}, u32[]{:S(2)}, u32[]{:S(2)}) %collective-permute-start.19) | collective-permute-done | bytes 2883616 | tf_op jit(solution)/shard_map/ppermute | solution.py:434
  170.4 10.3 %expand.14 = (bf16[64,32,16,128]{3,2,1,0:T(8,128)(2,1)}, f32[8,128]{1,0:T(8,128)}) custom-call(s32[1]{0:T(128)} %bitcast.32.at, bf16[512,1024]{1,0:T(8,128)(2,1)S(1)} %spread_blocks.1.spread, bf16[64,32,16,128]{3,2,1,0:T(8,128)(2,1)} %bitcast.70, bf16[64,11,16,128]{3,2,1,0:T(8,128)(2,1)} %collective-permute-done.19.other, ...), custom_call_target="tpu_custom_call", output_to_operand_aliasing={{0}: (4, {})} | custom-call | flops 1024 | bytes 1024 | tf_op jit(solution)/shard_map/expand/pallas_call | solution.py:344
  180.7 2.6 %expand.15 = (bf16[64,32,16,128]{3,2,1,0:T(8,128)(2,1)}, f32[8,128]{1,0:T(8,128)}) custom-call(s32[1]{0:T(128)} %bitcast.30.at, bf16[512,1024]{1,0:T(8,128)(2,1)S(1)} %spread_blocks.1.spread, bf16[64,32,16,128]{3,2,1,0:T(8,128)(2,1)} %bitcast.71, bf16[64,2,16,128]{3,2,1,0:T(8,128)(2,1)S(1)} %collective-permute-done.18.other, ...), custom_call_target="tpu_custom_call", output_to_operand_aliasing={{0}: (4, {})} | custom-call | flops 1024 | bytes 1024 | tf_op jit(solution)/shard_map/expand/pallas_call | solution.py:344
  183.3 2.2 %collective-permute-done.17.other = bf16[64,1,16,128]{3,2,1,0:T(8,128)(2,1)S(1)} collective-permute-done((bf16[64,1,16,128]{3,2,1,0:T(8,128)(2,1)S(1)}, bf16[64,1,16,128]{3,2,1,0:T(8,128)(2,1)S(1)}, u32[]{:S(2)}, u32[]{:S(2)}) %collective-permute-start.17) | collective-permute-done | bytes 262176 | tf_op jit(solution)/shard_map/ppermute | solution.py:434
  (77 shorter events, 37.4 us)
Async XLA Ops:
  1.9 27.0 %collective-permute-start.2 = (bf16[64,4,16,128]{3,2,1,0:T(8,128)(2,1)S(1)}, bf16[64,4,16,128]{3,2,1,0:T(8,128)(2,1)S(1)}, u32[]{:S(2)}, u32[]{:S(2)}) collective-permute-start(bf16[64,4,16,128]{3,2,1,0:T(8,128)(2,1)S(1)} %cut_middle.1.rest_0_), channel_id=1, source_target_pairs={{0,1},{1,0},{2,3},{3,2},{4,5},{5,4},{6,7},{7,6},{8,9},{9,8},{10,11... | collective-permute-start | bytes 3145736 | tf_op jit(solution)/shard_map/ppermute | solution.py:434
  6.0 12.7 %collective-permute-start = (bf16[64,1,16,128]{3,2,1,0:T(8,128)(2,1)S(1)}, bf16[64,1,16,128]{3,2,1,0:T(8,128)(2,1)S(1)}, u32[]{:S(2)}, u32[]{:S(2)}) collective-permute-start(bf16[64,1,16,128]{3,2,1,0:T(8,128)(2,1)S(1)} %get-tuple-element.42), channel_id=1, source_target_pairs={{0,2},{2,4},{4,6},{1,3},{3,5},{5,7},{8,10},{10,12},{12,14},{9,11},... | collective-permute-start | bytes 786440 | tf_op jit(solution)/shard_map/ppermute | solution.py:504
  9.5 11.8 %collective-permute-start.1 = (bf16[64,1,16,128]{3,2,1,0:T(8,128)(2,1)S(1)}, bf16[64,1,16,128]{3,2,1,0:T(8,128)(2,1)S(1)}, u32[]{:S(2)}, u32[]{:S(2)}) collective-permute-start(bf16[64,1,16,128]{3,2,1,0:T(8,128)(2,1)S(1)} %get-tuple-element.41), channel_id=1, source_target_pairs={{2,0},{4,2},{6,4},{3,1},{5,3},{7,5},{10,8},{12,10},{14,12},{11,9},... | collective-permute-start | bytes 786440 | tf_op jit(solution)/shard_map/ppermute | solution.py:505
  12.7 69.0 %collective-permute-start.3 = (bf16[64,3,16,128]{3,2,1,0:T(8,128)(2,1)}, bf16[64,3,16,128]{3,2,1,0:T(8,128)(2,1)}, u32[]{:S(2)}, u32[]{:S(2)}) collective-permute-start(bf16[64,3,16,128]{3,2,1,0:T(8,128)(2,1)} %cut.9), channel_id=1, source_target_pairs={{0,1},{1,0},{2,3},{3,2},{4,5},{5,4},{6,7},{7,6},{8,9},{9,8},{10,11... | collective-permute-start | bytes 2359304 | tf_op jit(solution)/shard_map/ppermute | solution.py:434
  15.2 70.3 %collective-permute-start.4 = (bf16[64,3,16,128]{3,2,1,0:T(8,128)(2,1)}, bf16[64,3,16,128]{3,2,1,0:T(8,128)(2,1)}, u32[]{:S(2)}, u32[]{:S(2)}) collective-permute-start(bf16[64,3,16,128]{3,2,1,0:T(8,128)(2,1)} %cut.10), channel_id=1, source_target_pairs={{0,1},{1,0},{2,3},{3,2},{4,5},{5,4},{6,7},{7,6},{8,9},{9,8},{10,11... | collective-permute-start | bytes 2359304 | tf_op jit(solution)/shard_map/ppermute | solution.py:434
  18.7 5.9 %copy-start.2 = (bf16[64,1,16,128]{3,2,1,0:T(8,128)(2,1)}, bf16[64,1,16,128]{3,2,1,0:T(8,128)(2,1)S(1)}, u32[]{:S(2)}) copy-start(bf16[64,1,16,128]{3,2,1,0:T(8,128)(2,1)S(1)} %collective-permute-done.low) | copy-start | bytes 786436
  18.7 70.6 %collective-permute-start.5 = (bf16[64,3,16,128]{3,2,1,0:T(8,128)(2,1)}, bf16[64,3,16,128]{3,2,1,0:T(8,128)(2,1)}, u32[]{:S(2)}, u32[]{:S(2)}) collective-permute-start(bf16[64,3,16,128]{3,2,1,0:T(8,128)(2,1)} %cut.11), channel_id=1, source_target_pairs={{0,1},{1,0},{2,3},{3,2},{4,5},{5,4},{6,7},{7,6},{8,9},{9,8},{10,11... | collective-permute-start | bytes 2359304 | tf_op jit(solution)/shard_map/ppermute | solution.py:434
  19.3 5.4 %copy-start.7 = (bf16[1,128,64]{1,2,0:T(8,128)(2,1)S(1)}, bf16[1,128,64]{1,2,0:T(8,128)(2,1)}, u32[]{:S(2)}) copy-start(bf16[1,128,64]{1,2,0:T(8,128)(2,1)} %param.8) | copy-start | bytes 49156
  21.3 9.7 %copy-start.4 = (bf16[64,1,16,128]{3,2,1,0:T(8,128)(2,1)}, bf16[64,1,16,128]{3,2,1,0:T(8,128)(2,1)S(1)}, u32[]{:S(2)}) copy-start(bf16[64,1,16,128]{3,2,1,0:T(8,128)(2,1)S(1)} %collective-permute-done.1.high) | copy-start | bytes 786436
  21.3 75.1 %collective-permute-start.6 = (bf16[64,3,16,128]{3,2,1,0:T(8,128)(2,1)}, bf16[64,3,16,128]{3,2,1,0:T(8,128)(2,1)}, u32[]{:S(2)}, u32[]{:S(2)}) collective-permute-start(bf16[64,3,16,128]{3,2,1,0:T(8,128)(2,1)} %cut.12), channel_id=1, source_target_pairs={{0,1},{1,0},{2,3},{3,2},{4,5},{5,4},{6,7},{7,6},{8,9},{9,8},{10,11... | collective-permute-start | bytes 2359304 | tf_op jit(solution)/shard_map/ppermute | solution.py:434
  24.7 9.9 %copy-start = (f32[1,32,16,128]{3,2,1,0:T(8,128)S(1)}, f32[1,32,16,128]{3,2,1,0:T(8,128)}, u32[]{:S(2)}) copy-start(f32[1,32,16,128]{3,2,1,0:T(8,128)} %param.6) | copy-start | bytes 786436
  28.9 78.8 %collective-permute-start.7 = (bf16[64,2,16,128]{3,2,1,0:T(8,128)(2,1)}, bf16[64,2,16,128]{3,2,1,0:T(8,128)(2,1)}, u32[]{:S(2)}, u32[]{:S(2)}) collective-permute-start(bf16[64,2,16,128]{3,2,1,0:T(8,128)(2,1)} %cut.13), channel_id=1, source_target_pairs={{0,1},{1,0},{2,3},{3,2},{4,5},{5,4},{6,7},{7,6},{8,9},{9,8},{10,11... | collective-permute-start | bytes 1572872 | tf_op jit(solution)/shard_map/ppermute | solution.py:434
  34.5 1.0 copy-start.1
  35.5 0.9 copy-start.3
  36.4 0.9 copy-start.5
  81.7 87.9 %collective-permute-start.19 = (bf16[64,11,16,128]{3,2,1,0:T(8,128)(2,1)}, bf16[64,11,16,128]{3,2,1,0:T(8,128)(2,1)}, u32[]{:S(2)}, u32[]{:S(2)}) collective-permute-start(bf16[64,11,16,128]{3,2,1,0:T(8,128)(2,1)} %cut.17), channel_id=1, source_target_pairs={{0,1},{1,0},{2,3},{3,2},{4,5},{5,4},{6,7},{7,6},{8,9},{9,8},{10,11... | collective-permute-start | bytes 8650760 | tf_op jit(solution)/shard_map/ppermute | solution.py:434
  119.8 11.4 %copy-start.8 = (s32[4]{0:T(128)S(1)}, s32[4]{0:T(128)}, u32[]{:S(2)}) copy-start(s32[4]{0:T(128)} %param.9) | copy-start | bytes 52
  126.3 4.1 %collective-permute-start.8 = (f32[80,128]{1,0:T(8,128)S(1)}, f32[80,128]{1,0:T(8,128)S(1)}, u32[]{:S(2)}, u32[]{:S(2)}) collective-permute-start(f32[80,128]{1,0:T(8,128)S(1)} %maximum_maximum_fusion), channel_id=1, source_target_pairs={{0,2},{2,0},{4,6},{6,4},{1,3},{3,1},{5,7},{7,5},{8,10},{10,8},{12,... | collective-permute-start | bytes 122888 | tf_op jit(solution)/shard_map/ppermute | solution.py:468
  130.5 1.3 collective-permute-start.9
  131.8 9.9 %collective-permute-start.10 = (f32[80,128]{1,0:T(8,128)S(1)}, f32[80,128]{1,0:T(8,128)S(1)}, u32[]{:S(2)}, u32[]{:S(2)}) collective-permute-start(f32[80,128]{1,0:T(8,128)S(1)} %add.81), channel_id=1, source_target_pairs={{2,0},{4,6},{3,1},{5,7},{10,8},{12,14},{11,9},{13,15},{18,16},{20,... | collective-permute-start | bytes 122888 | tf_op jit(solution)/shard_map/ppermute | solution.py:470
  141.7 1.3 collective-permute-start.11
  143.1 4.5 %collective-permute-start.12 = (f32[2,80,128]{2,1,0:T(8,128)S(1)}, f32[2,80,128]{2,1,0:T(8,128)S(1)}, u32[]{:S(2)}, u32[]{:S(2)}) collective-permute-start(f32[2,80,128]{2,1,0:T(8,128)S(1)} %fusion.6), channel_id=1, source_target_pairs={{0,16},{8,24},{16,0},{24,8},{1,17},{9,25},{17,1},{25,9},{2,18},{10... | collective-permute-start | bytes 245768 | tf_op jit(solution)/shard_map/ppermute | solution.py:460
  148.8 31.9 %collective-permute-start.18 = (bf16[64,2,16,128]{3,2,1,0:T(8,128)(2,1)S(1)}, bf16[64,2,16,128]{3,2,1,0:T(8,128)(2,1)S(1)}, u32[]{:S(2)}, u32[]{:S(2)}) collective-permute-start(bf16[64,2,16,128]{3,2,1,0:T(8,128)(2,1)S(1)} %cut.16), channel_id=1, source_target_pairs={{0,1},{1,0},{2,3},{3,2},{4,5},{5,4},{6,7},{7,6},{8,9},{9,8},{10,11... | collective-permute-start | bytes 1572872 | tf_op jit(solution)/shard_map/ppermute | solution.py:434
  150.6 4.7 %collective-permute-start.13 = (f32[10,128]{1,0:T(8,128)S(1)}, f32[10,128]{1,0:T(8,128)S(1)}, u32[]{:S(2)}, u32[]{:S(2)}) collective-permute-start(f32[10,128]{1,0:T(8,128)S(1)} %fusion.5), channel_id=1, source_target_pairs={{0,17},{1,16},{8,25},{9,24},{16,1},{17,0},{24,9},{25,8},{2,19},{3,... | collective-permute-start | bytes 15368 | tf_op jit(solution)/shard_map/ppermute | solution.py:443
  155.2 3.7 %collective-permute-start.14 = (f32[10,128]{1,0:T(8,128)S(1)}, f32[10,128]{1,0:T(8,128)S(1)}, u32[]{:S(2)}, u32[]{:S(2)}) collective-permute-start(f32[10,128]{1,0:T(8,128)S(1)} %collective-permute-done.13), channel_id=1, source_target_pairs={{0,2},{2,0},{4,6},{6,4},{1,3},{3,1},{5,7},{7,5},{8,10},{10,8},{12,... | collective-permute-start | bytes 15368 | tf_op jit(solution)/shard_map/ppermute | solution.py:452
  156.2 29.3 %collective-permute-start.17 = (bf16[64,1,16,128]{3,2,1,0:T(8,128)(2,1)S(1)}, bf16[64,1,16,128]{3,2,1,0:T(8,128)(2,1)S(1)}, u32[]{:S(2)}, u32[]{:S(2)}) collective-permute-start(bf16[64,1,16,128]{3,2,1,0:T(8,128)(2,1)S(1)} %cut.15), channel_id=1, source_target_pairs={{0,1},{1,0},{2,3},{3,2},{4,5},{5,4},{6,7},{7,6},{8,9},{9,8},{10,11... | collective-permute-start | bytes 786440 | tf_op jit(solution)/shard_map/ppermute | solution.py:434
  158.9 4.7 %collective-permute-start.15 = (f32[20,128]{1,0:T(8,128)S(1)}, f32[20,128]{1,0:T(8,128)S(1)}, u32[]{:S(2)}, u32[]{:S(2)}) collective-permute-start(f32[20,128]{1,0:T(8,128)S(1)} %maximum_select_fusion.2), channel_id=1, source_target_pairs={{0,4},{2,6},{4,0},{6,2},{1,5},{3,7},{5,1},{7,3},{8,12},{10,14},{12... | collective-permute-start | bytes 30728 | tf_op jit(solution)/shard_map/ppermute | solution.py:452
  163.6 1.4 collective-permute-start.16
  169.6 0.8 copy-start.6

commit v10 on v9

--- a/solution.py
+++ b/solution.py
@@ -214,20 +214,35 @@
     )(at.reshape(1), whole, *orders)
 
 
-def cut_middle_kernel(start, whole, out, sem):
-    copy = pltpu.make_async_copy(whole.at[:, pl.ds(start, out.shape[1])], out, sem)
-    copy.start()
-    copy.wait()
+def cut_middle_kernel(start, whole, out, held, reads, writes):
+    layers = out.shape[1]
+    ins, outs = [], []
+    for i in range(layers):
+        piece = held.at[:, pl.ds(i, 1)]
+        ins.append(pltpu.make_async_copy(whole.at[:, pl.ds(start + i, 1)], piece, reads.at[i]))
+        outs.append(pltpu.make_async_copy(piece, out.at[:, pl.ds(i, 1)], writes.at[i]))
+    for copy in ins:
+        copy.start()
+    for i in range(layers):
+        ins[i].wait()
+        outs[i].start()
+    for copy in outs:
+        copy.wait()
 
 
 def cut_middle(whole, count):
     rows, layers, cells_y, cells_z = whole.shape
+    shape = (rows, count, cells_y, cells_z)
     return pl.pallas_call(
         functools.partial(cut_middle_kernel, (layers - count) // 2),
         in_specs=[pl.BlockSpec(memory_space=pl.ANY)],
         out_specs=pl.BlockSpec(memory_space=pl.ANY),
-        scratch_shapes=[pltpu.SemaphoreType.DMA],
-        out_shape=jax.ShapeDtypeStruct((rows, count, cells_y, cells_z), whole.dtype),
+        scratch_shapes=[
+            pltpu.VMEM(shape, whole.dtype),
+            pltpu.SemaphoreType.DMA((count,)),
+            pltpu.SemaphoreType.DMA((count,)),
+        ],
+        out_shape=jax.ShapeDtypeStruct(shape, whole.dtype),
         compiler_params=pltpu.CompilerParams(vmem_limit_bytes=VMEM_BYTES),
         cost_estimate=SMALL,
         name="cut_middle",

time: 189 us -> 189 us (level)
  no operation moved by 1% of the time
where the time goes in v10:
time: 189 us; the launch traced here: 187 us
  Pallas kernels  114 us (60%)
  waiting for transfers between devices  40 us (21%)
  starting transfers between devices  24.7 us (13%)
  local copies, waits for them, and re-layouts  5.52 us (3%)
    pallas_call x1, Pallas kernels, stiff_terms(): pl.pallas_call(stiff_kernel, grid=(layers,), in_specs=[pl.BlockSpec(block...  40.1 us
    pallas_call x8, Pallas kernels, expand(): pl.pallas_call(vector_kernel, grid_spec=pltpu.PrefetchScalarGridSpec(num_...  34.9 us
    pallas_call x6, Pallas kernels, cross_terms(): pl.pallas_call(cross_kernel, grid_spec=pltpu.PrefetchScalarGridSpec(num_s...  18.9 us
    ppermute x9, waiting for transfers between devices, swap(): return lax.ppermute(x, 'blk', [(0, 1), (1, 0)])  17.1 us
    pallas_call x9, Pallas kernels, cut(): pl.pallas_call(cut_kernel, grid_spec=pltpu.PrefetchScalarGridSpec(num_sca...  15.3 us
    ppermute x9, starting transfers between devices, swap(): return lax.ppermute(x, 'blk', [(0, 1), (1, 0)])  11.6 us
    ppermute x1, waiting for transfers between devices, line_sum(): outer = lax.ppermute(x, axis, [(1, 0), (2, 3)])  7.73 us
    ppermute x3, waiting for transfers between devices, joined(): lax.ppermute(part, axis, [(i, i ^ step) for i in range(lax.axis_size(axis...  5.66 us
  transfers between devices with their start and end apart: 20, of which 13 were waited for; matrix products, arithmetic and copies ran while one was open for 2% of the time, Pallas kernels for 60%

profile of v10, /device:TPU:0, one launch (start us, length us, event | category | flops | bytes accessed | tf_op | source)
XLA Modules:
  0.0 186.8 jit_solution(3270702515687557001)
XLA Ops:
  2.0 3.0 %collective-permute-start.2 = (bf16[64,4,16,128]{3,2,1,0:T(8,128)(2,1)S(1)}, bf16[64,4,16,128]{3,2,1,0:T(8,128)(2,1)S(1)}, u32[]{:S(2)}, u32[]{:S(2)}) collective-permute-start(bf16[64,4,16,128]{3,2,1,0:T(8,128)(2,1)S(1)} %cut_middle.1.rest_0_), channel_id=1, source_target_pairs={{0,1},{1,0},{2,3},{3,2},{4,5},{5,4},{6,7},{7,6},{8,9},{9,8},{10,11... | collective-permute-start | bytes 3145736 | tf_op jit(solution)/shard_map/ppermute | solution.py:449
  6.1 3.5 %collective-permute-start = (bf16[64,1,16,128]{3,2,1,0:T(8,128)(2,1)S(1)}, bf16[64,1,16,128]{3,2,1,0:T(8,128)(2,1)S(1)}, u32[]{:S(2)}, u32[]{:S(2)}) collective-permute-start(bf16[64,1,16,128]{3,2,1,0:T(8,128)(2,1)S(1)} %get-tuple-element.42), channel_id=1, source_target_pairs={{0,2},{2,4},{4,6},{1,3},{3,5},{5,7},{8,10},{10,12},{12,14},{9,11},... | collective-permute-start | bytes 786440 | tf_op jit(solution)/shard_map/ppermute | solution.py:519
  16.9 1.9 %cut.11 = bf16[64,3,16,128]{3,2,1,0:T(8,128)(2,1)} custom-call(s32[1]{0:T(128)} %bitcast.21.at, bf16[64,32,16,128]{3,2,1,0:T(8,128)(2,1)} %bitcast.54, bf16[64,4,16,128]{3,2,1,0:T(8,128)(2,1)S(1)} %cut_middle.1.rest_0_), custom_call_target="tpu_custom_call" | custom-call | flops 1024 | bytes 1024 | tf_op jit(solution)/shard_map/cut/pallas_call | solution.py:197
  24.8 4.1 %collective-permute-done.2.order.other = bf16[64,4,16,128]{3,2,1,0:T(8,128)(2,1)S(1)} collective-permute-done((bf16[64,4,16,128]{3,2,1,0:T(8,128)(2,1)S(1)}, bf16[64,4,16,128]{3,2,1,0:T(8,128)(2,1)S(1)}, u32[]{:S(2)}, u32[]{:S(2)}) %collective-permute-start.2) | collective-permute-done | bytes 1048608 | tf_op jit(solution)/shard_map/ppermute | solution.py:449
  29.0 2.1 %collective-permute-start.7 = (bf16[64,2,16,128]{3,2,1,0:T(8,128)(2,1)}, bf16[64,2,16,128]{3,2,1,0:T(8,128)(2,1)}, u32[]{:S(2)}, u32[]{:S(2)}) collective-permute-start(bf16[64,2,16,128]{3,2,1,0:T(8,128)(2,1)} %cut.13), channel_id=1, source_target_pairs={{0,1},{1,0},{2,3},{3,2},{4,5},{5,4},{6,7},{7,6},{8,9},{9,8},{10,11... | collective-permute-start | bytes 1572872 | tf_op jit(solution)/shard_map/ppermute | solution.py:449
  31.7 2.8 %cut.17 = bf16[64,11,16,128]{3,2,1,0:T(8,128)(2,1)} custom-call(s32[1]{0:T(128)} %bitcast.33.at, bf16[64,32,16,128]{3,2,1,0:T(8,128)(2,1)} %bitcast.57, bf16[64,4,16,128]{3,2,1,0:T(8,128)(2,1)S(1)} %cut_middle.1.rest_0_), custom_call_target="tpu_custom_call" | custom-call | flops 1024 | bytes 1024 | tf_op jit(solution)/shard_map/cut/pallas_call | solution.py:197
  37.5 40.1 %stiff_terms.1 = (bf16[32,512,256]{2,1,0:T(8,128)(2,1)}, f32[64,64]{1,0:T(8,128)S(1)}, f32[16,64]{1,0:T(8,128)S(1)}) custom-call(bf16[64,32,16,128]{3,2,1,0:T(8,128)(2,1)} %bitcast.58, bf16[64,32,16,128]{3,2,1,0:T(8,128)(2,1)} %bitcast.59, bf16[64,32,16,128]{3,2,1,0:T(8,128)(2,1)} %bitcast.60, bf16[64,1,16,128]{3,2,1,0:T(8,128)(2,1)S(1)} %copy-done.3, ...), custom_call_target="tpu_custom_call" | custom-call | flops 1024 | bytes 1024 | tf_op jit(solution)/shard_map/stiff_terms/pallas_call | solution.py:100
  77.6 4.2 %expand.8 = (bf16[64,32,16,128]{3,2,1,0:T(8,128)(2,1)}, f32[8,128]{1,0:T(8,128)S(1)}) custom-call(s32[1]{0:T(128)} %constant.95.clone.1.at, bf16[512,1024]{1,0:T(8,128)(2,1)S(1)} %spread_blocks.1.spread, bf16[64,32,16,128]{3,2,1,0:T(8,128)(2,1)} %bitcast.61, bf16[64,4,16,128]{3,2,1,0:T(8,128)(2,1)S(1)} %collective-permute-done.2.order.other, ...), custom_call_target="tpu_custom_call" | custom-call | flops 1024 | bytes 1024 | tf_op jit(solution)/shard_map/expand/pallas_call | solution.py:359
  81.8 3.8 %expand.9 = (bf16[64,32,16,128]{3,2,1,0:T(8,128)(2,1)}, f32[8,128]{1,0:T(8,128)S(1)}) custom-call(s32[1]{0:T(128)} %bitcast.16.at, bf16[512,1024]{1,0:T(8,128)(2,1)S(1)} %spread_blocks.1.spread, bf16[64,32,16,128]{3,2,1,0:T(8,128)(2,1)} %bitcast.62, bf16[64,3,16,128]{3,2,1,0:T(8,128)(2,1)} %collective-permute-done.3.other, ...), custom_call_target="tpu_custom_call", output_to_operand_aliasing={{0}: (4, {})} | custom-call | flops 1024 | bytes 1024 | tf_op jit(solution)/shard_map/expand/pallas_call | solution.py:359
  85.6 3.8 %expand.10 = (bf16[64,32,16,128]{3,2,1,0:T(8,128)(2,1)}, f32[8,128]{1,0:T(8,128)S(1)}) custom-call(s32[1]{0:T(128)} %bitcast.18.at, bf16[512,1024]{1,0:T(8,128)(2,1)S(1)} %spread_blocks.1.spread, bf16[64,32,16,128]{3,2,1,0:T(8,128)(2,1)} %bitcast.63, bf16[64,3,16,128]{3,2,1,0:T(8,128)(2,1)} %collective-permute-done.4.other, ...), custom_call_target="tpu_custom_call", output_to_operand_aliasing={{0}: (4, {})} | custom-call | flops 1024 | bytes 1024 | tf_op jit(solution)/shard_map/expand/pallas_call | solution.py:359
  89.4 3.8 %expand.11 = (bf16[64,32,16,128]{3,2,1,0:T(8,128)(2,1)}, f32[8,128]{1,0:T(8,128)S(1)}) custom-call(s32[1]{0:T(128)} %bitcast.20.at, bf16[512,1024]{1,0:T(8,128)(2,1)S(1)} %spread_blocks.1.spread, bf16[64,32,16,128]{3,2,1,0:T(8,128)(2,1)} %bitcast.64, bf16[64,3,16,128]{3,2,1,0:T(8,128)(2,1)} %collective-permute-done.5.other, ...), custom_call_target="tpu_custom_call", output_to_operand_aliasing={{0}: (4, {})} | custom-call | flops 1024 | bytes 1024 | tf_op jit(solution)/shard_map/expand/pallas_call | solution.py:359
  93.2 3.3 %collective-permute-done.6.other = bf16[64,3,16,128]{3,2,1,0:T(8,128)(2,1)} collective-permute-done((bf16[64,3,16,128]{3,2,1,0:T(8,128)(2,1)}, bf16[64,3,16,128]{3,2,1,0:T(8,128)(2,1)}, u32[]{:S(2)}, u32[]{:S(2)}) %collective-permute-start.6) | collective-permute-done | bytes 786464 | tf_op jit(solution)/shard_map/ppermute | solution.py:449
  96.5 3.8 %expand.12 = (bf16[64,32,16,128]{3,2,1,0:T(8,128)(2,1)}, f32[8,128]{1,0:T(8,128)S(1)}) custom-call(s32[1]{0:T(128)} %bitcast.22.at, bf16[512,1024]{1,0:T(8,128)(2,1)S(1)} %spread_blocks.1.spread, bf16[64,32,16,128]{3,2,1,0:T(8,128)(2,1)} %bitcast.65, bf16[64,3,16,128]{3,2,1,0:T(8,128)(2,1)} %collective-permute-done.6.other, ...), custom_call_target="tpu_custom_call", output_to_operand_aliasing={{0}: (4, {})} | custom-call | flops 1024 | bytes 1024 | tf_op jit(solution)/shard_map/expand/pallas_call | solution.py:359
  100.3 3.5 %cross_terms.10 = f32[64,64]{1,0:T(8,128)S(1)} custom-call(s32[1]{0:T(128)} %bitcast.22.at, s32[1]{0:T(128)} %constant.100.clone.1.skip, bf16[32,512,256]{2,1,0:T(8,128)(2,1)} %get-tuple-element.23.stiff, bf16[64,3,16,128]{3,2,1,0:T(8,128)(2,1)} %collective-permute-done.6.other, f32[8,128]{1,0:T(8,128)S(1)} %get-tuple-element.33.order), custom_call_target="tpu_custom_call" | custom-call | flops 1024 | bytes 1024 | tf_op jit(solution)/shard_map/cross_terms/pallas_call | solution.py:151
  103.8 3.9 %collective-permute-done.7.other = bf16[64,2,16,128]{3,2,1,0:T(8,128)(2,1)} collective-permute-done((bf16[64,2,16,128]{3,2,1,0:T(8,128)(2,1)}, bf16[64,2,16,128]{3,2,1,0:T(8,128)(2,1)}, u32[]{:S(2)}, u32[]{:S(2)}) %collective-permute-start.7) | collective-permute-done | bytes 524320 | tf_op jit(solution)/shard_map/ppermute | solution.py:449
  107.7 2.7 %expand.13 = (bf16[64,32,16,128]{3,2,1,0:T(8,128)(2,1)}, f32[8,128]{1,0:T(8,128)S(1)}) custom-call(s32[1]{0:T(128)} %bitcast.24.at, bf16[512,1024]{1,0:T(8,128)(2,1)S(1)} %spread_blocks.1.spread, bf16[64,32,16,128]{3,2,1,0:T(8,128)(2,1)} %bitcast.66, bf16[64,2,16,128]{3,2,1,0:T(8,128)(2,1)} %collective-permute-done.7.other, ...), custom_call_target="tpu_custom_call", output_to_operand_aliasing={{0}: (4, {})} | custom-call | flops 1024 | bytes 1024 | tf_op jit(solution)/shard_map/expand/pallas_call | solution.py:359
  110.4 2.5 %cross_terms.11 = f32[64,64]{1,0:T(8,128)S(1)} custom-call(s32[1]{0:T(128)} %bitcast.24.at, s32[1]{0:T(128)} %constant.100.clone.1.skip, bf16[32,512,256]{2,1,0:T(8,128)(2,1)} %get-tuple-element.23.stiff, bf16[64,2,16,128]{3,2,1,0:T(8,128)(2,1)} %collective-permute-done.7.other, f32[8,128]{1,0:T(8,128)S(1)} %get-tuple-element.35.order), custom_call_target="tpu_custom_call" | custom-call | flops 1024 | bytes 1024 | tf_op jit(solution)/shard_map/cross_terms/pallas_call | solution.py:151
  112.8 3.5 %cross_terms.9 = f32[64,64]{1,0:T(8,128)S(1)} custom-call(s32[1]{0:T(128)} %bitcast.20.at, s32[1]{0:T(128)} %constant.100.clone.1.skip, bf16[32,512,256]{2,1,0:T(8,128)(2,1)} %get-tuple-element.23.stiff, bf16[64,3,16,128]{3,2,1,0:T(8,128)(2,1)} %collective-permute-done.5.other, f32[8,128]{1,0:T(8,128)S(1)} %get-tuple-element.31.order), custom_call_target="tpu_custom_call" | custom-call | flops 1024 | bytes 1024 | tf_op jit(solution)/shard_map/cross_terms/pallas_call | solution.py:151
  116.4 3.5 %cross_terms.8 = f32[64,64]{1,0:T(8,128)S(1)} custom-call(s32[1]{0:T(128)} %bitcast.18.at, s32[1]{0:T(128)} %constant.100.clone.1.skip, bf16[32,512,256]{2,1,0:T(8,128)(2,1)} %get-tuple-element.23.stiff, bf16[64,3,16,128]{3,2,1,0:T(8,128)(2,1)} %collective-permute-done.4.other, f32[8,128]{1,0:T(8,128)S(1)} %get-tuple-element.29.order), custom_call_target="tpu_custom_call" | custom-call | flops 1024 | bytes 1024 | tf_op jit(solution)/shard_map/cross_terms/pallas_call | solution.py:151
  119.9 3.5 %cross_terms.7 = f32[64,64]{1,0:T(8,128)S(1)} custom-call(s32[1]{0:T(128)} %bitcast.16.at, s32[1]{0:T(128)} %constant.100.clone.1.skip, bf16[32,512,256]{2,1,0:T(8,128)(2,1)} %get-tuple-element.23.stiff, bf16[64,3,16,128]{3,2,1,0:T(8,128)(2,1)} %collective-permute-done.3.other, f32[8,128]{1,0:T(8,128)S(1)} %get-tuple-element.27.order), custom_call_target="tpu_custom_call" | custom-call | flops 1024 | bytes 1024 | tf_op jit(solution)/shard_map/cross_terms/pallas_call | solution.py:151
  123.4 2.4 %cross_terms.6 = f32[64,64]{1,0:T(8,128)S(1)} custom-call(s32[1]{0:T(128)} %bitcast.11.at, s32[1]{0:T(128)} %bitcast.12.skip, bf16[32,512,256]{2,1,0:T(8,128)(2,1)} %get-tuple-element.23.stiff, bf16[64,4,16,128]{3,2,1,0:T(8,128)(2,1)S(1)} %collective-permute-done.2.order.other, f32[8,128]{1,0:T(8,128)S(1)} %get-tuple-element.25.order), custom_call_target="tpu_custom_call" | custom-call | flops 1024 | bytes 1024 | tf_op jit(solution)/shard_map/cross_terms/pallas_call | solution.py:151
  126.4 2.1 %collective-permute-start.8 = (f32[80,128]{1,0:T(8,128)S(1)}, f32[80,128]{1,0:T(8,128)S(1)}, u32[]{:S(2)}, u32[]{:S(2)}) collective-permute-start(f32[80,128]{1,0:T(8,128)S(1)} %maximum_maximum_fusion), channel_id=1, source_target_pairs={{0,2},{2,0},{4,6},{6,4},{1,3},{3,1},{5,7},{7,5},{8,10},{10,8},{12,... | collective-permute-start | bytes 122888 | tf_op jit(solution)/shard_map/ppermute | solution.py:483
  128.5 2.0 %collective-permute-done.8 = f32[80,128]{1,0:T(8,128)S(1)} collective-permute-done((f32[80,128]{1,0:T(8,128)S(1)}, f32[80,128]{1,0:T(8,128)S(1)}, u32[]{:S(2)}, u32[]{:S(2)}) %collective-permute-start.8) | collective-permute-done | bytes 40992 | tf_op jit(solution)/shard_map/ppermute | solution.py:483
  134.0 7.7 %collective-permute-done.10 = f32[80,128]{1,0:T(8,128)S(1)} collective-permute-done((f32[80,128]{1,0:T(8,128)S(1)}, f32[80,128]{1,0:T(8,128)S(1)}, u32[]{:S(2)}, u32[]{:S(2)}) %collective-permute-start.10) | collective-permute-done | bytes 40992 | tf_op jit(solution)/shard_map/ppermute | solution.py:485
  144.7 3.0 %collective-permute-done.12 = f32[2,80,128]{2,1,0:T(8,128)S(1)} collective-permute-done((f32[2,80,128]{2,1,0:T(8,128)S(1)}, f32[2,80,128]{2,1,0:T(8,128)S(1)}, u32[]{:S(2)}, u32[]{:S(2)}) %collective-permute-start.12) | collective-permute-done | bytes 81952 | tf_op jit(solution)/shard_map/ppermute | solution.py:475
  152.1 3.2 %collective-permute-done.13 = f32[10,128]{1,0:T(8,128)S(1)} collective-permute-done((f32[10,128]{1,0:T(8,128)S(1)}, f32[10,128]{1,0:T(8,128)S(1)}, u32[]{:S(2)}, u32[]{:S(2)}) %collective-permute-start.13) | collective-permute-done | bytes 5152 | tf_op jit(solution)/shard_map/ppermute | solution.py:458
  156.9 2.1 %collective-permute-done.14 = f32[10,128]{1,0:T(8,128)S(1)} collective-permute-done((f32[10,128]{1,0:T(8,128)S(1)}, f32[10,128]{1,0:T(8,128)S(1)}, u32[]{:S(2)}, u32[]{:S(2)}) %collective-permute-start.14) | collective-permute-done | bytes 5152 | tf_op jit(solution)/shard_map/ppermute | solution.py:467
  160.1 3.6 %collective-permute-done.15 = f32[20,128]{1,0:T(8,128)S(1)} collective-permute-done((f32[20,128]{1,0:T(8,128)S(1)}, f32[20,128]{1,0:T(8,128)S(1)}, u32[]{:S(2)}, u32[]{:S(2)}) %collective-permute-start.15) | collective-permute-done | bytes 10272 | tf_op jit(solution)/shard_map/ppermute | solution.py:467
  166.2 3.5 %collective-permute-done.19.other = bf16[64,11,16,128]{3,2,1,0:T(8,128)(2,1)} collective-permute-done((bf16[64,11,16,128]{3,2,1,0:T(8,128)(2,1)}, bf16[64,11,16,128]{3,2,1,0:T(8,128)(2,1)}, u32[]{:S(2)}, u32[]{:S(2)}) %collective-permute-start.19) | collective-permute-done | bytes 2883616 | tf_op jit(solution)/shard_map/ppermute | solution.py:449
  170.5 10.3 %expand.14 = (bf16[64,32,16,128]{3,2,1,0:T(8,128)(2,1)}, f32[8,128]{1,0:T(8,128)}) custom-call(s32[1]{0:T(128)} %bitcast.32.at, bf16[512,1024]{1,0:T(8,128)(2,1)S(1)} %spread_blocks.1.spread, bf16[64,32,16,128]{3,2,1,0:T(8,128)(2,1)} %bitcast.70, bf16[64,11,16,128]{3,2,1,0:T(8,128)(2,1)} %collective-permute-done.19.other, ...), custom_call_target="tpu_custom_call", output_to_operand_aliasing={{0}: (4, {})} | custom-call | flops 1024 | bytes 1024 | tf_op jit(solution)/shard_map/expand/pallas_call | solution.py:359
  180.8 2.6 %expand.15 = (bf16[64,32,16,128]{3,2,1,0:T(8,128)(2,1)}, f32[8,128]{1,0:T(8,128)}) custom-call(s32[1]{0:T(128)} %bitcast.30.at, bf16[512,1024]{1,0:T(8,128)(2,1)S(1)} %spread_blocks.1.spread, bf16[64,32,16,128]{3,2,1,0:T(8,128)(2,1)} %bitcast.71, bf16[64,2,16,128]{3,2,1,0:T(8,128)(2,1)S(1)} %collective-permute-done.18.other, ...), custom_call_target="tpu_custom_call", output_to_operand_aliasing={{0}: (4, {})} | custom-call | flops 1024 | bytes 1024 | tf_op jit(solution)/shard_map/expand/pallas_call | solution.py:359
  183.4 2.2 %collective-permute-done.17.other = bf16[64,1,16,128]{3,2,1,0:T(8,128)(2,1)S(1)} collective-permute-done((bf16[64,1,16,128]{3,2,1,0:T(8,128)(2,1)S(1)}, bf16[64,1,16,128]{3,2,1,0:T(8,128)(2,1)S(1)}, u32[]{:S(2)}, u32[]{:S(2)}) %collective-permute-start.17) | collective-permute-done | bytes 262176 | tf_op jit(solution)/shard_map/ppermute | solution.py:449
  (77 shorter events, 37.4 us)
Async XLA Ops:
  2.0 27.0 %collective-permute-start.2 = (bf16[64,4,16,128]{3,2,1,0:T(8,128)(2,1)S(1)}, bf16[64,4,16,128]{3,2,1,0:T(8,128)(2,1)S(1)}, u32[]{:S(2)}, u32[]{:S(2)}) collective-permute-start(bf16[64,4,16,128]{3,2,1,0:T(8,128)(2,1)S(1)} %cut_middle.1.rest_0_), channel_id=1, source_target_pairs={{0,1},{1,0},{2,3},{3,2},{4,5},{5,4},{6,7},{7,6},{8,9},{9,8},{10,11... | collective-permute-start | bytes 3145736 | tf_op jit(solution)/shard_map/ppermute | solution.py:449
  6.1 12.7 %collective-permute-start = (bf16[64,1,16,128]{3,2,1,0:T(8,128)(2,1)S(1)}, bf16[64,1,16,128]{3,2,1,0:T(8,128)(2,1)S(1)}, u32[]{:S(2)}, u32[]{:S(2)}) collective-permute-start(bf16[64,1,16,128]{3,2,1,0:T(8,128)(2,1)S(1)} %get-tuple-element.42), channel_id=1, source_target_pairs={{0,2},{2,4},{4,6},{1,3},{3,5},{5,7},{8,10},{10,12},{12,14},{9,11},... | collective-permute-start | bytes 786440 | tf_op jit(solution)/shard_map/ppermute | solution.py:519
  9.6 11.8 %collective-permute-start.1 = (bf16[64,1,16,128]{3,2,1,0:T(8,128)(2,1)S(1)}, bf16[64,1,16,128]{3,2,1,0:T(8,128)(2,1)S(1)}, u32[]{:S(2)}, u32[]{:S(2)}) collective-permute-start(bf16[64,1,16,128]{3,2,1,0:T(8,128)(2,1)S(1)} %get-tuple-element.41), channel_id=1, source_target_pairs={{2,0},{4,2},{6,4},{3,1},{5,3},{7,5},{10,8},{12,10},{14,12},{11,9},... | collective-permute-start | bytes 786440 | tf_op jit(solution)/shard_map/ppermute | solution.py:520
  12.8 69.0 %collective-permute-start.3 = (bf16[64,3,16,128]{3,2,1,0:T(8,128)(2,1)}, bf16[64,3,16,128]{3,2,1,0:T(8,128)(2,1)}, u32[]{:S(2)}, u32[]{:S(2)}) collective-permute-start(bf16[64,3,16,128]{3,2,1,0:T(8,128)(2,1)} %cut.9), channel_id=1, source_target_pairs={{0,1},{1,0},{2,3},{3,2},{4,5},{5,4},{6,7},{7,6},{8,9},{9,8},{10,11... | collective-permute-start | bytes 2359304 | tf_op jit(solution)/shard_map/ppermute | solution.py:449
  15.3 70.3 %collective-permute-start.4 = (bf16[64,3,16,128]{3,2,1,0:T(8,128)(2,1)}, bf16[64,3,16,128]{3,2,1,0:T(8,128)(2,1)}, u32[]{:S(2)}, u32[]{:S(2)}) collective-permute-start(bf16[64,3,16,128]{3,2,1,0:T(8,128)(2,1)} %cut.10), channel_id=1, source_target_pairs={{0,1},{1,0},{2,3},{3,2},{4,5},{5,4},{6,7},{7,6},{8,9},{9,8},{10,11... | collective-permute-start | bytes 2359304 | tf_op jit(solution)/shard_map/ppermute | solution.py:449
  18.8 5.9 %copy-start.2 = (bf16[64,1,16,128]{3,2,1,0:T(8,128)(2,1)}, bf16[64,1,16,128]{3,2,1,0:T(8,128)(2,1)S(1)}, u32[]{:S(2)}) copy-start(bf16[64,1,16,128]{3,2,1,0:T(8,128)(2,1)S(1)} %collective-permute-done.low) | copy-start | bytes 786436
  18.8 70.6 %collective-permute-start.5 = (bf16[64,3,16,128]{3,2,1,0:T(8,128)(2,1)}, bf16[64,3,16,128]{3,2,1,0:T(8,128)(2,1)}, u32[]{:S(2)}, u32[]{:S(2)}) collective-permute-start(bf16[64,3,16,128]{3,2,1,0:T(8,128)(2,1)} %cut.11), channel_id=1, source_target_pairs={{0,1},{1,0},{2,3},{3,2},{4,5},{5,4},{6,7},{7,6},{8,9},{9,8},{10,11... | collective-permute-start | bytes 2359304 | tf_op jit(solution)/shard_map/ppermute | solution.py:449
  19.4 5.4 %copy-start.7 = (bf16[1,128,64]{1,2,0:T(8,128)(2,1)S(1)}, bf16[1,128,64]{1,2,0:T(8,128)(2,1)}, u32[]{:S(2)}) copy-start(bf16[1,128,64]{1,2,0:T(8,128)(2,1)} %param.8) | copy-start | bytes 49156
  21.3 9.7 %copy-start.4 = (bf16[64,1,16,128]{3,2,1,0:T(8,128)(2,1)}, bf16[64,1,16,128]{3,2,1,0:T(8,128)(2,1)S(1)}, u32[]{:S(2)}) copy-start(bf16[64,1,16,128]{3,2,1,0:T(8,128)(2,1)S(1)} %collective-permute-done.1.high) | copy-start | bytes 786436
  21.3 75.1 %collective-permute-start.6 = (bf16[64,3,16,128]{3,2,1,0:T(8,128)(2,1)}, bf16[64,3,16,128]{3,2,1,0:T(8,128)(2,1)}, u32[]{:S(2)}, u32[]{:S(2)}) collective-permute-start(bf16[64,3,16,128]{3,2,1,0:T(8,128)(2,1)} %cut.12), channel_id=1, source_target_pairs={{0,1},{1,0},{2,3},{3,2},{4,5},{5,4},{6,7},{7,6},{8,9},{9,8},{10,11... | collective-permute-start | bytes 2359304 | tf_op jit(solution)/shard_map/ppermute | solution.py:449
  24.7 9.9 %copy-start = (f32[1,32,16,128]{3,2,1,0:T(8,128)S(1)}, f32[1,32,16,128]{3,2,1,0:T(8,128)}, u32[]{:S(2)}) copy-start(f32[1,32,16,128]{3,2,1,0:T(8,128)} %param.6) | copy-start | bytes 786436
  29.0 78.8 %collective-permute-start.7 = (bf16[64,2,16,128]{3,2,1,0:T(8,128)(2,1)}, bf16[64,2,16,128]{3,2,1,0:T(8,128)(2,1)}, u32[]{:S(2)}, u32[]{:S(2)}) collective-permute-start(bf16[64,2,16,128]{3,2,1,0:T(8,128)(2,1)} %cut.13), channel_id=1, source_target_pairs={{0,1},{1,0},{2,3},{3,2},{4,5},{5,4},{6,7},{7,6},{8,9},{9,8},{10,11... | collective-permute-start | bytes 1572872 | tf_op jit(solution)/shard_map/ppermute | solution.py:449
  34.6 1.0 copy-start.1
  35.6 0.9 copy-start.3
  36.5 0.9 copy-start.5
  81.8 87.9 %collective-permute-start.19 = (bf16[64,11,16,128]{3,2,1,0:T(8,128)(2,1)}, bf16[64,11,16,128]{3,2,1,0:T(8,128)(2,1)}, u32[]{:S(2)}, u32[]{:S(2)}) collective-permute-start(bf16[64,11,16,128]{3,2,1,0:T(8,128)(2,1)} %cut.17), channel_id=1, source_target_pairs={{0,1},{1,0},{2,3},{3,2},{4,5},{5,4},{6,7},{7,6},{8,9},{9,8},{10,11... | collective-permute-start | bytes 8650760 | tf_op jit(solution)/shard_map/ppermute | solution.py:449
  119.9 11.4 %copy-start.8 = (s32[4]{0:T(128)S(1)}, s32[4]{0:T(128)}, u32[]{:S(2)}) copy-start(s32[4]{0:T(128)} %param.9) | copy-start | bytes 52
  126.4 4.1 %collective-permute-start.8 = (f32[80,128]{1,0:T(8,128)S(1)}, f32[80,128]{1,0:T(8,128)S(1)}, u32[]{:S(2)}, u32[]{:S(2)}) collective-permute-start(f32[80,128]{1,0:T(8,128)S(1)} %maximum_maximum_fusion), channel_id=1, source_target_pairs={{0,2},{2,0},{4,6},{6,4},{1,3},{3,1},{5,7},{7,5},{8,10},{10,8},{12,... | collective-permute-start | bytes 122888 | tf_op jit(solution)/shard_map/ppermute | solution.py:483
  130.6 1.3 collective-permute-start.9
  131.9 9.9 %collective-permute-start.10 = (f32[80,128]{1,0:T(8,128)S(1)}, f32[80,128]{1,0:T(8,128)S(1)}, u32[]{:S(2)}, u32[]{:S(2)}) collective-permute-start(f32[80,128]{1,0:T(8,128)S(1)} %add.81), channel_id=1, source_target_pairs={{2,0},{4,6},{3,1},{5,7},{10,8},{12,14},{11,9},{13,15},{18,16},{20,... | collective-permute-start | bytes 122888 | tf_op jit(solution)/shard_map/ppermute | solution.py:485
  141.8 1.3 collective-permute-start.11
  143.2 4.5 %collective-permute-start.12 = (f32[2,80,128]{2,1,0:T(8,128)S(1)}, f32[2,80,128]{2,1,0:T(8,128)S(1)}, u32[]{:S(2)}, u32[]{:S(2)}) collective-permute-start(f32[2,80,128]{2,1,0:T(8,128)S(1)} %fusion.6), channel_id=1, source_target_pairs={{0,16},{8,24},{16,0},{24,8},{1,17},{9,25},{17,1},{25,9},{2,18},{10... | collective-permute-start | bytes 245768 | tf_op jit(solution)/shard_map/ppermute | solution.py:475
  148.9 31.9 %collective-permute-start.18 = (bf16[64,2,16,128]{3,2,1,0:T(8,128)(2,1)S(1)}, bf16[64,2,16,128]{3,2,1,0:T(8,128)(2,1)S(1)}, u32[]{:S(2)}, u32[]{:S(2)}) collective-permute-start(bf16[64,2,16,128]{3,2,1,0:T(8,128)(2,1)S(1)} %cut.16), channel_id=1, source_target_pairs={{0,1},{1,0},{2,3},{3,2},{4,5},{5,4},{6,7},{7,6},{8,9},{9,8},{10,11... | collective-permute-start | bytes 1572872 | tf_op jit(solution)/shard_map/ppermute | solution.py:449
  150.7 4.7 %collective-permute-start.13 = (f32[10,128]{1,0:T(8,128)S(1)}, f32[10,128]{1,0:T(8,128)S(1)}, u32[]{:S(2)}, u32[]{:S(2)}) collective-permute-start(f32[10,128]{1,0:T(8,128)S(1)} %fusion.5), channel_id=1, source_target_pairs={{0,17},{1,16},{8,25},{9,24},{16,1},{17,0},{24,9},{25,8},{2,19},{3,... | collective-permute-start | bytes 15368 | tf_op jit(solution)/shard_map/ppermute | solution.py:458
  155.3 3.7 %collective-permute-start.14 = (f32[10,128]{1,0:T(8,128)S(1)}, f32[10,128]{1,0:T(8,128)S(1)}, u32[]{:S(2)}, u32[]{:S(2)}) collective-permute-start(f32[10,128]{1,0:T(8,128)S(1)} %collective-permute-done.13), channel_id=1, source_target_pairs={{0,2},{2,0},{4,6},{6,4},{1,3},{3,1},{5,7},{7,5},{8,10},{10,8},{12,... | collective-permute-start | bytes 15368 | tf_op jit(solution)/shard_map/ppermute | solution.py:467
  156.3 29.3 %collective-permute-start.17 = (bf16[64,1,16,128]{3,2,1,0:T(8,128)(2,1)S(1)}, bf16[64,1,16,128]{3,2,1,0:T(8,128)(2,1)S(1)}, u32[]{:S(2)}, u32[]{:S(2)}) collective-permute-start(bf16[64,1,16,128]{3,2,1,0:T(8,128)(2,1)S(1)} %cut.15), channel_id=1, source_target_pairs={{0,1},{1,0},{2,3},{3,2},{4,5},{5,4},{6,7},{7,6},{8,9},{9,8},{10,11... | collective-permute-start | bytes 786440 | tf_op jit(solution)/shard_map/ppermute | solution.py:449
  159.0 4.7 %collective-permute-start.15 = (f32[20,128]{1,0:T(8,128)S(1)}, f32[20,128]{1,0:T(8,128)S(1)}, u32[]{:S(2)}, u32[]{:S(2)}) collective-permute-start(f32[20,128]{1,0:T(8,128)S(1)} %maximum_select_fusion.2), channel_id=1, source_target_pairs={{0,4},{2,6},{4,0},{6,2},{1,5},{3,7},{5,1},{7,3},{8,12},{10,14},{12... | collective-permute-start | bytes 30728 | tf_op jit(solution)/shard_map/ppermute | solution.py:467
  163.7 1.4 collective-permute-start.16
  169.7 0.8 copy-start.6

commit v11 on v10

--- a/solution.py
+++ b/solution.py
@@ -9,7 +9,7 @@
 SUB = 8
 VMEM_BYTES = 48 * 1024 * 1024
 LAST_BYTES = 16 * 1024 * 1024
-PARTS = 5
+PARTS = 4
 SMALL = pl.CostEstimate(flops=1024, bytes_accessed=1024, transcendentals=0)
 
 

time: 189 us -> 189 us (level)
  Pallas kernels: 114 us -> 108 us
  waiting for transfers between devices: 40 us -> 45 us
  local copies, waits for them, and re-layouts: 5.52 us -> 7.56 us
    pallas_call x9 -> x8, Pallas kernels: 15.3 us -> 12.9 us  [cut(): pl.pallas_call(cut_kernel, grid_spec=pltpu.PrefetchScalarGridSpec(num_sca...]
    ppermute x9 -> x8, waiting for transfers between devices: 17.1 us -> 19.3 us  [swap(): return lax.ppermute(x, 'blk', [(0, 1), (1, 0)])]
    pallas_call x6 -> x5, Pallas kernels: 18.9 us -> 17.2 us  [cross_terms(): pl.pallas_call(cross_kernel, grid_spec=pltpu.PrefetchScalarGridSpec(num_s...]
    ppermute x9 -> x8, starting transfers between devices: 11.6 us -> 9.94 us  [swap(): return lax.ppermute(x, 'blk', [(0, 1), (1, 0)])]
    pallas_call x8 -> x7, Pallas kernels: 34.9 us -> 33.5 us  [expand(): pl.pallas_call(vector_kernel, grid_spec=pltpu.PrefetchScalarGridSpec(num_...]
    unnamed x18 -> x16, local copies, waits for them, and re-layouts: 3.63 us -> 4.97 us
  transfers between devices with their start and end apart: 20 -> 19, of which waited for: 13 -> 14; matrix products, arithmetic and copies ran while one was open for 2% -> 2% of each run, Pallas kernels for 60% -> 57%
where the time goes in v11:
time: 189 us; the launch traced here: 187 us
  Pallas kernels  108 us (57%)
  waiting for transfers between devices  45 us (24%)
  starting transfers between devices  23.1 us (12%)
  local copies, waits for them, and re-layouts  7.56 us (4%)
    pallas_call x1, Pallas kernels, stiff_terms(): pl.pallas_call(stiff_kernel, grid=(layers,), in_specs=[pl.BlockSpec(block...  40.4 us
    pallas_call x7, Pallas kernels, expand(): pl.pallas_call(vector_kernel, grid_spec=pltpu.PrefetchScalarGridSpec(num_...  33.5 us
    ppermute x8, waiting for transfers between devices, swap(): return lax.ppermute(x, 'blk', [(0, 1), (1, 0)])  19.3 us
    pallas_call x5, Pallas kernels, cross_terms(): pl.pallas_call(cross_kernel, grid_spec=pltpu.PrefetchScalarGridSpec(num_s...  17.2 us
    pallas_call x8, Pallas kernels, cut(): pl.pallas_call(cut_kernel, grid_spec=pltpu.PrefetchScalarGridSpec(num_sca...  12.9 us
    ppermute x8, starting transfers between devices, swap(): return lax.ppermute(x, 'blk', [(0, 1), (1, 0)])  9.94 us
    ppermute x1, waiting for transfers between devices, line_sum(): outer = lax.ppermute(x, axis, [(1, 0), (2, 3)])  7.73 us
    ppermute x3, waiting for transfers between devices, joined(): lax.ppermute(part, axis, [(i, i ^ step) for i in range(lax.axis_size(axis...  5.66 us
  transfers between devices with their start and end apart: 19, of which 14 were waited for; matrix products, arithmetic and copies ran while one was open for 2% of the time, Pallas kernels for 57%

profile of v11, /device:TPU:0, one launch (start us, length us, event | category | flops | bytes accessed | tf_op | source)
XLA Modules:
  0.0 186.8 jit_solution(13786305811002668808)
XLA Ops:
  2.0 3.0 %collective-permute-start.2 = (bf16[64,4,16,128]{3,2,1,0:T(8,128)(2,1)S(1)}, bf16[64,4,16,128]{3,2,1,0:T(8,128)(2,1)S(1)}, u32[]{:S(2)}, u32[]{:S(2)}) collective-permute-start(bf16[64,4,16,128]{3,2,1,0:T(8,128)(2,1)S(1)} %cut_middle.1.rest_0_), channel_id=1, source_target_pairs={{0,1},{1,0},{2,3},{3,2},{4,5},{5,4},{6,7},{7,6},{8,9},{9,8},{10,11... | collective-permute-start | bytes 3145736 | tf_op jit(solution)/shard_map/ppermute | solution.py:449
  5.0 2.0 %cut.8 = bf16[64,4,16,128]{3,2,1,0:T(8,128)(2,1)} custom-call(s32[1]{0:T(128)} %bitcast.17.at, bf16[64,32,16,128]{3,2,1,0:T(8,128)(2,1)} %bitcast.49, bf16[64,4,16,128]{3,2,1,0:T(8,128)(2,1)S(1)} %cut_middle.1.rest_0_), custom_call_target="tpu_custom_call" | custom-call | flops 1024 | bytes 1024 | tf_op jit(solution)/shard_map/cut/pallas_call | solution.py:197
  7.1 2.0 %cut.9 = bf16[64,4,16,128]{3,2,1,0:T(8,128)(2,1)} custom-call(s32[1]{0:T(128)} %bitcast.19.at, bf16[64,32,16,128]{3,2,1,0:T(8,128)(2,1)} %bitcast.50, bf16[64,4,16,128]{3,2,1,0:T(8,128)(2,1)S(1)} %cut_middle.1.rest_0_), custom_call_target="tpu_custom_call" | custom-call | flops 1024 | bytes 1024 | tf_op jit(solution)/shard_map/cut/pallas_call | solution.py:197
  9.2 2.1 %collective-permute-start.4 = (bf16[64,4,16,128]{3,2,1,0:T(8,128)(2,1)}, bf16[64,4,16,128]{3,2,1,0:T(8,128)(2,1)}, u32[]{:S(2)}, u32[]{:S(2)}) collective-permute-start(bf16[64,4,16,128]{3,2,1,0:T(8,128)(2,1)} %cut.9), channel_id=1, source_target_pairs={{0,1},{1,0},{2,3},{3,2},{4,5},{5,4},{6,7},{7,6},{8,9},{9,8},{10,11... | collective-permute-start | bytes 3145736 | tf_op jit(solution)/shard_map/ppermute | solution.py:449
  13.0 3.5 %collective-permute-start = (bf16[64,1,16,128]{3,2,1,0:T(8,128)(2,1)S(1)}, bf16[64,1,16,128]{3,2,1,0:T(8,128)(2,1)S(1)}, u32[]{:S(2)}, u32[]{:S(2)}) collective-permute-start(bf16[64,1,16,128]{3,2,1,0:T(8,128)(2,1)S(1)} %get-tuple-element.38), channel_id=1, source_target_pairs={{0,2},{2,4},{4,6},{1,3},{3,5},{5,7},{8,10},{10,12},{12,14},{9,11},... | collective-permute-start | bytes 786440 | tf_op jit(solution)/shard_map/ppermute | solution.py:519
  17.8 1.9 %cut.10 = bf16[64,3,16,128]{3,2,1,0:T(8,128)(2,1)} custom-call(s32[1]{0:T(128)} %bitcast.21.at, bf16[64,32,16,128]{3,2,1,0:T(8,128)(2,1)} %bitcast.52, bf16[64,4,16,128]{3,2,1,0:T(8,128)(2,1)S(1)} %cut_middle.1.rest_0_), custom_call_target="tpu_custom_call" | custom-call | flops 1024 | bytes 1024 | tf_op jit(solution)/shard_map/cut/pallas_call | solution.py:197
  22.4 1.9 %cut.11 = bf16[64,3,16,128]{3,2,1,0:T(8,128)(2,1)} custom-call(s32[1]{0:T(128)} %bitcast.23.at, bf16[64,32,16,128]{3,2,1,0:T(8,128)(2,1)} %bitcast.53, bf16[64,4,16,128]{3,2,1,0:T(8,128)(2,1)S(1)} %cut_middle.1.rest_0_), custom_call_target="tpu_custom_call" | custom-call | flops 1024 | bytes 1024 | tf_op jit(solution)/shard_map/cut/pallas_call | solution.py:197
  26.9 1.9 %cut.15 = bf16[64,11,16,128]{3,2,1,0:T(8,128)(2,1)S(1)} custom-call(s32[1]{0:T(128)} %bitcast.31.at, bf16[64,32,16,128]{3,2,1,0:T(8,128)(2,1)} %bitcast.54, bf16[64,4,16,128]{3,2,1,0:T(8,128)(2,1)S(1)} %cut_middle.1.rest_0_), custom_call_target="tpu_custom_call" | custom-call | flops 1024 | bytes 1024 | tf_op jit(solution)/shard_map/cut/pallas_call | solution.py:197
  33.9 40.4 %stiff_terms.1 = (bf16[32,512,256]{2,1,0:T(8,128)(2,1)}, f32[64,64]{1,0:T(8,128)S(1)}, f32[16,64]{1,0:T(8,128)S(1)}) custom-call(bf16[64,32,16,128]{3,2,1,0:T(8,128)(2,1)} %bitcast.55, bf16[64,32,16,128]{3,2,1,0:T(8,128)(2,1)} %bitcast.56, bf16[64,32,16,128]{3,2,1,0:T(8,128)(2,1)} %bitcast.57, bf16[64,1,16,128]{3,2,1,0:T(8,128)(2,1)S(1)} %copy-done.4, ...), custom_call_target="tpu_custom_call" | custom-call | flops 1024 | bytes 1024 | tf_op jit(solution)/shard_map/stiff_terms/pallas_call | solution.py:100
  74.4 4.2 %expand.7 = (bf16[64,32,16,128]{3,2,1,0:T(8,128)(2,1)}, f32[8,128]{1,0:T(8,128)S(1)}) custom-call(s32[1]{0:T(128)} %constant.91.clone.1.at, bf16[512,1024]{1,0:T(8,128)(2,1)S(1)} %spread_blocks.1.spread, bf16[64,32,16,128]{3,2,1,0:T(8,128)(2,1)} %bitcast.58, bf16[64,4,16,128]{3,2,1,0:T(8,128)(2,1)S(1)} %collective-permute-done.2.order.other, ...), custom_call_target="tpu_custom_call" | custom-call | flops 1024 | bytes 1024 | tf_op jit(solution)/shard_map/expand/pallas_call | solution.py:359
  78.6 4.4 %expand.8 = (bf16[64,32,16,128]{3,2,1,0:T(8,128)(2,1)}, f32[8,128]{1,0:T(8,128)S(1)}) custom-call(s32[1]{0:T(128)} %bitcast.16.at, bf16[512,1024]{1,0:T(8,128)(2,1)S(1)} %spread_blocks.1.spread, bf16[64,32,16,128]{3,2,1,0:T(8,128)(2,1)} %bitcast.59, bf16[64,4,16,128]{3,2,1,0:T(8,128)(2,1)} %collective-permute-done.3.other, ...), custom_call_target="tpu_custom_call", output_to_operand_aliasing={{0}: (4, {})} | custom-call | flops 1024 | bytes 1024 | tf_op jit(solution)/shard_map/expand/pallas_call | solution.py:359
  83.0 4.4 %expand.9 = (bf16[64,32,16,128]{3,2,1,0:T(8,128)(2,1)}, f32[8,128]{1,0:T(8,128)S(1)}) custom-call(s32[1]{0:T(128)} %bitcast.18.at, bf16[512,1024]{1,0:T(8,128)(2,1)S(1)} %spread_blocks.1.spread, bf16[64,32,16,128]{3,2,1,0:T(8,128)(2,1)} %bitcast.60, bf16[64,4,16,128]{3,2,1,0:T(8,128)(2,1)} %collective-permute-done.4.other, ...), custom_call_target="tpu_custom_call", output_to_operand_aliasing={{0}: (4, {})} | custom-call | flops 1024 | bytes 1024 | tf_op jit(solution)/shard_map/expand/pallas_call | solution.py:359
  87.4 3.4 %collective-permute-done.5.other = bf16[64,3,16,128]{3,2,1,0:T(8,128)(2,1)} collective-permute-done((bf16[64,3,16,128]{3,2,1,0:T(8,128)(2,1)}, bf16[64,3,16,128]{3,2,1,0:T(8,128)(2,1)}, u32[]{:S(2)}, u32[]{:S(2)}) %collective-permute-start.5) | collective-permute-done | bytes 786464 | tf_op jit(solution)/shard_map/ppermute | solution.py:449
  90.9 3.8 %expand.10 = (bf16[64,32,16,128]{3,2,1,0:T(8,128)(2,1)}, f32[8,128]{1,0:T(8,128)S(1)}) custom-call(s32[1]{0:T(128)} %bitcast.20.at, bf16[512,1024]{1,0:T(8,128)(2,1)S(1)} %spread_blocks.1.spread, bf16[64,32,16,128]{3,2,1,0:T(8,128)(2,1)} %bitcast.61, bf16[64,3,16,128]{3,2,1,0:T(8,128)(2,1)} %collective-permute-done.5.other, ...), custom_call_target="tpu_custom_call", output_to_operand_aliasing={{0}: (4, {})} | custom-call | flops 1024 | bytes 1024 | tf_op jit(solution)/shard_map/expand/pallas_call | solution.py:359
  94.7 3.5 %cross_terms.8 = f32[64,64]{1,0:T(8,128)S(1)} custom-call(s32[1]{0:T(128)} %bitcast.20.at, s32[1]{0:T(128)} %constant.96.clone.1.skip, bf16[32,512,256]{2,1,0:T(8,128)(2,1)} %get-tuple-element.21.stiff, bf16[64,3,16,128]{3,2,1,0:T(8,128)(2,1)} %collective-permute-done.5.other, f32[8,128]{1,0:T(8,128)S(1)} %get-tuple-element.29.order), custom_call_target="tpu_custom_call" | custom-call | flops 1024 | bytes 1024 | tf_op jit(solution)/shard_map/cross_terms/pallas_call | solution.py:151
  98.2 9.5 %collective-permute-done.6.other = bf16[64,3,16,128]{3,2,1,0:T(8,128)(2,1)} collective-permute-done((bf16[64,3,16,128]{3,2,1,0:T(8,128)(2,1)}, bf16[64,3,16,128]{3,2,1,0:T(8,128)(2,1)}, u32[]{:S(2)}, u32[]{:S(2)}) %collective-permute-start.6) | collective-permute-done | bytes 786464 | tf_op jit(solution)/shard_map/ppermute | solution.py:449
  107.7 3.8 %expand.11 = (bf16[64,32,16,128]{3,2,1,0:T(8,128)(2,1)}, f32[8,128]{1,0:T(8,128)S(1)}) custom-call(s32[1]{0:T(128)} %bitcast.22.at, bf16[512,1024]{1,0:T(8,128)(2,1)S(1)} %spread_blocks.1.spread, bf16[64,32,16,128]{3,2,1,0:T(8,128)(2,1)} %bitcast.62, bf16[64,3,16,128]{3,2,1,0:T(8,128)(2,1)} %collective-permute-done.6.other, ...), custom_call_target="tpu_custom_call", output_to_operand_aliasing={{0}: (4, {})} | custom-call | flops 1024 | bytes 1024 | tf_op jit(solution)/shard_map/expand/pallas_call | solution.py:359
  111.5 3.5 %cross_terms.9 = f32[64,64]{1,0:T(8,128)S(1)} custom-call(s32[1]{0:T(128)} %bitcast.22.at, s32[1]{0:T(128)} %constant.96.clone.1.skip, bf16[32,512,256]{2,1,0:T(8,128)(2,1)} %get-tuple-element.21.stiff, bf16[64,3,16,128]{3,2,1,0:T(8,128)(2,1)} %collective-permute-done.6.other, f32[8,128]{1,0:T(8,128)S(1)} %get-tuple-element.31.order), custom_call_target="tpu_custom_call" | custom-call | flops 1024 | bytes 1024 | tf_op jit(solution)/shard_map/cross_terms/pallas_call | solution.py:151
  115.0 3.9 %cross_terms.7 = f32[64,64]{1,0:T(8,128)S(1)} custom-call(s32[1]{0:T(128)} %bitcast.18.at, s32[1]{0:T(128)} %constant.96.clone.1.skip, bf16[32,512,256]{2,1,0:T(8,128)(2,1)} %get-tuple-element.21.stiff, bf16[64,4,16,128]{3,2,1,0:T(8,128)(2,1)} %collective-permute-done.4.other, f32[8,128]{1,0:T(8,128)S(1)} %get-tuple-element.27.order), custom_call_target="tpu_custom_call" | custom-call | flops 1024 | bytes 1024 | tf_op jit(solution)/shard_map/cross_terms/pallas_call | solution.py:151
  118.9 3.9 %cross_terms.6 = f32[64,64]{1,0:T(8,128)S(1)} custom-call(s32[1]{0:T(128)} %bitcast.16.at, s32[1]{0:T(128)} %constant.96.clone.1.skip, bf16[32,512,256]{2,1,0:T(8,128)(2,1)} %get-tuple-element.21.stiff, bf16[64,4,16,128]{3,2,1,0:T(8,128)(2,1)} %collective-permute-done.3.other, f32[8,128]{1,0:T(8,128)S(1)} %get-tuple-element.25.order), custom_call_target="tpu_custom_call" | custom-call | flops 1024 | bytes 1024 | tf_op jit(solution)/shard_map/cross_terms/pallas_call | solution.py:151
  122.9 2.4 %cross_terms.5 = f32[64,64]{1,0:T(8,128)S(1)} custom-call(s32[1]{0:T(128)} %bitcast.11.at, s32[1]{0:T(128)} %bitcast.12.skip, bf16[32,512,256]{2,1,0:T(8,128)(2,1)} %get-tuple-element.21.stiff, bf16[64,4,16,128]{3,2,1,0:T(8,128)(2,1)S(1)} %collective-permute-done.2.order.other, f32[8,128]{1,0:T(8,128)S(1)} %get-tuple-element.23.order), custom_call_target="tpu_custom_call" | custom-call | flops 1024 | bytes 1024 | tf_op jit(solution)/shard_map/cross_terms/pallas_call | solution.py:151
  125.8 2.1 %collective-permute-start.7 = (f32[80,128]{1,0:T(8,128)S(1)}, f32[80,128]{1,0:T(8,128)S(1)}, u32[]{:S(2)}, u32[]{:S(2)}) collective-permute-start(f32[80,128]{1,0:T(8,128)S(1)} %maximum_maximum_fusion), channel_id=1, source_target_pairs={{0,2},{2,0},{4,6},{6,4},{1,3},{3,1},{5,7},{7,5},{8,10},{10,8},{12,... | collective-permute-start | bytes 122888 | tf_op jit(solution)/shard_map/ppermute | solution.py:483
  128.0 2.0 %collective-permute-done.7 = f32[80,128]{1,0:T(8,128)S(1)} collective-permute-done((f32[80,128]{1,0:T(8,128)S(1)}, f32[80,128]{1,0:T(8,128)S(1)}, u32[]{:S(2)}, u32[]{:S(2)}) %collective-permute-start.7) | collective-permute-done | bytes 40992 | tf_op jit(solution)/shard_map/ppermute | solution.py:483
  133.4 7.7 %collective-permute-done.9 = f32[80,128]{1,0:T(8,128)S(1)} collective-permute-done((f32[80,128]{1,0:T(8,128)S(1)}, f32[80,128]{1,0:T(8,128)S(1)}, u32[]{:S(2)}, u32[]{:S(2)}) %collective-permute-start.9) | collective-permute-done | bytes 40992 | tf_op jit(solution)/shard_map/ppermute | solution.py:485
  144.1 3.0 %collective-permute-done.11 = f32[2,80,128]{2,1,0:T(8,128)S(1)} collective-permute-done((f32[2,80,128]{2,1,0:T(8,128)S(1)}, f32[2,80,128]{2,1,0:T(8,128)S(1)}, u32[]{:S(2)}, u32[]{:S(2)}) %collective-permute-start.11) | collective-permute-done | bytes 81952 | tf_op jit(solution)/shard_map/ppermute | solution.py:475
  151.5 3.2 %collective-permute-done.12 = f32[10,128]{1,0:T(8,128)S(1)} collective-permute-done((f32[10,128]{1,0:T(8,128)S(1)}, f32[10,128]{1,0:T(8,128)S(1)}, u32[]{:S(2)}, u32[]{:S(2)}) %collective-permute-start.12) | collective-permute-done | bytes 5152 | tf_op jit(solution)/shard_map/ppermute | solution.py:458
  156.3 2.1 %collective-permute-done.13 = f32[10,128]{1,0:T(8,128)S(1)} collective-permute-done((f32[10,128]{1,0:T(8,128)S(1)}, f32[10,128]{1,0:T(8,128)S(1)}, u32[]{:S(2)}, u32[]{:S(2)}) %collective-permute-start.13) | collective-permute-done | bytes 5152 | tf_op jit(solution)/shard_map/ppermute | solution.py:467
  159.5 3.6 %collective-permute-done.14 = f32[20,128]{1,0:T(8,128)S(1)} collective-permute-done((f32[20,128]{1,0:T(8,128)S(1)}, f32[20,128]{1,0:T(8,128)S(1)}, u32[]{:S(2)}, u32[]{:S(2)}) %collective-permute-start.14) | collective-permute-done | bytes 10272 | tf_op jit(solution)/shard_map/ppermute | solution.py:467
  165.6 4.1 %collective-permute-done.18.other = bf16[64,11,16,128]{3,2,1,0:T(8,128)(2,1)} collective-permute-done((bf16[64,11,16,128]{3,2,1,0:T(8,128)(2,1)}, bf16[64,11,16,128]{3,2,1,0:T(8,128)(2,1)}, u32[]{:S(2)}, u32[]{:S(2)}) %collective-permute-start.18) | collective-permute-done | bytes 2883616 | tf_op jit(solution)/shard_map/ppermute | solution.py:449
  170.5 10.3 %expand.12 = (bf16[64,32,16,128]{3,2,1,0:T(8,128)(2,1)}, f32[8,128]{1,0:T(8,128)}) custom-call(s32[1]{0:T(128)} %bitcast.30.at, bf16[512,1024]{1,0:T(8,128)(2,1)S(1)} %spread_blocks.1.spread, bf16[64,32,16,128]{3,2,1,0:T(8,128)(2,1)} %bitcast.66, bf16[64,11,16,128]{3,2,1,0:T(8,128)(2,1)} %collective-permute-done.18.other, ...), custom_call_target="tpu_custom_call", output_to_operand_aliasing={{0}: (4, {})} | custom-call | flops 1024 | bytes 1024 | tf_op jit(solution)/shard_map/expand/pallas_call | solution.py:359
  180.8 2.6 %expand.13 = (bf16[64,32,16,128]{3,2,1,0:T(8,128)(2,1)}, f32[8,128]{1,0:T(8,128)}) custom-call(s32[1]{0:T(128)} %bitcast.28.at, bf16[512,1024]{1,0:T(8,128)(2,1)S(1)} %spread_blocks.1.spread, bf16[64,32,16,128]{3,2,1,0:T(8,128)(2,1)} %bitcast.67, bf16[64,2,16,128]{3,2,1,0:T(8,128)(2,1)S(1)} %collective-permute-done.17.other, ...), custom_call_target="tpu_custom_call", output_to_operand_aliasing={{0}: (4, {})} | custom-call | flops 1024 | bytes 1024 | tf_op jit(solution)/shard_map/expand/pallas_call | solution.py:359
  183.4 2.2 %collective-permute-done.16.other = bf16[64,1,16,128]{3,2,1,0:T(8,128)(2,1)S(1)} collective-permute-done((bf16[64,1,16,128]{3,2,1,0:T(8,128)(2,1)S(1)}, bf16[64,1,16,128]{3,2,1,0:T(8,128)(2,1)S(1)}, u32[]{:S(2)}, u32[]{:S(2)}) %collective-permute-start.16) | collective-permute-done | bytes 262176 | tf_op jit(solution)/shard_map/ppermute | solution.py:449
  (70 shorter events, 33.1 us)
Async XLA Ops:
  2.0 28.5 %collective-permute-start.2 = (bf16[64,4,16,128]{3,2,1,0:T(8,128)(2,1)S(1)}, bf16[64,4,16,128]{3,2,1,0:T(8,128)(2,1)S(1)}, u32[]{:S(2)}, u32[]{:S(2)}) collective-permute-start(bf16[64,4,16,128]{3,2,1,0:T(8,128)(2,1)S(1)} %cut_middle.1.rest_0_), channel_id=1, source_target_pairs={{0,1},{1,0},{2,3},{3,2},{4,5},{5,4},{6,7},{7,6},{8,9},{9,8},{10,11... | collective-permute-start | bytes 3145736 | tf_op jit(solution)/shard_map/ppermute | solution.py:449
  7.0 71.6 %collective-permute-start.3 = (bf16[64,4,16,128]{3,2,1,0:T(8,128)(2,1)}, bf16[64,4,16,128]{3,2,1,0:T(8,128)(2,1)}, u32[]{:S(2)}, u32[]{:S(2)}) collective-permute-start(bf16[64,4,16,128]{3,2,1,0:T(8,128)(2,1)} %cut.8), channel_id=1, source_target_pairs={{0,1},{1,0},{2,3},{3,2},{4,5},{5,4},{6,7},{7,6},{8,9},{9,8},{10,11... | collective-permute-start | bytes 3145736 | tf_op jit(solution)/shard_map/ppermute | solution.py:449
  9.2 73.8 %collective-permute-start.4 = (bf16[64,4,16,128]{3,2,1,0:T(8,128)(2,1)}, bf16[64,4,16,128]{3,2,1,0:T(8,128)(2,1)}, u32[]{:S(2)}, u32[]{:S(2)}) collective-permute-start(bf16[64,4,16,128]{3,2,1,0:T(8,128)(2,1)} %cut.9), channel_id=1, source_target_pairs={{0,1},{1,0},{2,3},{3,2},{4,5},{5,4},{6,7},{7,6},{8,9},{9,8},{10,11... | collective-permute-start | bytes 3145736 | tf_op jit(solution)/shard_map/ppermute | solution.py:449
  13.0 8.2 %collective-permute-start = (bf16[64,1,16,128]{3,2,1,0:T(8,128)(2,1)S(1)}, bf16[64,1,16,128]{3,2,1,0:T(8,128)(2,1)S(1)}, u32[]{:S(2)}, u32[]{:S(2)}) collective-permute-start(bf16[64,1,16,128]{3,2,1,0:T(8,128)(2,1)S(1)} %get-tuple-element.38), channel_id=1, source_target_pairs={{0,2},{2,4},{4,6},{1,3},{3,5},{5,7},{8,10},{10,12},{12,14},{9,11},... | collective-permute-start | bytes 786440 | tf_op jit(solution)/shard_map/ppermute | solution.py:519
  16.5 9.1 %collective-permute-start.1 = (bf16[64,1,16,128]{3,2,1,0:T(8,128)(2,1)}, bf16[64,1,16,128]{3,2,1,0:T(8,128)(2,1)}, u32[]{:S(2)}, u32[]{:S(2)}) collective-permute-start(bf16[64,1,16,128]{3,2,1,0:T(8,128)(2,1)} %get-tuple-element.37), channel_id=1, source_target_pairs={{2,0},{4,2},{6,4},{3,1},{5,3},{7,5},{10,8},{12,10},{14,12},{11,9},... | collective-permute-start | bytes 786440 | tf_op jit(solution)/shard_map/ppermute | solution.py:520
  17.8 8.3 %copy-start.6 = (bf16[1,128,64]{1,2,0:T(8,128)(2,1)S(1)}, bf16[1,128,64]{1,2,0:T(8,128)(2,1)}, u32[]{:S(2)}) copy-start(bf16[1,128,64]{1,2,0:T(8,128)(2,1)} %param.8) | copy-start | bytes 49156
  21.2 0.7 copy-start.3
  21.9 69.0 %collective-permute-start.5 = (bf16[64,3,16,128]{3,2,1,0:T(8,128)(2,1)}, bf16[64,3,16,128]{3,2,1,0:T(8,128)(2,1)}, u32[]{:S(2)}, u32[]{:S(2)}) collective-permute-start(bf16[64,3,16,128]{3,2,1,0:T(8,128)(2,1)} %cut.10), channel_id=1, source_target_pairs={{0,1},{1,0},{2,3},{3,2},{4,5},{5,4},{6,7},{7,6},{8,9},{9,8},{10,11... | collective-permute-start | bytes 2359304 | tf_op jit(solution)/shard_map/ppermute | solution.py:449
  24.3 7.7 %copy-start.1 = (f32[1,32,16,128]{3,2,1,0:T(8,128)S(1)}, f32[1,32,16,128]{3,2,1,0:T(8,128)}, u32[]{:S(2)}) copy-start(f32[1,32,16,128]{3,2,1,0:T(8,128)} %param.6) | copy-start | bytes 786436
  25.6 82.1 %collective-permute-start.6 = (bf16[64,3,16,128]{3,2,1,0:T(8,128)(2,1)}, bf16[64,3,16,128]{3,2,1,0:T(8,128)(2,1)}, u32[]{:S(2)}, u32[]{:S(2)}) collective-permute-start(bf16[64,3,16,128]{3,2,1,0:T(8,128)(2,1)} %cut.11), channel_id=1, source_target_pairs={{0,1},{1,0},{2,3},{3,2},{4,5},{5,4},{6,7},{7,6},{8,9},{9,8},{10,11... | collective-permute-start | bytes 2359304 | tf_op jit(solution)/shard_map/ppermute | solution.py:449
  28.8 1.6 copy-start
  30.5 139.2 %collective-permute-start.18 = (bf16[64,11,16,128]{3,2,1,0:T(8,128)(2,1)}, bf16[64,11,16,128]{3,2,1,0:T(8,128)(2,1)}, u32[]{:S(2)}, u32[]{:S(2)}) collective-permute-start(bf16[64,11,16,128]{3,2,1,0:T(8,128)(2,1)} %copy-done), channel_id=1, source_target_pairs={{0,1},{1,0},{2,3},{3,2},{4,5},{5,4},{6,7},{7,6},{8,9},{9,8},{10,11... | collective-permute-start | bytes 8650760 | tf_op jit(solution)/shard_map/ppermute | solution.py:449
  32.0 1.0 copy-start.2
  33.0 0.9 copy-start.4
  118.9 11.8 %copy-start.7 = (s32[4]{0:T(128)S(1)}, s32[4]{0:T(128)}, u32[]{:S(2)}) copy-start(s32[4]{0:T(128)} %param.9) | copy-start | bytes 52
  125.8 4.1 %collective-permute-start.7 = (f32[80,128]{1,0:T(8,128)S(1)}, f32[80,128]{1,0:T(8,128)S(1)}, u32[]{:S(2)}, u32[]{:S(2)}) collective-permute-start(f32[80,128]{1,0:T(8,128)S(1)} %maximum_maximum_fusion), channel_id=1, source_target_pairs={{0,2},{2,0},{4,6},{6,4},{1,3},{3,1},{5,7},{7,5},{8,10},{10,8},{12,... | collective-permute-start | bytes 122888 | tf_op jit(solution)/shard_map/ppermute | solution.py:483
  130.0 1.3 collective-permute-start.8
  131.3 9.9 %collective-permute-start.9 = (f32[80,128]{1,0:T(8,128)S(1)}, f32[80,128]{1,0:T(8,128)S(1)}, u32[]{:S(2)}, u32[]{:S(2)}) collective-permute-start(f32[80,128]{1,0:T(8,128)S(1)} %add.77), channel_id=1, source_target_pairs={{2,0},{4,6},{3,1},{5,7},{10,8},{12,14},{11,9},{13,15},{18,16},{20,... | collective-permute-start | bytes 122888 | tf_op jit(solution)/shard_map/ppermute | solution.py:485
  141.3 1.3 collective-permute-start.10
  142.6 4.5 %collective-permute-start.11 = (f32[2,80,128]{2,1,0:T(8,128)S(1)}, f32[2,80,128]{2,1,0:T(8,128)S(1)}, u32[]{:S(2)}, u32[]{:S(2)}) collective-permute-start(f32[2,80,128]{2,1,0:T(8,128)S(1)} %fusion.6), channel_id=1, source_target_pairs={{0,16},{8,24},{16,0},{24,8},{1,17},{9,25},{17,1},{25,9},{2,18},{10... | collective-permute-start | bytes 245768 | tf_op jit(solution)/shard_map/ppermute | solution.py:475
  148.3 32.5 %collective-permute-start.17 = (bf16[64,2,16,128]{3,2,1,0:T(8,128)(2,1)S(1)}, bf16[64,2,16,128]{3,2,1,0:T(8,128)(2,1)S(1)}, u32[]{:S(2)}, u32[]{:S(2)}) collective-permute-start(bf16[64,2,16,128]{3,2,1,0:T(8,128)(2,1)S(1)} %cut.14), channel_id=1, source_target_pairs={{0,1},{1,0},{2,3},{3,2},{4,5},{5,4},{6,7},{7,6},{8,9},{9,8},{10,11... | collective-permute-start | bytes 1572872 | tf_op jit(solution)/shard_map/ppermute | solution.py:449
  150.1 4.7 %collective-permute-start.12 = (f32[10,128]{1,0:T(8,128)S(1)}, f32[10,128]{1,0:T(8,128)S(1)}, u32[]{:S(2)}, u32[]{:S(2)}) collective-permute-start(f32[10,128]{1,0:T(8,128)S(1)} %fusion.5), channel_id=1, source_target_pairs={{0,17},{1,16},{8,25},{9,24},{16,1},{17,0},{24,9},{25,8},{2,19},{3,... | collective-permute-start | bytes 15368 | tf_op jit(solution)/shard_map/ppermute | solution.py:458
  154.8 3.7 %collective-permute-start.13 = (f32[10,128]{1,0:T(8,128)S(1)}, f32[10,128]{1,0:T(8,128)S(1)}, u32[]{:S(2)}, u32[]{:S(2)}) collective-permute-start(f32[10,128]{1,0:T(8,128)S(1)} %collective-permute-done.12), channel_id=1, source_target_pairs={{0,2},{2,0},{4,6},{6,4},{1,3},{3,1},{5,7},{7,5},{8,10},{10,8},{12,... | collective-permute-start | bytes 15368 | tf_op jit(solution)/shard_map/ppermute | solution.py:467
  155.8 29.8 %collective-permute-start.16 = (bf16[64,1,16,128]{3,2,1,0:T(8,128)(2,1)S(1)}, bf16[64,1,16,128]{3,2,1,0:T(8,128)(2,1)S(1)}, u32[]{:S(2)}, u32[]{:S(2)}) collective-permute-start(bf16[64,1,16,128]{3,2,1,0:T(8,128)(2,1)S(1)} %cut.13), channel_id=1, source_target_pairs={{0,1},{1,0},{2,3},{3,2},{4,5},{5,4},{6,7},{7,6},{8,9},{9,8},{10,11... | collective-permute-start | bytes 786440 | tf_op jit(solution)/shard_map/ppermute | solution.py:449
  158.4 4.7 %collective-permute-start.14 = (f32[20,128]{1,0:T(8,128)S(1)}, f32[20,128]{1,0:T(8,128)S(1)}, u32[]{:S(2)}, u32[]{:S(2)}) collective-permute-start(f32[20,128]{1,0:T(8,128)S(1)} %maximum_select_fusion.2), channel_id=1, source_target_pairs={{0,4},{2,6},{4,0},{6,2},{1,5},{3,7},{5,1},{7,3},{8,12},{10,14},{12... | collective-permute-start | bytes 30728 | tf_op jit(solution)/shard_map/ppermute | solution.py:467
  163.1 1.4 collective-permute-start.15
  169.7 0.8 copy-start.5
